TPU v7x, 32 devices: a whole 2x2x4 slice. The times are simulated.
32 devices in a mesh: dp: 4 (over z), blk: 2 (over x), tensor: 4 (over y, core).
Axes of the slice: x: 2, y: 2, z: 4, core: 2. Of those that a mesh axis runs over, the one named last changes fastest.
Arguments:
- tokens: bfloat16 [4, 1024, 2048], P('dp', ('blk', 'tensor')), may hold values from -6 to 6
- doc_lengths: int32 [4, 3], P('dp'), may hold values from 1 to 768, as said below
- weight_qkv: bfloat16 [2048, 3, 2048], P(('dp', 'blk'), None, 'tensor'), may hold values from -0.125 to 0.125
- weight_out: bfloat16 [2048, 2048], P(('dp', 'blk'), 'tensor'), may hold values from -1 to 1
- weight_gate_up: bfloat16 [2048, 2, 8192], P(('dp', 'blk'), None, 'tensor'), may hold values from -0.125 to 0.125
- weight_down: bfloat16 [2048, 8192], P(('dp', 'blk'), 'tensor'), may hold values from -0.0625 to 0.0625
- norm_gains: float32 [2, 2048], P(None, ('dp', 'blk', 'tensor')), may hold values from 0.5 to 1.5
- cotangent: bfloat16 [4, 1024, 2048], P('dp', ('blk', 'tensor')), may hold values from -6 to 6
Outputs:
- block_output: bfloat16 [4, 1024, 2048], P('dp', ('blk', 'tensor'))
- input_grad: float32 [4, 1024, 2048], P('dp', ('blk', 'tensor'))
- grad_qkv: float32 [2048, 3, 2048], P(('dp', 'blk'), None, 'tensor')
- grad_out: float32 [2048, 2048], P(('dp', 'blk'), 'tensor')
- grad_gate_up: float32 [2048, 2, 8192], P(('dp', 'blk'), None, 'tensor')
- grad_down: float32 [2048, 8192], P(('dp', 'blk'), 'tensor')
- grad_gains: float32 [2, 2048], P(None, ('dp', 'blk', 'tensor'))
Inputs may be any that keep to these rules, and one draw needn't show every extreme that they name: `doc_lengths`: each row holds 3 documents of one position or more, laid from the row's start; the positions after them are padding. One document of each row, which one drawn, is 1024 - 2 * (128) positions long; the others have at most 128 each, so that the long one starts within the row's first 512 positions and ends within its last 512.
All inputs are finite; a program needn't handle non-finite values.
Results may differ from a plain program's by a relative error of at most 0.02.
Values may be sent and summed in bfloat16 or wider, within the bound.
No kernel may reach another device: no remote copies, remote signals or barrier semaphores. Data moves between devices by JAX's collectives and lax.ppermute only.
A program may use at most 192 MiB of HBM per device.

v0:
```python
import jax
import jax.numpy as jnp
from jax import lax
from jax.sharding import PartitionSpec as P

HEAD_DIM = 64


EPSILON = 1e-05
ROPE_BASE = 130000.0
NEGATIVE = -1e30


def layout(lengths, places):
    doc_ends = jnp.cumsum(lengths)
    passed = places[:, None] >= doc_ends[None, :]
    segment = jnp.sum(passed.astype(jnp.int32), axis=1)
    begins = jnp.sum(jnp.where(passed, lengths[None, :], 0), axis=1)
    return (segment, places - begins)


def rope_tables(within, half_width):
    steps_up = jnp.arange(half_width, dtype=jnp.float32)
    frequency = ROPE_BASE ** (-2.0 * steps_up / (2 * half_width))
    angles = within.astype(jnp.float32)[:, None] * frequency[None, :]
    return (jnp.cos(angles), jnp.sin(angles))


def rotate(vectors, cosine_table, sine_table):
    half_width = vectors.shape[-1] // 2
    first_half = vectors[..., :half_width]
    second_half = vectors[..., half_width:]
    cosine_part = cosine_table[:, None, :]
    sine_part = sine_table[:, None, :]
    return jnp.concatenate(
        [
            first_half * cosine_part - second_half * sine_part,
            second_half * cosine_part + first_half * sine_part,
        ],
        axis=-1,
    )


def rotate_back(vectors, cosine_table, sine_table):
    half_width = vectors.shape[-1] // 2
    first_half = vectors[..., :half_width]
    second_half = vectors[..., half_width:]
    cosine_part = cosine_table[:, None, :]
    sine_part = sine_table[:, None, :]
    return jnp.concatenate(
        [
            first_half * cosine_part + second_half * sine_part,
            second_half * cosine_part - first_half * sine_part,
        ],
        axis=-1,
    )


def rms_unit(values):
    factor = lax.rsqrt(jnp.mean(values * values, axis=-1, keepdims=True) + EPSILON)
    return (values * factor, factor)


def norm_back(grad_normed, unit_rows, factor, gain_row):
    scaled_grad = grad_normed * gain_row
    inner_mean = jnp.mean(scaled_grad * unit_rows, axis=-1, keepdims=True)
    return (
        factor * (scaled_grad - unit_rows * inner_mean),
        jnp.sum(grad_normed * unit_rows, axis=0),
    )


def split_product(weights, operand, formula):
    high_part = weights.astype(jnp.bfloat16)
    rest_part = (weights - high_part.astype(jnp.float32)).astype(jnp.bfloat16)
    leading = jnp.einsum(formula, high_part, operand, preferred_element_type=jnp.float32)
    return leading + jnp.einsum(formula, rest_part, operand, preferred_element_type=jnp.float32)


def keep_state(current):
    return current


def fold_blocks(step_fn, running, pieces):
    piece_rows = pieces[0].shape[0]
    count_blocks = piece_rows // 512
    stacked = tuple((member.reshape((count_blocks, 512) + member.shape[1:]) for member in pieces))

    def scan_step(current, element):
        return (step_fn(current, element[0], element[1] * 512), None)

    return lax.scan(scan_step, running, (stacked, jnp.arange(count_blocks, dtype=jnp.int32)))[0]


def spread_rows(rows_here):
    return lax.all_gather(rows_here, "tensor", axis=0, tiled=True)


def spread_grads(rows_here):
    return lax.all_gather(rows_here, "tensor", axis=0, tiled=True)


def collect_rows(partial_sum):
    return lax.psum_scatter(
        partial_sum.astype(jnp.bfloat16), "tensor", scatter_dimension=0, tiled=True
    ).astype(jnp.float32)


def collect_grads(partial_sum):
    return lax.psum_scatter(
        partial_sum.astype(jnp.bfloat16), "tensor", scatter_dimension=0, tiled=True
    ).astype(jnp.float32)


def body(
    tokens, doc_lengths, weight_qkv, weight_out, weight_gate_up, weight_down, norm_gains, cotangent
):
    local_rows = tokens.shape[1]
    block_rows = local_rows * lax.axis_size("tensor")
    feature_local = weight_qkv.shape[2]
    heads_local = feature_local // HEAD_DIM
    score_scale = HEAD_DIM ** (-0.5)
    lengths = doc_lengths[0]
    places = lax.axis_index("blk") * block_rows + jnp.arange(block_rows, dtype=jnp.int32)
    segment, within = layout(lengths, places)
    present = (segment < lengths.shape[0]).astype(jnp.float32)
    cosine_table, sine_table = rope_tables(within, HEAD_DIM // 2)
    last_place = places[block_rows - 1]
    first_segment = segment[0]
    shape_heads = (block_rows, heads_local, HEAD_DIM)
    full_qkv, full_out, full_gate_up, full_down = (
        lax.all_gather(weight_qkv, ("dp", "blk"), axis=0, tiled=True),
        lax.all_gather(weight_out, ("dp", "blk"), axis=0, tiled=True),
        lax.all_gather(weight_gate_up, ("dp", "blk"), axis=0, tiled=True),
        lax.all_gather(weight_down, ("dp", "blk"), axis=0, tiled=True),
    )
    gain_pair = lax.all_gather(norm_gains, ("dp", "blk", "tensor"), axis=1, tiled=True)
    inputs = tokens[0].astype(jnp.float32)
    unit_first, factor_first = rms_unit(inputs)
    normed_first = spread_rows((unit_first * gain_pair[0]).astype(jnp.bfloat16))
    projected = jnp.einsum(
        "td,dcf->tcf", normed_first, full_qkv, preferred_element_type=jnp.float32
    )
    queries = rotate(projected[:, 0].reshape(shape_heads), cosine_table, sine_table).astype(
        jnp.bfloat16
    )
    keys_flat = (
        rotate(projected[:, 1].reshape(shape_heads), cosine_table, sine_table)
        .astype(jnp.bfloat16)
        .reshape(block_rows, feature_local)
    )
    values_flat = projected[:, 2].astype(jnp.bfloat16)

    def key_layout(piece_rows, offset):
        key_places = offset + jnp.arange(piece_rows, dtype=jnp.int32)
        key_segment = layout(lengths, key_places)[0]
        allowed = (segment[:, None] == key_segment[None, :]) & (
            key_places[None, :] <= places[:, None]
        )
        reaches = (key_places[0] <= last_place) & (key_segment[piece_rows - 1] >= first_segment)
        return (allowed, reaches)

    def attend_piece(running, pieces, offset):
        piece_rows = pieces[0].shape[0]
        piece_keys = pieces[0].reshape(piece_rows, heads_local, HEAD_DIM)
        piece_values = pieces[1].reshape(piece_rows, heads_local, HEAD_DIM)
        allowed, reaches = key_layout(piece_rows, offset)

        def attend_update(current):
            highest, denominator, accumulated = current
            scores = (
                jnp.einsum("qhd,khd->hqk", queries, piece_keys, preferred_element_type=jnp.float32)
                * score_scale
            )
            masked = jnp.where(allowed[None], scores, NEGATIVE)
            new_highest = jnp.maximum(highest, jnp.max(masked, axis=-1))
            weights = jnp.where(allowed[None], jnp.exp(masked - new_highest[..., None]), 0.0)
            shrink = jnp.exp(highest - new_highest)
            denominator = denominator * shrink + jnp.sum(weights, axis=-1)
            accumulated = accumulated * shrink.T[:, :, None] + split_product(
                weights, piece_values, "hqk,khd->qhd"
            )
            return (new_highest, denominator, accumulated)

        return lax.cond(reaches, attend_update, keep_state, running)

    empty_state = (
        jnp.full((heads_local, block_rows), NEGATIVE, jnp.float32),
        jnp.zeros((heads_local, block_rows), jnp.float32),
        jnp.zeros(shape_heads, jnp.float32),
    )
    highest, denominator, accumulated = fold_blocks(
        attend_piece,
        empty_state,
        (
            lax.all_gather(keys_flat, "blk", axis=0, tiled=True),
            lax.all_gather(values_flat, "blk", axis=0, tiled=True),
        ),
    )
    attention_raw = accumulated / denominator.T[:, :, None]
    log_total = highest + jnp.log(denominator)
    attended = (
        (attention_raw * present[:, None, None])
        .reshape(block_rows, feature_local)
        .astype(jnp.bfloat16)
    )
    branch = collect_rows(
        lax.dot_general(
            attended, full_out, (((1,), (1,)), ((), ())), preferred_element_type=jnp.float32
        )
    )
    middle = inputs + branch
    unit_second, factor_second = rms_unit(middle)
    normed_second = spread_rows((unit_second * gain_pair[1]).astype(jnp.bfloat16))
    gate_up = jnp.einsum(
        "td,dcf->tcf", normed_second, full_gate_up, preferred_element_type=jnp.float32
    )
    gate_part = gate_up[:, 0]
    up_part = gate_up[:, 1]
    sigmoid_gate = jax.nn.sigmoid(gate_part)
    activated = gate_part * sigmoid_gate
    hidden = (activated * up_part).astype(jnp.bfloat16)
    feed_out = collect_rows(
        lax.dot_general(
            hidden, full_down, (((1,), (1,)), ((), ())), preferred_element_type=jnp.float32
        )
    )
    outcome = (middle + feed_out).astype(jnp.bfloat16)
    grad_output = cotangent[0].astype(jnp.float32)
    grad_feed = spread_grads(grad_output.astype(jnp.bfloat16))
    grad_down = lax.dot_general(
        grad_feed, hidden, (((0,), (0,)), ((), ())), preferred_element_type=jnp.float32
    )
    grad_hidden = jnp.dot(grad_feed, full_down, preferred_element_type=jnp.float32)
    silu_slope = sigmoid_gate * (1.0 + gate_part * (1.0 - sigmoid_gate))
    grad_gates = jnp.stack(
        [grad_hidden * up_part * silu_slope, grad_hidden * activated], axis=1
    ).astype(jnp.bfloat16)
    grad_gate_up = jnp.einsum(
        "td,tcf->dcf", normed_second, grad_gates, preferred_element_type=jnp.float32
    )
    grad_normed_second = collect_grads(
        jnp.einsum("tcf,dcf->td", grad_gates, full_gate_up, preferred_element_type=jnp.float32)
    )
    grad_middle_norm, gain_second = norm_back(
        grad_normed_second, unit_second, factor_second, gain_pair[1]
    )
    grad_middle = grad_output + grad_middle_norm
    grad_branch = spread_grads(grad_middle.astype(jnp.bfloat16))
    grad_out = lax.dot_general(
        grad_branch, attended, (((0,), (0,)), ((), ())), preferred_element_type=jnp.float32
    )
    grad_attended = jnp.dot(grad_branch, full_out, preferred_element_type=jnp.float32).astype(
        jnp.bfloat16
    )
    grad_heads = (grad_attended * present[:, None].astype(jnp.bfloat16)).reshape(shape_heads)
    row_inner = jnp.sum(grad_heads.astype(jnp.float32) * attention_raw, axis=-1)

    def back_piece(running, pieces, offset):
        piece_rows = pieces[0].shape[0]
        piece_keys = pieces[0].reshape(piece_rows, heads_local, HEAD_DIM)
        piece_values = pieces[1].reshape(piece_rows, heads_local, HEAD_DIM)
        allowed, reaches = key_layout(piece_rows, offset)

        def back_update(current):
            grad_queries, grad_table = current
            scores = (
                jnp.einsum("qhd,khd->hqk", queries, piece_keys, preferred_element_type=jnp.float32)
                * score_scale
            )
            masked = jnp.where(allowed[None], scores, NEGATIVE)
            weights = jnp.where(allowed[None], jnp.exp(masked - log_total[..., None]), 0.0)
            grad_weights = jnp.einsum(
                "qhd,khd->hqk", grad_heads, piece_values, preferred_element_type=jnp.float32
            )
            grad_scores = (weights * (grad_weights - row_inner.T[:, :, None])).astype(jnp.bfloat16)
            grad_queries = grad_queries + score_scale * jnp.einsum(
                "hqk,khd->qhd", grad_scores, piece_keys, preferred_element_type=jnp.float32
            )
            grad_keys = score_scale * jnp.einsum(
                "hqk,qhd->khd", grad_scores, queries, preferred_element_type=jnp.float32
            )
            grad_values = split_product(weights, grad_heads, "hqk,qhd->khd")
            key_terms = jnp.stack(
                [
                    grad_keys.reshape(piece_rows, feature_local),
                    grad_values.reshape(piece_rows, feature_local),
                ],
                axis=1,
            )
            grad_table = lax.dynamic_update_slice_in_dim(grad_table, key_terms, offset, 0)
            return (grad_queries, grad_table)

        return lax.cond(reaches, back_update, keep_state, running)

    empty_grads = (
        jnp.zeros(shape_heads, jnp.float32),
        jnp.zeros((block_rows * lax.axis_size("blk"), 2, feature_local), jnp.float32),
    )
    grad_queries, grad_table = fold_blocks(
        back_piece,
        empty_grads,
        (
            lax.all_gather(keys_flat, "blk", axis=0, tiled=True),
            lax.all_gather(values_flat, "blk", axis=0, tiled=True),
        ),
    )
    key_value_grads = lax.psum_scatter(
        grad_table.astype(jnp.bfloat16), "blk", scatter_dimension=0, tiled=True
    ).astype(jnp.float32)
    grad_keys_here = key_value_grads[:, 0].reshape(shape_heads)
    grad_projected = jnp.stack(
        [
            rotate_back(grad_queries, cosine_table, sine_table).reshape(block_rows, feature_local),
            rotate_back(grad_keys_here, cosine_table, sine_table).reshape(
                block_rows, feature_local
            ),
            key_value_grads[:, 1],
        ],
        axis=1,
    ).astype(jnp.bfloat16)
    grad_qkv = jnp.einsum(
        "td,tcf->dcf", normed_first, grad_projected, preferred_element_type=jnp.float32
    )
    grad_normed_first = collect_grads(
        jnp.einsum("tcf,dcf->td", grad_projected, full_qkv, preferred_element_type=jnp.float32)
    )
    grad_input_norm, gain_first = norm_back(
        grad_normed_first, unit_first, factor_first, gain_pair[0]
    )
    grad_input = grad_middle + grad_input_norm
    sum_qkv, sum_out, sum_gate_up, sum_down = (
        lax.psum_scatter(
            grad_qkv.astype(jnp.bfloat16), ("dp", "blk"), scatter_dimension=0, tiled=True
        ).astype(jnp.float32),
        lax.psum_scatter(
            grad_out.astype(jnp.bfloat16), ("dp", "blk"), scatter_dimension=0, tiled=True
        ).astype(jnp.float32),
        lax.psum_scatter(
            grad_gate_up.astype(jnp.bfloat16), ("dp", "blk"), scatter_dimension=0, tiled=True
        ).astype(jnp.float32),
        lax.psum_scatter(
            grad_down.astype(jnp.bfloat16), ("dp", "blk"), scatter_dimension=0, tiled=True
        ).astype(jnp.float32),
    )
    gain_sums = lax.psum_scatter(
        jnp.stack([gain_first, gain_second]),
        ("dp", "blk", "tensor"),
        scatter_dimension=1,
        tiled=True,
    )
    return (outcome[None], grad_input[None], sum_qkv, sum_out, sum_gate_up, sum_down, gain_sums)


def solution(mesh):
    return jax.shard_map(
        body,
        mesh=mesh,
        in_specs=(
            P("dp", ("blk", "tensor"), None),
            P("dp", None),
            P(("dp", "blk"), None, "tensor"),
            P(("dp", "blk"), "tensor"),
            P(("dp", "blk"), None, "tensor"),
            P(("dp", "blk"), "tensor"),
            P(None, ("dp", "blk", "tensor")),
            P("dp", ("blk", "tensor"), None),
        ),
        out_specs=(
            P("dp", ("blk", "tensor"), None),
            P("dp", ("blk", "tensor"), None),
            P(("dp", "blk"), None, "tensor"),
            P(("dp", "blk"), "tensor"),
            P(("dp", "blk"), None, "tensor"),
            P(("dp", "blk"), "tensor"),
            P(None, ("dp", "blk", "tensor")),
        ),
        check_vma=False,
    )
```

profile of v0, /device:TPU:0, one launch (start us, length us, event | category | flops | bytes accessed | tf_op | source)
XLA Modules:
  0.0 1765.0 jit_solution(11293509838964499129)
XLA Ops:
  7.2 43.5 %all-gather.2 = f32[32,64,2]{1,2,0:T(2,128)S(1)} all-gather(f32[1,64,2]{1,2,0:T(2,128)} %bitcast.254), channel_id=1, replica_groups=mesh['dp'=4,'blk'=2,'tensor'=4] {'dp','blk','tensor'}, dimensions={0}, use_global_device_ids=true | all-gather | bytes 16896 | tf_op jit(solution)/shard_map/all_gather | solution.py:137
  52.1 2.0 fusion.67
  54.2 2.3 copy.111
  57.2 15.8 all-gather.14.cloned.1.call-done
  73.0 102.6 %all-gather.16.cloned.1.call-done = bf16[2048,3,512]{0,2,1:T(8,128)(2,1)} async-done(((bf16[256,3,512]{0,2,1:T(8,128)(2,1)}), bf16[2048,3,512]{0,2,1:T(8,128)(2,1)}) %all-gather.16.cloned.1.call-update) | async-done | bytes 6291472 | tf_op jit(solution)/shard_map/all_gather | solution.py:132
  175.6 6.2 fusion.49
  183.8 2.1 slice.156
  188.2 15.3 all-gather.18.cloned.1.call-done
  203.4 1.5 copy.112
  206.2 20.5 %all-gather.30.cloned.1.call-done = bf16[1024,1,512]{0,2,1:T(8,128)(2,1)} async-done(((bf16[512,1,512]{0,2,1:T(8,128)(2,1)}), bf16[1024,1,512]{0,2,1:T(8,128)(2,1)}) %all-gather.30.cloned.1.call-update) | async-done | bytes 1048592 | tf_op jit(solution)/shard_map/all_gather | solution.py:197
  226.7 1.8 reshape.240
  229.9 20.5 %while.32 = (s32[]{:T(128)}, f32[8,512]{1,0:T(8,128)S(1)}, f32[8,512]{1,0:T(8,128)S(1)}, f32[512,8,64]{0,2,1:T(8,128)S(1)}, s32[2]{0:T(128)S(1)}, /*index=5*/s32...) while((s32[]{:T(128)}, f32[8,512]{1,0:T(8,128)S(1)}, ...), condition=%wide.region_11.12_spmd.clone, body=%wide.region_5.11_spmd.clone.sunk | while | flops 850937344 | bytes 43559304 | solution.py:92
  235.0 10.3 conditional.6
  236.6 1.5 fusion.4
  238.1 2.7 fusion.5
  240.8 2.4 fusion.17
  243.2 2.0 fusion.7
  250.6 27.5 %all-gather.20.cloned.1.call-done = bf16[2048,512]{1,0:T(8,128)(2,1)} async-done(((bf16[256,512]{1,0:T(8,128)(2,1)}), bf16[2048,512]{1,0:T(8,128)(2,1)}) %all-gather.20.cloned.1.call-update) | async-done | bytes 2097168 | tf_op jit(solution)/shard_map/all_gather | solution.py:133
  278.1 4.3 convolution_convert_fusion.4
  282.4 30.0 %reduce-scatter.13.cloned.1.call-done = bf16[128,2048]{1,0:T(8,128)(2,1)} async-done(((bf16[512,2048]{1,0:T(8,128)(2,1)}), bf16[128,2048]{1,0:T(8,128)(2,1)}) %reduce-scatter.13.cloned.1.call-update) | async-done | bytes 524304 | tf_op jit(solution)/shard_map/reduce_scatter | solution.py:104
  313.8 2.0 multiply_convert_fusion.3
  315.9 3.8 copy.115
  321.5 17.1 all-gather.22.cloned.1.call-done
  338.6 230.6 %all-gather.24.cloned.1.call-done = bf16[2048,2,2048]{2,0,1:T(8,128)(2,1)} async-done(((bf16[256,2,2048]{2,0,1:T(8,128)(2,1)}), bf16[2048,2,2048]{2,0,1:T(8,128)(2,1)}) %all-gather.24.cloned.1.call-update) | async-done | bytes 16777232 | tf_op jit(solution)/shard_map/all_gather | solution.py:134
  569.2 15.0 fusion.46
  584.1 7.5 all-gather.32.cloned.1.call-done
  591.6 127.2 %all-gather.26.cloned.1.call-done = bf16[2048,2048]{1,0:T(8,128)(2,1)} async-done(((bf16[256,2048]{1,0:T(8,128)(2,1)}), bf16[2048,2048]{1,0:T(8,128)(2,1)}) %all-gather.26.cloned.1.call-update) | async-done | bytes 8388624 | tf_op jit(solution)/shard_map/all_gather | solution.py:135
  718.8 13.6 fusion.51
  734.4 13.5 bitcast_convert_fusion.1
  748.1 29.5 %reduce-scatter.17.cloned.1.call-done = bf16[128,2048]{1,0:T(8,128)(2,1)} async-done(((bf16[512,2048]{1,0:T(8,128)(2,1)}), bf16[128,2048]{1,0:T(8,128)(2,1)}) %reduce-scatter.17.cloned.1.call-update) | async-done | bytes 524304 | tf_op jit(solution)/shard_map/reduce_scatter | solution.py:110
  777.6 1.6 fusion.66
  779.2 2.3 fusion.80
  781.6 22.7 %all-gather.28.cloned.1.call-done = bf16[512,2048]{1,0:T(8,128)(2,1)} async-done(((bf16[128,2048]{1,0:T(8,128)(2,1)}), bf16[512,2048]{1,0:T(8,128)(2,1)}) %all-gather.28.cloned.1.call-update) | async-done | bytes 2097168 | tf_op jit(solution)/shard_map/all_gather | solution.py:100
  804.3 3.6 multiply_reduce_fusion
  807.9 1.6 broadcast_in_dim.123
  810.6 36.4 %while.33 = (s32[]{:T(128)}, f32[512,8,64]{0,2,1:T(8,128)}, bf16[1024,2,512]{0,2,1:T(8,128)(2,1)}, s32[2]{0:T(128)S(1)}, s32[]{:T(128)}, /*index=5*/s32[1,3]{1,0...) while((s32[]{:T(128)}, f32[512,8,64]{0,2,1:T(8,128)}, ...), condition=%wide.region_22.23_spmd.clone, body=%wide.region_18.22_spmd.clone.sunk | while | flops 1638667776 | bytes 79227360 | solution.py:92
  815.6 26.2 %conditional.7 = ((f32[512,8,64]{0,2,1:T(8,128)}, bf16[1024,2,512]{0,2,1:T(8,128)(2,1)})) conditional(s32[]{:T(128)} %convert_element_type.353, (f32[512,8,64]{0,2,1:T(8,128)}, bf16[1024,2,512]{0,2,1:T(8,128)(2,1)}) %tuple.129, (s32[512]{0:T(512)S(1)}, s32[512]{0:T(512)S(1)}, s32[]{:T(128)}, s32[1,512]{1,0:T(1,128)S(1)}, s32[]{:T(128)}, ...), branch_computations={%region_20.20_spmd, %region_21.21_spmd} | conditional | flops 1638663168 | bytes 79216744 | solution.py:294
  817.2 2.7 fusion.30
  824.0 2.0 copy-done
  827.5 10.1 dynamic_update_slice.4
  837.6 4.3 fusion.39
  847.0 3.9 copy.118
  851.2 57.1 %reduce-scatter.19.cloned.1.call-done = bf16[512,2,512]{2,0,1:T(8,128)(2,1)} async-done(((bf16[1024,2,512]{2,0,1:T(8,128)(2,1)}), bf16[512,2,512]{2,0,1:T(8,128)(2,1)}) %reduce-scatter.19.cloned.1.call-update) | async-done | bytes 1048592 | tf_op jit(solution)/shard_map/reduce_scatter | solution.py:308
  908.3 2.2 slice_convert_fusion.1
  910.8 1.5 add_convert_fusion.2
  914.4 8.1 bitcast_convert_fusion
  922.6 2.6 convolution_convert_fusion.2
  925.4 10.2 convolution_convert_fusion.3
  935.7 18.5 %reduce-scatter.21.cloned.1.call-done = bf16[128,2048]{1,0:T(8,128)(2,1)} async-done(((bf16[512,2048]{1,0:T(8,128)(2,1)}), bf16[128,2048]{1,0:T(8,128)(2,1)}) %reduce-scatter.21.cloned.1.call-update) | async-done | bytes 524304 | tf_op jit(solution)/shard_map/reduce_scatter | solution.py:110
  954.2 1.5 fusion.69
  957.3 10.1 convert_bitcast_fusion
  968.8 7.0 convolution_convert_fusion.1
  976.2 15.1 convolution_convert_fusion
  991.3 34.3 %reduce-scatter.25.cloned.1.call-done = bf16[256,512]{1,0:T(8,128)(2,1)} async-done(((bf16[2048,512]{1,0:T(8,128)(2,1)}), bf16[256,512]{1,0:T(8,128)(2,1)}) %reduce-scatter.25.cloned.1.call-update) | async-done | bytes 262160 | tf_op jit(solution)/shard_map/reduce_scatter | solution.py:336
  1025.6 1.8 convert_element_type.218
  1027.4 31.5 %reduce-scatter.15.cloned.1.call-done = bf16[128,2048]{1,0:T(8,128)(2,1)} async-done(((bf16[512,2048]{1,0:T(8,128)(2,1)}), bf16[128,2048]{1,0:T(8,128)(2,1)}) %reduce-scatter.15.cloned.1.call-update) | async-done | bytes 524304 | tf_op jit(solution)/shard_map/reduce_scatter | solution.py:104
  1058.9 3.0 fusion.62
  1061.9 134.5 %reduce-scatter.31.cloned.1.call-done = f32[64,2]{1,0:T(8,128)} async-done(((f32[2048,2]{1,0:T(8,128)}), f32[64,2]{1,0:T(8,128)}) %reduce-scatter.31.cloned.1.call-update) | async-done | bytes 528
  1197.8 147.4 %reduce-scatter.29.cloned.1.call-done = bf16[256,2048]{0,1:T(8,128)(2,1)} async-done(((bf16[2048,2048]{0,1:T(8,128)(2,1)}), bf16[256,2048]{0,1:T(8,128)(2,1)}) %reduce-scatter.29.cloned.1.call-update) | async-done | bytes 1048592 | tf_op jit(solution)/shard_map/reduce_scatter | solution.py:342
  1345.2 2.6 copy.126
  1347.8 118.8 %reduce-scatter.23.cloned.1.call-done = bf16[256,3,512]{2,0,1:T(8,128)(2,1)} async-done(((bf16[2048,3,512]{2,0,1:T(8,128)(2,1)}), bf16[256,3,512]{2,0,1:T(8,128)(2,1)}) %reduce-scatter.23.cloned.1.call-update) | async-done | bytes 786448 | tf_op jit(solution)/shard_map/reduce_scatter | solution.py:333
  1466.6 2.5 convert_element_type.216
  1469.1 282.8 %reduce-scatter.27.cloned.1.call-done = bf16[256,2,2048]{2,0,1:T(8,128)(2,1)} async-done(((bf16[2048,2,2048]{2,0,1:T(8,128)(2,1)}), bf16[256,2,2048]{2,0,1:T(8,128)(2,1)}) %reduce-scatter.27.cloned.1.call-update) | async-done | bytes 2097168 | tf_op jit(solution)/shard_map/reduce_scatter | solution.py:339
  1751.9 5.8 copy.125
  (189 shorter events, 39.2 us)
Async XLA Ops:
  7.2 49.4 %copy-start.29 = (s32[1,3]{1,0:T(1,128)S(1)}, s32[1,3]{1,0:T(1,128)}, u32[]{:S(2)}) copy-start(s32[1,3]{1,0:T(1,128)} %param.17) | copy-start | bytes 40
  7.2 65.8 %all-gather.14.cloned.1.call-start = ((), (), s32[]{:S(2)}) async-start(), calls=%async_computation.10 | async-start | bytes 2621440 | tf_op jit(solution)/shard_map/all_gather | solution.py:96
  50.9 124.7 %copy-start.21 = (f32[1,2048]{1,0:T(1,128)}, f32[1,2048]{1,0:T(1,128)S(1)}, u32[]{:S(2)}) copy-start(f32[1,2048]{1,0:T(1,128)S(1)} %get-tuple-element.924) | copy-start | bytes 24580
  50.9 728.3 %copy-start.19 = (f32[1,2048]{1,0:T(1,128)}, f32[1,2048]{1,0:T(1,128)S(1)}, u32[]{:S(2)}) copy-start(f32[1,2048]{1,0:T(1,128)S(1)} %get-tuple-element.923) | copy-start | bytes 24580
  52.1 4.8 copy-start.25
  54.2 121.4 %all-gather.16.cloned.1.call-start = ((), (), s32[]{:S(2)}) async-start(), calls=%async_computation.11 | async-start | bytes 7077888 | tf_op jit(solution)/shard_map/all_gather | solution.py:132
  56.5 146.9 %all-gather.18.cloned.1.call-start = ((), (), s32[]{:S(2)}) async-start(), calls=%async_computation.12 | async-start | bytes 1572864 | tf_op jit(solution)/shard_map/all_gather | solution.py:196
  57.2 124.8 %copy-start.10 = (f32[512,32]{0,1:T(8,128)}, f32[512,32]{0,1:T(8,128)S(1)}, u32[]{:S(2)}) copy-start(f32[512,32]{0,1:T(8,128)S(1)} %get-tuple-element.925) | copy-start | bytes 196612
  57.2 124.8 %copy-start.12 = (f32[512,32]{0,1:T(8,128)}, f32[512,32]{0,1:T(8,128)S(1)}, u32[]{:S(2)}) copy-start(f32[512,32]{0,1:T(8,128)S(1)} %get-tuple-element.926) | copy-start | bytes 196612
  181.8 1.9 copy-start.7
  183.7 43.0 %all-gather.30.cloned.1.call-start = ((), (), s32[]{:S(2)}) async-start(), calls=%async_computation.27 | async-start | bytes 1572864 | tf_op jit(solution)/shard_map/all_gather | solution.py:197
  185.9 92.2 %all-gather.20.cloned.1.call-start = ((), (), s32[]{:S(2)}) async-start(), calls=%async_computation.13 | async-start | bytes 2359296 | tf_op jit(solution)/shard_map/all_gather | solution.py:133
  186.5 126.0 %reduce-scatter.13.cloned.1.call-start = ((), (), s32[]{:S(2)}) async-start(), calls=%async_computation.14 | async-start | bytes 2621440 | tf_op jit(solution)/shard_map/reduce_scatter | solution.py:104
  250.6 31.8 %copy-start.15 = (bf16[512,8,64]{0,2,1:T(8,128)(2,1)}, bf16[512,8,64]{0,2,1:T(8,128)(2,1)S(1)}, u32[]{:S(2)}) copy-start(bf16[512,8,64]{0,2,1:T(8,128)(2,1)S(1)} %multiply_convert_fusion.4) | copy-start | bytes 1572868
  278.1 34.4 %copy-start.1 = (bf16[1,128,2048]{2,1,0:T(8,128)(2,1)S(1)}, bf16[1,128,2048]{2,1,0:T(8,128)(2,1)}, u32[]{:S(2)}) copy-start(bf16[1,128,2048]{2,1,0:T(8,128)(2,1)} %param.16) | copy-start | bytes 1572868
  282.4 56.2 %all-gather.22.cloned.1.call-start = ((), (), s32[]{:S(2)}) async-start(), calls=%async_computation.15 | async-start | bytes 2621440 | tf_op jit(solution)/shard_map/all_gather | solution.py:96
  313.8 465.5 %copy-start.23 = (f32[128]{0:T(128)}, f32[128]{0:T(128)S(1)}, u32[]{:S(2)}) copy-start(f32[128]{0:T(128)S(1)} %add_rsqrt_fusion) | copy-start | bytes 1540
  315.8 253.3 %all-gather.24.cloned.1.call-start = ((), (), s32[]{:S(2)}) async-start(), calls=%async_computation.16 | async-start | bytes 18874368 | tf_op jit(solution)/shard_map/all_gather | solution.py:134
  319.7 271.9 %all-gather.32.cloned.1.call-start = ((), (), s32[]{:S(2)}) async-start(), calls=%async_computation.28 | async-start | bytes 2621440 | tf_op jit(solution)/shard_map/all_gather | solution.py:100
  320.4 398.3 %all-gather.26.cloned.1.call-start = ((), (), s32[]{:S(2)}) async-start(), calls=%async_computation.17 | async-start | bytes 9437184 | tf_op jit(solution)/shard_map/all_gather | solution.py:135
  321.0 456.6 %reduce-scatter.17.cloned.1.call-start = ((), (), s32[]{:S(2)}) async-start(), calls=%async_computation.19 | async-start | bytes 2621440 | tf_op jit(solution)/shard_map/reduce_scatter | solution.py:110
  732.4 1.3 copy-start.30
  732.4 2.0 copy-start.31
  734.3 43.3 %copy-start.2 = (bf16[128,2048]{1,0:T(8,128)(2,1)S(1)}, bf16[128,2048]{1,0:T(8,128)(2,1)}, u32[]{:S(2)}) copy-start(bf16[128,2048]{1,0:T(8,128)(2,1)} %reduce-scatter.13.cloned.1.call-done) | copy-start | bytes 1572868
  734.4 44.9 %copy-start.4 = (bf16[1,128,2048]{2,1,0:T(8,128)(2,1)S(1)}, bf16[1,128,2048]{2,1,0:T(8,128)(2,1)}, u32[]{:S(2)}) copy-start(bf16[1,128,2048]{2,1,0:T(8,128)(2,1)} %param.23) | copy-start | bytes 1572868
  747.9 56.4 %all-gather.28.cloned.1.call-start = ((), (), s32[]{:S(2)}) async-start(), calls=%async_computation.20 | async-start | bytes 2621440 | tf_op jit(solution)/shard_map/all_gather | solution.py:100
  779.2 2.4 copy-start.27
  781.6 126.7 %reduce-scatter.19.cloned.1.call-start = ((), (), s32[]{:S(2)}) async-start(), calls=%async_computation.21 | async-start | bytes 3145728 | tf_op jit(solution)/shard_map/reduce_scatter | solution.py:308
  824.0 2.0 copy-start
  850.9 59.8 %copy-start.11 = (f32[512,32]{0,1:T(8,128)S(1)}, f32[512,32]{0,1:T(8,128)}, u32[]{:S(2)}) copy-start(f32[512,32]{0,1:T(8,128)} %copy-done.10) | copy-start | bytes 196612
  850.9 59.9 %copy-start.13 = (f32[512,32]{0,1:T(8,128)S(1)}, f32[512,32]{0,1:T(8,128)}, u32[]{:S(2)}) copy-start(f32[512,32]{0,1:T(8,128)} %copy-done.12) | copy-start | bytes 196612
  850.9 103.2 %reduce-scatter.21.cloned.1.call-start = ((), (), s32[]{:S(2)}) async-start(), calls=%async_computation.22 | async-start | bytes 2621440 | tf_op jit(solution)/shard_map/reduce_scatter | solution.py:110
  914.4 8.2 copy-start.8
  914.4 8.2 copy-start.16
  922.6 103.0 %reduce-scatter.25.cloned.1.call-start = ((), (), s32[]{:S(2)}) async-start(), calls=%async_computation.24 | async-start | bytes 2359296 | tf_op jit(solution)/shard_map/reduce_scatter | solution.py:336
  925.3 133.5 %reduce-scatter.15.cloned.1.call-start = ((), (), s32[]{:S(2)}) async-start(), calls=%async_computation.18 | async-start | bytes 2621440 | tf_op jit(solution)/shard_map/reduce_scatter | solution.py:104
  925.4 28.8 %copy-start.22 = (f32[1,2048]{1,0:T(1,128)S(1)}, f32[1,2048]{1,0:T(1,128)}, u32[]{:S(2)}) copy-start(f32[1,2048]{1,0:T(1,128)} %copy-done.21) | copy-start | bytes 24580
  925.4 28.8 %copy-start.26 = (f32[128]{0:T(128)S(1)}, f32[128]{0:T(128)}, u32[]{:S(2)}) copy-start(f32[128]{0:T(128)} %copy-done.25) | copy-start | bytes 1540
  935.6 260.8 %reduce-scatter.31.cloned.1.call-start = ((), (), s32[]{:S(2)}) async-start(), calls=%async_computation.29 | async-start | bytes 1081344
  957.0 388.2 %reduce-scatter.29.cloned.1.call-start = ((), (), s32[]{:S(2)}) async-start(), calls=%async_computation.26 | async-start | bytes 9437184 | tf_op jit(solution)/shard_map/reduce_scatter | solution.py:342
  967.4 1.0 copy-start.14
  967.4 1.2 copy-start.17
  967.4 1.4 copy-start.18
  967.4 499.2 %reduce-scatter.23.cloned.1.call-start = ((), (), s32[]{:S(2)}) async-start(), calls=%async_computation.23 | async-start | bytes 7077888 | tf_op jit(solution)/shard_map/reduce_scatter | solution.py:333
  975.8 776.1 %reduce-scatter.27.cloned.1.call-start = ((), (), s32[]{:S(2)}) async-start(), calls=%async_computation.25 | async-start | bytes 18874368 | tf_op jit(solution)/shard_map/reduce_scatter | solution.py:339
  991.2 67.6 %copy-start.3 = (bf16[128,2048]{1,0:T(8,128)(2,1)S(1)}, bf16[128,2048]{1,0:T(8,128)(2,1)}, u32[]{:S(2)}) copy-start(bf16[128,2048]{1,0:T(8,128)(2,1)} %reduce-scatter.13.cloned.1.call-done) | copy-start | bytes 1572868
  991.2 67.6 %copy-start.5 = (bf16[1,128,2048]{2,1,0:T(8,128)(2,1)S(1)}, bf16[1,128,2048]{2,1,0:T(8,128)(2,1)}, u32[]{:S(2)}) copy-start(bf16[1,128,2048]{2,1,0:T(8,128)(2,1)} %param.23) | copy-start | bytes 1572868
  991.2 67.6 %copy-start.6 = (bf16[128,2048]{1,0:T(8,128)(2,1)S(1)}, bf16[128,2048]{1,0:T(8,128)(2,1)}, u32[]{:S(2)}) copy-start(bf16[128,2048]{1,0:T(8,128)(2,1)} %reduce-scatter.17.cloned.1.call-done) | copy-start | bytes 1572868
  991.2 67.6 %copy-start.9 = (bf16[128,2048]{1,0:T(8,128)(2,1)S(1)}, bf16[128,2048]{1,0:T(8,128)(2,1)}, u32[]{:S(2)}) copy-start(bf16[128,2048]{1,0:T(8,128)(2,1)} %reduce-scatter.21.cloned.1.call-done) | copy-start | bytes 1572868
  991.2 67.6 %copy-start.20 = (f32[1,2048]{1,0:T(1,128)S(1)}, f32[1,2048]{1,0:T(1,128)}, u32[]{:S(2)}) copy-start(f32[1,2048]{1,0:T(1,128)} %copy-done.19) | copy-start | bytes 24580
  991.2 67.6 %copy-start.24 = (f32[128]{0:T(128)S(1)}, f32[128]{0:T(128)}, u32[]{:S(2)}) copy-start(f32[128]{0:T(128)} %copy-done.23) | copy-start | bytes 1540
  991.3 67.6 %copy-start.28 = (f32[128]{0:T(128)S(1)}, f32[128]{0:T(128)}, u32[]{:S(2)}) copy-start(f32[128]{0:T(128)} %copy-done.27) | copy-start | bytes 1540
Sparse Core Ops, SparseCore 0:
  54.3 18.6 all-gather.13
  75.6 99.9 all-gather.15
  183.8 19.5 all-gather.17
  205.4 21.2 all-gather.29
  228.7 49.3 all-gather.19
  282.5 29.9 reduce-scatter.12
  316.0 22.5 all-gather.21
  341.5 227.5 all-gather.23
  570.8 20.7 all-gather.31
  593.8 124.9 all-gather.25
  748.0 29.6 reduce-scatter.16
  781.7 22.5 all-gather.27
  851.1 57.1 reduce-scatter.18
  922.7 31.4 reduce-scatter.20
  957.5 68.0 reduce-scatter.24
  1028.5 30.2 reduce-scatter.14
  1061.6 134.7 reduce-scatter.30
  1199.9 145.2 reduce-scatter.28
  1349.2 117.3 reduce-scatter.22
  1470.7 281.1 reduce-scatter.26
where the time goes:
time: 1770 us
  waiting for transfers between devices  1470 us (83%)
  matrix products  128 us (7%)
  local copies, waits for them, and re-layouts  60.5 us (3%)
  blocking collectives  43.5 us (2%)
  other arithmetic  28.7 us (2%)
    reduce_scatter x1, waiting for transfers between devices, body(): lax.psum_scatter(grad_gate_up.astype(jnp.bfloat16), ('dp', 'blk'), scatte...  283 us
    all_gather x1, waiting for transfers between devices, body(): lax.all_gather(weight_gate_up, ('dp', 'blk'), axis=0, tiled=True)  231 us
    reduce_scatter x1, waiting for transfers between devices, body(): lax.psum_scatter(grad_down.astype(jnp.bfloat16), ('dp', 'blk'), scatter_d...  147 us
    unnamed x21, waiting for transfers between devices  137 us
    all_gather x1, waiting for transfers between devices, body(): lax.all_gather(weight_down, ('dp', 'blk'), axis=0, tiled=True)  127 us
    reduce_scatter x1, waiting for transfers between devices, body(): lax.psum_scatter(grad_qkv.astype(jnp.bfloat16), ('dp', 'blk'), scatter_di...  119 us
    all_gather x1, waiting for transfers between devices, body(): lax.all_gather(weight_qkv, ('dp', 'blk'), axis=0, tiled=True)  103 us
    reduce_scatter x2, waiting for transfers between devices, collect_rows(): lax.psum_scatter(partial_sum.astype(jnp.bfloat16), 'tensor', scatter_dime...  61.5 us
  transfers between devices with their start and end apart: 20, of which 20 were waited for; matrix products, arithmetic and copies ran while one was open for 6% of the time, Pallas kernels for 0%

commit v1 on v0

v1 whole, which is shorter than its diff:
```python
import functools

import jax
import jax.numpy as jnp
from jax import lax
from jax.experimental import pallas as pl
from jax.experimental.pallas import tpu as pltpu
from jax.sharding import PartitionSpec as P

HEAD_DIM = 64
PAIR = 2 * HEAD_DIM
EPSILON = 1e-05
ROPE_BASE = 130000.0
NEGATIVE = -1e30
QUERY_BLOCK = 256
UNROLLED = 4
LONG_ROW = 2048
PLANE = ("blk", "tensor")
F32 = jnp.float32
BF16 = jnp.bfloat16


def dot_nn(a, b):
    return lax.dot_general(a, b, (((1,), (0,)), ((), ())), preferred_element_type=F32)


def dot_nt(a, b):
    return lax.dot_general(a, b, (((1,), (1,)), ((), ())), preferred_element_type=F32)


def dot_tn(a, b):
    return lax.dot_general(a, b, (((0,), (0,)), ((), ())), preferred_element_type=F32)


def swap_by(value, axes, size, bits):
    return lax.ppermute(value, axes, [(i, i ^ bits) for i in range(size)])


def spread(rows, axes, size):
    near = jnp.concatenate(
        [rows] + [swap_by(rows, axes, size, bits) for bits in range(2, size, 2)], axis=0
    )
    return jnp.concatenate([near, swap_by(near, axes, size, 1)], axis=0)


def collect(left, right, product, axes, size):
    half = left.shape[0] // 2
    sent = product(left[half:], right).astype(BF16)
    received = swap_by(sent, axes, size, 1)
    near = (product(left[:half], right) + received.astype(F32)).astype(BF16)
    rows = near.shape[0] // (size // 2)
    total = near[:rows].astype(F32)
    for place in range(1, size // 2):
        block = near[place * rows : (place + 1) * rows]
        total = total + swap_by(block, axes, size, 2 * place).astype(F32)
    return total


def gather_small(value, axis_sizes):
    for axis, size in reversed(axis_sizes):
        index = lax.axis_index(axis)
        bit = 1
        while bit < size:
            other = swap_by(value, axis, size, bit)
            low = (index & bit) == 0
            value = jnp.concatenate(
                [jnp.where(low, value, other), jnp.where(low, other, value)], axis=1
            )
            bit *= 2
    return value


def scatter_small(value, axis_sizes):
    for axis, size in axis_sizes:
        index = lax.axis_index(axis)
        bit = size // 2
        while bit >= 1:
            half = value.shape[1] // 2
            low = (index & bit) == 0
            kept = jnp.where(low, value[:, :half], value[:, half:])
            sent = jnp.where(low, value[:, half:], value[:, :half])
            value = kept + swap_by(sent, axis, size, bit)
            bit //= 2
    return value


def gather_weight(weight, blocks):
    rows, kinds, columns = weight.shape
    own = columns // blocks
    parted = weight.reshape(rows, kinds, blocks, own).transpose(2, 0, 1, 3)
    parted = parted.reshape(blocks, rows, kinds * own)
    mixed = lax.all_to_all(parted, "blk", 0, 0, tiled=True).reshape(blocks * rows, kinds * own)
    return lax.all_gather(mixed, "dp", axis=0, tiled=True)


def scatter_weight(grads, blocks, kinds):
    own = grads.shape[1] // kinds
    summed = lax.psum_scatter(grads.astype(BF16), "dp", scatter_dimension=0, tiled=True)
    rows = summed.shape[0] // blocks
    parted = lax.all_to_all(
        summed.reshape(blocks, rows, kinds * own), "blk", 0, 0, tiled=True
    )
    parted = parted.reshape(blocks, rows, kinds, own).transpose(1, 2, 0, 3)
    return parted.reshape(rows, kinds, blocks * own).astype(F32)


def swap_halves(values):
    lane = lax.broadcasted_iota(jnp.int32, values.shape, 1)
    half = HEAD_DIM // 2
    return jnp.where(
        lane % HEAD_DIM < half,
        pltpu.roll(values, PAIR - half, 1),
        pltpu.roll(values, half, 1),
    )


def relative_place(block, info_ref, blocks, rows):
    bits = lax.bitwise_xor(jnp.int32(block), info_ref[0])
    place = lax.shift_right_logical(bits, 1) + (bits & 1) * (blocks // 2)
    return pl.ds(pl.multiple_of(place * rows, rows), rows)


def document_start(places, info_ref):
    end_0 = info_ref[1]
    end_1 = info_ref[2]
    end_2 = info_ref[3]
    start = jnp.where(places >= end_0, end_0, 0)
    start = jnp.where(places >= end_1, end_1, start)
    return jnp.where(places >= end_2, end_2, start)


def head_lanes(shape, head):
    lane = lax.broadcasted_iota(jnp.int32, shape, 1)
    return (lane < HEAD_DIM) if head == 0 else (lane >= HEAD_DIM)


def only_head(values, head):
    return jnp.where(head_lanes(values.shape, head), values, jnp.zeros_like(values))


def attend_kernel(
    blocks,
    info_ref,
    q_ref,
    k_ref,
    v_ref,
    cos_ref,
    sin_ref,
    out_ref,
    q_row,
    k_row,
    v_row,
    log_ref,
):
    length = q_ref.shape[0]
    rows = length // blocks
    score_scale = HEAD_DIM ** (-0.5)
    for block in range(blocks):
        here = relative_place(block, info_ref, blocks, rows)
        there = pl.ds(block * rows, rows)
        cosine, sine = cos_ref[here, :], sin_ref[here, :]
        q, k = q_ref[here, :], k_ref[here, :]
        q_row[there, :] = ((q * cosine + swap_halves(q) * sine) * score_scale).astype(BF16)
        k_row[there, :] = (k * cosine + swap_halves(k) * sine).astype(BF16)
        v_row[there, :] = v_ref[here, :].astype(BF16)

    tall = max(QUERY_BLOCK, rows)

    def query_step(first, width):
        queries = q_row[pl.ds(first, tall), :]
        places = first + lax.broadcasted_iota(jnp.int32, (tall, 1), 0)
        keys_at = lax.broadcasted_iota(jnp.int32, (tall, width), 1)
        allowed = (keys_at <= places) & (keys_at >= document_start(places, info_ref))
        results = []
        logs = []
        for head in range(2):
            scores = dot_nt(only_head(queries, head), k_row[:width, :])
            scores = jnp.where(allowed, scores, NEGATIVE)
            highest = jnp.max(scores, axis=1, keepdims=True)
            weights = jnp.exp(scores - highest)
            total = jnp.sum(weights, axis=1, keepdims=True)
            results.append(dot_nn(weights.astype(BF16), v_row[:width, :]) / total)
            logs.append(highest + jnp.log(total))
        first_head = head_lanes((tall, PAIR), 0)
        present = (places < info_ref[3]).astype(F32)
        merged = (jnp.where(first_head, results[0], results[1]) * present).astype(BF16)
        log_ref[pl.ds(first, tall), :] = jnp.where(first_head, logs[0], logs[1])
        return merged

    def put(merged, first_block):
        for part in range(tall // rows):
            here = relative_place(first_block + part, info_ref, blocks, rows)
            out_ref[here, :] = merged[part * rows : (part + 1) * rows]

    steps = length // tall
    if steps <= UNROLLED:
        for step in range(steps):
            put(query_step(step * tall, (step + 1) * tall), step * (tall // rows))
    else:

        @pl.loop(0, steps)
        def _(step):
            put(query_step(pl.multiple_of(step * tall, tall), length), step * (tall // rows))


def attend(info, projected, cosine, sine, blocks):
    length, width = projected.shape
    pairs = width // 3 // PAIR
    whole = lambda kind: pl.BlockSpec((length, PAIR), lambda p, _: (0, kind * pairs + p))
    table = pl.BlockSpec((length, PAIR), lambda p, _: (0, 0))
    shape = lambda kind: jax.ShapeDtypeStruct((length, pairs * PAIR), kind)
    return pl.pallas_call(
        functools.partial(attend_kernel, blocks),
        grid_spec=pltpu.PrefetchScalarGridSpec(
            num_scalar_prefetch=1,
            grid=(pairs,),
            in_specs=[whole(0), whole(1), whole(2), table, table],
            out_specs=[whole(0)] * 5,
        ),
        out_shape=[shape(BF16), shape(BF16), shape(BF16), shape(BF16), shape(F32)],
        compiler_params=pltpu.CompilerParams(vmem_limit_bytes=48 * 2**20),
        cost_estimate=pl.CostEstimate(
            flops=8 * pairs * length * length * PAIR // 2,
            bytes_accessed=6 * length * width,
            transcendentals=pairs * length * length,
        ),
        name="attend",
    )(info, projected, projected, projected, cosine, sine)


def attend_back_kernel(
    blocks,
    info_ref,
    q_row,
    k_row,
    v_row,
    log_ref,
    out_ref,
    grad_ref,
    cos_ref,
    sin_ref,
    back_ref,
    g_row,
    q_sum,
    k_sum,
    v_sum,
    log_flat,
    inner_flat,
):
    length = q_row.shape[0]
    rows = length // blocks
    score_scale = HEAD_DIM ** (-0.5)
    kind = pl.program_id(1)
    tall = max(QUERY_BLOCK, rows)

    @pl.when(kind == 0)
    def _():
        for block in range(blocks):
            here = relative_place(block, info_ref, blocks, rows)
            there = pl.ds(block * rows, rows)
            places = block * rows + lax.broadcasted_iota(jnp.int32, (rows, 1), 0)
            present = (places < info_ref[3]).astype(F32)
            grads = grad_ref[here, :].astype(F32) * present
            g_row[there, :] = grads.astype(BF16)
            inner = (grads * out_ref[here, :].astype(F32)).T
            for head in range(2):
                span = slice(head * HEAD_DIM, (head + 1) * HEAD_DIM)
                inner_flat[head : head + 1, there] = jnp.sum(inner[span], axis=0, keepdims=True)
            logs = log_ref[there, :].T
            for head in range(2):
                log_flat[head : head + 1, there] = logs[head * HEAD_DIM : head * HEAD_DIM + 1]
        q_sum[...] = jnp.zeros_like(q_sum)

        def key_step(first, from_query):
            width = length - from_query
            span = slice(from_query, length)
            keys = k_row[pl.ds(first, tall), :]
            values = v_row[pl.ds(first, tall), :]
            keys_at = first + lax.broadcasted_iota(jnp.int32, (tall, 1), 0)
            places = from_query + lax.broadcasted_iota(jnp.int32, (1, width), 1)
            allowed = (keys_at <= places) & (keys_at >= document_start(places, info_ref))
            queries, grads = q_row[span, :], g_row[span, :]
            k_parts = []
            v_parts = []
            for head in range(2):
                keys_head = only_head(keys, head)
                scores = dot_nt(keys_head, queries)
                raised = jnp.exp(scores - log_flat[head : head + 1, span])
                weights = jnp.where(allowed, raised, 0.0)
                grad_weights = dot_nt(only_head(values, head), grads)
                grad_scores = weights * (grad_weights - inner_flat[head : head + 1, span])
                grad_scores = grad_scores.astype(BF16)
                v_parts.append(dot_nn(weights.astype(BF16), grads))
                k_parts.append(dot_nn(grad_scores, queries))
                q_sum[span, :] += dot_tn(grad_scores, keys_head)
            first_head = head_lanes((tall, PAIR), 0)
            k_sum[pl.ds(first, tall), :] = jnp.where(first_head, k_parts[0], k_parts[1])
            v_sum[pl.ds(first, tall), :] = jnp.where(first_head, v_parts[0], v_parts[1])

        steps = length // tall
        if steps <= UNROLLED:
            for step in range(steps):
                key_step(step * tall, step * tall)
        else:

            @pl.loop(0, steps)
            def _(step):
                key_step(pl.multiple_of(step * tall, tall), 0)

    def give(source, turned, scale):
        for block in range(blocks):
            here = relative_place(block, info_ref, blocks, rows)
            grads = source[pl.ds(block * rows, rows), :] * scale
            if turned:
                grads = grads * cos_ref[here, :] - swap_halves(grads) * sin_ref[here, :]
            back_ref[here, :] = grads.astype(BF16)

    pl.when(kind == 0)(lambda: give(q_sum, True, score_scale))
    pl.when(kind == 1)(lambda: give(k_sum, True, 1.0))
    pl.when(kind == 2)(lambda: give(v_sum, False, 1.0))


def attend_back(info, q_row, k_row, v_row, logs, attended, grads, cosine, sine, blocks):
    length, width = q_row.shape
    pairs = width // PAIR
    one = pl.BlockSpec((length, PAIR), lambda p, c, _: (0, p))
    table = pl.BlockSpec((length, PAIR), lambda p, c, _: (0, 0))
    return pl.pallas_call(
        functools.partial(attend_back_kernel, blocks),
        grid_spec=pltpu.PrefetchScalarGridSpec(
            num_scalar_prefetch=1,
            grid=(pairs, 3),
            in_specs=[one] * 6 + [table] * 2,
            out_specs=pl.BlockSpec((length, PAIR), lambda p, c, _: (0, c * pairs + p)),
            scratch_shapes=[
                pltpu.VMEM((length, PAIR), BF16),
                pltpu.VMEM((length, PAIR), F32),
                pltpu.VMEM((length, PAIR), F32),
                pltpu.VMEM((length, PAIR), F32),
                pltpu.VMEM((8, length), F32),
                pltpu.VMEM((8, length), F32),
            ],
        ),
        out_shape=jax.ShapeDtypeStruct((length, 3 * width), BF16),
        compiler_params=pltpu.CompilerParams(vmem_limit_bytes=48 * 2**20),
        cost_estimate=pl.CostEstimate(
            flops=20 * pairs * length * length * PAIR // 2,
            bytes_accessed=20 * length * width,
            transcendentals=pairs * length * length,
        ),
        name="attend_back",
    )(info, q_row, k_row, v_row, logs, attended, grads, cosine, sine)


def whole_pairs(values, kinds):
    own = values.shape[1] // kinds
    if own % PAIR == 0:
        return values
    values = jnp.pad(values.reshape(-1, kinds, own), ((0, 0), (0, 0), (0, PAIR - own % PAIR)))
    return values.reshape(values.shape[0], -1)


def own_heads(values, kinds, own):
    return values.reshape(values.shape[0], kinds, -1)[:, :, :own].reshape(values.shape[0], -1)


def rms_unit(values):
    factor = lax.rsqrt(jnp.mean(values * values, axis=-1, keepdims=True) + EPSILON)
    return (values * factor, factor)


def norm_back(grad_normed, unit_rows, factor, gain_row):
    scaled_grad = grad_normed * gain_row
    inner_mean = jnp.mean(scaled_grad * unit_rows, axis=-1, keepdims=True)
    return (
        factor * (scaled_grad - unit_rows * inner_mean),
        jnp.sum(grad_normed * unit_rows, axis=0),
    )


def row_layout(lengths, places):
    ends = [jnp.sum(lengths[: i + 1]) for i in range(lengths.shape[0])]
    begins = jnp.zeros_like(places)
    for end in ends:
        begins = jnp.where(places >= end, end, begins)
    return ends, places - begins


def rope_tables(within):
    half = HEAD_DIM // 2
    steps_up = jnp.arange(half, dtype=F32)
    frequency = ROPE_BASE ** (-2.0 * steps_up / HEAD_DIM)
    angles = within.astype(F32)[:, None] * frequency[None, :]
    cosine, sine = jnp.cos(angles), jnp.sin(angles)
    return (
        jnp.concatenate([cosine] * 4, axis=1),
        jnp.concatenate([-sine, sine, -sine, sine], axis=1),
    )


def body(
    tokens, doc_lengths, weight_qkv, weight_out, weight_gate_up, weight_down, norm_gains, cotangent
):
    sizes = [(axis, lax.axis_size(axis)) for axis in ("dp", "blk", "tensor")]
    (_, _), (_, size_blk), (_, size_tensor) = sizes
    group = size_blk * size_tensor
    local_rows = tokens.shape[1]
    lengths = doc_lengths[0]

    me = (lax.axis_index("blk") * size_tensor + lax.axis_index("tensor")).astype(jnp.int32)
    order = jnp.array([*range(0, group, 2), *range(1, group, 2)], jnp.int32)
    places = (lax.bitwise_xor(order, me)[:, None] * local_rows) + jnp.arange(
        local_rows, dtype=jnp.int32
    )[None, :]
    ends, within = row_layout(lengths, places.reshape(-1))
    info = jnp.stack([me] + ends).astype(jnp.int32)
    cosine, sine = rope_tables(within)

    full_qkv = gather_weight(weight_qkv, size_blk)
    full_out = gather_weight(weight_out[:, None, :], size_blk)
    full_gate_up = gather_weight(weight_gate_up, size_blk)
    full_down = gather_weight(weight_down[:, None, :], size_blk)
    gain_pair = gather_small(norm_gains, sizes)
    gain_first, gain_second = gain_pair[0], gain_pair[1]

    inputs = tokens[0].astype(F32)
    unit_first, factor_first = rms_unit(inputs)
    normed_first = spread((unit_first * gain_first).astype(BF16), PLANE, group)
    projected = dot_nn(normed_first, full_qkv)
    features = full_out.shape[1]
    attended, q_row, k_row, v_row, logs = attend(
        info, whole_pairs(projected, 3), cosine, sine, group
    )
    attended_here = own_heads(attended, 1, features)
    branch = collect(attended_here, full_out, dot_nt, PLANE, group)
    middle = inputs + branch
    unit_second, factor_second = rms_unit(middle)
    normed_second = spread((unit_second * gain_second).astype(BF16), PLANE, group)
    hidden_here = full_gate_up.shape[1] // 2
    gate = dot_nn(normed_second, full_gate_up[:, :hidden_here])
    up = dot_nn(normed_second, full_gate_up[:, hidden_here:])
    sigmoid_gate = jax.nn.sigmoid(gate)
    activated = gate * sigmoid_gate
    hidden = (activated * up).astype(BF16)
    feed_out = collect(hidden, full_down, dot_nt, PLANE, group)
    grad_output = cotangent[0].astype(F32)
    last_rows = cotangent[0]
    if normed_second.shape[0] > LONG_ROW:
        last_rows, feed_out = lax.optimization_barrier((last_rows, feed_out))
    grad_feed = spread(last_rows, PLANE, group)
    outcome = (middle + feed_out).astype(BF16)
    grad_down = dot_tn(grad_feed, hidden)
    grad_hidden = dot_nn(grad_feed, full_down)
    silu_slope = sigmoid_gate * (1.0 + gate * (1.0 - sigmoid_gate))
    grad_gates = jnp.concatenate(
        [
            (grad_hidden * up * silu_slope).astype(BF16),
            (grad_hidden * activated).astype(BF16),
        ],
        axis=1,
    )
    grad_gate_up = dot_tn(normed_second, grad_gates)
    grad_normed_second = collect(grad_gates, full_gate_up, dot_nt, PLANE, group)
    grad_middle_norm, sum_second = norm_back(
        grad_normed_second, unit_second, factor_second, gain_second
    )
    grad_middle = grad_output + grad_middle_norm
    grad_branch = spread(grad_middle.astype(BF16), PLANE, group)
    grad_out = dot_tn(grad_branch, attended_here)
    grad_attended = dot_nn(grad_branch, full_out).astype(BF16)
    grad_projected = attend_back(
        info,
        q_row,
        k_row,
        v_row,
        logs,
        attended,
        whole_pairs(grad_attended, 1),
        cosine,
        sine,
        group,
    )
    grad_projected = own_heads(grad_projected, 3, features)
    grad_qkv = dot_tn(normed_first, grad_projected)
    grad_normed_first = collect(grad_projected, full_qkv, dot_nt, PLANE, group)
    grad_input_norm, sum_first = norm_back(grad_normed_first, unit_first, factor_first, gain_first)
    grad_input = grad_middle + grad_input_norm

    total_down = scatter_weight(grad_down, size_blk, 1)[:, 0]
    total_gate_up = scatter_weight(grad_gate_up, size_blk, 2)
    total_out = scatter_weight(grad_out, size_blk, 1)[:, 0]
    total_qkv = scatter_weight(grad_qkv, size_blk, 3)
    gain_sums = scatter_small(jnp.stack([sum_first, sum_second]), sizes)
    return (
        outcome[None],
        grad_input[None],
        total_qkv,
        total_out,
        total_gate_up,
        total_down,
        gain_sums,
    )


def solution(mesh):
    return jax.shard_map(
        body,
        mesh=mesh,
        in_specs=(
            P("dp", ("blk", "tensor"), None),
            P("dp", None),
            P(("dp", "blk"), None, "tensor"),
            P(("dp", "blk"), "tensor"),
            P(("dp", "blk"), None, "tensor"),
            P(("dp", "blk"), "tensor"),
            P(None, ("dp", "blk", "tensor")),
            P("dp", ("blk", "tensor"), None),
        ),
        out_specs=(
            P("dp", ("blk", "tensor"), None),
            P("dp", ("blk", "tensor"), None),
            P(("dp", "blk"), None, "tensor"),
            P(("dp", "blk"), "tensor"),
            P(("dp", "blk"), None, "tensor"),
            P(("dp", "blk"), "tensor"),
            P(None, ("dp", "blk", "tensor")),
        ),
        check_vma=False,
    )
```

time: 1770 us -> 847 us (0.48)
  waiting for transfers between devices: 1470 us -> 476 us
  starting transfers between devices: 2.37 us -> 64.9 us
  Pallas kernels: 0 us -> 23.3 us
    reduce_scatter x9 -> x4, waiting for transfers between devices: 750 us -> 191 us  [scatter_weight(): lax.psum_scatter(grads.astype(BF16), 'dp', scatter_dimension=0, tiled=True)]
    all_gather x10 -> x4, waiting for transfers between devices: 587 us -> 85.5 us  [gather_weight(): return lax.all_gather(mixed, 'dp', axis=0, tiled=True)]
    ppermute x0 -> x42, waiting for transfers between devices: none -> 167 us  [swap_by(): return lax.ppermute(value, axes, [(i, i ^ bits) for i in range(size)])]
    unnamed x21 -> x8, waiting for transfers between devices: 137 us -> 0.13 us
    all_to_all x0 -> x3, blocking collectives: none -> 47.7 us  [gather_weight(): lax.all_to_all(parted, 'blk', 0, 0, tiled=True)]
    ppermute x0 -> x42, starting transfers between devices: none -> 45.6 us  [swap_by(): return lax.ppermute(value, axes, [(i, i ^ bits) for i in range(size)])]
    all_gather x1 -> x0, blocking collectives: 43.5 us -> none  [body(): lax.all_gather(norm_gains, ('dp', 'blk', 'tensor'), axis=1, tiled=True)]
    all_to_all x0 -> x5, waiting for transfers between devices: none -> 33.7 us  [the longest x4 25.4 us: scatter_weight(): lax.all_to_all(summed.reshape(blocks, rows, kinds * own), 'blk', 0, 0, ti...]
  transfers between devices with their start and end apart: 20 -> 55, of which waited for: 20 -> 33; matrix products, arithmetic and copies ran while one was open for 6% -> 18% of each run, Pallas kernels for 0% -> 3%
where the time goes in v1:
time: 847 us; the launch traced here: 836 us
  waiting for transfers between devices  476 us (56%)
  matrix products  111 us (13%)
  local copies, waits for them, and re-layouts  73.6 us (9%)
  starting transfers between devices  64.9 us (8%)
  blocking collectives  47.7 us (6%)
  other arithmetic  23.5 us (3%)
  Pallas kernels  23.3 us (3%)
  between operations  15.4 us (2%)
    reduce_scatter x4, waiting for transfers between devices, scatter_weight(): lax.psum_scatter(grads.astype(BF16), 'dp', scatter_dimension=0, tiled=True)  191 us
    ppermute x42, waiting for transfers between devices, swap_by(): return lax.ppermute(value, axes, [(i, i ^ bits) for i in range(size)])  167 us
    all_gather x4, waiting for transfers between devices, gather_weight(): return lax.all_gather(mixed, 'dp', axis=0, tiled=True)  85.5 us
    all_to_all x3, blocking collectives, gather_weight(): lax.all_to_all(parted, 'blk', 0, 0, tiled=True)  47.7 us
    ppermute x42, starting transfers between devices, swap_by(): return lax.ppermute(value, axes, [(i, i ^ bits) for i in range(size)])  45.6 us
    dot_general x5, matrix products, dot_nn(): lax.dot_general(a, b, (((1,), (0,)), ((), ())), preferred_element_type=F32)  45.2 us
    dot_general x8, matrix products, dot_nt(): lax.dot_general(a, b, (((1,), (1,)), ((), ())), preferred_element_type=F32)  33.6 us
    unnamed x106, local copies, waits for them, and re-layouts  32.5 us
  transfers between devices with their start and end apart: 55, of which 33 were waited for; matrix products, arithmetic and copies ran while one was open for 18% of the time, Pallas kernels for 3%

profile of v1, /device:TPU:0, one launch (start us, length us, event | category | flops | bytes accessed | tf_op | source)
XLA Modules:
  0.0 836.1 jit_solution(17259003688429205553)
XLA Ops:
  8.7 14.8 %all_to_all.40 = bf16[2,256,768]{1,2,0:T(8,128)(2,1)S(1)} all-to-all(bf16[2,256,768]{1,2,0:T(8,128)(2,1)S(1)} %bitcast.129), channel_id=1, replica_groups=mesh['dp'=4,'blk'=2,'tensor'=4] {'blk'}, dimensions={0} | all-to-all | bytes 1572864 | tf_op jit(solution)/shard_map/all_to_all | solution.py:92
  24.9 7.6 all_to_all.41
  33.4 4.7 copy.46
  38.2 25.4 %all_to_all.42 = bf16[2,256,2048]{1,2,0:T(8,128)(2,1)S(1)} all-to-all(bf16[2,256,2048]{1,2,0:T(8,128)(2,1)S(1)} %bitcast.118), channel_id=1, replica_groups=mesh['dp'=4,'blk'=2,'tensor'=4] {'blk'}, dimensions={0} | all-to-all | bytes 4194304 | tf_op jit(solution)/shard_map/all_to_all | solution.py:92
  63.6 2.4 copy.48
  71.3 3.3 collective-permute-done.2
  78.4 3.0 collective-permute-start.4
  86.3 4.8 collective-permute-start.6
  91.1 9.0 %collective-permute-done.7 = bf16[128,2048]{1,0:T(8,128)(2,1)S(1)} collective-permute-done((bf16[128,2048]{1,0:T(8,128)(2,1)S(1)}, bf16[128,2048]{1,0:T(8,128)(2,1)S(1)}, u32[]{:S(2)}, u32[]{:S(2)}) %collective-permute-start.7) | collective-permute-done | bytes 524320 | tf_op jit(solution)/shard_map/ppermute | solution.py:36
  100.1 8.0 collective-permute-done.6
  118.5 3.2 constant_dynamic-update-slice_fusion
  121.6 8.3 fusion.52.q_ref.k_ref.v_ref
  129.9 10.9 %attend.1 = (bf16[1024,256]{1,0:T(8,128)(2,1)S(1)}, bf16[1024,256]{1,0:T(8,128)(2,1)S(1)}, bf16[1024,256]{1,0:T(8,128)(2,1)S(1)}, bf16[1024,256]{1,0:T(8,128)(2,1)S(1)}, f32[1024,256]{1,0:T(8,128)S(1)}) custom-call(s32[4]{0:T(128)S(1)} %pad_add_fusion.info_ref, f32[1024,768]{1,0:T(8,128)} %fusion.52.q_ref.k_ref.v_ref, f32[1024,768]{1,0:T(8,128)} %fusion.52.q_ref.k_ref.v_ref, ...), custom_call_target="tpu_custom_call" | custom-call | flops 1073741824 | bytes 4718592 | tf_op jit(solution)/shard_map/attend/pallas_call | solution.py:212
  142.4 3.3 convolution_convert_fusion.4
  149.7 2.3 copy.49
  151.9 4.4 all-to-all-start.3
  156.4 2.7 add_convert_fusion.3
  165.2 8.0 collective-permute-done.22
  173.2 2.9 pad_maximum_fusion.4
  176.2 8.3 all-to-all-done.3
  184.4 2.3 copy.50
  186.8 9.1 %collective-permute-done.12 = bf16[128,2048]{1,0:T(8,128)(2,1)} collective-permute-done((bf16[128,2048]{1,0:T(8,128)(2,1)}, bf16[128,2048]{1,0:T(8,128)(2,1)}, u32[]{:S(2)}, u32[]{:S(2)}) %collective-permute-start.12) | collective-permute-done | bytes 524320 | tf_op jit(solution)/shard_map/ppermute | solution.py:36
  195.9 10.0 %collective-permute-done.11 = bf16[128,2048]{1,0:T(8,128)(2,1)} collective-permute-done((bf16[128,2048]{1,0:T(8,128)(2,1)}, bf16[128,2048]{1,0:T(8,128)(2,1)}, u32[]{:S(2)}, u32[]{:S(2)}) %collective-permute-start.11) | collective-permute-done | bytes 524320 | tf_op jit(solution)/shard_map/ppermute | solution.py:36
  213.6 12.3 %collective-permute-done.15 = bf16[128,2048]{1,0:T(8,128)(2,1)S(1)} collective-permute-done((bf16[128,2048]{1,0:T(8,128)(2,1)S(1)}, bf16[128,2048]{1,0:T(8,128)(2,1)S(1)}, u32[]{:S(2)}, u32[]{:S(2)}) %collective-permute-start.15) | collective-permute-done | bytes 524320 | tf_op jit(solution)/shard_map/ppermute | solution.py:36
  225.9 8.7 %collective-permute-done.14 = bf16[128,2048]{1,0:T(8,128)(2,1)S(1)} collective-permute-done((bf16[128,2048]{1,0:T(8,128)(2,1)S(1)}, bf16[128,2048]{1,0:T(8,128)(2,1)S(1)}, u32[]{:S(2)}, u32[]{:S(2)}) %collective-permute-start.14) | collective-permute-done | bytes 524320 | tf_op jit(solution)/shard_map/ppermute | solution.py:36
  245.3 23.3 %all-gather.9.cloned.1.call-done = bf16[2048,2048]{1,0:T(8,128)(2,1)} async-done(((bf16[512,2048]{1,0:T(8,128)(2,1)}), bf16[2048,2048]{1,0:T(8,128)(2,1)}) %all-gather.9.cloned.1.call-update) | async-done | bytes 8388624 | tf_op jit(solution)/shard_map/all_gather | solution.py:93
  268.6 10.2 %fusion = f32[1024,1024]{0,1:T(8,128)} fusion(bf16[1024,2048]{1,0:T(8,128)(2,1)} %constant_dynamic-update-slice_fusion.5, bf16[2048,2048]{1,0:T(8,128)(2,1)} %all-gather.9.cloned.1.call-done), kind=kOutput, calls=%fused_computation.6 | convolution fusion | flops 4294967296 | bytes 12582912 | tf_op jit(solution)/shard_map/dot_general | solution.py:24
  278.8 8.6 %fusion.2 = f32[1024,1024]{0,1:T(8,128)} fusion(bf16[1024,2048]{1,0:T(8,128)(2,1)} %constant_dynamic-update-slice_fusion.5, bf16[2048,2048]{1,0:T(8,128)(2,1)S(1)} %copy-done.34), kind=kOutput, calls=%fused_computation.8 | convolution fusion | flops 4294967296 | bytes 12582912 | tf_op jit(solution)/shard_map/dot_general | solution.py:24
  287.4 62.2 %all-gather.11.cloned.1.call-done = bf16[2048,1024]{1,0:T(8,128)(2,1)} async-done(((bf16[512,1024]{1,0:T(8,128)(2,1)}), bf16[2048,1024]{1,0:T(8,128)(2,1)}) %all-gather.11.cloned.1.call-update) | async-done | bytes 4194320 | tf_op jit(solution)/shard_map/all_gather | solution.py:93
  349.6 14.3 %multiply_convert_fusion = (bf16[1024,1024]{0,1:T(8,128)(2,1)}, bf16[1024,1024]{0,1:T(8,128)(2,1)}, bf16[1024,1024]{0,1:T(8,128)(2,1)S(1)}) fusion(f32[1024,1024]{0,1:T(8,128)} %fusion.2, f32[1024,1024]{0,1:T(8,128)} %fusion, bf16[1024,2048]{1,0:T(8,128)(2,1)} %copy-done.29, bf16[2048,1024]{1,0:T(8,128)(2,1)} %all-gather.11.cloned.1.call-done), kind=kOutput, calls=%fused_computation.13 | convolution fusion | flops 4310695936 | bytes 23068672 | tf_op jit(solution)/shard_map/dot_general | solution.py:24
  363.9 2.4 convolution_convert_fusion.3
  366.4 9.1 %convolution_convert_fusion.6 = bf16[512,2048]{1,0:T(8,128)(2,1)S(1)} fusion(bf16[2048,2048]{1,0:T(8,128)(2,1)} %all-gather.9.cloned.1.call-done, bf16[1024,1024]{0,1:T(8,128)(2,1)} %get-tuple-element.45, bf16[1024,1024]{0,1:T(8,128)(2,1)} %get-tuple-element.44), kind=kOutput, calls=%fused_computation.25 | convolution fusion | flops 4300210176 | bytes 14680064 | tf_op jit(solution)/shard_map/dot_general | solution.py:28
  376.1 2.4 add_convert_fusion.2
  382.3 8.6 %add_convert_fusion.1 = bf16[512,2048]{1,0:T(8,128)(2,1)S(1)} fusion(bf16[512,2048]{1,0:T(8,128)(2,1)S(1)} %collective-permute-done.25, bf16[2048,2048]{1,0:T(8,128)(2,1)} %all-gather.9.cloned.1.call-done, bf16[1024,1024]{0,1:T(8,128)(2,1)} %get-tuple-element.45, bf16[1024,1024]{0,1:T(8,128)(2,1)} %get-tuple-element.44), kind=kOutput, calls=%fused_computation.12 | convolution fusion | flops 4302307328 | bytes 16777216 | tf_op jit(solution)/shard_map/dot_general | solution.py:28
  394.2 10.7 %collective-permute-done.18 = bf16[128,2048]{1,0:T(8,128)(2,1)S(1)} collective-permute-done((bf16[128,2048]{1,0:T(8,128)(2,1)S(1)}, bf16[128,2048]{1,0:T(8,128)(2,1)S(1)}, u32[]{:S(2)}, u32[]{:S(2)}) %collective-permute-start.18) | collective-permute-done | bytes 524320 | tf_op jit(solution)/shard_map/ppermute | solution.py:36
  406.4 20.0 %collective-permute-done.26 = bf16[128,2048]{1,0:T(8,128)(2,1)S(1)} collective-permute-done((bf16[128,2048]{1,0:T(8,128)(2,1)S(1)}, bf16[128,2048]{1,0:T(8,128)(2,1)S(1)}, u32[]{:S(2)}, u32[]{:S(2)}) %collective-permute-start.26) | collective-permute-done | bytes 524320 | tf_op jit(solution)/shard_map/ppermute | solution.py:36
  431.0 2.4 collective-permute-start.31
  434.5 12.3 %collective-permute-done.31 = bf16[128,2048]{1,0:T(8,128)(2,1)S(1)} collective-permute-done((bf16[128,2048]{1,0:T(8,128)(2,1)S(1)}, bf16[128,2048]{1,0:T(8,128)(2,1)S(1)}, u32[]{:S(2)}, u32[]{:S(2)}) %collective-permute-start.31) | collective-permute-done | bytes 524320 | tf_op jit(solution)/shard_map/ppermute | solution.py:36
  446.8 9.2 %collective-permute-done.30 = bf16[128,2048]{1,0:T(8,128)(2,1)S(1)} collective-permute-done((bf16[128,2048]{1,0:T(8,128)(2,1)S(1)}, bf16[128,2048]{1,0:T(8,128)(2,1)S(1)}, u32[]{:S(2)}, u32[]{:S(2)}) %collective-permute-start.30) | collective-permute-done | bytes 524320 | tf_op jit(solution)/shard_map/ppermute | solution.py:36
  456.4 4.0 collective-permute-done.32
  462.5 2.7 convolution_convert_fusion.7
  465.2 9.5 %convolution_convert_fusion.1 = bf16[2048,1024]{1,0:T(8,128)(2,1)} fusion(bf16[1024,2048]{1,0:T(8,128)(2,1)} %copy-done.29, bf16[1024,1024]{0,1:T(8,128)(2,1)} %copy-done.40), kind=kOutput, calls=%fused_computation.20 | convolution fusion | flops 4297064448 | bytes 10485760 | tf_op jit(solution)/shard_map/dot_general | solution.py:32
  474.9 3.8 convolution_convert_fusion.8.grad_ref
  478.7 12.4 %attend_back.1 = bf16[1024,768]{1,0:T(8,128)(2,1)} custom-call(s32[4]{0:T(128)S(1)} %pad_add_fusion.info_ref, bf16[1024,256]{1,0:T(8,128)(2,1)S(1)} %get-tuple-element.13.q_row, bf16[1024,256]{1,0:T(8,128)(2,1)S(1)} %copy-done.1, bf16[1024,256]{1,0:T(8,128)(2,1)S(1)} %copy-done.3, f32[1024,256]{1,0:T(8,128)S(1)} %get-tuple-element.16.log_ref, ...), custom_call_target="tpu_custom_call" | custom-call | flops 2684354560 | bytes 5242880 | tf_op jit(solution)/shard_map/attend_back/pallas_call | solution.py:328
  491.2 6.4 convolution_convert_fusion.2
  497.7 13.8 %convolution_convert_fusion = bf16[2048,2048]{1,0:T(8,128)(2,1)} fusion(bf16[1024,2048]{1,0:T(8,128)(2,1)} %constant_dynamic-update-slice_fusion.5, bf16[1024,1024]{0,1:T(8,128)(2,1)S(1)} %copy-done.42, bf16[1024,1024]{0,1:T(8,128)(2,1)} %get-tuple-element.45), kind=kOutput, calls=%fused_computation | convolution fusion | flops 8602517504 | bytes 16777216 | tf_op jit(solution)/shard_map/dot_general | solution.py:32
  513.4 3.1 convolution_convert_fusion.5
  516.9 3.9 collective-permute-done.33
  526.4 21.8 %collective-permute-done.34 = bf16[128,2048]{1,0:T(8,128)(2,1)S(1)} collective-permute-done((bf16[128,2048]{1,0:T(8,128)(2,1)S(1)}, bf16[128,2048]{1,0:T(8,128)(2,1)S(1)}, u32[]{:S(2)}, u32[]{:S(2)}) %collective-permute-start.34) | collective-permute-done | bytes 524320 | tf_op jit(solution)/shard_map/ppermute | solution.py:36
  551.3 4.8 collective-permute-done.37
  556.3 3.5 all-to-all-start.5
  568.8 3.6 all-to-all-start.7
  574.0 58.5 %reduce-scatter.5.cloned.1.call-done = bf16[512,768]{1,0:T(8,128)(2,1)} async-done(((bf16[2048,768]{1,0:T(8,128)(2,1)}), bf16[512,768]{1,0:T(8,128)(2,1)}) %reduce-scatter.5.cloned.1.call-update) | async-done | bytes 786448 | tf_op jit(solution)/shard_map/reduce_scatter | solution.py:98
  632.5 2.3 copy.51
  634.8 3.5 all-to-all-start.4
  638.4 10.8 %all-to-all-done.4 = bf16[2,256,768]{1,2,0:T(8,128)(2,1)S(1)} async-done(((bf16[2,256,768]{1,2,0:T(8,128)(2,1)}), bf16[2,256,768]{1,2,0:T(8,128)(2,1)S(1)}, u32[]{:S(2)}, u32[]{:S(2)}) %all-to-all-start.4) | async-done | bytes 786464 | tf_op jit(solution)/shard_map/all_to_all | solution.py:100
  649.2 130.2 %reduce-scatter.9.cloned.1.call-done = bf16[512,2048]{1,0:T(8,128)(2,1)} async-done(((bf16[2048,2048]{1,0:T(8,128)(2,1)}), bf16[512,2048]{1,0:T(8,128)(2,1)}) %reduce-scatter.9.cloned.1.call-update) | async-done | bytes 2097168 | tf_op jit(solution)/shard_map/reduce_scatter | solution.py:98
  779.4 4.0 all-to-all-start.6
  783.4 3.4 fusion.21
  792.9 3.0 copy.56
  796.0 12.4 %all-to-all-done.6 = bf16[2,256,2048]{2,1,0:T(8,128)(2,1)S(1)} async-done(((bf16[2,256,2048]{2,1,0:T(8,128)(2,1)}), bf16[2,256,2048]{2,1,0:T(8,128)(2,1)S(1)}, u32[]{:S(2)}, u32[]{:S(2)}) %all-to-all-start.6) | async-done | bytes 2097184 | tf_op jit(solution)/shard_map/all_to_all | solution.py:100
  808.3 5.1 reshape.168
  813.4 7.7 copy.60
  821.1 7.7 reshape.164
  (250 shorter events, 103.4 us)
Async XLA Ops:
  7.2 114.5 %all-gather.5.cloned.1.call-start = ((), (), s32[]{:S(2)}) async-start(), calls=%async_computation.12 | async-start | bytes 3932160 | tf_op jit(solution)/shard_map/all_gather | solution.py:93
  24.7 117.7 %all-gather.7.cloned.1.call-start = ((), (), s32[]{:S(2)}) async-start(), calls=%async_computation.13 | async-start | bytes 1310720 | tf_op jit(solution)/shard_map/all_gather | solution.py:93
  33.3 235.2 %all-gather.9.cloned.1.call-start = ((), (), s32[]{:S(2)}) async-start(), calls=%async_computation.14 | async-start | bytes 10485760 | tf_op jit(solution)/shard_map/all_gather | solution.py:93
  66.0 43.0 %copy-start.32 = (s32[1,3]{1,0:T(1,128)S(1)}, s32[1,3]{1,0:T(1,128)}, u32[]{:S(2)}) copy-start(s32[1,3]{1,0:T(1,128)} %param.10) | copy-start | bytes 40
  66.0 45.7 %copy-start.38 = (s32[8]{0:T(128)S(1)}, s32[8]{0:T(128)}, u32[]{:S(2)}) copy-start(s32[8]{0:T(128)} %constant.44.clone) | copy-start | bytes 100
  66.1 1.2 collective-permute-start
  67.3 3.6 collective-permute-start.1
  71.0 3.6 collective-permute-start.2
  74.6 3.8 collective-permute-start.3
  78.4 4.9 collective-permute-start.4
  84.3 15.8 %collective-permute-start.7 = (bf16[128,2048]{1,0:T(8,128)(2,1)S(1)}, bf16[128,2048]{1,0:T(8,128)(2,1)S(1)}, u32[]{:S(2)}, u32[]{:S(2)}) collective-permute-start(bf16[128,2048]{1,0:T(8,128)(2,1)S(1)} %get-tuple-element.43), channel_id=1, source_target_pairs={{0,6},{1,7},{2,4},{3,5},{4,2},{5,3},{6,0},{7,1},{8,14},{9,15},{10,... | collective-permute-start | bytes 1572872 | tf_op jit(solution)/shard_map/ppermute | solution.py:36
  86.3 21.8 %collective-permute-start.6 = (bf16[128,2048]{1,0:T(8,128)(2,1)S(1)}, bf16[128,2048]{1,0:T(8,128)(2,1)S(1)}, u32[]{:S(2)}, u32[]{:S(2)}) collective-permute-start(bf16[128,2048]{1,0:T(8,128)(2,1)S(1)} %get-tuple-element.43), channel_id=1, source_target_pairs={{0,4},{1,5},{2,6},{3,7},{4,0},{5,1},{6,2},{7,3},{8,12},{9,13},{10,... | collective-permute-start | bytes 1572872 | tf_op jit(solution)/shard_map/ppermute | solution.py:36
  91.1 17.0 %collective-permute-start.5 = (bf16[128,2048]{1,0:T(8,128)(2,1)S(1)}, bf16[128,2048]{1,0:T(8,128)(2,1)S(1)}, u32[]{:S(2)}, u32[]{:S(2)}) collective-permute-start(bf16[128,2048]{1,0:T(8,128)(2,1)S(1)} %get-tuple-element.43), channel_id=1, source_target_pairs={{0,2},{1,3},{2,0},{3,1},{4,6},{5,7},{6,4},{7,5},{8,10},{9,11},{10,... | collective-permute-start | bytes 1572872 | tf_op jit(solution)/shard_map/ppermute | solution.py:36
  109.1 9.4 %collective-permute-start.8 = (bf16[512,2048]{1,0:T(8,128)(2,1)S(1)}, bf16[512,2048]{1,0:T(8,128)(2,1)}, u32[]{:S(2)}, u32[]{:S(2)}) collective-permute-start(bf16[512,2048]{1,0:T(8,128)(2,1)S(1)} %pad_maximum_fusion.2), channel_id=1, source_target_pairs={{0,1},{1,0},{2,3},{3,2},{4,5},{5,4},{6,7},{7,6},{8,9},{9,8},{10,11... | collective-permute-start | bytes 6291464 | tf_op jit(solution)/shard_map/ppermute | solution.py:36
  145.7 10.8 %collective-permute-start.9 = (bf16[512,2048]{1,0:T(8,128)(2,1)}, bf16[512,2048]{1,0:T(8,128)(2,1)}, u32[]{:S(2)}, u32[]{:S(2)}) collective-permute-start(bf16[512,2048]{1,0:T(8,128)(2,1)} %convolution_convert_fusion.4), channel_id=1, source_target_pairs={{0,1},{1,0},{2,3},{3,2},{4,5},{5,4},{6,7},{7,6},{8,9},{9,8},{10,11... | collective-permute-start | bytes 6291464 | tf_op jit(solution)/shard_map/ppermute | solution.py:36
  146.2 19.0 %collective-permute-start.23 = (bf16[128,2048]{1,0:T(8,128)(2,1)}, bf16[128,2048]{1,0:T(8,128)(2,1)}, u32[]{:S(2)}, u32[]{:S(2)}) collective-permute-start(bf16[128,2048]{1,0:T(8,128)(2,1)} %bitcast.122), channel_id=1, source_target_pairs={{0,6},{1,7},{2,4},{3,5},{4,2},{5,3},{6,0},{7,1},{8,14},{9,15},{10,... | collective-permute-start | bytes 1572872 | tf_op jit(solution)/shard_map/ppermute | solution.py:36
  147.9 25.3 %collective-permute-start.22 = (bf16[128,2048]{1,0:T(8,128)(2,1)}, bf16[128,2048]{1,0:T(8,128)(2,1)}, u32[]{:S(2)}, u32[]{:S(2)}) collective-permute-start(bf16[128,2048]{1,0:T(8,128)(2,1)} %bitcast.123), channel_id=1, source_target_pairs={{0,4},{1,5},{2,6},{3,7},{4,0},{5,1},{6,2},{7,3},{8,12},{9,13},{10,... | collective-permute-start | bytes 1572872 | tf_op jit(solution)/shard_map/ppermute | solution.py:36
  148.8 24.4 %collective-permute-start.21 = (bf16[128,2048]{1,0:T(8,128)(2,1)}, bf16[128,2048]{1,0:T(8,128)(2,1)}, u32[]{:S(2)}, u32[]{:S(2)}) collective-permute-start(bf16[128,2048]{1,0:T(8,128)(2,1)} %bitcast.124), channel_id=1, source_target_pairs={{0,2},{1,3},{2,0},{3,1},{4,6},{5,7},{6,4},{7,5},{8,10},{9,11},{10,... | collective-permute-start | bytes 1572872 | tf_op jit(solution)/shard_map/ppermute | solution.py:36
  151.9 32.5 %all-to-all-start.3 = ((bf16[2,256,1024]{1,2,0:T(8,128)(2,1)}), bf16[2,256,1024]{1,2,0:T(8,128)(2,1)}, u32[]{:S(2)}, u32[]{:S(2)}) async-start(bf16[2,256,1024]{1,2,0:T(8,128)(2,1)} %bitcast.127), calls=%async_computation.3 | async-start | bytes 2097152 | tf_op jit(solution)/shard_map/all_to_all | solution.py:92
  156.4 193.2 %all-gather.11.cloned.1.call-start = ((), (), s32[]{:S(2)}) async-start(), calls=%async_computation.15 | async-start | bytes 5242880 | tf_op jit(solution)/shard_map/all_gather | solution.py:93
  161.7 25.1 %collective-permute-start.10 = (bf16[128,2048]{1,0:T(8,128)(2,1)}, bf16[128,2048]{1,0:T(8,128)(2,1)}, u32[]{:S(2)}, u32[]{:S(2)}) collective-permute-start(bf16[128,2048]{1,0:T(8,128)(2,1)} %get-tuple-element.56), channel_id=1, source_target_pairs={{0,2},{1,3},{2,0},{3,1},{4,6},{5,7},{6,4},{7,5},{8,10},{9,11},{10,... | collective-permute-start | bytes 1572872 | tf_op jit(solution)/shard_map/ppermute | solution.py:36
  162.9 33.0 %collective-permute-start.12 = (bf16[128,2048]{1,0:T(8,128)(2,1)}, bf16[128,2048]{1,0:T(8,128)(2,1)}, u32[]{:S(2)}, u32[]{:S(2)}) collective-permute-start(bf16[128,2048]{1,0:T(8,128)(2,1)} %get-tuple-element.57), channel_id=1, source_target_pairs={{0,6},{1,7},{2,4},{3,5},{4,2},{5,3},{6,0},{7,1},{8,14},{9,15},{10,... | collective-permute-start | bytes 1572872 | tf_op jit(solution)/shard_map/ppermute | solution.py:36
  165.1 40.8 %collective-permute-start.11 = (bf16[128,2048]{1,0:T(8,128)(2,1)}, bf16[128,2048]{1,0:T(8,128)(2,1)}, u32[]{:S(2)}, u32[]{:S(2)}) collective-permute-start(bf16[128,2048]{1,0:T(8,128)(2,1)} %get-tuple-element.58), channel_id=1, source_target_pairs={{0,4},{1,5},{2,6},{3,7},{4,0},{5,1},{6,2},{7,3},{8,12},{9,13},{10,... | collective-permute-start | bytes 1572872 | tf_op jit(solution)/shard_map/ppermute | solution.py:36
  176.1 62.8 %collective-permute-start.24 = (bf16[512,2048]{1,0:T(8,128)(2,1)}, bf16[512,2048]{1,0:T(8,128)(2,1)}, u32[]{:S(2)}, u32[]{:S(2)}) collective-permute-start(bf16[512,2048]{1,0:T(8,128)(2,1)} %pad_maximum_fusion.4), channel_id=1, source_target_pairs={{0,1},{1,0},{2,3},{3,2},{4,5},{5,4},{6,7},{7,6},{8,9},{9,8},{10,11... | collective-permute-start | bytes 6291464 | tf_op jit(solution)/shard_map/ppermute | solution.py:36
  186.7 369.6 %reduce-scatter.7.cloned.1.call-start = ((), (), s32[]{:S(2)}) async-start(), calls=%async_computation.17 | async-start | bytes 1310720 | tf_op jit(solution)/shard_map/reduce_scatter | solution.py:98
  186.8 48.9 %copy-start.10 = (bf16[1,128,2048]{2,1,0:T(8,128)(2,1)S(1)}, bf16[1,128,2048]{2,1,0:T(8,128)(2,1)}, u32[]{:S(2)}) copy-start(bf16[1,128,2048]{2,1,0:T(8,128)(2,1)} %param.16) | copy-start | bytes 1572868
  210.1 15.8 %collective-permute-start.15 = (bf16[128,2048]{1,0:T(8,128)(2,1)S(1)}, bf16[128,2048]{1,0:T(8,128)(2,1)S(1)}, u32[]{:S(2)}, u32[]{:S(2)}) collective-permute-start(bf16[128,2048]{1,0:T(8,128)(2,1)S(1)} %get-tuple-element.39), channel_id=1, source_target_pairs={{0,6},{1,7},{2,4},{3,5},{4,2},{5,3},{6,0},{7,1},{8,14},{9,15},{10,... | collective-permute-start | bytes 1572872 | tf_op jit(solution)/shard_map/ppermute | solution.py:36
  211.5 23.2 %collective-permute-start.14 = (bf16[128,2048]{1,0:T(8,128)(2,1)S(1)}, bf16[128,2048]{1,0:T(8,128)(2,1)S(1)}, u32[]{:S(2)}, u32[]{:S(2)}) collective-permute-start(bf16[128,2048]{1,0:T(8,128)(2,1)S(1)} %get-tuple-element.39), channel_id=1, source_target_pairs={{0,4},{1,5},{2,6},{3,7},{4,0},{5,1},{6,2},{7,3},{8,12},{9,13},{10,... | collective-permute-start | bytes 1572872 | tf_op jit(solution)/shard_map/ppermute | solution.py:36
  212.4 22.8 %collective-permute-start.13 = (bf16[128,2048]{1,0:T(8,128)(2,1)S(1)}, bf16[128,2048]{1,0:T(8,128)(2,1)S(1)}, u32[]{:S(2)}, u32[]{:S(2)}) collective-permute-start(bf16[128,2048]{1,0:T(8,128)(2,1)S(1)} %get-tuple-element.39), channel_id=1, source_target_pairs={{0,2},{1,3},{2,0},{3,1},{4,6},{5,7},{6,4},{7,5},{8,10},{9,11},{10,... | collective-permute-start | bytes 1572872 | tf_op jit(solution)/shard_map/ppermute | solution.py:36
  235.5 8.3 collective-permute-start.16
  366.3 9.8 %collective-permute-start.17 = (bf16[512,2048]{1,0:T(8,128)(2,1)S(1)}, bf16[512,2048]{1,0:T(8,128)(2,1)S(1)}, u32[]{:S(2)}, u32[]{:S(2)}) collective-permute-start(bf16[512,2048]{1,0:T(8,128)(2,1)S(1)} %convolution_convert_fusion.3), channel_id=1, source_target_pairs={{0,1},{1,0},{2,3},{3,2},{4,5},{5,4},{6,7},{7,6},{8,9},{9,8},{10,11... | collective-permute-start | bytes 6291464 | tf_op jit(solution)/shard_map/ppermute | solution.py:36
  375.6 6.7 collective-permute-start.25
  378.8 26.1 %collective-permute-start.18 = (bf16[128,2048]{1,0:T(8,128)(2,1)S(1)}, bf16[128,2048]{1,0:T(8,128)(2,1)S(1)}, u32[]{:S(2)}, u32[]{:S(2)}) collective-permute-start(bf16[128,2048]{1,0:T(8,128)(2,1)S(1)} %get-tuple-element.53), channel_id=1, source_target_pairs={{0,2},{1,3},{2,0},{3,1},{4,6},{5,7},{6,4},{7,5},{8,10},{9,11},{10,... | collective-permute-start | bytes 1572872 | tf_op jit(solution)/shard_map/ppermute | solution.py:36
  380.3 26.0 %collective-permute-start.20 = (bf16[128,2048]{1,0:T(8,128)(2,1)S(1)}, bf16[128,2048]{1,0:T(8,128)(2,1)S(1)}, u32[]{:S(2)}, u32[]{:S(2)}) collective-permute-start(bf16[128,2048]{1,0:T(8,128)(2,1)S(1)} %get-tuple-element.54), channel_id=1, source_target_pairs={{0,6},{1,7},{2,4},{3,5},{4,2},{5,3},{6,0},{7,1},{8,14},{9,15},{10,... | collective-permute-start | bytes 1572872 | tf_op jit(solution)/shard_map/ppermute | solution.py:36
  381.8 45.9 %copy-start.5 = (f32[128,2048]{1,0:T(8,128)S(1)}, f32[128,2048]{1,0:T(8,128)}, u32[]{:S(2)}) copy-start(f32[128,2048]{1,0:T(8,128)} %copy-done.4) | copy-start | bytes 3145732
  381.8 24.6 %collective-permute-start.19 = (bf16[128,2048]{1,0:T(8,128)(2,1)S(1)}, bf16[128,2048]{1,0:T(8,128)(2,1)S(1)}, u32[]{:S(2)}, u32[]{:S(2)}) collective-permute-start(bf16[128,2048]{1,0:T(8,128)(2,1)S(1)} %get-tuple-element.55), channel_id=1, source_target_pairs={{0,4},{1,5},{2,6},{3,7},{4,0},{5,1},{6,2},{7,3},{8,12},{9,13},{10,... | collective-permute-start | bytes 1572872 | tf_op jit(solution)/shard_map/ppermute | solution.py:36
  391.0 38.4 %copy-start.11 = (bf16[1,128,2048]{2,1,0:T(8,128)(2,1)S(1)}, bf16[1,128,2048]{2,1,0:T(8,128)(2,1)}, u32[]{:S(2)}) copy-start(bf16[1,128,2048]{2,1,0:T(8,128)(2,1)} %param.16) | copy-start | bytes 1572868
  391.1 35.2 %collective-permute-start.26 = (bf16[128,2048]{1,0:T(8,128)(2,1)S(1)}, bf16[128,2048]{1,0:T(8,128)(2,1)S(1)}, u32[]{:S(2)}, u32[]{:S(2)}) collective-permute-start(bf16[128,2048]{1,0:T(8,128)(2,1)S(1)} %get-tuple-element.50), channel_id=1, source_target_pairs={{0,2},{1,3},{2,0},{3,1},{4,6},{5,7},{6,4},{7,5},{8,10},{9,11},{10,... | collective-permute-start | bytes 1572872 | tf_op jit(solution)/shard_map/ppermute | solution.py:36
  392.7 33.7 %collective-permute-start.28 = (bf16[128,2048]{1,0:T(8,128)(2,1)S(1)}, bf16[128,2048]{1,0:T(8,128)(2,1)S(1)}, u32[]{:S(2)}, u32[]{:S(2)}) collective-permute-start(bf16[128,2048]{1,0:T(8,128)(2,1)S(1)} %get-tuple-element.51), channel_id=1, source_target_pairs={{0,6},{1,7},{2,4},{3,5},{4,2},{5,3},{6,0},{7,1},{8,14},{9,15},{10,... | collective-permute-start | bytes 1572872 | tf_op jit(solution)/shard_map/ppermute | solution.py:36
  404.8 22.8 %collective-permute-start.27 = (bf16[128,2048]{1,0:T(8,128)(2,1)S(1)}, bf16[128,2048]{1,0:T(8,128)(2,1)S(1)}, u32[]{:S(2)}, u32[]{:S(2)}) collective-permute-start(bf16[128,2048]{1,0:T(8,128)(2,1)S(1)} %get-tuple-element.52), channel_id=1, source_target_pairs={{0,4},{1,5},{2,6},{3,7},{4,0},{5,1},{6,2},{7,3},{8,12},{9,13},{10,... | collective-permute-start | bytes 1572872 | tf_op jit(solution)/shard_map/ppermute | solution.py:36
  431.0 15.8 %collective-permute-start.31 = (bf16[128,2048]{1,0:T(8,128)(2,1)S(1)}, bf16[128,2048]{1,0:T(8,128)(2,1)S(1)}, u32[]{:S(2)}, u32[]{:S(2)}) collective-permute-start(bf16[128,2048]{1,0:T(8,128)(2,1)S(1)} %get-tuple-element.36), channel_id=1, source_target_pairs={{0,6},{1,7},{2,4},{3,5},{4,2},{5,3},{6,0},{7,1},{8,14},{9,15},{10,... | collective-permute-start | bytes 1572872 | tf_op jit(solution)/shard_map/ppermute | solution.py:36
  433.4 22.5 %collective-permute-start.30 = (bf16[128,2048]{1,0:T(8,128)(2,1)S(1)}, bf16[128,2048]{1,0:T(8,128)(2,1)S(1)}, u32[]{:S(2)}, u32[]{:S(2)}) collective-permute-start(bf16[128,2048]{1,0:T(8,128)(2,1)S(1)} %get-tuple-element.36), channel_id=1, source_target_pairs={{0,4},{1,5},{2,6},{3,7},{4,0},{5,1},{6,2},{7,3},{8,12},{9,13},{10,... | collective-permute-start | bytes 1572872 | tf_op jit(solution)/shard_map/ppermute | solution.py:36
  434.0 22.0 %collective-permute-start.29 = (bf16[128,2048]{1,0:T(8,128)(2,1)S(1)}, bf16[128,2048]{1,0:T(8,128)(2,1)S(1)}, u32[]{:S(2)}, u32[]{:S(2)}) collective-permute-start(bf16[128,2048]{1,0:T(8,128)(2,1)S(1)} %get-tuple-element.36), channel_id=1, source_target_pairs={{0,2},{1,3},{2,0},{3,1},{4,6},{5,7},{6,4},{7,5},{8,10},{9,11},{10,... | collective-permute-start | bytes 1572872 | tf_op jit(solution)/shard_map/ppermute | solution.py:36
  456.1 4.2 collective-permute-start.32
  465.2 103.7 %reduce-scatter.11.cloned.1.call-start = ((), (), s32[]{:S(2)}) async-start(), calls=%async_computation.19 | async-start | bytes 5242880 | tf_op jit(solution)/shard_map/reduce_scatter | solution.py:98
  474.8 157.7 %reduce-scatter.5.cloned.1.call-start = ((), (), s32[]{:S(2)}) async-start(), calls=%async_computation.16 | async-start | bytes 3932160 | tf_op jit(solution)/shard_map/reduce_scatter | solution.py:98
  497.6 281.7 %reduce-scatter.9.cloned.1.call-start = ((), (), s32[]{:S(2)}) async-start(), calls=%async_computation.18 | async-start | bytes 10485760 | tf_op jit(solution)/shard_map/reduce_scatter | solution.py:98
  516.6 32.8 %copy-start.7 = (bf16[1,128,2048]{2,1,0:T(8,128)(2,1)S(1)}, bf16[1,128,2048]{2,1,0:T(8,128)(2,1)}, u32[]{:S(2)}) copy-start(bf16[1,128,2048]{2,1,0:T(8,128)(2,1)} %param.9) | copy-start | bytes 1572868
  516.6 32.8 %copy-start.26 = (f32[1,2048]{1,0:T(1,128)S(1)}, f32[1,2048]{1,0:T(1,128)}, u32[]{:S(2)}) copy-start(f32[1,2048]{1,0:T(1,128)} %copy-done.25) | copy-start | bytes 24580
  516.6 32.8 %copy-start.31 = (f32[128]{0:T(128)S(1)}, f32[128]{0:T(128)}, u32[]{:S(2)}) copy-start(f32[128]{0:T(128)} %copy-done.30) | copy-start | bytes 1540
  516.6 4.2 collective-permute-start.33
  522.8 25.3 %collective-permute-start.34 = (bf16[128,2048]{1,0:T(8,128)(2,1)S(1)}, bf16[128,2048]{1,0:T(8,128)(2,1)S(1)}, u32[]{:S(2)}, u32[]{:S(2)}) collective-permute-start(bf16[128,2048]{1,0:T(8,128)(2,1)S(1)} %get-tuple-element.47), channel_id=1, source_target_pairs={{0,2},{1,3},{2,0},{3,1},{4,6},{5,7},{6,4},{7,5},{8,10},{9,11},{10,... | collective-permute-start | bytes 1572872 | tf_op jit(solution)/shard_map/ppermute | solution.py:36
  524.5 23.6 %collective-permute-start.36 = (bf16[128,2048]{1,0:T(8,128)(2,1)S(1)}, bf16[128,2048]{1,0:T(8,128)(2,1)S(1)}, u32[]{:S(2)}, u32[]{:S(2)}) collective-permute-start(bf16[128,2048]{1,0:T(8,128)(2,1)S(1)} %get-tuple-element.48), channel_id=1, source_target_pairs={{0,6},{1,7},{2,4},{3,5},{4,2},{5,3},{6,0},{7,1},{8,14},{9,15},{10,... | collective-permute-start | bytes 1572872 | tf_op jit(solution)/shard_map/ppermute | solution.py:36
  526.0 23.4 %collective-permute-start.35 = (bf16[128,2048]{1,0:T(8,128)(2,1)S(1)}, bf16[128,2048]{1,0:T(8,128)(2,1)S(1)}, u32[]{:S(2)}, u32[]{:S(2)}) collective-permute-start(bf16[128,2048]{1,0:T(8,128)(2,1)S(1)} %get-tuple-element.49), channel_id=1, source_target_pairs={{0,4},{1,5},{2,6},{3,7},{4,0},{5,1},{6,2},{7,3},{8,12},{9,13},{10,... | collective-permute-start | bytes 1572872 | tf_op jit(solution)/shard_map/ppermute | solution.py:36
  550.2 6.0 collective-permute-start.37
  556.2 5.5 collective-permute-start.38
  556.3 9.2 %all-to-all-start.5 = ((bf16[2,256,256]{2,1,0:T(8,128)(2,1)}), bf16[2,256,256]{2,1,0:T(8,128)(2,1)S(1)}, u32[]{:S(2)}, u32[]{:S(2)}) async-start(bf16[2,256,256]{2,1,0:T(8,128)(2,1)} %bitcast.140), calls=%async_computation.7 | async-start | bytes 524288 | tf_op jit(solution)/shard_map/all_to_all | solution.py:100
  561.7 10.7 %collective-permute-start.39 = (f32[2,256]{1,0:T(2,128)S(1)}, f32[2,256]{1,0:T(2,128)S(1)}, u32[]{:S(2)}, u32[]{:S(2)}) collective-permute-start(f32[2,256]{1,0:T(2,128)S(1)} %broadcast_select_fusion.6), channel_id=1, source_target_pairs={{0,4},{4,0},{1,5},{5,1},{2,6},{6,2},{3,7},{7,3},{8,12},{12,8},{9,1... | collective-permute-start | bytes 6152 | tf_op jit(solution)/shard_map/ppermute | solution.py:36
  568.8 65.9 %all-to-all-start.7 = ((bf16[2,256,1024]{2,1,0:T(8,128)(2,1)}), bf16[2,256,1024]{2,1,0:T(8,128)(2,1)S(1)}, u32[]{:S(2)}, u32[]{:S(2)}) async-start(bf16[2,256,1024]{2,1,0:T(8,128)(2,1)} %bitcast.135), calls=%async_computation.11 | async-start | bytes 2097152 | tf_op jit(solution)/shard_map/all_to_all | solution.py:100
  572.5 65.9 %collective-permute-start.40 = (f32[2,128]{1,0:T(2,128)S(1)}, f32[2,128]{1,0:T(2,128)S(1)}, u32[]{:S(2)}, u32[]{:S(2)}) collective-permute-start(f32[2,128]{1,0:T(2,128)S(1)} %broadcast_select_fusion.12), channel_id=1, source_target_pairs={{0,2},{1,3},{2,0},{3,1},{4,6},{5,7},{6,4},{7,5},{8,10},{9,11},{10,... | collective-permute-start | bytes 3080 | tf_op jit(solution)/shard_map/ppermute | solution.py:36
  634.8 144.6 %copy-start.12 = (bf16[2,256,1024]{2,1,0:T(8,128)(2,1)}, bf16[2,256,1024]{2,1,0:T(8,128)(2,1)S(1)}, u32[]{:S(2)}) copy-start(bf16[2,256,1024]{2,1,0:T(8,128)(2,1)S(1)} %all-to-all-done.7) | copy-start | bytes 3145732
  634.8 14.4 %all-to-all-start.4 = ((bf16[2,256,768]{1,2,0:T(8,128)(2,1)}), bf16[2,256,768]{1,2,0:T(8,128)(2,1)S(1)}, u32[]{:S(2)}, u32[]{:S(2)}) async-start(bf16[2,256,768]{1,2,0:T(8,128)(2,1)} %copy.51), calls=%async_computation.5 | async-start | bytes 1572864 | tf_op jit(solution)/shard_map/all_to_all | solution.py:100
  638.4 148.4 %collective-permute-start.41 = (f32[2,64]{1,0:T(2,128)S(1)}, f32[2,64]{1,0:T(2,128)S(1)}, u32[]{:S(2)}, u32[]{:S(2)}) collective-permute-start(f32[2,64]{1,0:T(2,128)S(1)} %broadcast_select_fusion.9), channel_id=1, source_target_pairs={{0,1},{1,0},{2,3},{3,2},{4,5},{5,4},{6,7},{7,6},{8,9},{9,8},{10,11... | collective-permute-start | bytes 1544 | tf_op jit(solution)/shard_map/ppermute | solution.py:36
  779.4 28.9 %all-to-all-start.6 = ((bf16[2,256,2048]{2,1,0:T(8,128)(2,1)}), bf16[2,256,2048]{2,1,0:T(8,128)(2,1)S(1)}, u32[]{:S(2)}, u32[]{:S(2)}) async-start(bf16[2,256,2048]{2,1,0:T(8,128)(2,1)} %bitcast.132), calls=%async_computation.9 | async-start | bytes 4194304 | tf_op jit(solution)/shard_map/all_to_all | solution.py:100
  (34 other events, 256.7 us)
Sparse Core Ops, SparseCore 0:
  24.8 64.2 all-gather.4
  91.3 26.4 all-gather.6
  119.4 149.1 all-gather.8
  270.6 78.9 all-gather.10
  465.3 25.5 reduce-scatter.6
  493.1 75.6 reduce-scatter.10
  571.7 60.7 reduce-scatter.4
  634.8 144.4 reduce-scatter.8

commit v2 on v1

--- a/solution.py
+++ b/solution.py
@@ -32,28 +32,77 @@
     return lax.dot_general(a, b, (((0,), (0,)), ((), ())), preferred_element_type=F32)
 
 
+def named(name, function, *args):
+    with jax.named_scope(name):
+        return function(*args)
+
+
+def after(value, *events):
+    return lax.optimization_barrier((value, *events))[0]
+
+
+def together(*values):
+    return lax.optimization_barrier(values)
+
+
 def swap_by(value, axes, size, bits):
     return lax.ppermute(value, axes, [(i, i ^ bits) for i in range(size)])
+
+
+def join_kernel(steps, near_ref, far_ref, out_ref):
+    step = pl.program_id(0)
+
+    @pl.when(step < steps)
+    def _():
+        out_ref[...] = near_ref[...]
+
+    @pl.when(step >= steps)
+    def _():
+        out_ref[...] = far_ref[...]
+
+
+def join_halves(near, far):
+    rows, width = near.shape
+    steps = max(1, rows // 128)
+    block = (rows // steps, width)
+    return pl.pallas_call(
+        functools.partial(join_kernel, steps),
+        grid=(2 * steps,),
+        in_specs=[
+            pl.BlockSpec(block, lambda i: (jnp.minimum(i, steps - 1), 0)),
+            pl.BlockSpec(block, lambda i: (jnp.maximum(i - steps, 0), 0)),
+        ],
+        out_specs=pl.BlockSpec(block, lambda i: (i, 0)),
+        out_shape=jax.ShapeDtypeStruct((2 * rows, width), near.dtype),
+        cost_estimate=pl.CostEstimate(
+            flops=0, bytes_accessed=8 * rows * width, transcendentals=0
+        ),
+        name="join_halves",
+    )(near, far)
 
 
 def spread(rows, axes, size):
     near = jnp.concatenate(
         [rows] + [swap_by(rows, axes, size, bits) for bits in range(2, size, 2)], axis=0
     )
-    return jnp.concatenate([near, swap_by(near, axes, size, 1)], axis=0)
-
-
-def collect(left, right, product, axes, size):
+    return join_halves(near, swap_by(near, axes, size, 1))
+
+
+def collect(left, right, product, axes, size, *tied, begin=()):
     half = left.shape[0] // 2
-    sent = product(left[half:], right).astype(BF16)
-    received = swap_by(sent, axes, size, 1)
+    received = swap_by(product(left[half:], right).astype(BF16), axes, size, 1)
     near = (product(left[:half], right) + received.astype(F32)).astype(BF16)
+    if tied:
+        near, *tied = together(near, *tied)
+    if begin:
+        near = after(near, *begin)
     rows = near.shape[0] // (size // 2)
-    total = near[:rows].astype(F32)
-    for place in range(1, size // 2):
-        block = near[place * rows : (place + 1) * rows]
-        total = total + swap_by(block, axes, size, 2 * place).astype(F32)
-    return total
+    blocks = [
+        swap_by(near[place * rows : (place + 1) * rows], axes, size, 2 * place)
+        for place in range(1, size // 2)
+    ]
+    summed = sum([block.astype(F32) for block in blocks], near[:rows].astype(F32))
+    return summed, blocks[0], *tied
 
 
 def gather_small(value, axis_sizes):
@@ -71,7 +120,12 @@
 
 
 def scatter_small(value, axis_sizes):
-    for axis, size in axis_sizes:
+    sizes = [size for _, size in axis_sizes]
+    kinds = value.shape[0]
+    value = value.reshape(kinds, sizes[0], -1).swapaxes(1, 2).reshape(kinds, *sizes[1:], -1)
+    value = value.reshape(kinds, -1, value.shape[-1] // sizes[0], sizes[0])
+    value = value.swapaxes(2, 3).reshape(kinds, -1)
+    for axis, size in (*axis_sizes[1:], axis_sizes[0]):
         index = lax.axis_index(axis)
         bit = size // 2
         while bit >= 1:
@@ -84,24 +138,48 @@
     return value
 
 
-def gather_weight(weight, blocks):
+def trade(blocks, axis):
+    return lax.all_to_all(blocks, axis, 0, 0, tiled=True)
+
+
+def split_columns(weight, blocks):
     rows, kinds, columns = weight.shape
-    own = columns // blocks
-    parted = weight.reshape(rows, kinds, blocks, own).transpose(2, 0, 1, 3)
-    parted = parted.reshape(blocks, rows, kinds * own)
-    mixed = lax.all_to_all(parted, "blk", 0, 0, tiled=True).reshape(blocks * rows, kinds * own)
-    return lax.all_gather(mixed, "dp", axis=0, tiled=True)
-
-
-def scatter_weight(grads, blocks, kinds):
-    own = grads.shape[1] // kinds
-    summed = lax.psum_scatter(grads.astype(BF16), "dp", scatter_dimension=0, tiled=True)
-    rows = summed.shape[0] // blocks
-    parted = lax.all_to_all(
-        summed.reshape(blocks, rows, kinds * own), "blk", 0, 0, tiled=True
-    )
-    parted = parted.reshape(blocks, rows, kinds, own).transpose(1, 2, 0, 3)
-    return parted.reshape(rows, kinds, blocks * own).astype(F32)
+    parted = weight.reshape(rows, kinds, blocks, columns // blocks).transpose(2, 0, 1, 3)
+    return parted.reshape(blocks, rows, -1)
+
+
+def swap_columns(weights, blocks):
+    parts = [split_columns(weight, blocks) for weight in weights]
+    traded = trade(jnp.concatenate(parts, axis=2), "blk")
+    traded = traded.reshape(-1, traded.shape[2])
+    cuts = []
+    start = 0
+    for part in parts:
+        cuts.append(traded[:, start : start + part.shape[2]])
+        start += part.shape[2]
+    return cuts
+
+
+def gather_rows(weight, *events):
+    return lax.all_gather(after(weight, *events), "dp", axis=0, tiled=True)
+
+
+def sum_rows(grads):
+    return lax.psum_scatter(grads, "dp", scatter_dimension=0, tiled=True)
+
+
+def return_columns(summed, blocks, kinds, own):
+    parted = trade(summed.reshape(blocks, -1, summed.shape[1]), "blk").astype(F32)
+    totals = []
+    start = 0
+    for kind in kinds:
+        columns = [
+            [parted[b, :, start + i * own : start + (i + 1) * own] for b in range(blocks)]
+            for i in range(kind)
+        ]
+        totals.append(jnp.stack([jnp.concatenate(part, axis=1) for part in columns], axis=1))
+        start += kind * own
+    return totals
 
 
 def swap_halves(values):
@@ -402,7 +480,7 @@
     tokens, doc_lengths, weight_qkv, weight_out, weight_gate_up, weight_down, norm_gains, cotangent
 ):
     sizes = [(axis, lax.axis_size(axis)) for axis in ("dp", "blk", "tensor")]
-    (_, _), (_, size_blk), (_, size_tensor) = sizes
+    size_dp, size_blk, size_tensor = (size for _, size in sizes)
     group = size_blk * size_tensor
     local_rows = tokens.shape[1]
     lengths = doc_lengths[0]
@@ -416,40 +494,51 @@
     info = jnp.stack([me] + ends).astype(jnp.int32)
     cosine, sine = rope_tables(within)
 
-    full_qkv = gather_weight(weight_qkv, size_blk)
-    full_out = gather_weight(weight_out[:, None, :], size_blk)
-    full_gate_up = gather_weight(weight_gate_up, size_blk)
-    full_down = gather_weight(weight_down[:, None, :], size_blk)
-    gain_pair = gather_small(norm_gains, sizes)
+    held_qkv, held_out = named(
+        "attention_weights", swap_columns, [weight_qkv, weight_out[:, None, :]], size_blk
+    )
+    full_qkv = named("qkv_gather", gather_rows, held_qkv)
+    gain_pair = named("gain_gather", gather_small, norm_gains, sizes)
     gain_first, gain_second = gain_pair[0], gain_pair[1]
 
     inputs = tokens[0].astype(F32)
     unit_first, factor_first = rms_unit(inputs)
-    normed_first = spread((unit_first * gain_first).astype(BF16), PLANE, group)
+    normed_first = named("first_spread", spread, (unit_first * gain_first).astype(BF16), PLANE, group)
+    held_gate_up, held_down = named(
+        "feed_weights", swap_columns, [weight_gate_up, weight_down[:, None, :]], size_blk
+    )
+    full_out = named("out_gather", gather_rows, held_out, full_qkv, normed_first)
+    full_gate_up = named("gate_up_gather", gather_rows, held_gate_up, full_out)
     projected = dot_nn(normed_first, full_qkv)
     features = full_out.shape[1]
     attended, q_row, k_row, v_row, logs = attend(
         info, whole_pairs(projected, 3), cosine, sine, group
     )
     attended_here = own_heads(attended, 1, features)
-    branch = collect(attended_here, full_out, dot_nt, PLANE, group)
+    branch, _ = named(
+        "branch_collect", collect, attended_here, full_out, dot_nt, PLANE, group
+    )
     middle = inputs + branch
     unit_second, factor_second = rms_unit(middle)
-    normed_second = spread((unit_second * gain_second).astype(BF16), PLANE, group)
+    normed_second = named("second_spread", spread, (unit_second * gain_second).astype(BF16), PLANE, group)
     hidden_here = full_gate_up.shape[1] // 2
+    grad_output = cotangent[0].astype(F32)
+    last_rows = cotangent[0]
+    if normed_second.shape[0] > LONG_ROW:
+        last_rows = after(last_rows, normed_second)
+    grad_feed = named("cotangent_spread", spread, last_rows, PLANE, group)
+    full_down = named(
+        "down_gather", gather_rows, held_down, full_gate_up, normed_second, grad_feed
+    )
     gate = dot_nn(normed_second, full_gate_up[:, :hidden_here])
     up = dot_nn(normed_second, full_gate_up[:, hidden_here:])
     sigmoid_gate = jax.nn.sigmoid(gate)
     activated = gate * sigmoid_gate
     hidden = (activated * up).astype(BF16)
-    feed_out = collect(hidden, full_down, dot_nt, PLANE, group)
-    grad_output = cotangent[0].astype(F32)
-    last_rows = cotangent[0]
-    if normed_second.shape[0] > LONG_ROW:
-        last_rows, feed_out = lax.optimization_barrier((last_rows, feed_out))
-    grad_feed = spread(last_rows, PLANE, group)
-    outcome = (middle + feed_out).astype(BF16)
-    grad_down = dot_tn(grad_feed, hidden)
+    grad_down = dot_tn(grad_feed, hidden).astype(BF16)
+    wide = full_down.shape[1]
+    full_down = after(full_down, grad_down)
+    down_sum = named("down_back", sum_rows, after(grad_down, full_down))
     grad_hidden = dot_nn(grad_feed, full_down)
     silu_slope = sigmoid_gate * (1.0 + gate * (1.0 - sigmoid_gate))
     grad_gates = jnp.concatenate(
@@ -459,14 +548,26 @@
         ],
         axis=1,
     )
-    grad_gate_up = dot_tn(normed_second, grad_gates)
-    grad_normed_second = collect(grad_gates, full_gate_up, dot_nt, PLANE, group)
+    grad_gate_up = dot_tn(normed_second, grad_gates).astype(BF16)
+    grad_normed_second, first_second = named(
+        "second_grad_collect", collect, grad_gates, full_gate_up, dot_nt, PLANE, group
+    )
+    grad_gate_up = after(grad_gate_up, down_sum, first_second)
+    gate_up_sum = named("gate_up_back", sum_rows, grad_gate_up)
     grad_middle_norm, sum_second = norm_back(
         grad_normed_second, unit_second, factor_second, gain_second
     )
     grad_middle = grad_output + grad_middle_norm
-    grad_branch = spread(grad_middle.astype(BF16), PLANE, group)
-    grad_out = dot_tn(grad_branch, attended_here)
+    grad_branch = named("branch_grad_spread", spread, grad_middle.astype(BF16), PLANE, group)
+    with jax.named_scope("feed_collect"):
+        feed_hidden = after(hidden, first_second)
+        feed_out, _ = collect(
+            feed_hidden, full_down, dot_nt, PLANE, group, begin=(grad_branch,)
+        )
+    [total_down] = named(
+        "down_return", return_columns, after(down_sum, grad_branch), size_blk, [1], wide
+    )
+    grad_out = dot_tn(grad_branch, attended_here).astype(BF16)
     grad_attended = dot_nn(grad_branch, full_out).astype(BF16)
     grad_projected = attend_back(
         info,
@@ -481,23 +582,39 @@
         group,
     )
     grad_projected = own_heads(grad_projected, 3, features)
-    grad_qkv = dot_tn(normed_first, grad_projected)
-    grad_normed_first = collect(grad_projected, full_qkv, dot_nt, PLANE, group)
+    grad_qkv = dot_tn(normed_first, grad_projected).astype(BF16)
+    grad_normed_first, _, feed_out, total_down = named(
+        "first_grad_collect",
+        collect,
+        grad_projected,
+        full_qkv,
+        dot_nt,
+        PLANE,
+        group,
+        feed_out,
+        total_down,
+    )
+    both = jnp.concatenate([grad_qkv, grad_out], axis=1)
+    both_sum = named("attention_back", sum_rows, after(both, gate_up_sum, grad_normed_first))
+
+    outcome = (middle + feed_out).astype(BF16)
     grad_input_norm, sum_first = norm_back(grad_normed_first, unit_first, factor_first, gain_first)
     grad_input = grad_middle + grad_input_norm
-
-    total_down = scatter_weight(grad_down, size_blk, 1)[:, 0]
-    total_gate_up = scatter_weight(grad_gate_up, size_blk, 2)
-    total_out = scatter_weight(grad_out, size_blk, 1)[:, 0]
-    total_qkv = scatter_weight(grad_qkv, size_blk, 3)
-    gain_sums = scatter_small(jnp.stack([sum_first, sum_second]), sizes)
+    gain_sums = named("gain_scatter", scatter_small, jnp.stack([sum_first, sum_second]), sizes)
+    [total_gate_up] = named(
+        "gate_up_return", return_columns, gate_up_sum, size_blk, [2], wide
+    )
+    both_sum = after(both_sum, total_gate_up, outcome, grad_input, gain_sums)
+    total_qkv, total_out = named(
+        "attention_return", return_columns, both_sum, size_blk, [3, 1], features
+    )
     return (
         outcome[None],
         grad_input[None],
         total_qkv,
-        total_out,
+        total_out[:, 0],
         total_gate_up,
-        total_down,
+        total_down[:, 0],
         gain_sums,
     )
 

time: 847 us -> 718 us (0.85)
  waiting for transfers between devices: 476 us -> 389 us
  blocking collectives: 47.7 us -> 0 us
  local copies, waits for them, and re-layouts: 73.6 us -> 37.1 us
  Pallas kernels: 23.3 us -> 52 us
  other arithmetic: 23.5 us -> 40.5 us
    reduce_scatter x4 -> x3, waiting for transfers between devices: 191 us -> 55.9 us  [sum_rows(): return lax.psum_scatter(grads, 'dp', scatter_dimension=0, tiled=True)]
    all_to_all x3 -> x0, blocking collectives: 47.7 us -> none  [gather_weight(): lax.all_to_all(parted, 'blk', 0, 0, tiled=True)]
    all_to_all x5, waiting for transfers between devices: 33.7 us -> 67.6 us  [trade(): return lax.all_to_all(blocks, axis, 0, 0, tiled=True)]
    pallas_call x0 -> x4, Pallas kernels: none -> 28.5 us  [join_halves(): pl.pallas_call(functools.partial(join_kernel, steps), grid=(2 * steps,),...]
    convert_element_type x6 -> x0, local copies, waits for them, and re-layouts: 23.8 us -> none  [scatter_weight(): return parted.reshape(rows, kinds, blocks * own).astype(F32)]
    unnamed x106 -> x83, local copies, waits for them, and re-layouts: 32.5 us -> 20 us
    ppermute x42, waiting for transfers between devices: 167 us -> 176 us  [swap_by(): return lax.ppermute(value, axes, [(i, i ^ bits) for i in range(size)])]
  transfers between devices with their start and end apart: 55 -> 54, of which waited for: 33 -> 41; matrix products, arithmetic and copies ran while one was open for 18% -> 25% of each run, Pallas kernels for 3% -> 7%
where the time goes in v2:
time: 718 us; the launch traced here: 710 us
  waiting for transfers between devices  389 us (54%)
  matrix products  106 us (15%)
  starting transfers between devices  70.8 us (10%)
  Pallas kernels  52 us (7%)
  other arithmetic  40.5 us (6%)
  local copies, waits for them, and re-layouts  37.1 us (5%)
  between operations  15.4 us (2%)
    ppermute x42, waiting for transfers between devices, swap_by(): return lax.ppermute(value, axes, [(i, i ^ bits) for i in range(size)])  176 us
    all_gather x4, waiting for transfers between devices, gather_rows(): return lax.all_gather(after(weight, *events), 'dp', axis=0, tiled=True)  89 us
    all_to_all x5, waiting for transfers between devices, trade(): return lax.all_to_all(blocks, axis, 0, 0, tiled=True)  67.6 us
    reduce_scatter x3, waiting for transfers between devices, sum_rows(): return lax.psum_scatter(grads, 'dp', scatter_dimension=0, tiled=True)  55.9 us
    ppermute x42, starting transfers between devices, swap_by(): return lax.ppermute(value, axes, [(i, i ^ bits) for i in range(size)])  49 us
    dot_general x5, matrix products, dot_nn(): lax.dot_general(a, b, (((1,), (0,)), ((), ())), preferred_element_type=F32)  42 us
    dot_general x8, matrix products, dot_nt(): lax.dot_general(a, b, (((1,), (1,)), ((), ())), preferred_element_type=F32)  36.8 us
    pallas_call x4, Pallas kernels, join_halves(): pl.pallas_call(functools.partial(join_kernel, steps), grid=(2 * steps,),...  28.5 us
  transfers between devices with their start and end apart: 54, of which 41 were waited for; matrix products, arithmetic and copies ran while one was open for 25% of the time, Pallas kernels for 7%

profile of v2, /device:TPU:0, one launch (start us, length us, event | category | flops | bytes accessed | tf_op | source)
XLA Modules:
  0.0 710.0 jit_solution(6317499332419853879)
XLA Ops:
  11.3 3.8 all-to-all-start
  21.2 9.0 %all-to-all-done = bf16[2,256,1024]{1,2,0:T(8,128)(2,1)S(1)} async-done(((bf16[2,256,1024]{1,2,0:T(8,128)(2,1)}), bf16[2,256,1024]{1,2,0:T(8,128)(2,1)S(1)}, u32[]{:S(2)}, u32[]{:S(2)}) %all-to-all-start) | async-done | bytes 1048608 | tf_op jit(solution)/shard_map/attention_weights/all_to_all | solution.py:142
  35.4 2.9 collective-permute-start.4
  44.4 10.5 %collective-permute-done.5 = bf16[128,2048]{1,0:T(8,128)(2,1)S(1)} collective-permute-done((bf16[128,2048]{1,0:T(8,128)(2,1)S(1)}, bf16[128,2048]{1,0:T(8,128)(2,1)S(1)}, u32[]{:S(2)}, u32[]{:S(2)}) %collective-permute-start.5) | collective-permute-done | bytes 524320 | tf_op jit(solution)/shard_map/first_spread/ppermute | solution.py:49
  54.9 2.7 collective-permute-done.6
  57.6 7.2 %collective-permute-done.7 = bf16[128,2048]{1,0:T(8,128)(2,1)S(1)} collective-permute-done((bf16[128,2048]{1,0:T(8,128)(2,1)S(1)}, bf16[128,2048]{1,0:T(8,128)(2,1)S(1)}, u32[]{:S(2)}, u32[]{:S(2)}) %collective-permute-start.7) | collective-permute-done | bytes 524320 | tf_op jit(solution)/shard_map/first_spread/ppermute | solution.py:49
  66.4 4.1 copy.40
  74.5 3.1 pad_maximum_fusion.4
  77.5 5.2 all-to-all-start.1
  83.5 7.1 join_halves.4
  90.6 5.3 all-gather.5.cloned.1.call-done
  96.0 23.9 %all-to-all-done.1 = bf16[2,256,3072]{1,2,0:T(8,128)(2,1)} async-done(((bf16[2,256,3072]{1,2,0:T(8,128)(2,1)}), bf16[2,256,3072]{1,2,0:T(8,128)(2,1)}, u32[]{:S(2)}, u32[]{:S(2)}) %all-to-all-start.1) | async-done | bytes 3145760 | tf_op jit(solution)/shard_map/feed_weights/all_to_all | solution.py:142
  119.9 3.2 copy.43
  132.0 7.4 %fusion.46.q_ref.k_ref.v_ref = f32[1024,768]{1,0:T(8,128)} fusion(bf16[1024,2048]{1,0:T(8,128)(2,1)S(1)} %copy-done.11, bf16[2048,768]{1,0:T(8,128)(2,1)} %all-gather.5.cloned.1.call-done), kind=kOutput, calls=%fused_computation.147 | convolution fusion | flops 3221225472 | bytes 10485760 | tf_op jit(solution)/shard_map/dot_general | solution.py:24
  139.4 10.9 %attend.1 = (bf16[1024,256]{1,0:T(8,128)(2,1)S(1)}, bf16[1024,256]{1,0:T(8,128)(2,1)S(1)}, bf16[1024,256]{1,0:T(8,128)(2,1)S(1)}, bf16[1024,256]{1,0:T(8,128)(2,1)S(1)}, f32[1024,256]{1,0:T(8,128)S(1)}) custom-call(s32[4]{0:T(128)S(1)} %pad_add_fusion.info_ref, f32[1024,768]{1,0:T(8,128)} %fusion.46.q_ref.k_ref.v_ref, f32[1024,768]{1,0:T(8,128)} %fusion.46.q_ref.k_ref.v_ref, ...), custom_call_target="tpu_custom_call" | custom-call | flops 1073741824 | bytes 4718592 | tf_op jit(solution)/shard_map/attend/pallas_call | solution.py:290
  151.2 4.1 collective-permute-done.9
  162.6 9.2 %collective-permute-done.10 = bf16[128,2048]{1,0:T(8,128)(2,1)S(1)} collective-permute-done((bf16[128,2048]{1,0:T(8,128)(2,1)S(1)}, bf16[128,2048]{1,0:T(8,128)(2,1)S(1)}, u32[]{:S(2)}, u32[]{:S(2)}) %collective-permute-start.10) | collective-permute-done | bytes 524320 | tf_op jit(solution)/shard_map/branch_collect/ppermute | solution.py:49
  174.1 9.7 %collective-permute-done.12 = bf16[128,2048]{1,0:T(8,128)(2,1)S(1)} collective-permute-done((bf16[128,2048]{1,0:T(8,128)(2,1)S(1)}, bf16[128,2048]{1,0:T(8,128)(2,1)S(1)}, u32[]{:S(2)}, u32[]{:S(2)}) %collective-permute-start.12) | collective-permute-done | bytes 524320 | tf_op jit(solution)/shard_map/branch_collect/ppermute | solution.py:49
  188.4 5.8 collective-permute-done.13
  196.5 9.8 %collective-permute-done.15 = bf16[128,2048]{1,0:T(8,128)(2,1)S(1)} collective-permute-done((bf16[128,2048]{1,0:T(8,128)(2,1)S(1)}, bf16[128,2048]{1,0:T(8,128)(2,1)S(1)}, u32[]{:S(2)}, u32[]{:S(2)}) %collective-permute-start.15) | collective-permute-done | bytes 524320 | tf_op jit(solution)/shard_map/cotangent_spread/ppermute | solution.py:49
  207.9 7.3 %collective-permute-done.17 = bf16[128,2048]{1,0:T(8,128)(2,1)S(1)} collective-permute-done((bf16[128,2048]{1,0:T(8,128)(2,1)S(1)}, bf16[128,2048]{1,0:T(8,128)(2,1)S(1)}, u32[]{:S(2)}, u32[]{:S(2)}) %collective-permute-start.17) | collective-permute-done | bytes 524320 | tf_op jit(solution)/shard_map/second_spread/ppermute | solution.py:49
  215.2 2.5 collective-permute-done.18
  217.6 10.0 %collective-permute-done.19 = bf16[128,2048]{1,0:T(8,128)(2,1)S(1)} collective-permute-done((bf16[128,2048]{1,0:T(8,128)(2,1)S(1)}, bf16[128,2048]{1,0:T(8,128)(2,1)S(1)}, u32[]{:S(2)}, u32[]{:S(2)}) %collective-permute-start.19) | collective-permute-done | bytes 524320 | tf_op jit(solution)/shard_map/second_spread/ppermute | solution.py:49
  231.5 7.1 %join_halves.5 = bf16[1024,2048]{1,0:T(8,128)(2,1)} custom-call(bf16[512,2048]{1,0:T(8,128)(2,1)} %pad_maximum_fusion.6.near_ref, bf16[512,2048]{1,0:T(8,128)(2,1)} %collective-permute-done.16.far_ref), custom_call_target="tpu_custom_call" | custom-call | bytes 8388608 | tf_op jit(solution)/shard_map/cotangent_spread/join_halves/pallas_call | solution.py:68
  238.7 7.1 %join_halves.6 = bf16[1024,2048]{1,0:T(8,128)(2,1)} custom-call(bf16[512,2048]{1,0:T(8,128)(2,1)} %pad_maximum_fusion.7.near_ref, bf16[512,2048]{1,0:T(8,128)(2,1)} %collective-permute-done.20.far_ref), custom_call_target="tpu_custom_call" | custom-call | bytes 8388608 | tf_op jit(solution)/shard_map/second_spread/join_halves/pallas_call | solution.py:68
  245.8 29.6 %all-gather.9.cloned.1.call-done = bf16[2048,2048]{1,0:T(8,128)(2,1)} async-done(((bf16[512,2048]{1,0:T(8,128)(2,1)}), bf16[2048,2048]{1,0:T(8,128)(2,1)}) %all-gather.9.cloned.1.call-update) | async-done | bytes 8388624 | tf_op jit(solution)/shard_map/gate_up_gather/all_gather | solution.py:164
  275.7 10.2 %fusion.2 = f32[1024,1024]{0,1:T(8,128)} fusion(bf16[1024,2048]{1,0:T(8,128)(2,1)} %join_halves.6, bf16[2048,2048]{1,0:T(8,128)(2,1)} %all-gather.9.cloned.1.call-done), kind=kOutput, calls=%fused_computation.8 | convolution fusion | flops 4294967296 | bytes 12582912 | tf_op jit(solution)/shard_map/dot_general | solution.py:24
  285.9 8.6 %multiply_convert_fusion.2 = (bf16[1024,1024]{0,1:T(8,128)(2,1)}, f32[1024,1024]{0,1:T(8,128)}) fusion(f32[1024,1024]{0,1:T(8,128)} %fusion.2, bf16[1024,2048]{1,0:T(8,128)(2,1)S(1)} %copy-done.14, bf16[2048,2048]{1,0:T(8,128)(2,1)S(1)} %copy-done.31), kind=kOutput, calls=%fused_computation.17 | convolution fusion | flops 4301258752 | bytes 18874368 | tf_op jit(solution)/shard_map/dot_general | solution.py:24
  294.6 7.8 %convolution_convert_fusion.1 = bf16[2048,1024]{1,0:T(8,128)(2,1)} fusion(bf16[1024,2048]{1,0:T(8,128)(2,1)S(1)} %copy-done.16, bf16[1024,1024]{0,1:T(8,128)(2,1)} %get-tuple-element.35), kind=kOutput, calls=%fused_computation.21 | convolution fusion | flops 4297064448 | bytes 10485760 | tf_op jit(solution)/shard_map/dot_general | solution.py:32
  302.4 54.0 %all-gather.11.cloned.1.call-done = bf16[2048,1024]{1,0:T(8,128)(2,1)} async-done(((bf16[512,1024]{1,0:T(8,128)(2,1)}), bf16[2048,1024]{1,0:T(8,128)(2,1)}) %all-gather.11.cloned.1.call-update) | async-done | bytes 4194320 | tf_op jit(solution)/shard_map/down_gather/all_gather | solution.py:164
  356.7 11.9 %multiply_convert_fusion = (bf16[1024,1024]{0,1:T(8,128)(2,1)S(1)}, bf16[1024,1024]{0,1:T(8,128)(2,1)S(1)}) fusion(f32[1024,1024]{0,1:T(8,128)} %fusion.2, f32[1024,1024]{0,1:T(8,128)} %get-tuple-element.119, bf16[1024,2048]{1,0:T(8,128)(2,1)} %join_halves.5, bf16[2048,1024]{1,0:T(8,128)(2,1)} %all-gather.11.cloned.1.call-done), kind=kOutput, calls=%fused_computation.15 | convolution fusion | flops 4308598784 | bytes 20971520 | tf_op jit(solution)/shard_map/dot_general | solution.py:24
  368.7 8.7 %convolution_convert_fusion.6 = bf16[512,2048]{1,0:T(8,128)(2,1)S(1)} fusion(bf16[2048,2048]{1,0:T(8,128)(2,1)} %all-gather.9.cloned.1.call-done, bf16[1024,1024]{0,1:T(8,128)(2,1)S(1)} %get-tuple-element.76, bf16[1024,1024]{0,1:T(8,128)(2,1)S(1)} %get-tuple-element.75), kind=kOutput, calls=%fused_computation.27 | convolution fusion | flops 4300210176 | bytes 14680064 | tf_op jit(solution)/shard_map/second_grad_collect/dot_general | solution.py:28
  377.4 4.1 collective-permute-done.21
  381.6 8.4 %add_convert_fusion.2 = bf16[512,2048]{1,0:T(8,128)(2,1)S(1)} fusion(bf16[512,2048]{1,0:T(8,128)(2,1)S(1)} %collective-permute-done.21, bf16[2048,2048]{1,0:T(8,128)(2,1)} %all-gather.9.cloned.1.call-done, bf16[1024,1024]{0,1:T(8,128)(2,1)S(1)} %get-tuple-element.76, bf16[1024,1024]{0,1:T(8,128)(2,1)S(1)} %get-tuple-element.75), kind=kOutput, calls=%fused_computation.14 | convolution fusion | flops 4302307328 | bytes 16777216 | tf_op jit(solution)/shard_map/second_grad_collect/dot_general | solution.py:28
  394.0 12.6 %convolution_convert_fusion = bf16[2048,2048]{1,0:T(8,128)(2,1)} fusion(bf16[1024,2048]{1,0:T(8,128)(2,1)S(1)} %copy-done.15, bf16[1024,1024]{0,1:T(8,128)(2,1)S(1)} %get-tuple-element.75, bf16[1024,1024]{0,1:T(8,128)(2,1)S(1)} %get-tuple-element.76), kind=kOutput, calls=%fused_computation | convolution fusion | flops 8602517504 | bytes 16777216 | tf_op jit(solution)/shard_map/dot_general | solution.py:32
  406.8 27.1 %reduce-scatter.4.cloned.1.call-done = bf16[512,1024]{1,0:T(8,128)(2,1)} async-done(((bf16[2048,1024]{1,0:T(8,128)(2,1)}), bf16[512,1024]{1,0:T(8,128)(2,1)}) %reduce-scatter.4.cloned.1.call-update) | async-done | bytes 1048592 | tf_op jit(solution)/shard_map/down_back/reduce_scatter | solution.py:168
  436.9 12.1 %collective-permute-done.23 = bf16[128,2048]{1,0:T(8,128)(2,1)S(1)} collective-permute-done((bf16[128,2048]{1,0:T(8,128)(2,1)}, bf16[128,2048]{1,0:T(8,128)(2,1)S(1)}, u32[]{:S(2)}, u32[]{:S(2)}) %collective-permute-start.23) | collective-permute-done | bytes 524320 | tf_op jit(solution)/shard_map/second_grad_collect/ppermute | solution.py:49
  449.0 11.0 %collective-permute-done.24 = bf16[128,2048]{1,0:T(8,128)(2,1)S(1)} collective-permute-done((bf16[128,2048]{1,0:T(8,128)(2,1)}, bf16[128,2048]{1,0:T(8,128)(2,1)S(1)}, u32[]{:S(2)}, u32[]{:S(2)}) %collective-permute-start.24) | collective-permute-done | bytes 524320 | tf_op jit(solution)/shard_map/second_grad_collect/ppermute | solution.py:49
  462.1 3.5 fusion.41
  469.1 10.5 %collective-permute-done.25 = bf16[128,2048]{1,0:T(8,128)(2,1)S(1)} collective-permute-done((bf16[128,2048]{1,0:T(8,128)(2,1)S(1)}, bf16[128,2048]{1,0:T(8,128)(2,1)S(1)}, u32[]{:S(2)}, u32[]{:S(2)}) %collective-permute-start.25) | collective-permute-done | bytes 524320 | tf_op jit(solution)/shard_map/branch_grad_spread/ppermute | solution.py:49
  481.0 10.0 %collective-permute-done.27 = bf16[128,2048]{1,0:T(8,128)(2,1)S(1)} collective-permute-done((bf16[128,2048]{1,0:T(8,128)(2,1)S(1)}, bf16[128,2048]{1,0:T(8,128)(2,1)S(1)}, u32[]{:S(2)}, u32[]{:S(2)}) %collective-permute-start.27) | collective-permute-done | bytes 524320 | tf_op jit(solution)/shard_map/branch_grad_spread/ppermute | solution.py:49
  491.3 3.7 convolution_convert_fusion.3
  495.5 7.1 %join_halves.7 = bf16[1024,2048]{1,0:T(8,128)(2,1)} custom-call(bf16[512,2048]{1,0:T(8,128)(2,1)} %copy-done.10, bf16[512,2048]{1,0:T(8,128)(2,1)} %collective-permute-done.28.far_ref), custom_call_target="tpu_custom_call" | custom-call | bytes 8388608 | tf_op jit(solution)/shard_map/branch_grad_spread/join_halves/pallas_call | solution.py:68
  502.7 3.9 convolution_convert_fusion.8.grad_ref
  506.6 12.6 %attend_back.1 = bf16[1024,768]{1,0:T(8,128)(2,1)} custom-call(s32[4]{0:T(128)S(1)} %pad_add_fusion.info_ref, bf16[1024,256]{1,0:T(8,128)(2,1)S(1)} %get-tuple-element.28.q_row, bf16[1024,256]{1,0:T(8,128)(2,1)S(1)} %copy-done.1, bf16[1024,256]{1,0:T(8,128)(2,1)S(1)} %copy-done.3, f32[1024,256]{1,0:T(8,128)S(1)} %get-tuple-element.31.log_ref, ...), custom_call_target="tpu_custom_call" | custom-call | flops 2684354560 | bytes 5242880 | tf_op jit(solution)/shard_map/attend_back/pallas_call | solution.py:406
  519.2 4.4 convolution_convert_fusion.5
  523.9 4.2 add_convert_fusion
  531.8 5.0 convolution_convert_fusion.2
  536.8 5.7 collective-permute-done.31
  543.5 11.4 %collective-permute-done.33 = bf16[128,2048]{1,0:T(8,128)(2,1)S(1)} collective-permute-done((bf16[128,2048]{1,0:T(8,128)(2,1)S(1)}, bf16[128,2048]{1,0:T(8,128)(2,1)S(1)}, u32[]{:S(2)}, u32[]{:S(2)}) %collective-permute-start.33) | collective-permute-done | bytes 524320 | tf_op jit(solution)/shard_map/feed_collect/ppermute | solution.py:49
  555.2 3.6 all-to-all-start.2
  558.9 5.9 add_convert_fusion.1
  564.8 7.3 %all-to-all-done.2 = bf16[2,256,1024]{2,1,0:T(8,128)(2,1)S(1)} async-done(((bf16[2,256,1024]{2,1,0:T(8,128)(2,1)}), bf16[2,256,1024]{2,1,0:T(8,128)(2,1)S(1)}, u32[]{:S(2)}, u32[]{:S(2)}) %all-to-all-start.2) | async-done | bytes 1048608 | tf_op jit(solution)/shard_map/down_return/all_to_all | solution.py:142
  583.1 7.0 collective-permute-done.34
  592.1 8.7 %collective-permute-done.36 = bf16[128,2048]{1,0:T(8,128)(2,1)} collective-permute-done((bf16[128,2048]{1,0:T(8,128)(2,1)}, bf16[128,2048]{1,0:T(8,128)(2,1)}, u32[]{:S(2)}, u32[]{:S(2)}) %collective-permute-start.36) | collective-permute-done | bytes 524320 | tf_op jit(solution)/shard_map/first_grad_collect/ppermute | solution.py:49
  600.9 2.8 fusion.21
  604.5 3.1 collective-permute-done.37
  612.6 3.0 collective-permute-start.40
  615.6 5.1 all-to-all-start.3
  624.9 21.1 %all-to-all-done.3 = bf16[2,256,2048]{2,1,0:T(8,128)(2,1)} async-done(((bf16[2,256,2048]{2,1,0:T(8,128)(2,1)}), bf16[2,256,2048]{2,1,0:T(8,128)(2,1)}, u32[]{:S(2)}, u32[]{:S(2)}) %all-to-all-start.3) | async-done | bytes 2097184 | tf_op jit(solution)/shard_map/gate_up_return/all_to_all | solution.py:142
  651.5 28.7 %reduce-scatter.8.cloned.1.call-done = bf16[512,1024]{0,1:T(8,128)(2,1)} async-done(((bf16[2048,1024]{0,1:T(8,128)(2,1)}), bf16[512,1024]{0,1:T(8,128)(2,1)}) %reduce-scatter.8.cloned.1.call-update) | async-done | bytes 1048592 | tf_op jit(solution)/shard_map/attention_back/reduce_scatter | solution.py:168
  682.5 3.6 all-to-all-start.4
  686.0 7.4 %copy.46 = f32[256,2,2048]{2,1,0:T(2,128)} copy(f32[256,2,2048]{2,0,1:T(8,128)} %pad_maximum_fusion.3) | data formatting | bytes 8388608
  693.5 6.5 all-to-all-done.4
  (240 shorter events, 113.8 us)
Async XLA Ops:
  7.2 7.9 %collective-permute-start = (f32[2,64]{1,0:T(2,128)}, f32[2,64]{1,0:T(2,128)S(1)}, u32[]{:S(2)}, u32[]{:S(2)}) collective-permute-start(f32[2,64]{1,0:T(2,128)} %param.15), channel_id=1, source_target_pairs={{0,1},{1,0},{2,3},{3,2},{4,5},{5,4},{6,7},{7,6},{8,9},{9,8},{10,11... | collective-permute-start | bytes 1544 | tf_op jit(solution)/shard_map/gain_gather/ppermute | solution.py:49
  10.3 23.4 %copy-start.6 = (bf16[1,128,2048]{2,1,0:T(8,128)(2,1)S(1)}, bf16[1,128,2048]{2,1,0:T(8,128)(2,1)}, u32[]{:S(2)}) copy-start(bf16[1,128,2048]{2,1,0:T(8,128)(2,1)} %param.9) | copy-start | bytes 1572868
  11.3 18.9 %all-to-all-start = ((bf16[2,256,1024]{1,2,0:T(8,128)(2,1)}), bf16[2,256,1024]{1,2,0:T(8,128)(2,1)S(1)}, u32[]{:S(2)}, u32[]{:S(2)}) async-start(bf16[2,256,1024]{1,2,0:T(8,128)(2,1)} %pad_maximum_fusion.10), calls=%async_computation | async-start | bytes 2097152 | tf_op jit(solution)/shard_map/attention_weights/all_to_all | solution.py:142
  15.1 80.9 %all-gather.5.cloned.1.call-start = ((), (), s32[]{:S(2)}) async-start(), calls=%async_computation.8 | async-start | bytes 3932160 | tf_op jit(solution)/shard_map/qkv_gather/all_gather | solution.py:164
  15.2 4.0 collective-permute-start.1
  19.2 12.5 %collective-permute-start.2 = (f32[2,256]{1,0:T(2,128)S(1)}, f32[2,256]{1,0:T(2,128)S(1)}, u32[]{:S(2)}, u32[]{:S(2)}) collective-permute-start(f32[2,256]{1,0:T(2,128)S(1)} %pad_maximum_fusion.17), channel_id=1, source_target_pairs={{0,4},{4,0},{1,5},{5,1},{2,6},{6,2},{3,7},{7,3},{8,12},{12,8},{9,1... | collective-permute-start | bytes 6152 | tf_op jit(solution)/shard_map/gain_gather/ppermute | solution.py:49
  31.7 3.7 collective-permute-start.3
  35.4 4.6 collective-permute-start.4
  38.3 32.1 %copy-start.27 = (f32[128]{0:T(128)}, f32[128]{0:T(128)S(1)}, u32[]{:S(2)}) copy-start(f32[128]{0:T(128)S(1)} %add_rsqrt_fusion.1) | copy-start | bytes 1540
  40.9 25.5 %copy-start.22 = (bf16[256,2,2048]{2,1,0:T(2,128)(2,1)S(1)}, bf16[256,2,2048]{2,1,0:T(2,128)(2,1)}, u32[]{:S(2)}) copy-start(bf16[256,2,2048]{2,1,0:T(2,128)(2,1)} %param.13) | copy-start | bytes 6291460
  40.9 14.0 %collective-permute-start.5 = (bf16[128,2048]{1,0:T(8,128)(2,1)S(1)}, bf16[128,2048]{1,0:T(8,128)(2,1)S(1)}, u32[]{:S(2)}, u32[]{:S(2)}) collective-permute-start(bf16[128,2048]{1,0:T(8,128)(2,1)S(1)} %fusion.16), channel_id=1, source_target_pairs={{0,2},{1,3},{2,0},{3,1},{4,6},{5,7},{6,4},{7,5},{8,10},{9,11},{10,... | collective-permute-start | bytes 1572872 | tf_op jit(solution)/shard_map/first_spread/ppermute | solution.py:49
  42.7 14.9 %collective-permute-start.6 = (bf16[128,2048]{1,0:T(8,128)(2,1)S(1)}, bf16[128,2048]{1,0:T(8,128)(2,1)S(1)}, u32[]{:S(2)}, u32[]{:S(2)}) collective-permute-start(bf16[128,2048]{1,0:T(8,128)(2,1)S(1)} %fusion.16), channel_id=1, source_target_pairs={{0,4},{1,5},{2,6},{3,7},{4,0},{5,1},{6,2},{7,3},{8,12},{9,13},{10,... | collective-permute-start | bytes 1572872 | tf_op jit(solution)/shard_map/first_spread/ppermute | solution.py:49
  43.0 21.8 %collective-permute-start.7 = (bf16[128,2048]{1,0:T(8,128)(2,1)S(1)}, bf16[128,2048]{1,0:T(8,128)(2,1)S(1)}, u32[]{:S(2)}, u32[]{:S(2)}) collective-permute-start(bf16[128,2048]{1,0:T(8,128)(2,1)S(1)} %fusion.16), channel_id=1, source_target_pairs={{0,6},{1,7},{2,4},{3,5},{4,2},{5,3},{6,0},{7,1},{8,14},{9,15},{10,... | collective-permute-start | bytes 1572872 | tf_op jit(solution)/shard_map/first_spread/ppermute | solution.py:49
  66.4 17.2 %collective-permute-start.8 = (bf16[512,2048]{1,0:T(8,128)(2,1)}, bf16[512,2048]{1,0:T(8,128)(2,1)}, u32[]{:S(2)}, u32[]{:S(2)}) collective-permute-start(bf16[512,2048]{1,0:T(8,128)(2,1)} %pad_maximum_fusion.5.near_ref), channel_id=1, source_target_pairs={{0,1},{1,0},{2,3},{3,2},{4,5},{5,4},{6,7},{7,6},{8,9},{9,8},{10,11... | collective-permute-start | bytes 6291464 | tf_op jit(solution)/shard_map/first_spread/ppermute | solution.py:49
  77.5 42.3 %all-to-all-start.1 = ((bf16[2,256,3072]{1,2,0:T(8,128)(2,1)}), bf16[2,256,3072]{1,2,0:T(8,128)(2,1)}, u32[]{:S(2)}, u32[]{:S(2)}) async-start(bf16[2,256,3072]{1,2,0:T(8,128)(2,1)} %pad_maximum_fusion.4), calls=%async_computation.1 | async-start | bytes 6291456 | tf_op jit(solution)/shard_map/feed_weights/all_to_all | solution.py:142
  82.8 42.0 %all-gather.7.cloned.1.call-start = ((), (), s32[]{:S(2)}) async-start(), calls=%async_computation.9 | async-start | bytes 1310720 | tf_op jit(solution)/shard_map/out_gather/all_gather | solution.py:164
  96.0 179.5 %all-gather.9.cloned.1.call-start = ((), (), s32[]{:S(2)}) async-start(), calls=%async_computation.10 | async-start | bytes 10485760 | tf_op jit(solution)/shard_map/gate_up_gather/all_gather | solution.py:164
  124.8 231.7 %all-gather.11.cloned.1.call-start = ((), (), s32[]{:S(2)}) async-start(), calls=%async_computation.11 | async-start | bytes 5242880 | tf_op jit(solution)/shard_map/down_gather/all_gather | solution.py:164
  151.1 32.7 %copy-start.7 = (bf16[1,128,2048]{2,1,0:T(8,128)(2,1)S(1)}, bf16[1,128,2048]{2,1,0:T(8,128)(2,1)}, u32[]{:S(2)}) copy-start(bf16[1,128,2048]{2,1,0:T(8,128)(2,1)} %param.9) | copy-start | bytes 1572868
  151.1 4.2 collective-permute-start.9
  156.2 15.6 %collective-permute-start.10 = (bf16[128,2048]{1,0:T(8,128)(2,1)S(1)}, bf16[128,2048]{1,0:T(8,128)(2,1)S(1)}, u32[]{:S(2)}, u32[]{:S(2)}) collective-permute-start(bf16[128,2048]{1,0:T(8,128)(2,1)S(1)} %get-tuple-element.100), channel_id=1, source_target_pairs={{0,2},{1,3},{2,0},{3,1},{4,6},{5,7},{6,4},{7,5},{8,10},{9,11},{10,... | collective-permute-start | bytes 1572872 | tf_op jit(solution)/shard_map/branch_collect/ppermute | solution.py:49
  157.8 16.3 %collective-permute-start.11 = (bf16[128,2048]{1,0:T(8,128)(2,1)S(1)}, bf16[128,2048]{1,0:T(8,128)(2,1)S(1)}, u32[]{:S(2)}, u32[]{:S(2)}) collective-permute-start(bf16[128,2048]{1,0:T(8,128)(2,1)S(1)} %get-tuple-element.102), channel_id=1, source_target_pairs={{0,4},{1,5},{2,6},{3,7},{4,0},{5,1},{6,2},{7,3},{8,12},{9,13},{10,... | collective-permute-start | bytes 1572872 | tf_op jit(solution)/shard_map/branch_collect/ppermute | solution.py:49
  159.1 24.7 %collective-permute-start.12 = (bf16[128,2048]{1,0:T(8,128)(2,1)S(1)}, bf16[128,2048]{1,0:T(8,128)(2,1)S(1)}, u32[]{:S(2)}, u32[]{:S(2)}) collective-permute-start(bf16[128,2048]{1,0:T(8,128)(2,1)S(1)} %get-tuple-element.101), channel_id=1, source_target_pairs={{0,6},{1,7},{2,4},{3,5},{4,2},{5,3},{6,0},{7,1},{8,14},{9,15},{10,... | collective-permute-start | bytes 1572872 | tf_op jit(solution)/shard_map/branch_collect/ppermute | solution.py:49
  159.7 34.5 %collective-permute-start.13 = (bf16[128,2048]{1,0:T(8,128)(2,1)S(1)}, bf16[128,2048]{1,0:T(8,128)(2,1)S(1)}, u32[]{:S(2)}, u32[]{:S(2)}) collective-permute-start(bf16[128,2048]{1,0:T(8,128)(2,1)S(1)} %bitcast.138), channel_id=1, source_target_pairs={{0,2},{1,3},{2,0},{3,1},{4,6},{5,7},{6,4},{7,5},{8,10},{9,11},{10,... | collective-permute-start | bytes 1572872 | tf_op jit(solution)/shard_map/cotangent_spread/ppermute | solution.py:49
  161.3 35.2 %collective-permute-start.14 = (bf16[128,2048]{1,0:T(8,128)(2,1)S(1)}, bf16[128,2048]{1,0:T(8,128)(2,1)S(1)}, u32[]{:S(2)}, u32[]{:S(2)}) collective-permute-start(bf16[128,2048]{1,0:T(8,128)(2,1)S(1)} %bitcast.139), channel_id=1, source_target_pairs={{0,4},{1,5},{2,6},{3,7},{4,0},{5,1},{6,2},{7,3},{8,12},{9,13},{10,... | collective-permute-start | bytes 1572872 | tf_op jit(solution)/shard_map/cotangent_spread/ppermute | solution.py:49
  171.8 34.6 %collective-permute-start.15 = (bf16[128,2048]{1,0:T(8,128)(2,1)S(1)}, bf16[128,2048]{1,0:T(8,128)(2,1)S(1)}, u32[]{:S(2)}, u32[]{:S(2)}) collective-permute-start(bf16[128,2048]{1,0:T(8,128)(2,1)S(1)} %bitcast.140), channel_id=1, source_target_pairs={{0,6},{1,7},{2,4},{3,5},{4,2},{5,3},{6,0},{7,1},{8,14},{9,15},{10,... | collective-permute-start | bytes 1572872 | tf_op jit(solution)/shard_map/cotangent_spread/ppermute | solution.py:49
  185.5 29.7 %collective-permute-start.17 = (bf16[128,2048]{1,0:T(8,128)(2,1)S(1)}, bf16[128,2048]{1,0:T(8,128)(2,1)S(1)}, u32[]{:S(2)}, u32[]{:S(2)}) collective-permute-start(bf16[128,2048]{1,0:T(8,128)(2,1)S(1)} %multiply_convert_fusion.3), channel_id=1, source_target_pairs={{0,2},{1,3},{2,0},{3,1},{4,6},{5,7},{6,4},{7,5},{8,10},{9,11},{10,... | collective-permute-start | bytes 1572872 | tf_op jit(solution)/shard_map/second_spread/ppermute | solution.py:49
  187.1 30.5 %collective-permute-start.18 = (bf16[128,2048]{1,0:T(8,128)(2,1)S(1)}, bf16[128,2048]{1,0:T(8,128)(2,1)S(1)}, u32[]{:S(2)}, u32[]{:S(2)}) collective-permute-start(bf16[128,2048]{1,0:T(8,128)(2,1)S(1)} %multiply_convert_fusion.3), channel_id=1, source_target_pairs={{0,4},{1,5},{2,6},{3,7},{4,0},{5,1},{6,2},{7,3},{8,12},{9,13},{10,... | collective-permute-start | bytes 1572872 | tf_op jit(solution)/shard_map/second_spread/ppermute | solution.py:49
  194.2 33.5 %collective-permute-start.19 = (bf16[128,2048]{1,0:T(8,128)(2,1)S(1)}, bf16[128,2048]{1,0:T(8,128)(2,1)S(1)}, u32[]{:S(2)}, u32[]{:S(2)}) collective-permute-start(bf16[128,2048]{1,0:T(8,128)(2,1)S(1)} %multiply_convert_fusion.3), channel_id=1, source_target_pairs={{0,6},{1,7},{2,4},{3,5},{4,2},{5,3},{6,0},{7,1},{8,14},{9,15},{10,... | collective-permute-start | bytes 1572872 | tf_op jit(solution)/shard_map/second_spread/ppermute | solution.py:49
  207.9 23.6 %collective-permute-start.16 = (bf16[512,2048]{1,0:T(8,128)(2,1)}, bf16[512,2048]{1,0:T(8,128)(2,1)}, u32[]{:S(2)}, u32[]{:S(2)}) collective-permute-start(bf16[512,2048]{1,0:T(8,128)(2,1)} %pad_maximum_fusion.6.near_ref), channel_id=1, source_target_pairs={{0,1},{1,0},{2,3},{3,2},{4,5},{5,4},{6,7},{7,6},{8,9},{9,8},{10,11... | collective-permute-start | bytes 6291464 | tf_op jit(solution)/shard_map/cotangent_spread/ppermute | solution.py:49
  229.2 9.4 %collective-permute-start.20 = (bf16[512,2048]{1,0:T(8,128)(2,1)}, bf16[512,2048]{1,0:T(8,128)(2,1)}, u32[]{:S(2)}, u32[]{:S(2)}) collective-permute-start(bf16[512,2048]{1,0:T(8,128)(2,1)} %pad_maximum_fusion.7.near_ref), channel_id=1, source_target_pairs={{0,1},{1,0},{2,3},{3,2},{4,5},{5,4},{6,7},{7,6},{8,9},{9,8},{10,11... | collective-permute-start | bytes 6291464 | tf_op jit(solution)/shard_map/second_spread/ppermute | solution.py:49
  275.4 158.5 %reduce-scatter.4.cloned.1.call-start = ((), (), s32[]{:S(2)}) async-start(), calls=%async_computation.12 | async-start | bytes 5242880 | tf_op jit(solution)/shard_map/down_back/reduce_scatter | solution.py:168
  356.5 247.2 %reduce-scatter.6.cloned.1.call-start = ((), (), s32[]{:S(2)}) async-start(), calls=%async_computation.13 | async-start | bytes 10485760 | tf_op jit(solution)/shard_map/gate_up_back/reduce_scatter | solution.py:168
  377.3 4.2 collective-permute-start.21
  392.5 14.3 %collective-permute-start.22 = (bf16[128,2048]{1,0:T(8,128)(2,1)}, bf16[128,2048]{1,0:T(8,128)(2,1)}, u32[]{:S(2)}, u32[]{:S(2)}) collective-permute-start(bf16[128,2048]{1,0:T(8,128)(2,1)} %get-tuple-element.97), channel_id=1, source_target_pairs={{0,2},{1,3},{2,0},{3,1},{4,6},{5,7},{6,4},{7,5},{8,10},{9,11},{10,... | collective-permute-start | bytes 1572872 | tf_op jit(solution)/shard_map/second_grad_collect/ppermute | solution.py:49
  433.9 15.1 %collective-permute-start.23 = (bf16[128,2048]{1,0:T(8,128)(2,1)}, bf16[128,2048]{1,0:T(8,128)(2,1)S(1)}, u32[]{:S(2)}, u32[]{:S(2)}) collective-permute-start(bf16[128,2048]{1,0:T(8,128)(2,1)} %get-tuple-element.99), channel_id=1, source_target_pairs={{0,4},{1,5},{2,6},{3,7},{4,0},{5,1},{6,2},{7,3},{8,12},{9,13},{10,... | collective-permute-start | bytes 1572872 | tf_op jit(solution)/shard_map/second_grad_collect/ppermute | solution.py:49
  435.5 24.6 %collective-permute-start.24 = (bf16[128,2048]{1,0:T(8,128)(2,1)}, bf16[128,2048]{1,0:T(8,128)(2,1)S(1)}, u32[]{:S(2)}, u32[]{:S(2)}) collective-permute-start(bf16[128,2048]{1,0:T(8,128)(2,1)} %get-tuple-element.98), channel_id=1, source_target_pairs={{0,6},{1,7},{2,4},{3,5},{4,2},{5,3},{6,0},{7,1},{8,14},{9,15},{10,... | collective-permute-start | bytes 1572872 | tf_op jit(solution)/shard_map/second_grad_collect/ppermute | solution.py:49
  462.1 29.2 %copy-start.32 = (bf16[2048,1024]{1,0:T(8,128)(2,1)S(1)}, bf16[2048,1024]{1,0:T(8,128)(2,1)}, u32[]{:S(2)}) copy-start(bf16[2048,1024]{1,0:T(8,128)(2,1)} %all-gather.11.cloned.1.call-done) | copy-start | bytes 12582916
  462.1 29.2 %copy-start.37 = (bf16[1024,1024]{0,1:T(8,128)(2,1)S(1)}, bf16[1024,1024]{0,1:T(8,128)(2,1)}, u32[]{:S(2)}) copy-start(bf16[1024,1024]{0,1:T(8,128)(2,1)} %get-tuple-element.35) | copy-start | bytes 6291460
  465.6 14.0 %collective-permute-start.25 = (bf16[128,2048]{1,0:T(8,128)(2,1)S(1)}, bf16[128,2048]{1,0:T(8,128)(2,1)S(1)}, u32[]{:S(2)}, u32[]{:S(2)}) collective-permute-start(bf16[128,2048]{1,0:T(8,128)(2,1)S(1)} %get-tuple-element.71), channel_id=1, source_target_pairs={{0,2},{1,3},{2,0},{3,1},{4,6},{5,7},{6,4},{7,5},{8,10},{9,11},{10,... | collective-permute-start | bytes 1572872 | tf_op jit(solution)/shard_map/branch_grad_spread/ppermute | solution.py:49
  466.1 14.9 %collective-permute-start.26 = (bf16[128,2048]{1,0:T(8,128)(2,1)S(1)}, bf16[128,2048]{1,0:T(8,128)(2,1)S(1)}, u32[]{:S(2)}, u32[]{:S(2)}) collective-permute-start(bf16[128,2048]{1,0:T(8,128)(2,1)S(1)} %get-tuple-element.71), channel_id=1, source_target_pairs={{0,4},{1,5},{2,6},{3,7},{4,0},{5,1},{6,2},{7,3},{8,12},{9,13},{10,... | collective-permute-start | bytes 1572872 | tf_op jit(solution)/shard_map/branch_grad_spread/ppermute | solution.py:49
  467.6 23.3 %collective-permute-start.27 = (bf16[128,2048]{1,0:T(8,128)(2,1)S(1)}, bf16[128,2048]{1,0:T(8,128)(2,1)S(1)}, u32[]{:S(2)}, u32[]{:S(2)}) collective-permute-start(bf16[128,2048]{1,0:T(8,128)(2,1)S(1)} %get-tuple-element.71), channel_id=1, source_target_pairs={{0,6},{1,7},{2,4},{3,5},{4,2},{5,3},{6,0},{7,1},{8,14},{9,15},{10,... | collective-permute-start | bytes 1572872 | tf_op jit(solution)/shard_map/branch_grad_spread/ppermute | solution.py:49
  491.2 4.4 collective-permute-start.28
  495.0 28.8 %collective-permute-start.30 = (bf16[512,2048]{1,0:T(8,128)(2,1)}, bf16[512,2048]{1,0:T(8,128)(2,1)}, u32[]{:S(2)}, u32[]{:S(2)}) collective-permute-start(bf16[512,2048]{1,0:T(8,128)(2,1)} %convolution_convert_fusion.3), channel_id=1, source_target_pairs={{0,1},{1,0},{2,3},{3,2},{4,5},{5,4},{6,7},{7,6},{8,9},{9,8},{10,11... | collective-permute-start | bytes 6291464 | tf_op jit(solution)/shard_map/feed_collect/ppermute | solution.py:49
  523.7 35.2 %collective-permute-start.29 = (bf16[512,2048]{1,0:T(8,128)(2,1)}, bf16[512,2048]{1,0:T(8,128)(2,1)}, u32[]{:S(2)}, u32[]{:S(2)}) collective-permute-start(bf16[512,2048]{1,0:T(8,128)(2,1)} %convolution_convert_fusion.5), channel_id=1, source_target_pairs={{0,1},{1,0},{2,3},{3,2},{4,5},{5,4},{6,7},{7,6},{8,9},{9,8},{10,11... | collective-permute-start | bytes 6291464 | tf_op jit(solution)/shard_map/first_grad_collect/ppermute | solution.py:49
  528.3 14.3 %collective-permute-start.31 = (bf16[128,2048]{1,0:T(8,128)(2,1)S(1)}, bf16[128,2048]{1,0:T(8,128)(2,1)S(1)}, u32[]{:S(2)}, u32[]{:S(2)}) collective-permute-start(bf16[128,2048]{1,0:T(8,128)(2,1)S(1)} %get-tuple-element.94), channel_id=1, source_target_pairs={{0,2},{1,3},{2,0},{3,1},{4,6},{5,7},{6,4},{7,5},{8,10},{9,11},{10,... | collective-permute-start | bytes 1572872 | tf_op jit(solution)/shard_map/feed_collect/ppermute | solution.py:49
  528.8 14.8 %collective-permute-start.32 = (bf16[128,2048]{1,0:T(8,128)(2,1)S(1)}, bf16[128,2048]{1,0:T(8,128)(2,1)S(1)}, u32[]{:S(2)}, u32[]{:S(2)}) collective-permute-start(bf16[128,2048]{1,0:T(8,128)(2,1)S(1)} %get-tuple-element.96), channel_id=1, source_target_pairs={{0,4},{1,5},{2,6},{3,7},{4,0},{5,1},{6,2},{7,3},{8,12},{9,13},{10,... | collective-permute-start | bytes 1572872 | tf_op jit(solution)/shard_map/feed_collect/ppermute | solution.py:49
  530.2 24.7 %collective-permute-start.33 = (bf16[128,2048]{1,0:T(8,128)(2,1)S(1)}, bf16[128,2048]{1,0:T(8,128)(2,1)S(1)}, u32[]{:S(2)}, u32[]{:S(2)}) collective-permute-start(bf16[128,2048]{1,0:T(8,128)(2,1)S(1)} %get-tuple-element.95), channel_id=1, source_target_pairs={{0,6},{1,7},{2,4},{3,5},{4,2},{5,3},{6,0},{7,1},{8,14},{9,15},{10,... | collective-permute-start | bytes 1572872 | tf_op jit(solution)/shard_map/feed_collect/ppermute | solution.py:49
  555.2 16.9 %all-to-all-start.2 = ((bf16[2,256,1024]{2,1,0:T(8,128)(2,1)}), bf16[2,256,1024]{2,1,0:T(8,128)(2,1)S(1)}, u32[]{:S(2)}, u32[]{:S(2)}) async-start(bf16[2,256,1024]{2,1,0:T(8,128)(2,1)} %bitcast.142), calls=%async_computation.3 | async-start | bytes 2097152 | tf_op jit(solution)/shard_map/down_return/all_to_all | solution.py:142
  558.8 121.3 %reduce-scatter.8.cloned.1.call-start = ((), (), s32[]{:S(2)}) async-start(), calls=%async_computation.14 | async-start | bytes 5242880 | tf_op jit(solution)/shard_map/attention_back/reduce_scatter | solution.py:168
  575.9 14.2 %collective-permute-start.34 = (bf16[128,2048]{1,0:T(8,128)(2,1)}, bf16[128,2048]{1,0:T(8,128)(2,1)S(1)}, u32[]{:S(2)}, u32[]{:S(2)}) collective-permute-start(bf16[128,2048]{1,0:T(8,128)(2,1)} %get-tuple-element.89), channel_id=1, source_target_pairs={{0,2},{1,3},{2,0},{3,1},{4,6},{5,7},{6,4},{7,5},{8,10},{9,11},{10,... | collective-permute-start | bytes 1572872 | tf_op jit(solution)/shard_map/first_grad_collect/ppermute | solution.py:49
  577.0 15.2 %collective-permute-start.35 = (bf16[128,2048]{1,0:T(8,128)(2,1)}, bf16[128,2048]{1,0:T(8,128)(2,1)}, u32[]{:S(2)}, u32[]{:S(2)}) collective-permute-start(bf16[128,2048]{1,0:T(8,128)(2,1)} %get-tuple-element.91), channel_id=1, source_target_pairs={{0,4},{1,5},{2,6},{3,7},{4,0},{5,1},{6,2},{7,3},{8,12},{9,13},{10,... | collective-permute-start | bytes 1572872 | tf_op jit(solution)/shard_map/first_grad_collect/ppermute | solution.py:49
  577.2 23.6 %collective-permute-start.36 = (bf16[128,2048]{1,0:T(8,128)(2,1)}, bf16[128,2048]{1,0:T(8,128)(2,1)}, u32[]{:S(2)}, u32[]{:S(2)}) collective-permute-start(bf16[128,2048]{1,0:T(8,128)(2,1)} %get-tuple-element.90), channel_id=1, source_target_pairs={{0,6},{1,7},{2,4},{3,5},{4,2},{5,3},{6,0},{7,1},{8,14},{9,15},{10,... | collective-permute-start | bytes 1572872 | tf_op jit(solution)/shard_map/first_grad_collect/ppermute | solution.py:49
  580.7 20.2 %copy-start.8 = (bf16[1,128,2048]{2,1,0:T(8,128)(2,1)S(1)}, bf16[1,128,2048]{2,1,0:T(8,128)(2,1)}, u32[]{:S(2)}) copy-start(bf16[1,128,2048]{2,1,0:T(8,128)(2,1)} %param.9) | copy-start | bytes 1572868
  580.7 20.2 %copy-start.26 = (f32[1,2048]{1,0:T(1,128)S(1)}, f32[1,2048]{1,0:T(1,128)}, u32[]{:S(2)}) copy-start(f32[1,2048]{1,0:T(1,128)} %copy-done.25) | copy-start | bytes 24580
  580.7 20.1 %copy-start.28 = (f32[128]{0:T(128)S(1)}, f32[128]{0:T(128)}, u32[]{:S(2)}) copy-start(f32[128]{0:T(128)} %copy-done.27) | copy-start | bytes 1540
  583.1 28.3 %copy-start.5 = (f32[128,2048]{1,0:T(8,128)S(1)}, f32[128,2048]{1,0:T(8,128)}, u32[]{:S(2)}) copy-start(f32[128,2048]{1,0:T(8,128)} %copy-done.4) | copy-start | bytes 3145732
  603.9 3.7 collective-permute-start.37
  607.6 3.7 collective-permute-start.38
  611.3 1.2 collective-permute-start.39
  612.6 8.1 %collective-permute-start.40 = (f32[2,128]{1,0:T(2,128)S(1)}, f32[2,128]{1,0:T(2,128)S(1)}, u32[]{:S(2)}, u32[]{:S(2)}) collective-permute-start(f32[2,128]{1,0:T(2,128)S(1)} %broadcast_select_fusion.9), channel_id=1, source_target_pairs={{0,16},{8,24},{16,0},{24,8},{1,17},{9,25},{17,1},{25,9},{2,18},{10... | collective-permute-start | bytes 3080 | tf_op jit(solution)/shard_map/gain_scatter/ppermute | solution.py:49
  615.6 30.4 %all-to-all-start.3 = ((bf16[2,256,2048]{2,1,0:T(8,128)(2,1)}), bf16[2,256,2048]{2,1,0:T(8,128)(2,1)}, u32[]{:S(2)}, u32[]{:S(2)}) async-start(bf16[2,256,2048]{2,1,0:T(8,128)(2,1)} %bitcast.136), calls=%async_computation.6 | async-start | bytes 4194304 | tf_op jit(solution)/shard_map/gate_up_return/all_to_all | solution.py:142
  620.7 3.6 collective-permute-start.41
  682.5 17.5 %all-to-all-start.4 = ((bf16[2,256,1024]{2,1,0:T(8,128)(2,1)}), bf16[2,256,1024]{2,1,0:T(8,128)(2,1)S(1)}, u32[]{:S(2)}, u32[]{:S(2)}) async-start(bf16[2,256,1024]{2,1,0:T(8,128)(2,1)} %bitcast.40), calls=%async_computation.7 | async-start | bytes 2097152 | tf_op jit(solution)/shard_map/attention_return/all_to_all | solution.py:142
  (29 other events, 186.0 us)
Sparse Core Ops, SparseCore 0:
  31.8 64.0 all-gather.4
  98.1 26.5 all-gather.6
  126.3 149.1 all-gather.8
  277.4 78.9 all-gather.10
  358.6 75.2 reduce-scatter.3
  436.2 144.9 reduce-scatter.5
  603.8 76.3 reduce-scatter.7

commit v3 on v2

--- a/solution.py
+++ b/solution.py
@@ -82,10 +82,9 @@
 
 
 def spread(rows, axes, size):
-    near = jnp.concatenate(
-        [rows] + [swap_by(rows, axes, size, bits) for bits in range(2, size, 2)], axis=0
-    )
-    return join_halves(near, swap_by(near, axes, size, 1))
+    pieces = [swap_by(rows, axes, size, bits) for bits in range(2, size, 2)]
+    near = jnp.concatenate([rows] + pieces, axis=0)
+    return join_halves(near, swap_by(near, axes, size, 1)), pieces[-1]
 
 
 def collect(left, right, product, axes, size, *tied, begin=()):
@@ -102,7 +101,7 @@
         for place in range(1, size // 2)
     ]
     summed = sum([block.astype(F32) for block in blocks], near[:rows].astype(F32))
-    return summed, blocks[0], *tied
+    return summed, blocks[-1], *tied
 
 
 def gather_small(value, axis_sizes):
@@ -494,21 +493,30 @@
     info = jnp.stack([me] + ends).astype(jnp.int32)
     cosine, sine = rope_tables(within)
 
-    held_qkv, held_out = named(
+    held_attention = named(
         "attention_weights", swap_columns, [weight_qkv, weight_out[:, None, :]], size_blk
     )
-    full_qkv = named("qkv_gather", gather_rows, held_qkv)
+    full_attention = jnp.concatenate(held_attention, axis=1)
+    full_attention = named("attention_gather", gather_rows, full_attention)
+    cut = held_attention[0].shape[1]
+    full_qkv, full_out = full_attention[:, :cut], full_attention[:, cut:]
+    held_gate_up, held_down = named(
+        "feed_weights",
+        swap_columns,
+        [after(weight_gate_up, *held_attention), weight_down[:, None, :]],
+        size_blk,
+    )
     gain_pair = named("gain_gather", gather_small, norm_gains, sizes)
     gain_first, gain_second = gain_pair[0], gain_pair[1]
 
     inputs = tokens[0].astype(F32)
     unit_first, factor_first = rms_unit(inputs)
-    normed_first = named("first_spread", spread, (unit_first * gain_first).astype(BF16), PLANE, group)
-    held_gate_up, held_down = named(
-        "feed_weights", swap_columns, [weight_gate_up, weight_down[:, None, :]], size_blk
-    )
-    full_out = named("out_gather", gather_rows, held_out, full_qkv, normed_first)
-    full_gate_up = named("gate_up_gather", gather_rows, held_gate_up, full_out)
+    rows_first = (unit_first * gain_first).astype(BF16)
+    rows_first, held_gate_up, held_down = together(rows_first, held_gate_up, held_down)
+    normed_first, last_first = named("first_spread", spread, rows_first, PLANE, group)
+    full_gate_up = named(
+        "gate_up_gather", gather_rows, held_gate_up, full_attention, last_first
+    )
     projected = dot_nn(normed_first, full_qkv)
     features = full_out.shape[1]
     attended, q_row, k_row, v_row, logs = attend(
@@ -520,13 +528,13 @@
     )
     middle = inputs + branch
     unit_second, factor_second = rms_unit(middle)
-    normed_second = named("second_spread", spread, (unit_second * gain_second).astype(BF16), PLANE, group)
+    normed_second, _ = named("second_spread", spread, (unit_second * gain_second).astype(BF16), PLANE, group)
     hidden_here = full_gate_up.shape[1] // 2
     grad_output = cotangent[0].astype(F32)
     last_rows = cotangent[0]
     if normed_second.shape[0] > LONG_ROW:
         last_rows = after(last_rows, normed_second)
-    grad_feed = named("cotangent_spread", spread, last_rows, PLANE, group)
+    grad_feed, _ = named("cotangent_spread", spread, last_rows, PLANE, group)
     full_down = named(
         "down_gather", gather_rows, held_down, full_gate_up, normed_second, grad_feed
     )
@@ -549,18 +557,18 @@
         axis=1,
     )
     grad_gate_up = dot_tn(normed_second, grad_gates).astype(BF16)
-    grad_normed_second, first_second = named(
+    grad_normed_second, last_second = named(
         "second_grad_collect", collect, grad_gates, full_gate_up, dot_nt, PLANE, group
     )
-    grad_gate_up = after(grad_gate_up, down_sum, first_second)
+    grad_gate_up = after(grad_gate_up, down_sum, last_second)
     gate_up_sum = named("gate_up_back", sum_rows, grad_gate_up)
     grad_middle_norm, sum_second = norm_back(
         grad_normed_second, unit_second, factor_second, gain_second
     )
     grad_middle = grad_output + grad_middle_norm
-    grad_branch = named("branch_grad_spread", spread, grad_middle.astype(BF16), PLANE, group)
+    grad_branch, _ = named("branch_grad_spread", spread, grad_middle.astype(BF16), PLANE, group)
     with jax.named_scope("feed_collect"):
-        feed_hidden = after(hidden, first_second)
+        feed_hidden = after(hidden, last_second)
         feed_out, _ = collect(
             feed_hidden, full_down, dot_nt, PLANE, group, begin=(grad_branch,)
         )
@@ -583,19 +591,11 @@
     )
     grad_projected = own_heads(grad_projected, 3, features)
     grad_qkv = dot_tn(normed_first, grad_projected).astype(BF16)
-    grad_normed_first, _, feed_out, total_down = named(
-        "first_grad_collect",
-        collect,
-        grad_projected,
-        full_qkv,
-        dot_nt,
-        PLANE,
-        group,
-        feed_out,
-        total_down,
+    grad_normed_first, last_grad = named(
+        "first_grad_collect", collect, grad_projected, full_qkv, dot_nt, PLANE, group
     )
     both = jnp.concatenate([grad_qkv, grad_out], axis=1)
-    both_sum = named("attention_back", sum_rows, after(both, gate_up_sum, grad_normed_first))
+    both_sum = named("attention_back", sum_rows, after(both, gate_up_sum, last_grad))
 
     outcome = (middle + feed_out).astype(BF16)
     grad_input_norm, sum_first = norm_back(grad_normed_first, unit_first, factor_first, gain_first)
@@ -604,7 +604,7 @@
     [total_gate_up] = named(
         "gate_up_return", return_columns, gate_up_sum, size_blk, [2], wide
     )
-    both_sum = after(both_sum, total_gate_up, outcome, grad_input, gain_sums)
+    both_sum = after(both_sum, total_gate_up, total_down, outcome, grad_input, gain_sums)
     total_qkv, total_out = named(
         "attention_return", return_columns, both_sum, size_blk, [3, 1], features
     )

time: 718 us -> 691 us (0.962)
  waiting for transfers between devices: 389 us -> 349 us
  blocking collectives: 0 us -> 17.6 us
  local copies, waits for them, and re-layouts: 37.1 us -> 45 us
    all_gather x4 -> x3, waiting for transfers between devices: 89 us -> 66.3 us  [gather_rows(): return lax.all_gather(after(weight, *events), 'dp', axis=0, tiled=True)]
    all_to_all x5 -> x4, waiting for transfers between devices: 67.6 us -> 47.9 us  [trade(): return lax.all_to_all(blocks, axis, 0, 0, tiled=True)]
    all_to_all x0 -> x1, blocking collectives: none -> 17.6 us  [trade(): return lax.all_to_all(blocks, axis, 0, 0, tiled=True)]
    reduce_scatter x3, waiting for transfers between devices: 55.9 us -> 67.9 us  [sum_rows(): return lax.psum_scatter(grads, 'dp', scatter_dimension=0, tiled=True)]
    ppermute x42, waiting for transfers between devices: 176 us -> 166 us  [swap_by(): return lax.ppermute(value, axes, [(i, i ^ bits) for i in range(size)])]
    all_to_all x5 -> x4, starting transfers between devices: 21.2 us -> 16.4 us  [trade(): return lax.all_to_all(blocks, axis, 0, 0, tiled=True)]
  transfers between devices with their start and end apart: 54 -> 52, of which waited for: 41 -> 37; matrix products, arithmetic and copies ran while one was open for 25% -> 24% of each run, Pallas kernels for 7% -> 8%
where the time goes in v3:
time: 691 us; the launch traced here: 683 us
  waiting for transfers between devices  349 us (51%)
  matrix products  103 us (15%)
  starting transfers between devices  64.8 us (9%)
  Pallas kernels  52 us (8%)
  local copies, waits for them, and re-layouts  45 us (7%)
  other arithmetic  37.6 us (5%)
  blocking collectives  17.6 us (3%)
  between operations  15.1 us (2%)
    ppermute x42, waiting for transfers between devices, swap_by(): return lax.ppermute(value, axes, [(i, i ^ bits) for i in range(size)])  166 us
    reduce_scatter x3, waiting for transfers between devices, sum_rows(): return lax.psum_scatter(grads, 'dp', scatter_dimension=0, tiled=True)  67.9 us
    all_gather x3, waiting for transfers between devices, gather_rows(): return lax.all_gather(after(weight, *events), 'dp', axis=0, tiled=True)  66.3 us
    all_to_all x4, waiting for transfers between devices, trade(): return lax.all_to_all(blocks, axis, 0, 0, tiled=True)  47.9 us
    ppermute x42, starting transfers between devices, swap_by(): return lax.ppermute(value, axes, [(i, i ^ bits) for i in range(size)])  47.7 us
    dot_general x5, matrix products, dot_nn(): lax.dot_general(a, b, (((1,), (0,)), ((), ())), preferred_element_type=F32)  42.7 us
    dot_general x8, matrix products, dot_nt(): lax.dot_general(a, b, (((1,), (1,)), ((), ())), preferred_element_type=F32)  34 us
    pallas_call x4, Pallas kernels, join_halves(): pl.pallas_call(functools.partial(join_kernel, steps), grid=(2 * steps,),...  28.9 us
  transfers between devices with their start and end apart: 52, of which 37 were waited for; matrix products, arithmetic and copies ran while one was open for 24% of the time, Pallas kernels for 8%

profile of v3, /device:TPU:0, one launch (start us, length us, event | category | flops | bytes accessed | tf_op | source)
XLA Modules:
  0.0 683.2 jit_solution(17593067193662452074)
XLA Ops:
  9.9 17.6 %all_to_all.25 = bf16[2,256,1024]{1,2,0:T(8,128)(2,1)S(1)} all-to-all(bf16[2,256,1024]{1,2,0:T(8,128)(2,1)S(1)} %pad_maximum_fusion.10), channel_id=1, replica_groups=mesh['dp'=4,'blk'=2,'tensor'=4] {'blk'}, dimensions={0} | all-to-all | bytes 2097152 | tf_op jit(solution)/shard_map/attention_weights/all_to_all | solution.py:141
  31.8 6.2 copy.35
  43.7 5.3 all-to-all-start
  51.0 2.8 collective-permute-done.3
  55.5 3.2 collective-permute-done.4
  59.7 25.5 %all-to-all-done = bf16[2,256,3072]{1,2,0:T(8,128)(2,1)} async-done(((bf16[2,256,3072]{1,2,0:T(8,128)(2,1)}), bf16[2,256,3072]{1,2,0:T(8,128)(2,1)}, u32[]{:S(2)}, u32[]{:S(2)}) %all-to-all-start) | async-done | bytes 3145760 | tf_op jit(solution)/shard_map/feed_weights/all_to_all | solution.py:141
  85.2 3.2 copy.38
  91.0 13.5 %collective-permute-done.7 = bf16[128,2048]{1,0:T(8,128)(2,1)S(1)} collective-permute-done((bf16[128,2048]{1,0:T(8,128)(2,1)}, bf16[128,2048]{1,0:T(8,128)(2,1)S(1)}, u32[]{:S(2)}, u32[]{:S(2)}) %collective-permute-start.7) | collective-permute-done | bytes 524320 | tf_op jit(solution)/shard_map/first_spread/ppermute | solution.py:49
  104.5 6.1 all-gather.4.cloned.1.call-done
  115.6 9.0 %collective-permute-done.5 = bf16[128,2048]{1,0:T(8,128)(2,1)S(1)} collective-permute-done((bf16[128,2048]{1,0:T(8,128)(2,1)}, bf16[128,2048]{1,0:T(8,128)(2,1)S(1)}, u32[]{:S(2)}, u32[]{:S(2)}) %collective-permute-start.5) | collective-permute-done | bytes 524320 | tf_op jit(solution)/shard_map/first_spread/ppermute | solution.py:49
  134.3 7.3 %join_halves.4 = bf16[1024,2048]{1,0:T(8,128)(2,1)} custom-call(bf16[512,2048]{1,0:T(8,128)(2,1)} %constant_dynamic-update-slice_fusion.near_ref, bf16[512,2048]{1,0:T(8,128)(2,1)} %collective-permute-done.8.far_ref), custom_call_target="tpu_custom_call" | custom-call | bytes 8388608 | tf_op jit(solution)/shard_map/first_spread/join_halves/pallas_call | solution.py:68
  141.6 8.2 %fusion.8.q_ref.k_ref.v_ref = f32[1024,768]{1,0:T(8,128)} fusion(bf16[1024,2048]{1,0:T(8,128)(2,1)} %join_halves.4, bf16[2048,1024]{1,0:T(8,128)(2,1)} %all-gather.4.cloned.1.call-done), kind=kOutput, calls=%fused_computation.32 | convolution fusion | flops 3221225472 | bytes 10485760 | tf_op jit(solution)/shard_map/dot_general | solution.py:24
  149.8 10.6 %attend.1 = (bf16[1024,256]{1,0:T(8,128)(2,1)S(1)}, bf16[1024,256]{1,0:T(8,128)(2,1)S(1)}, bf16[1024,256]{1,0:T(8,128)(2,1)S(1)}, bf16[1024,256]{1,0:T(8,128)(2,1)S(1)}, f32[1024,256]{1,0:T(8,128)S(1)}) custom-call(s32[4]{0:T(128)S(1)} %pad_add_fusion.info_ref, f32[1024,768]{1,0:T(8,128)} %fusion.8.q_ref.k_ref.v_ref, f32[1024,768]{1,0:T(8,128)} %fusion.8.q_ref.k_ref.v_ref, ...), custom_call_target="tpu_custom_call" | custom-call | flops 1073741824 | bytes 4718592 | tf_op jit(solution)/shard_map/attend/pallas_call | solution.py:289
  161.8 3.8 collective-permute-done.9
  172.7 8.9 %collective-permute-done.10 = bf16[128,2048]{1,0:T(8,128)(2,1)S(1)} collective-permute-done((bf16[128,2048]{1,0:T(8,128)(2,1)S(1)}, bf16[128,2048]{1,0:T(8,128)(2,1)S(1)}, u32[]{:S(2)}, u32[]{:S(2)}) %collective-permute-start.10) | collective-permute-done | bytes 524320 | tf_op jit(solution)/shard_map/branch_collect/ppermute | solution.py:49
  183.6 10.5 %collective-permute-done.12 = bf16[128,2048]{1,0:T(8,128)(2,1)S(1)} collective-permute-done((bf16[128,2048]{1,0:T(8,128)(2,1)S(1)}, bf16[128,2048]{1,0:T(8,128)(2,1)S(1)}, u32[]{:S(2)}, u32[]{:S(2)}) %collective-permute-start.12) | collective-permute-done | bytes 524320 | tf_op jit(solution)/shard_map/branch_collect/ppermute | solution.py:49
  198.5 5.5 collective-permute-done.17
  206.1 10.6 %collective-permute-done.19 = bf16[128,2048]{1,0:T(8,128)(2,1)S(1)} collective-permute-done((bf16[128,2048]{1,0:T(8,128)(2,1)S(1)}, bf16[128,2048]{1,0:T(8,128)(2,1)S(1)}, u32[]{:S(2)}, u32[]{:S(2)}) %collective-permute-start.19) | collective-permute-done | bytes 524320 | tf_op jit(solution)/shard_map/cotangent_spread/ppermute | solution.py:49
  218.2 7.5 %collective-permute-done.13 = bf16[128,2048]{1,0:T(8,128)(2,1)S(1)} collective-permute-done((bf16[128,2048]{1,0:T(8,128)(2,1)S(1)}, bf16[128,2048]{1,0:T(8,128)(2,1)S(1)}, u32[]{:S(2)}, u32[]{:S(2)}) %collective-permute-start.13) | collective-permute-done | bytes 524320 | tf_op jit(solution)/shard_map/second_spread/ppermute | solution.py:49
  227.5 10.7 %collective-permute-done.15 = bf16[128,2048]{1,0:T(8,128)(2,1)S(1)} collective-permute-done((bf16[128,2048]{1,0:T(8,128)(2,1)S(1)}, bf16[128,2048]{1,0:T(8,128)(2,1)S(1)}, u32[]{:S(2)}, u32[]{:S(2)}) %collective-permute-start.15) | collective-permute-done | bytes 524320 | tf_op jit(solution)/shard_map/second_spread/ppermute | solution.py:49
  239.8 7.1 %join_halves.6 = bf16[1024,2048]{1,0:T(8,128)(2,1)} custom-call(bf16[512,2048]{1,0:T(8,128)(2,1)} %copy-done.11, bf16[512,2048]{1,0:T(8,128)(2,1)} %collective-permute-done.20.far_ref), custom_call_target="tpu_custom_call" | custom-call | bytes 8388608 | tf_op jit(solution)/shard_map/cotangent_spread/join_halves/pallas_call | solution.py:68
  247.0 7.2 %join_halves.5 = bf16[1024,2048]{1,0:T(8,128)(2,1)} custom-call(bf16[512,2048]{1,0:T(8,128)(2,1)} %pad_maximum_fusion.5.near_ref, bf16[512,2048]{1,0:T(8,128)(2,1)} %collective-permute-done.16.far_ref), custom_call_target="tpu_custom_call" | custom-call | bytes 8388608 | tf_op jit(solution)/shard_map/second_spread/join_halves/pallas_call | solution.py:68
  254.1 6.1 all-gather.6.cloned.1.call-done
  260.7 10.1 %fusion.2 = f32[1024,1024]{0,1:T(8,128)} fusion(bf16[1024,2048]{1,0:T(8,128)(2,1)} %join_halves.5, bf16[2048,2048]{1,0:T(8,128)(2,1)} %all-gather.6.cloned.1.call-done), kind=kOutput, calls=%fused_computation.8 | convolution fusion | flops 4294967296 | bytes 12582912 | tf_op jit(solution)/shard_map/dot_general | solution.py:24
  270.8 8.6 %multiply_convert_fusion.2 = (bf16[1024,1024]{0,1:T(8,128)(2,1)}, f32[1024,1024]{0,1:T(8,128)}) fusion(f32[1024,1024]{0,1:T(8,128)} %fusion.2, bf16[1024,2048]{1,0:T(8,128)(2,1)S(1)} %copy-done.16, bf16[2048,2048]{1,0:T(8,128)(2,1)S(1)} %copy-done.33), kind=kOutput, calls=%fused_computation.17 | convolution fusion | flops 4301258752 | bytes 18874368 | tf_op jit(solution)/shard_map/dot_general | solution.py:24
  279.4 7.8 %convolution_convert_fusion.1 = bf16[2048,1024]{1,0:T(8,128)(2,1)} fusion(bf16[1024,2048]{1,0:T(8,128)(2,1)S(1)} %copy-done.18, bf16[1024,1024]{0,1:T(8,128)(2,1)} %get-tuple-element.32), kind=kOutput, calls=%fused_computation.21 | convolution fusion | flops 4297064448 | bytes 10485760 | tf_op jit(solution)/shard_map/dot_general | solution.py:32
  287.3 54.1 %all-gather.8.cloned.1.call-done = bf16[2048,1024]{1,0:T(8,128)(2,1)} async-done(((bf16[512,1024]{1,0:T(8,128)(2,1)}), bf16[2048,1024]{1,0:T(8,128)(2,1)}) %all-gather.8.cloned.1.call-update) | async-done | bytes 4194320 | tf_op jit(solution)/shard_map/down_gather/all_gather | solution.py:163
  341.4 11.9 %multiply_convert_fusion = (bf16[1024,1024]{0,1:T(8,128)(2,1)S(1)}, bf16[1024,1024]{0,1:T(8,128)(2,1)S(1)}) fusion(f32[1024,1024]{0,1:T(8,128)} %fusion.2, f32[1024,1024]{0,1:T(8,128)} %get-tuple-element.116, bf16[1024,2048]{1,0:T(8,128)(2,1)} %join_halves.6, bf16[2048,1024]{1,0:T(8,128)(2,1)} %all-gather.8.cloned.1.call-done), kind=kOutput, calls=%fused_computation.15 | convolution fusion | flops 4308598784 | bytes 20971520 | tf_op jit(solution)/shard_map/dot_general | solution.py:24
  353.4 8.4 %convolution_convert_fusion.6 = bf16[512,2048]{1,0:T(8,128)(2,1)S(1)} fusion(bf16[2048,2048]{1,0:T(8,128)(2,1)} %all-gather.6.cloned.1.call-done, bf16[1024,1024]{0,1:T(8,128)(2,1)S(1)} %get-tuple-element.73, bf16[1024,1024]{0,1:T(8,128)(2,1)S(1)} %get-tuple-element.72), kind=kOutput, calls=%fused_computation.27 | convolution fusion | flops 4300210176 | bytes 14680064 | tf_op jit(solution)/shard_map/second_grad_collect/dot_general | solution.py:28
  361.9 4.1 collective-permute-done.21
  366.0 8.4 %add_convert_fusion.2 = bf16[512,2048]{1,0:T(8,128)(2,1)S(1)} fusion(bf16[512,2048]{1,0:T(8,128)(2,1)S(1)} %collective-permute-done.21, bf16[2048,2048]{1,0:T(8,128)(2,1)} %all-gather.6.cloned.1.call-done, bf16[1024,1024]{0,1:T(8,128)(2,1)S(1)} %get-tuple-element.73, bf16[1024,1024]{0,1:T(8,128)(2,1)S(1)} %get-tuple-element.72), kind=kOutput, calls=%fused_computation.14 | convolution fusion | flops 4302307328 | bytes 16777216 | tf_op jit(solution)/shard_map/second_grad_collect/dot_general | solution.py:28
  377.0 2.4 collective-permute-start.22
  379.4 12.5 %convolution_convert_fusion = bf16[2048,2048]{1,0:T(8,128)(2,1)} fusion(bf16[1024,2048]{1,0:T(8,128)(2,1)S(1)} %copy-done.17, bf16[1024,1024]{0,1:T(8,128)(2,1)S(1)} %get-tuple-element.72, bf16[1024,1024]{0,1:T(8,128)(2,1)S(1)} %get-tuple-element.73), kind=kOutput, calls=%fused_computation | convolution fusion | flops 8602517504 | bytes 16777216 | tf_op jit(solution)/shard_map/dot_general | solution.py:32
  392.2 26.6 %reduce-scatter.4.cloned.1.call-done = bf16[512,1024]{1,0:T(8,128)(2,1)} async-done(((bf16[2048,1024]{1,0:T(8,128)(2,1)}), bf16[512,1024]{1,0:T(8,128)(2,1)}) %reduce-scatter.4.cloned.1.call-update) | async-done | bytes 1048592 | tf_op jit(solution)/shard_map/down_back/reduce_scatter | solution.py:167
  421.9 11.0 %collective-permute-done.24 = bf16[128,2048]{1,0:T(8,128)(2,1)S(1)} collective-permute-done((bf16[128,2048]{1,0:T(8,128)(2,1)}, bf16[128,2048]{1,0:T(8,128)(2,1)S(1)}, u32[]{:S(2)}, u32[]{:S(2)}) %collective-permute-start.24) | collective-permute-done | bytes 524320 | tf_op jit(solution)/shard_map/second_grad_collect/ppermute | solution.py:49
  436.1 3.4 fusion.45
  443.0 10.5 %collective-permute-done.26 = bf16[128,2048]{1,0:T(8,128)(2,1)S(1)} collective-permute-done((bf16[128,2048]{1,0:T(8,128)(2,1)S(1)}, bf16[128,2048]{1,0:T(8,128)(2,1)S(1)}, u32[]{:S(2)}, u32[]{:S(2)}) %collective-permute-start.26) | collective-permute-done | bytes 524320 | tf_op jit(solution)/shard_map/branch_grad_spread/ppermute | solution.py:49
  454.8 9.6 %collective-permute-done.28 = bf16[128,2048]{1,0:T(8,128)(2,1)S(1)} collective-permute-done((bf16[128,2048]{1,0:T(8,128)(2,1)S(1)}, bf16[128,2048]{1,0:T(8,128)(2,1)S(1)}, u32[]{:S(2)}, u32[]{:S(2)}) %collective-permute-start.28) | collective-permute-done | bytes 524320 | tf_op jit(solution)/shard_map/branch_grad_spread/ppermute | solution.py:49
  466.1 4.3 collective-permute-done.29.far_ref
  470.4 7.3 %join_halves.7 = bf16[1024,2048]{1,0:T(8,128)(2,1)} custom-call(bf16[512,2048]{1,0:T(8,128)(2,1)} %copy-done.12, bf16[512,2048]{1,0:T(8,128)(2,1)} %collective-permute-done.29.far_ref), custom_call_target="tpu_custom_call" | custom-call | bytes 8388608 | tf_op jit(solution)/shard_map/branch_grad_spread/join_halves/pallas_call | solution.py:68
  477.7 3.8 convolution_convert_fusion.8.grad_ref
  481.6 12.4 %attend_back.1 = bf16[1024,768]{1,0:T(8,128)(2,1)} custom-call(s32[4]{0:T(128)S(1)} %pad_add_fusion.info_ref, bf16[1024,256]{1,0:T(8,128)(2,1)S(1)} %get-tuple-element.34.q_row, bf16[1024,256]{1,0:T(8,128)(2,1)S(1)} %copy-done.1, bf16[1024,256]{1,0:T(8,128)(2,1)S(1)} %copy-done.3, f32[1024,256]{1,0:T(8,128)S(1)} %get-tuple-element.37.log_ref, ...), custom_call_target="tpu_custom_call" | custom-call | flops 2684354560 | bytes 5242880 | tf_op jit(solution)/shard_map/attend_back/pallas_call | solution.py:405
  494.0 3.1 convolution_convert_fusion.5
  497.3 3.8 convolution_convert_fusion.3
  501.5 4.2 convolution_convert_fusion.2
  512.9 2.5 pad_maximum_fusion.2
  515.4 9.6 %collective-permute-done.36 = bf16[128,2048]{1,0:T(8,128)(2,1)S(1)} collective-permute-done((bf16[128,2048]{1,0:T(8,128)(2,1)S(1)}, bf16[128,2048]{1,0:T(8,128)(2,1)S(1)}, u32[]{:S(2)}, u32[]{:S(2)}) %collective-permute-start.36) | collective-permute-done | bytes 524320 | tf_op jit(solution)/shard_map/first_grad_collect/ppermute | solution.py:49
  524.9 41.3 %reduce-scatter.6.cloned.1.call-done = bf16[512,2048]{1,0:T(8,128)(2,1)} async-done(((bf16[2048,2048]{1,0:T(8,128)(2,1)}), bf16[512,2048]{1,0:T(8,128)(2,1)}) %reduce-scatter.6.cloned.1.call-update) | async-done | bytes 2097168 | tf_op jit(solution)/shard_map/gate_up_back/reduce_scatter | solution.py:167
  569.2 6.9 %add_convert_fusion.1 = bf16[512,2048]{1,0:T(8,128)(2,1)} fusion(bf16[512,2048]{1,0:T(8,128)(2,1)} %collective-permute-done.23, bf16[2048,1024]{1,0:T(8,128)(2,1)} %all-gather.8.cloned.1.call-done, bf16[1024,1024]{0,1:T(8,128)(2,1)} %get-tuple-element.32), kind=kOutput, calls=%fused_computation.13 | convolution fusion | flops 2150629376 | bytes 9437184 | tf_op jit(solution)/shard_map/feed_collect/dot_general | solution.py:28
  576.1 3.8 collective-permute-done.34
  587.4 2.4 collective-permute-start.32
  590.5 10.0 %collective-permute-done.38 = f32[2,512]{1,0:T(2,128)S(1)} collective-permute-done((f32[2,512]{1,0:T(2,128)S(1)}, f32[2,512]{1,0:T(2,128)S(1)}, u32[]{:S(2)}, u32[]{:S(2)}) %collective-permute-start.38) | collective-permute-done | bytes 4128 | tf_op jit(solution)/shard_map/gain_scatter/ppermute | solution.py:49
  601.8 9.1 %collective-permute-done.32 = bf16[128,2048]{1,0:T(8,128)(2,1)S(1)} collective-permute-done((bf16[128,2048]{1,0:T(8,128)(2,1)S(1)}, bf16[128,2048]{1,0:T(8,128)(2,1)S(1)}, u32[]{:S(2)}, u32[]{:S(2)}) %collective-permute-start.32) | collective-permute-done | bytes 524320 | tf_op jit(solution)/shard_map/feed_collect/ppermute | solution.py:49
  610.9 2.2 add_convert_fusion.4
  613.1 3.6 all-to-all-start.4
  616.7 3.7 collective-permute-start.40
  620.4 7.3 %all-to-all-done.4 = bf16[2,256,1024]{2,1,0:T(8,128)(2,1)S(1)} async-done(((bf16[2,256,1024]{2,1,0:T(8,128)(2,1)}), bf16[2,256,1024]{2,1,0:T(8,128)(2,1)S(1)}, u32[]{:S(2)}, u32[]{:S(2)}) %all-to-all-start.4) | async-done | bytes 1048608 | tf_op jit(solution)/shard_map/down_return/all_to_all | solution.py:141
  628.7 3.8 all-to-all-start.2
  634.5 3.3 fusion.24
  640.0 14.0 %all-to-all-done.2 = bf16[2,256,2048]{2,1,0:T(8,128)(2,1)S(1)} async-done(((bf16[2,256,2048]{2,1,0:T(8,128)(2,1)}), bf16[2,256,2048]{2,1,0:T(8,128)(2,1)S(1)}, u32[]{:S(2)}, u32[]{:S(2)}) %all-to-all-start.2) | async-done | bytes 2097184 | tf_op jit(solution)/shard_map/gate_up_return/all_to_all | solution.py:141
  655.5 2.3 pad_maximum_fusion.3
  657.8 2.4 copy.47
  660.2 3.8 all-to-all-start.3
  667.0 5.2 copy.46
  (234 shorter events, 106.2 us)
Async XLA Ops:
  7.2 103.4 %all-gather.4.cloned.1.call-start = ((), (), s32[]{:S(2)}) async-start(), calls=%async_computation.8 | async-start | bytes 5242880 | tf_op jit(solution)/shard_map/attention_gather/all_gather | solution.py:163
  8.7 20.1 %copy-start.32 = (f32[2,64]{1,0:T(2,128)S(1)}, f32[2,64]{1,0:T(2,128)}, u32[]{:S(2)}) copy-start(f32[2,64]{1,0:T(2,128)} %param.15) | copy-start | bytes 1540
  28.8 1.2 collective-permute-start
  30.1 11.3 %collective-permute-start.1 = (f32[2,128]{1,0:T(2,128)S(1)}, f32[2,128]{1,0:T(2,128)S(1)}, u32[]{:S(2)}, u32[]{:S(2)}) collective-permute-start(f32[2,128]{1,0:T(2,128)S(1)} %pad_maximum_fusion.18), channel_id=1, source_target_pairs={{0,2},{1,3},{2,0},{3,1},{4,6},{5,7},{6,4},{7,5},{8,10},{9,11},{10,... | collective-permute-start | bytes 3080 | tf_op jit(solution)/shard_map/gain_gather/ppermute | solution.py:49
  41.4 7.6 %collective-permute-start.2 = (f32[2,256]{1,0:T(2,128)S(1)}, f32[2,256]{1,0:T(2,128)S(1)}, u32[]{:S(2)}, u32[]{:S(2)}) collective-permute-start(f32[2,256]{1,0:T(2,128)S(1)} %pad_maximum_fusion.17), channel_id=1, source_target_pairs={{0,4},{4,0},{1,5},{5,1},{2,6},{6,2},{3,7},{7,3},{8,12},{12,8},{9,1... | collective-permute-start | bytes 6152 | tf_op jit(solution)/shard_map/gain_gather/ppermute | solution.py:49
  43.7 41.5 %all-to-all-start = ((bf16[2,256,3072]{1,2,0:T(8,128)(2,1)}), bf16[2,256,3072]{1,2,0:T(8,128)(2,1)}, u32[]{:S(2)}, u32[]{:S(2)}) async-start(bf16[2,256,3072]{1,2,0:T(8,128)(2,1)} %pad_maximum_fusion.4), calls=%async_computation | async-start | bytes 6291456 | tf_op jit(solution)/shard_map/feed_weights/all_to_all | solution.py:141
  49.0 211.2 %all-gather.6.cloned.1.call-start = ((), (), s32[]{:S(2)}) async-start(), calls=%async_computation.9 | async-start | bytes 10485760 | tf_op jit(solution)/shard_map/gate_up_gather/all_gather | solution.py:163
  49.1 4.7 collective-permute-start.3
  53.8 4.8 collective-permute-start.4
  89.9 37.5 %copy-start.31 = (s32[1,3]{1,0:T(1,128)S(1)}, s32[1,3]{1,0:T(1,128)}, u32[]{:S(2)}) copy-start(s32[1,3]{1,0:T(1,128)} %param.10) | copy-start | bytes 40
  89.9 40.2 %copy-start.35 = (s32[8]{0:T(128)S(1)}, s32[8]{0:T(128)}, u32[]{:S(2)}) copy-start(s32[8]{0:T(128)} %constant.44.clone) | copy-start | bytes 100
  90.9 13.6 %collective-permute-start.7 = (bf16[128,2048]{1,0:T(8,128)(2,1)}, bf16[128,2048]{1,0:T(8,128)(2,1)S(1)}, u32[]{:S(2)}, u32[]{:S(2)}) collective-permute-start(bf16[128,2048]{1,0:T(8,128)(2,1)} %fusion.20), channel_id=1, source_target_pairs={{0,6},{1,7},{2,4},{3,5},{4,2},{5,3},{6,0},{7,1},{8,14},{9,15},{10,... | collective-permute-start | bytes 1572872 | tf_op jit(solution)/shard_map/first_spread/ppermute | solution.py:49
  110.6 230.8 %all-gather.8.cloned.1.call-start = ((), (), s32[]{:S(2)}) async-start(), calls=%async_computation.10 | async-start | bytes 5242880 | tf_op jit(solution)/shard_map/down_gather/all_gather | solution.py:163
  110.6 14.0 %collective-permute-start.5 = (bf16[128,2048]{1,0:T(8,128)(2,1)}, bf16[128,2048]{1,0:T(8,128)(2,1)S(1)}, u32[]{:S(2)}, u32[]{:S(2)}) collective-permute-start(bf16[128,2048]{1,0:T(8,128)(2,1)} %fusion.20), channel_id=1, source_target_pairs={{0,2},{1,3},{2,0},{3,1},{4,6},{5,7},{6,4},{7,5},{8,10},{9,11},{10,... | collective-permute-start | bytes 1572872 | tf_op jit(solution)/shard_map/first_spread/ppermute | solution.py:49
  112.2 13.6 %collective-permute-start.6 = (bf16[128,2048]{1,0:T(8,128)(2,1)}, bf16[128,2048]{1,0:T(8,128)(2,1)S(1)}, u32[]{:S(2)}, u32[]{:S(2)}) collective-permute-start(bf16[128,2048]{1,0:T(8,128)(2,1)} %fusion.20), channel_id=1, source_target_pairs={{0,4},{1,5},{2,6},{3,7},{4,0},{5,1},{6,2},{7,3},{8,12},{9,13},{10,... | collective-permute-start | bytes 1572872 | tf_op jit(solution)/shard_map/first_spread/ppermute | solution.py:49
  127.4 6.9 %collective-permute-start.8 = (bf16[512,2048]{1,0:T(8,128)(2,1)}, bf16[512,2048]{1,0:T(8,128)(2,1)}, u32[]{:S(2)}, u32[]{:S(2)}) collective-permute-start(bf16[512,2048]{1,0:T(8,128)(2,1)} %constant_dynamic-update-slice_fusion.near_ref), channel_id=1, source_target_pairs={{0,1},{1,0},{2,3},{3,2},{4,5},{5,4},{6,7},{7,6},{8,9},{9,8},{10,11... | collective-permute-start | bytes 6291464 | tf_op jit(solution)/shard_map/first_spread/ppermute | solution.py:49
  161.3 32.9 %copy-start.8 = (bf16[1,128,2048]{2,1,0:T(8,128)(2,1)S(1)}, bf16[1,128,2048]{2,1,0:T(8,128)(2,1)}, u32[]{:S(2)}) copy-start(bf16[1,128,2048]{2,1,0:T(8,128)(2,1)} %param.9) | copy-start | bytes 1572868
  161.3 4.4 collective-permute-start.9
  166.5 15.1 %collective-permute-start.10 = (bf16[128,2048]{1,0:T(8,128)(2,1)S(1)}, bf16[128,2048]{1,0:T(8,128)(2,1)S(1)}, u32[]{:S(2)}, u32[]{:S(2)}) collective-permute-start(bf16[128,2048]{1,0:T(8,128)(2,1)S(1)} %get-tuple-element.97), channel_id=1, source_target_pairs={{0,2},{1,3},{2,0},{3,1},{4,6},{5,7},{6,4},{7,5},{8,10},{9,11},{10,... | collective-permute-start | bytes 1572872 | tf_op jit(solution)/shard_map/branch_collect/ppermute | solution.py:49
  167.7 15.9 %collective-permute-start.11 = (bf16[128,2048]{1,0:T(8,128)(2,1)S(1)}, bf16[128,2048]{1,0:T(8,128)(2,1)S(1)}, u32[]{:S(2)}, u32[]{:S(2)}) collective-permute-start(bf16[128,2048]{1,0:T(8,128)(2,1)S(1)} %get-tuple-element.99), channel_id=1, source_target_pairs={{0,4},{1,5},{2,6},{3,7},{4,0},{5,1},{6,2},{7,3},{8,12},{9,13},{10,... | collective-permute-start | bytes 1572872 | tf_op jit(solution)/shard_map/branch_collect/ppermute | solution.py:49
  169.2 24.9 %collective-permute-start.12 = (bf16[128,2048]{1,0:T(8,128)(2,1)S(1)}, bf16[128,2048]{1,0:T(8,128)(2,1)S(1)}, u32[]{:S(2)}, u32[]{:S(2)}) collective-permute-start(bf16[128,2048]{1,0:T(8,128)(2,1)S(1)} %get-tuple-element.98), channel_id=1, source_target_pairs={{0,6},{1,7},{2,4},{3,5},{4,2},{5,3},{6,0},{7,1},{8,14},{9,15},{10,... | collective-permute-start | bytes 1572872 | tf_op jit(solution)/shard_map/branch_collect/ppermute | solution.py:49
  170.1 33.9 %collective-permute-start.17 = (bf16[128,2048]{1,0:T(8,128)(2,1)S(1)}, bf16[128,2048]{1,0:T(8,128)(2,1)S(1)}, u32[]{:S(2)}, u32[]{:S(2)}) collective-permute-start(bf16[128,2048]{1,0:T(8,128)(2,1)S(1)} %bitcast.128), channel_id=1, source_target_pairs={{0,2},{1,3},{2,0},{3,1},{4,6},{5,7},{6,4},{7,5},{8,10},{9,11},{10,... | collective-permute-start | bytes 1572872 | tf_op jit(solution)/shard_map/cotangent_spread/ppermute | solution.py:49
  171.2 34.9 %collective-permute-start.18 = (bf16[128,2048]{1,0:T(8,128)(2,1)S(1)}, bf16[128,2048]{1,0:T(8,128)(2,1)S(1)}, u32[]{:S(2)}, u32[]{:S(2)}) collective-permute-start(bf16[128,2048]{1,0:T(8,128)(2,1)S(1)} %bitcast.129), channel_id=1, source_target_pairs={{0,4},{1,5},{2,6},{3,7},{4,0},{5,1},{6,2},{7,3},{8,12},{9,13},{10,... | collective-permute-start | bytes 1572872 | tf_op jit(solution)/shard_map/cotangent_spread/ppermute | solution.py:49
  181.6 35.1 %collective-permute-start.19 = (bf16[128,2048]{1,0:T(8,128)(2,1)S(1)}, bf16[128,2048]{1,0:T(8,128)(2,1)S(1)}, u32[]{:S(2)}, u32[]{:S(2)}) collective-permute-start(bf16[128,2048]{1,0:T(8,128)(2,1)S(1)} %bitcast.130), channel_id=1, source_target_pairs={{0,6},{1,7},{2,4},{3,5},{4,2},{5,3},{6,0},{7,1},{8,14},{9,15},{10,... | collective-permute-start | bytes 1572872 | tf_op jit(solution)/shard_map/cotangent_spread/ppermute | solution.py:49
  195.8 29.9 %collective-permute-start.13 = (bf16[128,2048]{1,0:T(8,128)(2,1)S(1)}, bf16[128,2048]{1,0:T(8,128)(2,1)S(1)}, u32[]{:S(2)}, u32[]{:S(2)}) collective-permute-start(bf16[128,2048]{1,0:T(8,128)(2,1)S(1)} %multiply_convert_fusion.3), channel_id=1, source_target_pairs={{0,2},{1,3},{2,0},{3,1},{4,6},{5,7},{6,4},{7,5},{8,10},{9,11},{10,... | collective-permute-start | bytes 1572872 | tf_op jit(solution)/shard_map/second_spread/ppermute | solution.py:49
  197.0 30.5 %collective-permute-start.14 = (bf16[128,2048]{1,0:T(8,128)(2,1)S(1)}, bf16[128,2048]{1,0:T(8,128)(2,1)S(1)}, u32[]{:S(2)}, u32[]{:S(2)}) collective-permute-start(bf16[128,2048]{1,0:T(8,128)(2,1)S(1)} %multiply_convert_fusion.3), channel_id=1, source_target_pairs={{0,4},{1,5},{2,6},{3,7},{4,0},{5,1},{6,2},{7,3},{8,12},{9,13},{10,... | collective-permute-start | bytes 1572872 | tf_op jit(solution)/shard_map/second_spread/ppermute | solution.py:49
  204.0 34.2 %collective-permute-start.15 = (bf16[128,2048]{1,0:T(8,128)(2,1)S(1)}, bf16[128,2048]{1,0:T(8,128)(2,1)S(1)}, u32[]{:S(2)}, u32[]{:S(2)}) collective-permute-start(bf16[128,2048]{1,0:T(8,128)(2,1)S(1)} %multiply_convert_fusion.3), channel_id=1, source_target_pairs={{0,6},{1,7},{2,4},{3,5},{4,2},{5,3},{6,0},{7,1},{8,14},{9,15},{10,... | collective-permute-start | bytes 1572872 | tf_op jit(solution)/shard_map/second_spread/ppermute | solution.py:49
  218.2 21.6 %collective-permute-start.20 = (bf16[512,2048]{1,0:T(8,128)(2,1)S(1)}, bf16[512,2048]{1,0:T(8,128)(2,1)}, u32[]{:S(2)}, u32[]{:S(2)}) collective-permute-start(bf16[512,2048]{1,0:T(8,128)(2,1)S(1)} %pad_maximum_fusion.6.near_ref), channel_id=1, source_target_pairs={{0,1},{1,0},{2,3},{3,2},{4,5},{5,4},{6,7},{7,6},{8,9},{9,8},{10,11... | collective-permute-start | bytes 6291464 | tf_op jit(solution)/shard_map/cotangent_spread/ppermute | solution.py:49
  239.8 7.1 %collective-permute-start.16 = (bf16[512,2048]{1,0:T(8,128)(2,1)}, bf16[512,2048]{1,0:T(8,128)(2,1)}, u32[]{:S(2)}, u32[]{:S(2)}) collective-permute-start(bf16[512,2048]{1,0:T(8,128)(2,1)} %pad_maximum_fusion.5.near_ref), channel_id=1, source_target_pairs={{0,1},{1,0},{2,3},{3,2},{4,5},{5,4},{6,7},{7,6},{8,9},{9,8},{10,11... | collective-permute-start | bytes 6291464 | tf_op jit(solution)/shard_map/second_spread/ppermute | solution.py:49
  260.2 158.6 %reduce-scatter.4.cloned.1.call-start = ((), (), s32[]{:S(2)}) async-start(), calls=%async_computation.11 | async-start | bytes 5242880 | tf_op jit(solution)/shard_map/down_back/reduce_scatter | solution.py:167
  341.4 224.8 %reduce-scatter.6.cloned.1.call-start = ((), (), s32[]{:S(2)}) async-start(), calls=%async_computation.12 | async-start | bytes 10485760 | tf_op jit(solution)/shard_map/gate_up_back/reduce_scatter | solution.py:167
  361.8 17.6 %copy-start.17 = (bf16[1024,2048]{1,0:T(8,128)(2,1)S(1)}, bf16[1024,2048]{1,0:T(8,128)(2,1)}, u32[]{:S(2)}) copy-start(bf16[1024,2048]{1,0:T(8,128)(2,1)} %join_halves.5) | copy-start | bytes 12582916
  361.8 4.2 collective-permute-start.21
  377.0 15.2 %collective-permute-start.22 = (bf16[128,2048]{1,0:T(8,128)(2,1)}, bf16[128,2048]{1,0:T(8,128)(2,1)}, u32[]{:S(2)}, u32[]{:S(2)}) collective-permute-start(bf16[128,2048]{1,0:T(8,128)(2,1)} %get-tuple-element.96), channel_id=1, source_target_pairs={{0,6},{1,7},{2,4},{3,5},{4,2},{5,3},{6,0},{7,1},{8,14},{9,15},{10,... | collective-permute-start | bytes 1572872 | tf_op jit(solution)/shard_map/second_grad_collect/ppermute | solution.py:49
  418.9 239.0 %reduce-scatter.8.cloned.1.call-start = ((), (), s32[]{:S(2)}) async-start(), calls=%async_computation.13 | async-start | bytes 5242880 | tf_op jit(solution)/shard_map/attention_back/reduce_scatter | solution.py:167
  418.9 14.0 %collective-permute-start.24 = (bf16[128,2048]{1,0:T(8,128)(2,1)}, bf16[128,2048]{1,0:T(8,128)(2,1)S(1)}, u32[]{:S(2)}, u32[]{:S(2)}) collective-permute-start(bf16[128,2048]{1,0:T(8,128)(2,1)} %get-tuple-element.94), channel_id=1, source_target_pairs={{0,2},{1,3},{2,0},{3,1},{4,6},{5,7},{6,4},{7,5},{8,10},{9,11},{10,... | collective-permute-start | bytes 1572872 | tf_op jit(solution)/shard_map/second_grad_collect/ppermute | solution.py:49
  420.5 13.6 %collective-permute-start.25 = (bf16[128,2048]{1,0:T(8,128)(2,1)}, bf16[128,2048]{1,0:T(8,128)(2,1)S(1)}, u32[]{:S(2)}, u32[]{:S(2)}) collective-permute-start(bf16[128,2048]{1,0:T(8,128)(2,1)} %get-tuple-element.95), channel_id=1, source_target_pairs={{0,4},{1,5},{2,6},{3,7},{4,0},{5,1},{6,2},{7,3},{8,12},{9,13},{10,... | collective-permute-start | bytes 1572872 | tf_op jit(solution)/shard_map/second_grad_collect/ppermute | solution.py:49
  439.5 14.0 %collective-permute-start.26 = (bf16[128,2048]{1,0:T(8,128)(2,1)S(1)}, bf16[128,2048]{1,0:T(8,128)(2,1)S(1)}, u32[]{:S(2)}, u32[]{:S(2)}) collective-permute-start(bf16[128,2048]{1,0:T(8,128)(2,1)S(1)} %get-tuple-element.68), channel_id=1, source_target_pairs={{0,2},{1,3},{2,0},{3,1},{4,6},{5,7},{6,4},{7,5},{8,10},{9,11},{10,... | collective-permute-start | bytes 1572872 | tf_op jit(solution)/shard_map/branch_grad_spread/ppermute | solution.py:49
  439.9 14.9 %collective-permute-start.27 = (bf16[128,2048]{1,0:T(8,128)(2,1)S(1)}, bf16[128,2048]{1,0:T(8,128)(2,1)S(1)}, u32[]{:S(2)}, u32[]{:S(2)}) collective-permute-start(bf16[128,2048]{1,0:T(8,128)(2,1)S(1)} %get-tuple-element.68), channel_id=1, source_target_pairs={{0,4},{1,5},{2,6},{3,7},{4,0},{5,1},{6,2},{7,3},{8,12},{9,13},{10,... | collective-permute-start | bytes 1572872 | tf_op jit(solution)/shard_map/branch_grad_spread/ppermute | solution.py:49
  441.4 23.0 %collective-permute-start.28 = (bf16[128,2048]{1,0:T(8,128)(2,1)S(1)}, bf16[128,2048]{1,0:T(8,128)(2,1)S(1)}, u32[]{:S(2)}, u32[]{:S(2)}) collective-permute-start(bf16[128,2048]{1,0:T(8,128)(2,1)S(1)} %get-tuple-element.68), channel_id=1, source_target_pairs={{0,6},{1,7},{2,4},{3,5},{4,2},{5,3},{6,0},{7,1},{8,14},{9,15},{10,... | collective-permute-start | bytes 1572872 | tf_op jit(solution)/shard_map/branch_grad_spread/ppermute | solution.py:49
  466.1 4.3 collective-permute-start.29
  481.6 12.4 %copy-start.26 = (bf16[2048,1024]{1,0:T(8,128)(2,1)S(1)}, bf16[2048,1024]{1,0:T(8,128)(2,1)}, u32[]{:S(2)}) copy-start(bf16[2048,1024]{1,0:T(8,128)(2,1)} %all-gather.4.cloned.1.call-done) | copy-start | bytes 12582916
  497.1 8.6 %collective-permute-start.33 = (bf16[512,2048]{1,0:T(8,128)(2,1)S(1)}, bf16[512,2048]{1,0:T(8,128)(2,1)S(1)}, u32[]{:S(2)}, u32[]{:S(2)}) collective-permute-start(bf16[512,2048]{1,0:T(8,128)(2,1)S(1)} %convolution_convert_fusion.5), channel_id=1, source_target_pairs={{0,1},{1,0},{2,3},{3,2},{4,5},{5,4},{6,7},{7,6},{8,9},{9,8},{10,11... | collective-permute-start | bytes 6291464 | tf_op jit(solution)/shard_map/first_grad_collect/ppermute | solution.py:49
  501.1 68.1 %collective-permute-start.23 = (bf16[512,2048]{1,0:T(8,128)(2,1)}, bf16[512,2048]{1,0:T(8,128)(2,1)}, u32[]{:S(2)}, u32[]{:S(2)}) collective-permute-start(bf16[512,2048]{1,0:T(8,128)(2,1)} %convolution_convert_fusion.3), channel_id=1, source_target_pairs={{0,1},{1,0},{2,3},{3,2},{4,5},{5,4},{6,7},{7,6},{8,9},{9,8},{10,11... | collective-permute-start | bytes 6291464 | tf_op jit(solution)/shard_map/feed_collect/ppermute | solution.py:49
  510.0 14.9 %collective-permute-start.36 = (bf16[128,2048]{1,0:T(8,128)(2,1)S(1)}, bf16[128,2048]{1,0:T(8,128)(2,1)S(1)}, u32[]{:S(2)}, u32[]{:S(2)}) collective-permute-start(bf16[128,2048]{1,0:T(8,128)(2,1)S(1)} %get-tuple-element.89), channel_id=1, source_target_pairs={{0,6},{1,7},{2,4},{3,5},{4,2},{5,3},{6,0},{7,1},{8,14},{9,15},{10,... | collective-permute-start | bytes 1572872 | tf_op jit(solution)/shard_map/first_grad_collect/ppermute | solution.py:49
  566.2 13.8 %collective-permute-start.34 = (bf16[128,2048]{1,0:T(8,128)(2,1)}, bf16[128,2048]{1,0:T(8,128)(2,1)S(1)}, u32[]{:S(2)}, u32[]{:S(2)}) collective-permute-start(bf16[128,2048]{1,0:T(8,128)(2,1)} %get-tuple-element.88), channel_id=1, source_target_pairs={{0,2},{1,3},{2,0},{3,1},{4,6},{5,7},{6,4},{7,5},{8,10},{9,11},{10,... | collective-permute-start | bytes 1572872 | tf_op jit(solution)/shard_map/first_grad_collect/ppermute | solution.py:49
  567.7 13.4 %copy-start.9 = (bf16[1,128,2048]{2,1,0:T(8,128)(2,1)S(1)}, bf16[1,128,2048]{2,1,0:T(8,128)(2,1)}, u32[]{:S(2)}) copy-start(bf16[1,128,2048]{2,1,0:T(8,128)(2,1)} %param.9) | copy-start | bytes 1572868
  567.7 13.4 %copy-start.28 = (f32[1,2048]{1,0:T(1,128)S(1)}, f32[1,2048]{1,0:T(1,128)}, u32[]{:S(2)}) copy-start(f32[1,2048]{1,0:T(1,128)} %copy-done.27) | copy-start | bytes 24580
  567.7 13.4 %copy-start.30 = (f32[128]{0:T(128)S(1)}, f32[128]{0:T(128)}, u32[]{:S(2)}) copy-start(f32[128]{0:T(128)} %copy-done.29) | copy-start | bytes 1540
  567.7 13.4 %collective-permute-start.35 = (bf16[128,2048]{1,0:T(8,128)(2,1)}, bf16[128,2048]{1,0:T(8,128)(2,1)S(1)}, u32[]{:S(2)}, u32[]{:S(2)}) collective-permute-start(bf16[128,2048]{1,0:T(8,128)(2,1)} %get-tuple-element.90), channel_id=1, source_target_pairs={{0,4},{1,5},{2,6},{3,7},{4,0},{5,1},{6,2},{7,3},{8,12},{9,13},{10,... | collective-permute-start | bytes 1572872 | tf_op jit(solution)/shard_map/first_grad_collect/ppermute | solution.py:49
  576.1 34.7 %copy-start.5 = (f32[128,2048]{1,0:T(8,128)S(1)}, f32[128,2048]{1,0:T(8,128)}, u32[]{:S(2)}) copy-start(f32[128,2048]{1,0:T(8,128)} %copy-done.4) | copy-start | bytes 3145732
  580.0 33.1 %copy-start.23 = (bf16[128,2048]{1,0:T(8,128)(2,1)}, bf16[128,2048]{1,0:T(8,128)(2,1)S(1)}, u32[]{:S(2)}) copy-start(bf16[128,2048]{1,0:T(8,128)(2,1)S(1)} %collective-permute-done.34) | copy-start | bytes 1572868
  581.2 31.9 %copy-start.24 = (bf16[128,2048]{1,0:T(8,128)(2,1)}, bf16[128,2048]{1,0:T(8,128)(2,1)S(1)}, u32[]{:S(2)}) copy-start(bf16[128,2048]{1,0:T(8,128)(2,1)S(1)} %collective-permute-done.35) | copy-start | bytes 1572868
  583.2 6.7 collective-permute-start.37
  586.3 14.3 %collective-permute-start.30 = (bf16[128,2048]{1,0:T(8,128)(2,1)S(1)}, bf16[128,2048]{1,0:T(8,128)(2,1)S(1)}, u32[]{:S(2)}, u32[]{:S(2)}) collective-permute-start(bf16[128,2048]{1,0:T(8,128)(2,1)S(1)} %get-tuple-element.91), channel_id=1, source_target_pairs={{0,2},{1,3},{2,0},{3,1},{4,6},{5,7},{6,4},{7,5},{8,10},{9,11},{10,... | collective-permute-start | bytes 1572872 | tf_op jit(solution)/shard_map/feed_collect/ppermute | solution.py:49
  586.9 14.9 %collective-permute-start.31 = (bf16[128,2048]{1,0:T(8,128)(2,1)S(1)}, bf16[128,2048]{1,0:T(8,128)(2,1)S(1)}, u32[]{:S(2)}, u32[]{:S(2)}) collective-permute-start(bf16[128,2048]{1,0:T(8,128)(2,1)S(1)} %get-tuple-element.93), channel_id=1, source_target_pairs={{0,4},{1,5},{2,6},{3,7},{4,0},{5,1},{6,2},{7,3},{8,12},{9,13},{10,... | collective-permute-start | bytes 1572872 | tf_op jit(solution)/shard_map/feed_collect/ppermute | solution.py:49
  587.4 23.4 %collective-permute-start.32 = (bf16[128,2048]{1,0:T(8,128)(2,1)S(1)}, bf16[128,2048]{1,0:T(8,128)(2,1)S(1)}, u32[]{:S(2)}, u32[]{:S(2)}) collective-permute-start(bf16[128,2048]{1,0:T(8,128)(2,1)S(1)} %get-tuple-element.92), channel_id=1, source_target_pairs={{0,6},{1,7},{2,4},{3,5},{4,2},{5,3},{6,0},{7,1},{8,14},{9,15},{10,... | collective-permute-start | bytes 1572872 | tf_op jit(solution)/shard_map/feed_collect/ppermute | solution.py:49
  589.9 10.6 %collective-permute-start.38 = (f32[2,512]{1,0:T(2,128)S(1)}, f32[2,512]{1,0:T(2,128)S(1)}, u32[]{:S(2)}, u32[]{:S(2)}) collective-permute-start(f32[2,512]{1,0:T(2,128)S(1)} %broadcast_select_fusion.3), channel_id=1, source_target_pairs={{0,2},{1,3},{2,0},{3,1},{4,6},{5,7},{6,4},{7,5},{8,10},{9,11},{10,... | collective-permute-start | bytes 12296 | tf_op jit(solution)/shard_map/gain_scatter/ppermute | solution.py:49
  600.5 16.2 %collective-permute-start.39 = (f32[2,256]{1,0:T(2,128)S(1)}, f32[2,256]{1,0:T(2,128)S(1)}, u32[]{:S(2)}, u32[]{:S(2)}) collective-permute-start(f32[2,256]{1,0:T(2,128)S(1)} %broadcast_select_fusion.6), channel_id=1, source_target_pairs={{0,1},{1,0},{2,3},{3,2},{4,5},{5,4},{6,7},{7,6},{8,9},{9,8},{10,11... | collective-permute-start | bytes 6152 | tf_op jit(solution)/shard_map/gain_scatter/ppermute | solution.py:49
  613.1 14.7 %all-to-all-start.4 = ((bf16[2,256,1024]{2,1,0:T(8,128)(2,1)}), bf16[2,256,1024]{2,1,0:T(8,128)(2,1)S(1)}, u32[]{:S(2)}, u32[]{:S(2)}) async-start(bf16[2,256,1024]{2,1,0:T(8,128)(2,1)} %bitcast.132), calls=%async_computation.7 | async-start | bytes 2097152 | tf_op jit(solution)/shard_map/down_return/all_to_all | solution.py:141
  616.7 15.8 %collective-permute-start.40 = (f32[2,128]{1,0:T(2,128)S(1)}, f32[2,128]{1,0:T(2,128)S(1)}, u32[]{:S(2)}, u32[]{:S(2)}) collective-permute-start(f32[2,128]{1,0:T(2,128)S(1)} %broadcast_select_fusion.9), channel_id=1, source_target_pairs={{0,16},{8,24},{16,0},{24,8},{1,17},{9,25},{17,1},{25,9},{2,18},{10... | collective-permute-start | bytes 3080 | tf_op jit(solution)/shard_map/gain_scatter/ppermute | solution.py:49
  628.7 25.3 %all-to-all-start.2 = ((bf16[2,256,2048]{2,1,0:T(8,128)(2,1)}), bf16[2,256,2048]{2,1,0:T(8,128)(2,1)S(1)}, u32[]{:S(2)}, u32[]{:S(2)}) async-start(bf16[2,256,2048]{2,1,0:T(8,128)(2,1)} %bitcast.127), calls=%async_computation.5 | async-start | bytes 4194304 | tf_op jit(solution)/shard_map/gate_up_return/all_to_all | solution.py:141
  632.6 5.2 collective-permute-start.41
  660.2 13.1 %all-to-all-start.3 = ((bf16[2,256,1024]{2,1,0:T(8,128)(2,1)}), bf16[2,256,1024]{2,1,0:T(8,128)(2,1)S(1)}, u32[]{:S(2)}, u32[]{:S(2)}) async-start(bf16[2,256,1024]{2,1,0:T(8,128)(2,1)} %bitcast.123), calls=%async_computation.6 | async-start | bytes 2097152 | tf_op jit(solution)/shard_map/attention_return/all_to_all | solution.py:141
  (26 other events, 123.9 us)
Sparse Core Ops, SparseCore 0:
  28.9 81.6 all-gather.3
  112.1 148.0 all-gather.5
  262.3 78.9 all-gather.7
  343.5 75.2 reduce-scatter.3
  421.1 144.9 reduce-scatter.5
  569.0 77.5 reduce-scatter.7

commit v4 on v3

--- a/solution.py
+++ b/solution.py
@@ -87,12 +87,10 @@
     return join_halves(near, swap_by(near, axes, size, 1)), pieces[-1]
 
 
-def collect(left, right, product, axes, size, *tied, begin=()):
+def collect(left, right, product, axes, size, begin=()):
     half = left.shape[0] // 2
     received = swap_by(product(left[half:], right).astype(BF16), axes, size, 1)
     near = (product(left[:half], right) + received.astype(F32)).astype(BF16)
-    if tied:
-        near, *tied = together(near, *tied)
     if begin:
         near = after(near, *begin)
     rows = near.shape[0] // (size // 2)
@@ -101,7 +99,7 @@
         for place in range(1, size // 2)
     ]
     summed = sum([block.astype(F32) for block in blocks], near[:rows].astype(F32))
-    return summed, blocks[-1], *tied
+    return summed, blocks
 
 
 def gather_small(value, axis_sizes):
@@ -167,17 +165,24 @@
     return lax.psum_scatter(grads, "dp", scatter_dimension=0, tiled=True)
 
 
-def return_columns(summed, blocks, kinds, own):
-    parted = trade(summed.reshape(blocks, -1, summed.shape[1]), "blk").astype(F32)
+def return_columns(summed, blocks, kinds, wide):
+    parted = summed.reshape(blocks, -1, summed.shape[1])
+    if blocks == 2:
+        first = lax.axis_index("blk") == 0
+        got = swap_by(jnp.where(first, parted[1], parted[0]), "blk", blocks, 1).astype(F32)
+        own = jnp.where(first, parted[0], parted[1]).astype(F32)
+        parted = [jnp.where(first, own, got), jnp.where(first, got, own)]
+    else:
+        parted = list(trade(parted, "blk").astype(F32))
     totals = []
     start = 0
     for kind in kinds:
         columns = [
-            [parted[b, :, start + i * own : start + (i + 1) * own] for b in range(blocks)]
+            [parted[b][:, start + i * wide : start + (i + 1) * wide] for b in range(blocks)]
             for i in range(kind)
         ]
         totals.append(jnp.stack([jnp.concatenate(part, axis=1) for part in columns], axis=1))
-        start += kind * own
+        start += kind * wide
     return totals
 
 
@@ -560,7 +565,7 @@
     grad_normed_second, last_second = named(
         "second_grad_collect", collect, grad_gates, full_gate_up, dot_nt, PLANE, group
     )
-    grad_gate_up = after(grad_gate_up, down_sum, last_second)
+    grad_gate_up = after(grad_gate_up, down_sum, *last_second)
     gate_up_sum = named("gate_up_back", sum_rows, grad_gate_up)
     grad_middle_norm, sum_second = norm_back(
         grad_normed_second, unit_second, factor_second, gain_second
@@ -568,7 +573,7 @@
     grad_middle = grad_output + grad_middle_norm
     grad_branch, _ = named("branch_grad_spread", spread, grad_middle.astype(BF16), PLANE, group)
     with jax.named_scope("feed_collect"):
-        feed_hidden = after(hidden, last_second)
+        feed_hidden = after(hidden, *last_second)
         feed_out, _ = collect(
             feed_hidden, full_down, dot_nt, PLANE, group, begin=(grad_branch,)
         )
@@ -595,7 +600,7 @@
         "first_grad_collect", collect, grad_projected, full_qkv, dot_nt, PLANE, group
     )
     both = jnp.concatenate([grad_qkv, grad_out], axis=1)
-    both_sum = named("attention_back", sum_rows, after(both, gate_up_sum, last_grad))
+    both_sum = named("attention_back", sum_rows, after(both, gate_up_sum, feed_out, total_down, *last_grad))
 
     outcome = (middle + feed_out).astype(BF16)
     grad_input_norm, sum_first = norm_back(grad_normed_first, unit_first, factor_first, gain_first)
@@ -604,7 +609,7 @@
     [total_gate_up] = named(
         "gate_up_return", return_columns, gate_up_sum, size_blk, [2], wide
     )
-    both_sum = after(both_sum, total_gate_up, total_down, outcome, grad_input, gain_sums)
+    both_sum = after(both_sum, total_gate_up, outcome, grad_input, gain_sums)
     total_qkv, total_out = named(
         "attention_return", return_columns, both_sum, size_blk, [3, 1], features
     )

time: 691 us -> 678 us (0.981)
  starting transfers between devices: 64.8 us -> 54.3 us
  local copies, waits for them, and re-layouts: 45 us -> 36.7 us
    all_to_all x4 -> x1, waiting for transfers between devices: 47.9 us -> 25.5 us  [trade(): return lax.all_to_all(blocks, axis, 0, 0, tiled=True)]
    ppermute x42 -> x45, waiting for transfers between devices: 166 us -> 183 us  [swap_by(): return lax.ppermute(value, axes, [(i, i ^ bits) for i in range(size)])]
    all_to_all x4 -> x1, starting transfers between devices: 16.4 us -> 5.33 us  [trade(): return lax.all_to_all(blocks, axis, 0, 0, tiled=True)]
    reduce_scatter x3, waiting for transfers between devices: 67.9 us -> 76.7 us  [sum_rows(): return lax.psum_scatter(grads, 'dp', scatter_dimension=0, tiled=True)]
    unnamed x83 -> x85, local copies, waits for them, and re-layouts: 21.5 us -> 17.4 us
    ppermute x42 -> x45, starting transfers between devices: 47.7 us -> 48.3 us  [swap_by(): return lax.ppermute(value, axes, [(i, i ^ bits) for i in range(size)])]
  transfers between devices with their start and end apart: 52 -> 52, of which waited for: 37 -> 38; matrix products, arithmetic and copies ran while one was open for 24% -> 25% of each run, Pallas kernels for 8% -> 8%
where the time goes in v4:
time: 678 us; the launch traced here: 671 us
  waiting for transfers between devices  352 us (52%)
  matrix products  104 us (15%)
  starting transfers between devices  54.3 us (8%)
  Pallas kernels  52.2 us (8%)
  other arithmetic  40.3 us (6%)
  local copies, waits for them, and re-layouts  36.7 us (5%)
  blocking collectives  17.6 us (3%)
  between operations  15.1 us (2%)
    ppermute x45, waiting for transfers between devices, swap_by(): return lax.ppermute(value, axes, [(i, i ^ bits) for i in range(size)])  183 us
    reduce_scatter x3, waiting for transfers between devices, sum_rows(): return lax.psum_scatter(grads, 'dp', scatter_dimension=0, tiled=True)  76.7 us
    all_gather x3, waiting for transfers between devices, gather_rows(): return lax.all_gather(after(weight, *events), 'dp', axis=0, tiled=True)  66.3 us
    ppermute x45, starting transfers between devices, swap_by(): return lax.ppermute(value, axes, [(i, i ^ bits) for i in range(size)])  48.3 us
    dot_general x5, matrix products, dot_nn(): lax.dot_general(a, b, (((1,), (0,)), ((), ())), preferred_element_type=F32)  42.7 us
    dot_general x8, matrix products, dot_nt(): lax.dot_general(a, b, (((1,), (1,)), ((), ())), preferred_element_type=F32)  35.4 us
    pallas_call x4, Pallas kernels, join_halves(): pl.pallas_call(functools.partial(join_kernel, steps), grid=(2 * steps,),...  29.1 us
    dot_general x4, matrix products, dot_tn(): lax.dot_general(a, b, (((0,), (0,)), ((), ())), preferred_element_type=F32)  25.6 us
  transfers between devices with their start and end apart: 52, of which 38 were waited for; matrix products, arithmetic and copies ran while one was open for 25% of the time, Pallas kernels for 8%

profile of v4, /device:TPU:0, one launch (start us, length us, event | category | flops | bytes accessed | tf_op | source)
XLA Modules:
  0.0 671.5 jit_solution(5781422656879797965)
XLA Ops:
  9.9 17.6 %all_to_all.10 = bf16[2,256,1024]{1,2,0:T(8,128)(2,1)S(1)} all-to-all(bf16[2,256,1024]{1,2,0:T(8,128)(2,1)S(1)} %pad_maximum_fusion.10), channel_id=1, replica_groups=mesh['dp'=4,'blk'=2,'tensor'=4] {'blk'}, dimensions={0} | all-to-all | bytes 2097152 | tf_op jit(solution)/shard_map/attention_weights/all_to_all | solution.py:139
  31.8 6.2 copy.38
  43.7 5.3 all-to-all-start
  51.0 2.8 collective-permute-done.3
  55.5 3.2 collective-permute-done.4
  59.7 25.5 %all-to-all-done = bf16[2,256,3072]{1,2,0:T(8,128)(2,1)} async-done(((bf16[2,256,3072]{1,2,0:T(8,128)(2,1)}), bf16[2,256,3072]{1,2,0:T(8,128)(2,1)}, u32[]{:S(2)}, u32[]{:S(2)}) %all-to-all-start) | async-done | bytes 3145760 | tf_op jit(solution)/shard_map/feed_weights/all_to_all | solution.py:139
  85.2 3.2 copy.41
  91.0 13.5 %collective-permute-done.7 = bf16[128,2048]{1,0:T(8,128)(2,1)S(1)} collective-permute-done((bf16[128,2048]{1,0:T(8,128)(2,1)}, bf16[128,2048]{1,0:T(8,128)(2,1)S(1)}, u32[]{:S(2)}, u32[]{:S(2)}) %collective-permute-start.7) | collective-permute-done | bytes 524320 | tf_op jit(solution)/shard_map/first_spread/ppermute | solution.py:49
  104.5 6.1 all-gather.4.cloned.1.call-done
  115.6 9.0 %collective-permute-done.5 = bf16[128,2048]{1,0:T(8,128)(2,1)S(1)} collective-permute-done((bf16[128,2048]{1,0:T(8,128)(2,1)}, bf16[128,2048]{1,0:T(8,128)(2,1)S(1)}, u32[]{:S(2)}, u32[]{:S(2)}) %collective-permute-start.5) | collective-permute-done | bytes 524320 | tf_op jit(solution)/shard_map/first_spread/ppermute | solution.py:49
  134.3 7.3 %join_halves.4 = bf16[1024,2048]{1,0:T(8,128)(2,1)} custom-call(bf16[512,2048]{1,0:T(8,128)(2,1)} %constant_dynamic-update-slice_fusion.near_ref, bf16[512,2048]{1,0:T(8,128)(2,1)} %collective-permute-done.8.far_ref), custom_call_target="tpu_custom_call" | custom-call | bytes 8388608 | tf_op jit(solution)/shard_map/first_spread/join_halves/pallas_call | solution.py:68
  141.6 8.2 %fusion.8.q_ref.k_ref.v_ref = f32[1024,768]{1,0:T(8,128)} fusion(bf16[1024,2048]{1,0:T(8,128)(2,1)} %join_halves.4, bf16[2048,1024]{1,0:T(8,128)(2,1)} %all-gather.4.cloned.1.call-done), kind=kOutput, calls=%fused_computation.34 | convolution fusion | flops 3221225472 | bytes 10485760 | tf_op jit(solution)/shard_map/dot_general | solution.py:24
  149.8 10.6 %attend.1 = (bf16[1024,256]{1,0:T(8,128)(2,1)S(1)}, bf16[1024,256]{1,0:T(8,128)(2,1)S(1)}, bf16[1024,256]{1,0:T(8,128)(2,1)S(1)}, bf16[1024,256]{1,0:T(8,128)(2,1)S(1)}, f32[1024,256]{1,0:T(8,128)S(1)}) custom-call(s32[4]{0:T(128)S(1)} %pad_add_fusion.info_ref, f32[1024,768]{1,0:T(8,128)} %fusion.8.q_ref.k_ref.v_ref, f32[1024,768]{1,0:T(8,128)} %fusion.8.q_ref.k_ref.v_ref, ...), custom_call_target="tpu_custom_call" | custom-call | flops 1073741824 | bytes 4718592 | tf_op jit(solution)/shard_map/attend/pallas_call | solution.py:294
  161.8 3.8 collective-permute-done.9
  172.7 8.9 %collective-permute-done.10 = bf16[128,2048]{1,0:T(8,128)(2,1)S(1)} collective-permute-done((bf16[128,2048]{1,0:T(8,128)(2,1)S(1)}, bf16[128,2048]{1,0:T(8,128)(2,1)S(1)}, u32[]{:S(2)}, u32[]{:S(2)}) %collective-permute-start.10) | collective-permute-done | bytes 524320 | tf_op jit(solution)/shard_map/branch_collect/ppermute | solution.py:49
  183.6 10.5 %collective-permute-done.12 = bf16[128,2048]{1,0:T(8,128)(2,1)S(1)} collective-permute-done((bf16[128,2048]{1,0:T(8,128)(2,1)S(1)}, bf16[128,2048]{1,0:T(8,128)(2,1)S(1)}, u32[]{:S(2)}, u32[]{:S(2)}) %collective-permute-start.12) | collective-permute-done | bytes 524320 | tf_op jit(solution)/shard_map/branch_collect/ppermute | solution.py:49
  198.5 5.5 collective-permute-done.17
  204.0 2.1 collective-permute-start.15
  206.1 10.6 %collective-permute-done.19 = bf16[128,2048]{1,0:T(8,128)(2,1)S(1)} collective-permute-done((bf16[128,2048]{1,0:T(8,128)(2,1)S(1)}, bf16[128,2048]{1,0:T(8,128)(2,1)S(1)}, u32[]{:S(2)}, u32[]{:S(2)}) %collective-permute-start.19) | collective-permute-done | bytes 524320 | tf_op jit(solution)/shard_map/cotangent_spread/ppermute | solution.py:49
  218.2 7.5 %collective-permute-done.13 = bf16[128,2048]{1,0:T(8,128)(2,1)S(1)} collective-permute-done((bf16[128,2048]{1,0:T(8,128)(2,1)S(1)}, bf16[128,2048]{1,0:T(8,128)(2,1)S(1)}, u32[]{:S(2)}, u32[]{:S(2)}) %collective-permute-start.13) | collective-permute-done | bytes 524320 | tf_op jit(solution)/shard_map/second_spread/ppermute | solution.py:49
  227.5 10.7 %collective-permute-done.15 = bf16[128,2048]{1,0:T(8,128)(2,1)S(1)} collective-permute-done((bf16[128,2048]{1,0:T(8,128)(2,1)S(1)}, bf16[128,2048]{1,0:T(8,128)(2,1)S(1)}, u32[]{:S(2)}, u32[]{:S(2)}) %collective-permute-start.15) | collective-permute-done | bytes 524320 | tf_op jit(solution)/shard_map/second_spread/ppermute | solution.py:49
  239.8 7.1 %join_halves.6 = bf16[1024,2048]{1,0:T(8,128)(2,1)} custom-call(bf16[512,2048]{1,0:T(8,128)(2,1)} %copy-done.11, bf16[512,2048]{1,0:T(8,128)(2,1)} %collective-permute-done.20.far_ref), custom_call_target="tpu_custom_call" | custom-call | bytes 8388608 | tf_op jit(solution)/shard_map/cotangent_spread/join_halves/pallas_call | solution.py:68
  246.9 7.1 %join_halves.5 = bf16[1024,2048]{1,0:T(8,128)(2,1)} custom-call(bf16[512,2048]{1,0:T(8,128)(2,1)} %pad_maximum_fusion.5.near_ref, bf16[512,2048]{1,0:T(8,128)(2,1)} %collective-permute-done.16.far_ref), custom_call_target="tpu_custom_call" | custom-call | bytes 8388608 | tf_op jit(solution)/shard_map/second_spread/join_halves/pallas_call | solution.py:68
  254.1 6.1 all-gather.6.cloned.1.call-done
  260.7 10.1 %fusion.2 = f32[1024,1024]{0,1:T(8,128)} fusion(bf16[1024,2048]{1,0:T(8,128)(2,1)} %join_halves.5, bf16[2048,2048]{1,0:T(8,128)(2,1)} %all-gather.6.cloned.1.call-done), kind=kOutput, calls=%fused_computation.8 | convolution fusion | flops 4294967296 | bytes 12582912 | tf_op jit(solution)/shard_map/dot_general | solution.py:24
  270.8 8.6 %multiply_convert_fusion.2 = (bf16[1024,1024]{0,1:T(8,128)(2,1)}, f32[1024,1024]{0,1:T(8,128)}) fusion(f32[1024,1024]{0,1:T(8,128)} %fusion.2, bf16[1024,2048]{1,0:T(8,128)(2,1)S(1)} %copy-done.14, bf16[2048,2048]{1,0:T(8,128)(2,1)S(1)} %copy-done.32), kind=kOutput, calls=%fused_computation.17 | convolution fusion | flops 4301258752 | bytes 18874368 | tf_op jit(solution)/shard_map/dot_general | solution.py:24
  279.4 7.8 %convolution_convert_fusion.1 = bf16[2048,1024]{1,0:T(8,128)(2,1)} fusion(bf16[1024,2048]{1,0:T(8,128)(2,1)S(1)} %copy-done.17, bf16[1024,1024]{0,1:T(8,128)(2,1)} %get-tuple-element.32), kind=kOutput, calls=%fused_computation.21 | convolution fusion | flops 4297064448 | bytes 10485760 | tf_op jit(solution)/shard_map/dot_general | solution.py:32
  287.3 54.1 %all-gather.8.cloned.1.call-done = bf16[2048,1024]{1,0:T(8,128)(2,1)} async-done(((bf16[512,1024]{1,0:T(8,128)(2,1)}), bf16[2048,1024]{1,0:T(8,128)(2,1)}) %all-gather.8.cloned.1.call-update) | async-done | bytes 4194320 | tf_op jit(solution)/shard_map/down_gather/all_gather | solution.py:161
  341.4 11.9 %multiply_convert_fusion = (bf16[1024,1024]{0,1:T(8,128)(2,1)S(1)}, bf16[1024,1024]{0,1:T(8,128)(2,1)S(1)}) fusion(f32[1024,1024]{0,1:T(8,128)} %fusion.2, f32[1024,1024]{0,1:T(8,128)} %get-tuple-element.129, bf16[1024,2048]{1,0:T(8,128)(2,1)} %join_halves.6, bf16[2048,1024]{1,0:T(8,128)(2,1)} %all-gather.8.cloned.1.call-done), kind=kOutput, calls=%fused_computation.15 | convolution fusion | flops 4308598784 | bytes 20971520 | tf_op jit(solution)/shard_map/dot_general | solution.py:24
  353.4 8.4 %convolution_convert_fusion.6 = bf16[512,2048]{1,0:T(8,128)(2,1)S(1)} fusion(bf16[2048,2048]{1,0:T(8,128)(2,1)} %all-gather.6.cloned.1.call-done, bf16[1024,1024]{0,1:T(8,128)(2,1)S(1)} %get-tuple-element.82, bf16[1024,1024]{0,1:T(8,128)(2,1)S(1)} %get-tuple-element.81), kind=kOutput, calls=%fused_computation.27 | convolution fusion | flops 4300210176 | bytes 14680064 | tf_op jit(solution)/shard_map/second_grad_collect/dot_general | solution.py:28
  361.9 4.1 collective-permute-done.21
  366.0 8.4 %add_convert_fusion.2 = bf16[512,2048]{1,0:T(8,128)(2,1)S(1)} fusion(bf16[512,2048]{1,0:T(8,128)(2,1)S(1)} %collective-permute-done.21, bf16[2048,2048]{1,0:T(8,128)(2,1)} %all-gather.6.cloned.1.call-done, bf16[1024,1024]{0,1:T(8,128)(2,1)S(1)} %get-tuple-element.82, bf16[1024,1024]{0,1:T(8,128)(2,1)S(1)} %get-tuple-element.81), kind=kOutput, calls=%fused_computation.14 | convolution fusion | flops 4302307328 | bytes 16777216 | tf_op jit(solution)/shard_map/second_grad_collect/dot_general | solution.py:28
  380.4 12.5 %convolution_convert_fusion = bf16[2048,2048]{1,0:T(8,128)(2,1)} fusion(bf16[1024,2048]{1,0:T(8,128)(2,1)S(1)} %copy-done.15, bf16[1024,1024]{0,1:T(8,128)(2,1)S(1)} %get-tuple-element.81, bf16[1024,1024]{0,1:T(8,128)(2,1)S(1)} %get-tuple-element.82), kind=kOutput, calls=%fused_computation | convolution fusion | flops 8602517504 | bytes 16777216 | tf_op jit(solution)/shard_map/dot_general | solution.py:32
  393.6 10.1 %collective-permute-done.24 = bf16[128,2048]{1,0:T(8,128)(2,1)} collective-permute-done((bf16[128,2048]{1,0:T(8,128)(2,1)}, bf16[128,2048]{1,0:T(8,128)(2,1)}, u32[]{:S(2)}, u32[]{:S(2)}) %collective-permute-start.24) | collective-permute-done | bytes 524320 | tf_op jit(solution)/shard_map/second_grad_collect/ppermute | solution.py:49
  403.6 15.2 %reduce-scatter.4.cloned.1.call-done = bf16[512,1024]{1,0:T(8,128)(2,1)} async-done(((bf16[2048,1024]{1,0:T(8,128)(2,1)}), bf16[512,1024]{1,0:T(8,128)(2,1)}) %reduce-scatter.4.cloned.1.call-update) | async-done | bytes 1048592 | tf_op jit(solution)/shard_map/down_back/reduce_scatter | solution.py:165
  418.9 2.3 multiply_reduce_fusion
  421.3 3.7 fusion.45
  428.5 10.4 %collective-permute-done.26 = bf16[128,2048]{1,0:T(8,128)(2,1)S(1)} collective-permute-done((bf16[128,2048]{1,0:T(8,128)(2,1)S(1)}, bf16[128,2048]{1,0:T(8,128)(2,1)S(1)}, u32[]{:S(2)}, u32[]{:S(2)}) %collective-permute-start.26) | collective-permute-done | bytes 524320 | tf_op jit(solution)/shard_map/branch_grad_spread/ppermute | solution.py:49
  439.0 2.4 collective-permute-done.27
  441.3 9.8 %collective-permute-done.28 = bf16[128,2048]{1,0:T(8,128)(2,1)S(1)} collective-permute-done((bf16[128,2048]{1,0:T(8,128)(2,1)S(1)}, bf16[128,2048]{1,0:T(8,128)(2,1)S(1)}, u32[]{:S(2)}, u32[]{:S(2)}) %collective-permute-start.28) | collective-permute-done | bytes 524320 | tf_op jit(solution)/shard_map/branch_grad_spread/ppermute | solution.py:49
  451.5 3.7 convolution_convert_fusion.3
  455.7 7.6 %join_halves.7 = bf16[1024,2048]{1,0:T(8,128)(2,1)} custom-call(bf16[512,2048]{1,0:T(8,128)(2,1)} %copy-done.12, bf16[512,2048]{1,0:T(8,128)(2,1)} %collective-permute-done.29.far_ref), custom_call_target="tpu_custom_call" | custom-call | bytes 8388608 | tf_op jit(solution)/shard_map/branch_grad_spread/join_halves/pallas_call | solution.py:68
  463.3 3.8 convolution_convert_fusion.8.grad_ref
  467.2 12.4 %attend_back.1 = bf16[1024,768]{1,0:T(8,128)(2,1)} custom-call(s32[4]{0:T(128)S(1)} %pad_add_fusion.info_ref, bf16[1024,256]{1,0:T(8,128)(2,1)S(1)} %get-tuple-element.34.q_row, bf16[1024,256]{1,0:T(8,128)(2,1)S(1)} %copy-done.1, bf16[1024,256]{1,0:T(8,128)(2,1)S(1)} %copy-done.3, f32[1024,256]{1,0:T(8,128)S(1)} %get-tuple-element.37.log_ref, ...), custom_call_target="tpu_custom_call" | custom-call | flops 2684354560 | bytes 5242880 | tf_op jit(solution)/shard_map/attend_back/pallas_call | solution.py:410
  479.6 4.5 convolution_convert_fusion.5
  484.3 4.1 add_convert_fusion.1
  495.4 3.9 convolution_convert_fusion.2
  499.3 2.6 pad_maximum_fusion.2
  501.9 4.7 add_convert_fusion
  510.4 7.0 %collective-permute-done.32 = bf16[128,2048]{1,0:T(8,128)(2,1)} collective-permute-done((bf16[128,2048]{1,0:T(8,128)(2,1)}, bf16[128,2048]{1,0:T(8,128)(2,1)}, u32[]{:S(2)}, u32[]{:S(2)}) %collective-permute-start.32) | collective-permute-done | bytes 524320 | tf_op jit(solution)/shard_map/feed_collect/ppermute | solution.py:49
  517.4 2.6 add_convert_fusion.4
  520.0 8.5 %collective-permute-done.34 = bf16[128,2048]{1,0:T(8,128)(2,1)S(1)} collective-permute-done((bf16[128,2048]{1,0:T(8,128)(2,1)S(1)}, bf16[128,2048]{1,0:T(8,128)(2,1)S(1)}, u32[]{:S(2)}, u32[]{:S(2)}) %collective-permute-start.34) | collective-permute-done | bytes 524320 | tf_op jit(solution)/shard_map/first_grad_collect/ppermute | solution.py:49
  528.7 10.4 %collective-permute-done.36 = bf16[128,2048]{1,0:T(8,128)(2,1)} collective-permute-done((bf16[128,2048]{1,0:T(8,128)(2,1)S(1)}, bf16[128,2048]{1,0:T(8,128)(2,1)}, u32[]{:S(2)}, u32[]{:S(2)}) %collective-permute-start.36) | collective-permute-done | bytes 524320 | tf_op jit(solution)/shard_map/first_grad_collect/ppermute | solution.py:49
  539.1 27.1 %reduce-scatter.6.cloned.1.call-done = bf16[512,2048]{1,0:T(8,128)(2,1)} async-done(((bf16[2048,2048]{1,0:T(8,128)(2,1)}), bf16[512,2048]{1,0:T(8,128)(2,1)}) %reduce-scatter.6.cloned.1.call-update) | async-done | bytes 2097168 | tf_op jit(solution)/shard_map/gate_up_back/reduce_scatter | solution.py:165
  566.3 2.1 fusion.25
  570.1 2.2 collective-permute-done.38
  573.8 2.1 collective-permute-done.39
  577.2 3.2 collective-permute-start.41
  584.6 3.2 fusion.24
  590.2 18.4 %collective-permute-done.37 = bf16[256,2048]{1,0:T(8,128)(2,1)S(1)} collective-permute-done((bf16[256,2048]{1,0:T(8,128)(2,1)S(1)}, bf16[256,2048]{1,0:T(8,128)(2,1)S(1)}, u32[]{:S(2)}, u32[]{:S(2)}) %collective-permute-start.37) | collective-permute-done | bytes 1048608 | tf_op jit(solution)/shard_map/gate_up_return/ppermute | solution.py:49
  609.8 2.3 pad_maximum_fusion.3
  612.1 34.4 %reduce-scatter.8.cloned.1.call-done = bf16[512,1024]{1,0:T(8,128)(2,1)} async-done(((bf16[2048,1024]{1,0:T(8,128)(2,1)}), bf16[512,1024]{1,0:T(8,128)(2,1)}) %reduce-scatter.8.cloned.1.call-update) | async-done | bytes 1048592 | tf_op jit(solution)/shard_map/attention_back/reduce_scatter | solution.py:165
  652.2 5.2 copy.50
  657.5 4.1 collective-permute-done.43
  (239 shorter events, 97.7 us)
Async XLA Ops:
  7.2 103.4 %all-gather.4.cloned.1.call-start = ((), (), s32[]{:S(2)}) async-start(), calls=%async_computation.5 | async-start | bytes 5242880 | tf_op jit(solution)/shard_map/attention_gather/all_gather | solution.py:161
  8.7 20.1 %copy-start.31 = (f32[2,64]{1,0:T(2,128)S(1)}, f32[2,64]{1,0:T(2,128)}, u32[]{:S(2)}) copy-start(f32[2,64]{1,0:T(2,128)} %param.15) | copy-start | bytes 1540
  28.8 1.2 collective-permute-start
  30.1 11.3 %collective-permute-start.1 = (f32[2,128]{1,0:T(2,128)S(1)}, f32[2,128]{1,0:T(2,128)S(1)}, u32[]{:S(2)}, u32[]{:S(2)}) collective-permute-start(f32[2,128]{1,0:T(2,128)S(1)} %pad_maximum_fusion.18), channel_id=1, source_target_pairs={{0,2},{1,3},{2,0},{3,1},{4,6},{5,7},{6,4},{7,5},{8,10},{9,11},{10,... | collective-permute-start | bytes 3080 | tf_op jit(solution)/shard_map/gain_gather/ppermute | solution.py:49
  41.4 7.6 %collective-permute-start.2 = (f32[2,256]{1,0:T(2,128)S(1)}, f32[2,256]{1,0:T(2,128)S(1)}, u32[]{:S(2)}, u32[]{:S(2)}) collective-permute-start(f32[2,256]{1,0:T(2,128)S(1)} %pad_maximum_fusion.17), channel_id=1, source_target_pairs={{0,4},{4,0},{1,5},{5,1},{2,6},{6,2},{3,7},{7,3},{8,12},{12,8},{9,1... | collective-permute-start | bytes 6152 | tf_op jit(solution)/shard_map/gain_gather/ppermute | solution.py:49
  43.7 41.5 %all-to-all-start = ((bf16[2,256,3072]{1,2,0:T(8,128)(2,1)}), bf16[2,256,3072]{1,2,0:T(8,128)(2,1)}, u32[]{:S(2)}, u32[]{:S(2)}) async-start(bf16[2,256,3072]{1,2,0:T(8,128)(2,1)} %pad_maximum_fusion.4), calls=%async_computation | async-start | bytes 6291456 | tf_op jit(solution)/shard_map/feed_weights/all_to_all | solution.py:139
  49.0 211.2 %all-gather.6.cloned.1.call-start = ((), (), s32[]{:S(2)}) async-start(), calls=%async_computation.6 | async-start | bytes 10485760 | tf_op jit(solution)/shard_map/gate_up_gather/all_gather | solution.py:161
  49.1 4.7 collective-permute-start.3
  53.8 4.8 collective-permute-start.4
  89.9 37.5 %copy-start.30 = (s32[1,3]{1,0:T(1,128)S(1)}, s32[1,3]{1,0:T(1,128)}, u32[]{:S(2)}) copy-start(s32[1,3]{1,0:T(1,128)} %param.10) | copy-start | bytes 40
  89.9 40.2 %copy-start.35 = (s32[8]{0:T(128)S(1)}, s32[8]{0:T(128)}, u32[]{:S(2)}) copy-start(s32[8]{0:T(128)} %constant.44.clone) | copy-start | bytes 100
  90.9 13.6 %collective-permute-start.7 = (bf16[128,2048]{1,0:T(8,128)(2,1)}, bf16[128,2048]{1,0:T(8,128)(2,1)S(1)}, u32[]{:S(2)}, u32[]{:S(2)}) collective-permute-start(bf16[128,2048]{1,0:T(8,128)(2,1)} %fusion.20), channel_id=1, source_target_pairs={{0,6},{1,7},{2,4},{3,5},{4,2},{5,3},{6,0},{7,1},{8,14},{9,15},{10,... | collective-permute-start | bytes 1572872 | tf_op jit(solution)/shard_map/first_spread/ppermute | solution.py:49
  110.6 230.8 %all-gather.8.cloned.1.call-start = ((), (), s32[]{:S(2)}) async-start(), calls=%async_computation.7 | async-start | bytes 5242880 | tf_op jit(solution)/shard_map/down_gather/all_gather | solution.py:161
  110.6 14.0 %collective-permute-start.5 = (bf16[128,2048]{1,0:T(8,128)(2,1)}, bf16[128,2048]{1,0:T(8,128)(2,1)S(1)}, u32[]{:S(2)}, u32[]{:S(2)}) collective-permute-start(bf16[128,2048]{1,0:T(8,128)(2,1)} %fusion.20), channel_id=1, source_target_pairs={{0,2},{1,3},{2,0},{3,1},{4,6},{5,7},{6,4},{7,5},{8,10},{9,11},{10,... | collective-permute-start | bytes 1572872 | tf_op jit(solution)/shard_map/first_spread/ppermute | solution.py:49
  112.2 13.6 %collective-permute-start.6 = (bf16[128,2048]{1,0:T(8,128)(2,1)}, bf16[128,2048]{1,0:T(8,128)(2,1)S(1)}, u32[]{:S(2)}, u32[]{:S(2)}) collective-permute-start(bf16[128,2048]{1,0:T(8,128)(2,1)} %fusion.20), channel_id=1, source_target_pairs={{0,4},{1,5},{2,6},{3,7},{4,0},{5,1},{6,2},{7,3},{8,12},{9,13},{10,... | collective-permute-start | bytes 1572872 | tf_op jit(solution)/shard_map/first_spread/ppermute | solution.py:49
  127.4 6.9 %collective-permute-start.8 = (bf16[512,2048]{1,0:T(8,128)(2,1)}, bf16[512,2048]{1,0:T(8,128)(2,1)}, u32[]{:S(2)}, u32[]{:S(2)}) collective-permute-start(bf16[512,2048]{1,0:T(8,128)(2,1)} %constant_dynamic-update-slice_fusion.near_ref), channel_id=1, source_target_pairs={{0,1},{1,0},{2,3},{3,2},{4,5},{5,4},{6,7},{7,6},{8,9},{9,8},{10,11... | collective-permute-start | bytes 6291464 | tf_op jit(solution)/shard_map/first_spread/ppermute | solution.py:49
  161.3 32.9 %copy-start.8 = (bf16[1,128,2048]{2,1,0:T(8,128)(2,1)S(1)}, bf16[1,128,2048]{2,1,0:T(8,128)(2,1)}, u32[]{:S(2)}) copy-start(bf16[1,128,2048]{2,1,0:T(8,128)(2,1)} %param.9) | copy-start | bytes 1572868
  161.3 4.3 collective-permute-start.9
  166.5 15.1 %collective-permute-start.10 = (bf16[128,2048]{1,0:T(8,128)(2,1)S(1)}, bf16[128,2048]{1,0:T(8,128)(2,1)S(1)}, u32[]{:S(2)}, u32[]{:S(2)}) collective-permute-start(bf16[128,2048]{1,0:T(8,128)(2,1)S(1)} %get-tuple-element.98), channel_id=1, source_target_pairs={{0,2},{1,3},{2,0},{3,1},{4,6},{5,7},{6,4},{7,5},{8,10},{9,11},{10,... | collective-permute-start | bytes 1572872 | tf_op jit(solution)/shard_map/branch_collect/ppermute | solution.py:49
  167.7 15.9 %collective-permute-start.11 = (bf16[128,2048]{1,0:T(8,128)(2,1)S(1)}, bf16[128,2048]{1,0:T(8,128)(2,1)S(1)}, u32[]{:S(2)}, u32[]{:S(2)}) collective-permute-start(bf16[128,2048]{1,0:T(8,128)(2,1)S(1)} %get-tuple-element.100), channel_id=1, source_target_pairs={{0,4},{1,5},{2,6},{3,7},{4,0},{5,1},{6,2},{7,3},{8,12},{9,13},{10,... | collective-permute-start | bytes 1572872 | tf_op jit(solution)/shard_map/branch_collect/ppermute | solution.py:49
  169.2 24.9 %collective-permute-start.12 = (bf16[128,2048]{1,0:T(8,128)(2,1)S(1)}, bf16[128,2048]{1,0:T(8,128)(2,1)S(1)}, u32[]{:S(2)}, u32[]{:S(2)}) collective-permute-start(bf16[128,2048]{1,0:T(8,128)(2,1)S(1)} %get-tuple-element.99), channel_id=1, source_target_pairs={{0,6},{1,7},{2,4},{3,5},{4,2},{5,3},{6,0},{7,1},{8,14},{9,15},{10,... | collective-permute-start | bytes 1572872 | tf_op jit(solution)/shard_map/branch_collect/ppermute | solution.py:49
  170.1 33.9 %collective-permute-start.17 = (bf16[128,2048]{1,0:T(8,128)(2,1)S(1)}, bf16[128,2048]{1,0:T(8,128)(2,1)S(1)}, u32[]{:S(2)}, u32[]{:S(2)}) collective-permute-start(bf16[128,2048]{1,0:T(8,128)(2,1)S(1)} %bitcast.95), channel_id=1, source_target_pairs={{0,2},{1,3},{2,0},{3,1},{4,6},{5,7},{6,4},{7,5},{8,10},{9,11},{10,... | collective-permute-start | bytes 1572872 | tf_op jit(solution)/shard_map/cotangent_spread/ppermute | solution.py:49
  171.2 34.9 %collective-permute-start.18 = (bf16[128,2048]{1,0:T(8,128)(2,1)S(1)}, bf16[128,2048]{1,0:T(8,128)(2,1)S(1)}, u32[]{:S(2)}, u32[]{:S(2)}) collective-permute-start(bf16[128,2048]{1,0:T(8,128)(2,1)S(1)} %bitcast.96), channel_id=1, source_target_pairs={{0,4},{1,5},{2,6},{3,7},{4,0},{5,1},{6,2},{7,3},{8,12},{9,13},{10,... | collective-permute-start | bytes 1572872 | tf_op jit(solution)/shard_map/cotangent_spread/ppermute | solution.py:49
  181.6 35.1 %collective-permute-start.19 = (bf16[128,2048]{1,0:T(8,128)(2,1)S(1)}, bf16[128,2048]{1,0:T(8,128)(2,1)S(1)}, u32[]{:S(2)}, u32[]{:S(2)}) collective-permute-start(bf16[128,2048]{1,0:T(8,128)(2,1)S(1)} %bitcast.97), channel_id=1, source_target_pairs={{0,6},{1,7},{2,4},{3,5},{4,2},{5,3},{6,0},{7,1},{8,14},{9,15},{10,... | collective-permute-start | bytes 1572872 | tf_op jit(solution)/shard_map/cotangent_spread/ppermute | solution.py:49
  195.8 29.9 %collective-permute-start.13 = (bf16[128,2048]{1,0:T(8,128)(2,1)S(1)}, bf16[128,2048]{1,0:T(8,128)(2,1)S(1)}, u32[]{:S(2)}, u32[]{:S(2)}) collective-permute-start(bf16[128,2048]{1,0:T(8,128)(2,1)S(1)} %multiply_convert_fusion.3), channel_id=1, source_target_pairs={{0,2},{1,3},{2,0},{3,1},{4,6},{5,7},{6,4},{7,5},{8,10},{9,11},{10,... | collective-permute-start | bytes 1572872 | tf_op jit(solution)/shard_map/second_spread/ppermute | solution.py:49
  197.0 30.5 %collective-permute-start.14 = (bf16[128,2048]{1,0:T(8,128)(2,1)S(1)}, bf16[128,2048]{1,0:T(8,128)(2,1)S(1)}, u32[]{:S(2)}, u32[]{:S(2)}) collective-permute-start(bf16[128,2048]{1,0:T(8,128)(2,1)S(1)} %multiply_convert_fusion.3), channel_id=1, source_target_pairs={{0,4},{1,5},{2,6},{3,7},{4,0},{5,1},{6,2},{7,3},{8,12},{9,13},{10,... | collective-permute-start | bytes 1572872 | tf_op jit(solution)/shard_map/second_spread/ppermute | solution.py:49
  204.0 34.2 %collective-permute-start.15 = (bf16[128,2048]{1,0:T(8,128)(2,1)S(1)}, bf16[128,2048]{1,0:T(8,128)(2,1)S(1)}, u32[]{:S(2)}, u32[]{:S(2)}) collective-permute-start(bf16[128,2048]{1,0:T(8,128)(2,1)S(1)} %multiply_convert_fusion.3), channel_id=1, source_target_pairs={{0,6},{1,7},{2,4},{3,5},{4,2},{5,3},{6,0},{7,1},{8,14},{9,15},{10,... | collective-permute-start | bytes 1572872 | tf_op jit(solution)/shard_map/second_spread/ppermute | solution.py:49
  218.2 21.6 %collective-permute-start.20 = (bf16[512,2048]{1,0:T(8,128)(2,1)S(1)}, bf16[512,2048]{1,0:T(8,128)(2,1)}, u32[]{:S(2)}, u32[]{:S(2)}) collective-permute-start(bf16[512,2048]{1,0:T(8,128)(2,1)S(1)} %pad_maximum_fusion.6.near_ref), channel_id=1, source_target_pairs={{0,1},{1,0},{2,3},{3,2},{4,5},{5,4},{6,7},{7,6},{8,9},{9,8},{10,11... | collective-permute-start | bytes 6291464 | tf_op jit(solution)/shard_map/cotangent_spread/ppermute | solution.py:49
  239.8 7.1 %collective-permute-start.16 = (bf16[512,2048]{1,0:T(8,128)(2,1)}, bf16[512,2048]{1,0:T(8,128)(2,1)}, u32[]{:S(2)}, u32[]{:S(2)}) collective-permute-start(bf16[512,2048]{1,0:T(8,128)(2,1)} %pad_maximum_fusion.5.near_ref), channel_id=1, source_target_pairs={{0,1},{1,0},{2,3},{3,2},{4,5},{5,4},{6,7},{7,6},{8,9},{9,8},{10,11... | collective-permute-start | bytes 6291464 | tf_op jit(solution)/shard_map/second_spread/ppermute | solution.py:49
  260.2 158.6 %reduce-scatter.4.cloned.1.call-start = ((), (), s32[]{:S(2)}) async-start(), calls=%async_computation.8 | async-start | bytes 5242880 | tf_op jit(solution)/shard_map/down_back/reduce_scatter | solution.py:165
  341.4 224.8 %reduce-scatter.6.cloned.1.call-start = ((), (), s32[]{:S(2)}) async-start(), calls=%async_computation.9 | async-start | bytes 10485760 | tf_op jit(solution)/shard_map/gate_up_back/reduce_scatter | solution.py:165
  361.8 18.6 %copy-start.15 = (bf16[1024,2048]{1,0:T(8,128)(2,1)S(1)}, bf16[1024,2048]{1,0:T(8,128)(2,1)}, u32[]{:S(2)}) copy-start(bf16[1024,2048]{1,0:T(8,128)(2,1)} %join_halves.5) | copy-start | bytes 12582916
  361.8 4.2 collective-permute-start.21
  376.9 16.0 %collective-permute-start.22 = (bf16[128,2048]{1,0:T(8,128)(2,1)}, bf16[128,2048]{1,0:T(8,128)(2,1)}, u32[]{:S(2)}, u32[]{:S(2)}) collective-permute-start(bf16[128,2048]{1,0:T(8,128)(2,1)} %get-tuple-element.97), channel_id=1, source_target_pairs={{0,2},{1,3},{2,0},{3,1},{4,6},{5,7},{6,4},{7,5},{8,10},{9,11},{10,... | collective-permute-start | bytes 1572872 | tf_op jit(solution)/shard_map/second_grad_collect/ppermute | solution.py:49
  378.4 15.1 %collective-permute-start.23 = (bf16[128,2048]{1,0:T(8,128)(2,1)}, bf16[128,2048]{1,0:T(8,128)(2,1)}, u32[]{:S(2)}, u32[]{:S(2)}) collective-permute-start(bf16[128,2048]{1,0:T(8,128)(2,1)} %get-tuple-element.96), channel_id=1, source_target_pairs={{0,4},{1,5},{2,6},{3,7},{4,0},{5,1},{6,2},{7,3},{8,12},{9,13},{10,... | collective-permute-start | bytes 1572872 | tf_op jit(solution)/shard_map/second_grad_collect/ppermute | solution.py:49
  379.9 23.7 %collective-permute-start.24 = (bf16[128,2048]{1,0:T(8,128)(2,1)}, bf16[128,2048]{1,0:T(8,128)(2,1)}, u32[]{:S(2)}, u32[]{:S(2)}) collective-permute-start(bf16[128,2048]{1,0:T(8,128)(2,1)} %get-tuple-element.95), channel_id=1, source_target_pairs={{0,6},{1,7},{2,4},{3,5},{4,2},{5,3},{6,0},{7,1},{8,14},{9,15},{10,... | collective-permute-start | bytes 1572872 | tf_op jit(solution)/shard_map/second_grad_collect/ppermute | solution.py:49
  418.9 227.7 %reduce-scatter.8.cloned.1.call-start = ((), (), s32[]{:S(2)}) async-start(), calls=%async_computation.10 | async-start | bytes 5242880 | tf_op jit(solution)/shard_map/attention_back/reduce_scatter | solution.py:165
  421.2 30.2 %copy-start.33 = (bf16[2048,1024]{1,0:T(8,128)(2,1)S(1)}, bf16[2048,1024]{1,0:T(8,128)(2,1)}, u32[]{:S(2)}) copy-start(bf16[2048,1024]{1,0:T(8,128)(2,1)} %all-gather.8.cloned.1.call-done) | copy-start | bytes 12582916
  421.3 30.2 %copy-start.37 = (bf16[1024,1024]{0,1:T(8,128)(2,1)S(1)}, bf16[1024,1024]{0,1:T(8,128)(2,1)}, u32[]{:S(2)}) copy-start(bf16[1024,1024]{0,1:T(8,128)(2,1)} %get-tuple-element.32) | copy-start | bytes 6291460
  425.0 13.9 %collective-permute-start.26 = (bf16[128,2048]{1,0:T(8,128)(2,1)S(1)}, bf16[128,2048]{1,0:T(8,128)(2,1)S(1)}, u32[]{:S(2)}, u32[]{:S(2)}) collective-permute-start(bf16[128,2048]{1,0:T(8,128)(2,1)S(1)} %get-tuple-element.77), channel_id=1, source_target_pairs={{0,2},{1,3},{2,0},{3,1},{4,6},{5,7},{6,4},{7,5},{8,10},{9,11},{10,... | collective-permute-start | bytes 1572872 | tf_op jit(solution)/shard_map/branch_grad_spread/ppermute | solution.py:49
  426.5 14.8 %collective-permute-start.27 = (bf16[128,2048]{1,0:T(8,128)(2,1)S(1)}, bf16[128,2048]{1,0:T(8,128)(2,1)S(1)}, u32[]{:S(2)}, u32[]{:S(2)}) collective-permute-start(bf16[128,2048]{1,0:T(8,128)(2,1)S(1)} %get-tuple-element.77), channel_id=1, source_target_pairs={{0,4},{1,5},{2,6},{3,7},{4,0},{5,1},{6,2},{7,3},{8,12},{9,13},{10,... | collective-permute-start | bytes 1572872 | tf_op jit(solution)/shard_map/branch_grad_spread/ppermute | solution.py:49
  428.0 23.2 %collective-permute-start.28 = (bf16[128,2048]{1,0:T(8,128)(2,1)S(1)}, bf16[128,2048]{1,0:T(8,128)(2,1)S(1)}, u32[]{:S(2)}, u32[]{:S(2)}) collective-permute-start(bf16[128,2048]{1,0:T(8,128)(2,1)S(1)} %get-tuple-element.77), channel_id=1, source_target_pairs={{0,6},{1,7},{2,4},{3,5},{4,2},{5,3},{6,0},{7,1},{8,14},{9,15},{10,... | collective-permute-start | bytes 1572872 | tf_op jit(solution)/shard_map/branch_grad_spread/ppermute | solution.py:49
  451.4 4.4 collective-permute-start.29
  455.2 29.0 %collective-permute-start.25 = (bf16[512,2048]{1,0:T(8,128)(2,1)}, bf16[512,2048]{1,0:T(8,128)(2,1)}, u32[]{:S(2)}, u32[]{:S(2)}) collective-permute-start(bf16[512,2048]{1,0:T(8,128)(2,1)} %convolution_convert_fusion.3), channel_id=1, source_target_pairs={{0,1},{1,0},{2,3},{3,2},{4,5},{5,4},{6,7},{7,6},{8,9},{9,8},{10,11... | collective-permute-start | bytes 6291464 | tf_op jit(solution)/shard_map/feed_collect/ppermute | solution.py:49
  484.1 17.8 %collective-permute-start.33 = (bf16[512,2048]{1,0:T(8,128)(2,1)}, bf16[512,2048]{1,0:T(8,128)(2,1)}, u32[]{:S(2)}, u32[]{:S(2)}) collective-permute-start(bf16[512,2048]{1,0:T(8,128)(2,1)} %convolution_convert_fusion.5), channel_id=1, source_target_pairs={{0,1},{1,0},{2,3},{3,2},{4,5},{5,4},{6,7},{7,6},{8,9},{9,8},{10,11... | collective-permute-start | bytes 6291464 | tf_op jit(solution)/shard_map/first_grad_collect/ppermute | solution.py:49
  489.6 19.4 %collective-permute-start.30 = (bf16[128,2048]{1,0:T(8,128)(2,1)}, bf16[128,2048]{1,0:T(8,128)(2,1)}, u32[]{:S(2)}, u32[]{:S(2)}) collective-permute-start(bf16[128,2048]{1,0:T(8,128)(2,1)} %get-tuple-element.92), channel_id=1, source_target_pairs={{0,2},{1,3},{2,0},{3,1},{4,6},{5,7},{6,4},{7,5},{8,10},{9,11},{10,... | collective-permute-start | bytes 1572872 | tf_op jit(solution)/shard_map/feed_collect/ppermute | solution.py:49
  491.1 19.3 %collective-permute-start.31 = (bf16[128,2048]{1,0:T(8,128)(2,1)}, bf16[128,2048]{1,0:T(8,128)(2,1)}, u32[]{:S(2)}, u32[]{:S(2)}) collective-permute-start(bf16[128,2048]{1,0:T(8,128)(2,1)} %get-tuple-element.94), channel_id=1, source_target_pairs={{0,4},{1,5},{2,6},{3,7},{4,0},{5,1},{6,2},{7,3},{8,12},{9,13},{10,... | collective-permute-start | bytes 1572872 | tf_op jit(solution)/shard_map/feed_collect/ppermute | solution.py:49
  492.5 24.9 %collective-permute-start.32 = (bf16[128,2048]{1,0:T(8,128)(2,1)}, bf16[128,2048]{1,0:T(8,128)(2,1)}, u32[]{:S(2)}, u32[]{:S(2)}) collective-permute-start(bf16[128,2048]{1,0:T(8,128)(2,1)} %get-tuple-element.93), channel_id=1, source_target_pairs={{0,6},{1,7},{2,4},{3,5},{4,2},{5,3},{6,0},{7,1},{8,14},{9,15},{10,... | collective-permute-start | bytes 1572872 | tf_op jit(solution)/shard_map/feed_collect/ppermute | solution.py:49
  506.8 59.4 %copy-start.9 = (bf16[1,128,2048]{2,1,0:T(8,128)(2,1)S(1)}, bf16[1,128,2048]{2,1,0:T(8,128)(2,1)}, u32[]{:S(2)}) copy-start(bf16[1,128,2048]{2,1,0:T(8,128)(2,1)} %param.9) | copy-start | bytes 1572868
  506.8 59.4 %copy-start.27 = (f32[1,2048]{1,0:T(1,128)S(1)}, f32[1,2048]{1,0:T(1,128)}, u32[]{:S(2)}) copy-start(f32[1,2048]{1,0:T(1,128)} %copy-done.26) | copy-start | bytes 24580
  506.8 59.4 %copy-start.29 = (f32[128]{0:T(128)S(1)}, f32[128]{0:T(128)}, u32[]{:S(2)}) copy-start(f32[128]{0:T(128)} %copy-done.28) | copy-start | bytes 1540
  506.8 21.6 %collective-permute-start.34 = (bf16[128,2048]{1,0:T(8,128)(2,1)S(1)}, bf16[128,2048]{1,0:T(8,128)(2,1)S(1)}, u32[]{:S(2)}, u32[]{:S(2)}) collective-permute-start(bf16[128,2048]{1,0:T(8,128)(2,1)S(1)} %get-tuple-element.89), channel_id=1, source_target_pairs={{0,2},{1,3},{2,0},{3,1},{4,6},{5,7},{6,4},{7,5},{8,10},{9,11},{10,... | collective-permute-start | bytes 1572872 | tf_op jit(solution)/shard_map/first_grad_collect/ppermute | solution.py:49
  507.5 21.1 %collective-permute-start.35 = (bf16[128,2048]{1,0:T(8,128)(2,1)S(1)}, bf16[128,2048]{1,0:T(8,128)(2,1)}, u32[]{:S(2)}, u32[]{:S(2)}) collective-permute-start(bf16[128,2048]{1,0:T(8,128)(2,1)S(1)} %get-tuple-element.91), channel_id=1, source_target_pairs={{0,4},{1,5},{2,6},{3,7},{4,0},{5,1},{6,2},{7,3},{8,12},{9,13},{10,... | collective-permute-start | bytes 1572872 | tf_op jit(solution)/shard_map/first_grad_collect/ppermute | solution.py:49
  509.0 30.1 %collective-permute-start.36 = (bf16[128,2048]{1,0:T(8,128)(2,1)S(1)}, bf16[128,2048]{1,0:T(8,128)(2,1)}, u32[]{:S(2)}, u32[]{:S(2)}) collective-permute-start(bf16[128,2048]{1,0:T(8,128)(2,1)S(1)} %get-tuple-element.90), channel_id=1, source_target_pairs={{0,6},{1,7},{2,4},{3,5},{4,2},{5,3},{6,0},{7,1},{8,14},{9,15},{10,... | collective-permute-start | bytes 1572872 | tf_op jit(solution)/shard_map/first_grad_collect/ppermute | solution.py:49
  566.2 16.2 %copy-start.10 = (bf16[512,2048]{1,0:T(8,128)(2,1)S(1)}, bf16[512,2048]{1,0:T(8,128)(2,1)}, u32[]{:S(2)}) copy-start(bf16[512,2048]{1,0:T(8,128)(2,1)} %reduce-scatter.6.cloned.1.call-done) | copy-start | bytes 6291460
  568.5 3.7 collective-permute-start.38
  572.3 3.7 collective-permute-start.39
  576.0 1.2 collective-permute-start.40
  577.2 5.2 collective-permute-start.41
  582.5 26.1 %collective-permute-start.37 = (bf16[256,2048]{1,0:T(8,128)(2,1)S(1)}, bf16[256,2048]{1,0:T(8,128)(2,1)S(1)}, u32[]{:S(2)}, u32[]{:S(2)}) collective-permute-start(bf16[256,2048]{1,0:T(8,128)(2,1)S(1)} %broadcast_select_fusion), channel_id=1, source_target_pairs={{0,4},{4,0},{1,5},{5,1},{2,6},{6,2},{3,7},{7,3},{8,12},{12,8},{9,1... | collective-permute-start | bytes 3145736 | tf_op jit(solution)/shard_map/gate_up_return/ppermute | solution.py:49
  584.1 4.0 collective-permute-start.42
  588.8 60.6 %collective-permute-start.44 = (bf16[256,1024]{1,0:T(8,128)(2,1)S(1)}, bf16[256,1024]{1,0:T(8,128)(2,1)}, u32[]{:S(2)}, u32[]{:S(2)}) collective-permute-start(bf16[256,1024]{1,0:T(8,128)(2,1)S(1)} %broadcast_select_fusion.2), channel_id=1, source_target_pairs={{0,4},{4,0},{1,5},{5,1},{2,6},{6,2},{3,7},{7,3},{8,12},{12,8},{9,1... | collective-permute-start | bytes 1572872 | tf_op jit(solution)/shard_map/down_return/ppermute | solution.py:49
  609.8 39.6 %copy-start.19 = (bf16[512,1024]{1,0:T(8,128)(2,1)S(1)}, bf16[512,1024]{1,0:T(8,128)(2,1)}, u32[]{:S(2)}) copy-start(bf16[512,1024]{1,0:T(8,128)(2,1)} %reduce-scatter.4.cloned.1.call-done) | copy-start | bytes 3145732
  647.8 13.8 %collective-permute-start.43 = (bf16[256,1024]{1,0:T(8,128)(2,1)S(1)}, bf16[256,1024]{1,0:T(8,128)(2,1)S(1)}, u32[]{:S(2)}, u32[]{:S(2)}) collective-permute-start(bf16[256,1024]{1,0:T(8,128)(2,1)S(1)} %broadcast_select_fusion.4), channel_id=1, source_target_pairs={{0,4},{4,0},{1,5},{5,1},{2,6},{6,2},{3,7},{7,3},{8,12},{12,8},{9,1... | collective-permute-start | bytes 1572872 | tf_op jit(solution)/shard_map/attention_return/ppermute | solution.py:49
  (27 other events, 178.9 us)
Sparse Core Ops, SparseCore 0:
  28.9 81.6 all-gather.3
  112.1 148.0 all-gather.5
  262.3 78.9 all-gather.7
  343.5 75.2 reduce-scatter.3
  421.1 144.9 reduce-scatter.5
  569.0 77.5 reduce-scatter.7

commit v5 on v4

--- a/solution.py
+++ b/solution.py
@@ -165,25 +165,39 @@
     return lax.psum_scatter(grads, "dp", scatter_dimension=0, tiled=True)
 
 
-def return_columns(summed, blocks, kinds, wide):
-    parted = summed.reshape(blocks, -1, summed.shape[1])
-    if blocks == 2:
-        first = lax.axis_index("blk") == 0
-        got = swap_by(jnp.where(first, parted[1], parted[0]), "blk", blocks, 1).astype(F32)
-        own = jnp.where(first, parted[0], parted[1]).astype(F32)
-        parted = [jnp.where(first, own, got), jnp.where(first, got, own)]
-    else:
-        parted = list(trade(parted, "blk").astype(F32))
+def own_then_other(blocks):
+    first = lax.axis_index("blk") == 0
+    return jnp.where(first, blocks[0], blocks[1]), jnp.where(first, blocks[1], blocks[0])
+
+
+def trade_rows(grads, size_dp):
+    split = grads.reshape(size_dp, 2, -1, grads.shape[1])
+    own, sent = own_then_other([split[:, 0], split[:, 1]])
+    return [part.reshape(-1, grads.shape[1]) for part in (own, swap_by(sent, "blk", 2, 1))]
+
+
+def join_columns(parted, kinds, wide):
     totals = []
     start = 0
     for kind in kinds:
         columns = [
-            [parted[b][:, start + i * wide : start + (i + 1) * wide] for b in range(blocks)]
+            [part[:, start + i * wide : start + (i + 1) * wide] for part in parted]
             for i in range(kind)
         ]
         totals.append(jnp.stack([jnp.concatenate(part, axis=1) for part in columns], axis=1))
         start += kind * wide
     return totals
+
+
+def return_columns(summed, blocks, kinds, wide):
+    parted = summed.reshape(blocks, -1, summed.shape[1])
+    if blocks == 2:
+        own, sent = own_then_other(parted)
+        got = swap_by(sent, "blk", blocks, 1)
+        parted = own_then_other([own.astype(F32), got.astype(F32)])
+    else:
+        parted = list(trade(parted, "blk").astype(F32))
+    return join_columns(parted, kinds, wide)
 
 
 def swap_halves(values):
@@ -572,16 +586,13 @@
     )
     grad_middle = grad_output + grad_middle_norm
     grad_branch, _ = named("branch_grad_spread", spread, grad_middle.astype(BF16), PLANE, group)
-    with jax.named_scope("feed_collect"):
-        feed_hidden = after(hidden, *last_second)
-        feed_out, _ = collect(
-            feed_hidden, full_down, dot_nt, PLANE, group, begin=(grad_branch,)
-        )
     [total_down] = named(
         "down_return", return_columns, after(down_sum, grad_branch), size_blk, [1], wide
     )
     grad_out = dot_tn(grad_branch, attended_here).astype(BF16)
     grad_attended = dot_nn(grad_branch, full_out).astype(BF16)
+    if size_blk == 2:
+        out_parts = named("out_trade", trade_rows, grad_out, size_dp)
     grad_projected = attend_back(
         info,
         q_row,
@@ -595,13 +606,23 @@
         group,
     )
     grad_projected = own_heads(grad_projected, 3, features)
-    grad_qkv = dot_tn(normed_first, grad_projected).astype(BF16)
+    if size_blk == 2:
+        grad_projected, *out_parts = together(grad_projected, *out_parts)
+        grad_qkv = dot_tn(normed_first, grad_projected).astype(BF16)
+        qkv_parts = named("qkv_trade", trade_rows, grad_qkv, size_dp)
+        parts = [qkv_parts[0], out_parts[0], qkv_parts[1], out_parts[1]]
+    else:
+        parts = [dot_tn(normed_first, grad_projected).astype(BF16), grad_out]
     grad_normed_first, last_grad = named(
         "first_grad_collect", collect, grad_projected, full_qkv, dot_nt, PLANE, group
     )
-    both = jnp.concatenate([grad_qkv, grad_out], axis=1)
-    both_sum = named("attention_back", sum_rows, after(both, gate_up_sum, feed_out, total_down, *last_grad))
-
+    both = after(jnp.concatenate(parts, axis=1), gate_up_sum, *last_grad)
+    both_sum = named("attention_back", sum_rows, both)
+    with jax.named_scope("feed_collect"):
+        feed_hidden = after(hidden, *last_second)
+        feed_out, _ = collect(
+            feed_hidden, full_down, dot_nt, PLANE, group, begin=last_grad
+        )
     outcome = (middle + feed_out).astype(BF16)
     grad_input_norm, sum_first = norm_back(grad_normed_first, unit_first, factor_first, gain_first)
     grad_input = grad_middle + grad_input_norm
@@ -609,10 +630,14 @@
     [total_gate_up] = named(
         "gate_up_return", return_columns, gate_up_sum, size_blk, [2], wide
     )
-    both_sum = after(both_sum, total_gate_up, outcome, grad_input, gain_sums)
-    total_qkv, total_out = named(
-        "attention_return", return_columns, both_sum, size_blk, [3, 1], features
-    )
+    both_sum = after(both_sum, total_gate_up, total_down, outcome, grad_input, gain_sums)
+    if size_blk == 2:
+        half = both_sum.shape[1] // 2
+        summed = both_sum.astype(F32)
+        parted = own_then_other([summed[:, :half], summed[:, half:]])
+        total_qkv, total_out = join_columns(parted, [3, 1], features)
+    else:
+        total_qkv, total_out = return_columns(both_sum, size_blk, [3, 1], features)
     return (
         outcome[None],
         grad_input[None],

time: 678 us -> 664 us (0.979)
    reduce_scatter x3, waiting for transfers between devices: 76.7 us -> 32 us  [sum_rows(): return lax.psum_scatter(grads, 'dp', scatter_dimension=0, tiled=True)]
    ppermute x45 -> x46, waiting for transfers between devices: 183 us -> 221 us  [swap_by(): return lax.ppermute(value, axes, [(i, i ^ bits) for i in range(size)])]
    ppermute x45 -> x46, starting transfers between devices: 48.3 us -> 43.5 us  [swap_by(): return lax.ppermute(value, axes, [(i, i ^ bits) for i in range(size)])]
  transfers between devices with their start and end apart: 52 -> 53, of which waited for: 38 -> 39; matrix products, arithmetic and copies ran while one was open for 25% -> 25% of each run, Pallas kernels for 8% -> 8%
where the time goes in v5:
time: 664 us; the launch traced here: 657 us
  waiting for transfers between devices  347 us (52%)
  matrix products  101 us (15%)
  Pallas kernels  52.2 us (8%)
  starting transfers between devices  49.4 us (7%)
  other arithmetic  40 us (6%)
  local copies, waits for them, and re-layouts  35.6 us (5%)
  blocking collectives  17.6 us (3%)
  between operations  15.2 us (2%)
    ppermute x46, waiting for transfers between devices, swap_by(): return lax.ppermute(value, axes, [(i, i ^ bits) for i in range(size)])  221 us
    all_gather x3, waiting for transfers between devices, gather_rows(): return lax.all_gather(after(weight, *events), 'dp', axis=0, tiled=True)  67.7 us
    ppermute x46, starting transfers between devices, swap_by(): return lax.ppermute(value, axes, [(i, i ^ bits) for i in range(size)])  43.5 us
    dot_general x5, matrix products, dot_nn(): lax.dot_general(a, b, (((1,), (0,)), ((), ())), preferred_element_type=F32)  40.2 us
    dot_general x8, matrix products, dot_nt(): lax.dot_general(a, b, (((1,), (1,)), ((), ())), preferred_element_type=F32)  32.6 us
    reduce_scatter x3, waiting for transfers between devices, sum_rows(): return lax.psum_scatter(grads, 'dp', scatter_dimension=0, tiled=True)  32 us
    pallas_call x4, Pallas kernels, join_halves(): pl.pallas_call(functools.partial(join_kernel, steps), grid=(2 * steps,),...  29.1 us
    dot_general x4, matrix products, dot_tn(): lax.dot_general(a, b, (((0,), (0,)), ((), ())), preferred_element_type=F32)  27.8 us
  transfers between devices with their start and end apart: 53, of which 39 were waited for; matrix products, arithmetic and copies ran while one was open for 25% of the time, Pallas kernels for 8%

profile of v5, /device:TPU:0, one launch (start us, length us, event | category | flops | bytes accessed | tf_op | source)
XLA Modules:
  0.0 657.3 jit_solution(15097638112422074188)
XLA Ops:
  9.9 17.6 %all_to_all.10 = bf16[2,256,1024]{1,2,0:T(8,128)(2,1)S(1)} all-to-all(bf16[2,256,1024]{1,2,0:T(8,128)(2,1)S(1)} %pad_maximum_fusion.10), channel_id=1, replica_groups=mesh['dp'=4,'blk'=2,'tensor'=4] {'blk'}, dimensions={0} | all-to-all | bytes 2097152 | tf_op jit(solution)/shard_map/attention_weights/all_to_all | solution.py:139
  31.8 6.2 copy.44
  38.0 1.9 copy.45
  41.8 1.9 pad_maximum_fusion.4
  43.7 5.3 all-to-all-start
  51.0 2.8 collective-permute-done.3
  55.5 3.2 collective-permute-done.4
  59.7 25.5 %all-to-all-done = bf16[2,256,3072]{1,2,0:T(8,128)(2,1)} async-done(((bf16[2,256,3072]{1,2,0:T(8,128)(2,1)}), bf16[2,256,3072]{1,2,0:T(8,128)(2,1)}, u32[]{:S(2)}, u32[]{:S(2)}) %all-to-all-start) | async-done | bytes 3145760 | tf_op jit(solution)/shard_map/feed_weights/all_to_all | solution.py:139
  85.2 3.2 copy.47
  91.0 13.5 %collective-permute-done.7 = bf16[128,2048]{1,0:T(8,128)(2,1)S(1)} collective-permute-done((bf16[128,2048]{1,0:T(8,128)(2,1)}, bf16[128,2048]{1,0:T(8,128)(2,1)S(1)}, u32[]{:S(2)}, u32[]{:S(2)}) %collective-permute-start.7) | collective-permute-done | bytes 524320 | tf_op jit(solution)/shard_map/first_spread/ppermute | solution.py:49
  104.5 6.1 all-gather.4.cloned.1.call-done
  114.8 9.8 %collective-permute-done.5 = bf16[128,2048]{1,0:T(8,128)(2,1)S(1)} collective-permute-done((bf16[128,2048]{1,0:T(8,128)(2,1)}, bf16[128,2048]{1,0:T(8,128)(2,1)S(1)}, u32[]{:S(2)}, u32[]{:S(2)}) %collective-permute-start.5) | collective-permute-done | bytes 524320 | tf_op jit(solution)/shard_map/first_spread/ppermute | solution.py:49
  130.2 1.9 fusion.39
  133.0 7.3 %join_halves.4 = bf16[1024,2048]{1,0:T(8,128)(2,1)} custom-call(bf16[512,2048]{1,0:T(8,128)(2,1)} %copy-done.21, bf16[512,2048]{1,0:T(8,128)(2,1)} %collective-permute-done.8.far_ref), custom_call_target="tpu_custom_call" | custom-call | bytes 8388608 | tf_op jit(solution)/shard_map/first_spread/join_halves/pallas_call | solution.py:68
  140.3 8.2 %fusion.8.q_ref.k_ref.v_ref = f32[1024,768]{1,0:T(8,128)} fusion(bf16[1024,2048]{1,0:T(8,128)(2,1)} %join_halves.4, bf16[2048,1024]{1,0:T(8,128)(2,1)} %all-gather.4.cloned.1.call-done), kind=kOutput, calls=%fused_computation.34 | convolution fusion | flops 3221225472 | bytes 10485760 | tf_op jit(solution)/shard_map/dot_general | solution.py:24
  148.5 10.7 %attend.1 = (bf16[1024,256]{1,0:T(8,128)(2,1)S(1)}, bf16[1024,256]{1,0:T(8,128)(2,1)S(1)}, bf16[1024,256]{1,0:T(8,128)(2,1)S(1)}, bf16[1024,256]{1,0:T(8,128)(2,1)S(1)}, f32[1024,256]{1,0:T(8,128)S(1)}) custom-call(s32[4]{0:T(128)S(1)} %pad_add_fusion.info_ref, f32[1024,768]{1,0:T(8,128)} %fusion.8.q_ref.k_ref.v_ref, f32[1024,768]{1,0:T(8,128)} %fusion.8.q_ref.k_ref.v_ref, ...), custom_call_target="tpu_custom_call" | custom-call | flops 1073741824 | bytes 4718592 | tf_op jit(solution)/shard_map/attend/pallas_call | solution.py:308
  160.4 3.9 collective-permute-done.9
  170.7 9.6 %collective-permute-done.10 = bf16[128,2048]{1,0:T(8,128)(2,1)S(1)} collective-permute-done((bf16[128,2048]{1,0:T(8,128)(2,1)S(1)}, bf16[128,2048]{1,0:T(8,128)(2,1)S(1)}, u32[]{:S(2)}, u32[]{:S(2)}) %collective-permute-start.10) | collective-permute-done | bytes 524320 | tf_op jit(solution)/shard_map/branch_collect/ppermute | solution.py:49
  181.8 11.0 %collective-permute-done.12 = bf16[128,2048]{1,0:T(8,128)(2,1)S(1)} collective-permute-done((bf16[128,2048]{1,0:T(8,128)(2,1)S(1)}, bf16[128,2048]{1,0:T(8,128)(2,1)S(1)}, u32[]{:S(2)}, u32[]{:S(2)}) %collective-permute-start.12) | collective-permute-done | bytes 524320 | tf_op jit(solution)/shard_map/branch_collect/ppermute | solution.py:49
  196.5 6.2 collective-permute-done.17
  204.2 11.1 %collective-permute-done.19 = bf16[128,2048]{1,0:T(8,128)(2,1)S(1)} collective-permute-done((bf16[128,2048]{1,0:T(8,128)(2,1)S(1)}, bf16[128,2048]{1,0:T(8,128)(2,1)S(1)}, u32[]{:S(2)}, u32[]{:S(2)}) %collective-permute-start.19) | collective-permute-done | bytes 524320 | tf_op jit(solution)/shard_map/cotangent_spread/ppermute | solution.py:49
  216.8 7.5 %collective-permute-done.13 = bf16[128,2048]{1,0:T(8,128)(2,1)S(1)} collective-permute-done((bf16[128,2048]{1,0:T(8,128)(2,1)S(1)}, bf16[128,2048]{1,0:T(8,128)(2,1)S(1)}, u32[]{:S(2)}, u32[]{:S(2)}) %collective-permute-start.13) | collective-permute-done | bytes 524320 | tf_op jit(solution)/shard_map/second_spread/ppermute | solution.py:49
  225.6 11.2 %collective-permute-done.15 = bf16[128,2048]{1,0:T(8,128)(2,1)S(1)} collective-permute-done((bf16[128,2048]{1,0:T(8,128)(2,1)S(1)}, bf16[128,2048]{1,0:T(8,128)(2,1)S(1)}, u32[]{:S(2)}, u32[]{:S(2)}) %collective-permute-start.15) | collective-permute-done | bytes 524320 | tf_op jit(solution)/shard_map/second_spread/ppermute | solution.py:49
  238.4 7.1 %join_halves.6 = bf16[1024,2048]{1,0:T(8,128)(2,1)} custom-call(bf16[512,2048]{1,0:T(8,128)(2,1)} %copy-done.10, bf16[512,2048]{1,0:T(8,128)(2,1)} %collective-permute-done.20.far_ref), custom_call_target="tpu_custom_call" | custom-call | bytes 8388608 | tf_op jit(solution)/shard_map/cotangent_spread/join_halves/pallas_call | solution.py:68
  245.5 7.2 %join_halves.5 = bf16[1024,2048]{1,0:T(8,128)(2,1)} custom-call(bf16[512,2048]{1,0:T(8,128)(2,1)} %pad_maximum_fusion.5.near_ref, bf16[512,2048]{1,0:T(8,128)(2,1)} %collective-permute-done.16.far_ref), custom_call_target="tpu_custom_call" | custom-call | bytes 8388608 | tf_op jit(solution)/shard_map/second_spread/join_halves/pallas_call | solution.py:68
  252.6 7.6 %all-gather.6.cloned.1.call-done = bf16[2048,2048]{1,0:T(8,128)(2,1)} async-done(((bf16[512,2048]{1,0:T(8,128)(2,1)}), bf16[2048,2048]{1,0:T(8,128)(2,1)}) %all-gather.6.cloned.1.call-update) | async-done | bytes 8388624 | tf_op jit(solution)/shard_map/gate_up_gather/all_gather | solution.py:161
  260.7 10.1 %fusion.2 = f32[1024,1024]{0,1:T(8,128)} fusion(bf16[1024,2048]{1,0:T(8,128)(2,1)} %join_halves.5, bf16[2048,2048]{1,0:T(8,128)(2,1)} %all-gather.6.cloned.1.call-done), kind=kOutput, calls=%fused_computation.8 | convolution fusion | flops 4294967296 | bytes 12582912 | tf_op jit(solution)/shard_map/dot_general | solution.py:24
  270.8 8.6 %multiply_convert_fusion.2 = (bf16[1024,1024]{0,1:T(8,128)(2,1)}, f32[1024,1024]{0,1:T(8,128)}) fusion(f32[1024,1024]{0,1:T(8,128)} %fusion.2, bf16[1024,2048]{1,0:T(8,128)(2,1)S(1)} %copy-done.12, bf16[2048,2048]{1,0:T(8,128)(2,1)S(1)} %copy-done.34), kind=kOutput, calls=%fused_computation.17 | convolution fusion | flops 4301258752 | bytes 18874368 | tf_op jit(solution)/shard_map/dot_general | solution.py:24
  279.4 7.8 %convolution_convert_fusion.1 = bf16[2048,1024]{1,0:T(8,128)(2,1)} fusion(bf16[1024,2048]{1,0:T(8,128)(2,1)S(1)} %copy-done.14, bf16[1024,1024]{0,1:T(8,128)(2,1)} %get-tuple-element.35), kind=kOutput, calls=%fused_computation.21 | convolution fusion | flops 4297064448 | bytes 10485760 | tf_op jit(solution)/shard_map/dot_general | solution.py:32
  287.3 54.1 %all-gather.8.cloned.1.call-done = bf16[2048,1024]{1,0:T(8,128)(2,1)} async-done(((bf16[512,1024]{1,0:T(8,128)(2,1)}), bf16[2048,1024]{1,0:T(8,128)(2,1)}) %all-gather.8.cloned.1.call-update) | async-done | bytes 4194320 | tf_op jit(solution)/shard_map/down_gather/all_gather | solution.py:161
  341.4 11.9 %multiply_convert_fusion = (bf16[1024,1024]{0,1:T(8,128)(2,1)S(1)}, bf16[1024,1024]{0,1:T(8,128)(2,1)S(1)}) fusion(f32[1024,1024]{0,1:T(8,128)} %fusion.2, f32[1024,1024]{0,1:T(8,128)} %get-tuple-element.137, bf16[1024,2048]{1,0:T(8,128)(2,1)} %join_halves.6, bf16[2048,1024]{1,0:T(8,128)(2,1)} %all-gather.8.cloned.1.call-done), kind=kOutput, calls=%fused_computation.15 | convolution fusion | flops 4308598784 | bytes 20971520 | tf_op jit(solution)/shard_map/dot_general | solution.py:24
  353.4 8.4 %convolution_convert_fusion.6 = bf16[512,2048]{1,0:T(8,128)(2,1)S(1)} fusion(bf16[2048,2048]{1,0:T(8,128)(2,1)} %all-gather.6.cloned.1.call-done, bf16[1024,1024]{0,1:T(8,128)(2,1)S(1)} %get-tuple-element.86, bf16[1024,1024]{0,1:T(8,128)(2,1)S(1)} %get-tuple-element.85), kind=kOutput, calls=%fused_computation.27 | convolution fusion | flops 4300210176 | bytes 14680064 | tf_op jit(solution)/shard_map/second_grad_collect/dot_general | solution.py:28
  361.9 4.1 collective-permute-done.21
  366.0 8.4 %add_convert_fusion.2 = bf16[512,2048]{1,0:T(8,128)(2,1)S(1)} fusion(bf16[512,2048]{1,0:T(8,128)(2,1)S(1)} %collective-permute-done.21, bf16[2048,2048]{1,0:T(8,128)(2,1)} %all-gather.6.cloned.1.call-done, bf16[1024,1024]{0,1:T(8,128)(2,1)S(1)} %get-tuple-element.86, bf16[1024,1024]{0,1:T(8,128)(2,1)S(1)} %get-tuple-element.85), kind=kOutput, calls=%fused_computation.14 | convolution fusion | flops 4302307328 | bytes 16777216 | tf_op jit(solution)/shard_map/second_grad_collect/dot_general | solution.py:28
  380.4 12.4 %convolution_convert_fusion = bf16[2048,2048]{1,0:T(8,128)(2,1)} fusion(bf16[1024,2048]{1,0:T(8,128)(2,1)S(1)} %copy-done.13, bf16[1024,1024]{0,1:T(8,128)(2,1)S(1)} %get-tuple-element.85, bf16[1024,1024]{0,1:T(8,128)(2,1)S(1)} %get-tuple-element.86), kind=kOutput, calls=%fused_computation | convolution fusion | flops 8602517504 | bytes 16777216 | tf_op jit(solution)/shard_map/dot_general | solution.py:32
  393.6 10.1 %collective-permute-done.24 = bf16[128,2048]{1,0:T(8,128)(2,1)} collective-permute-done((bf16[128,2048]{1,0:T(8,128)(2,1)}, bf16[128,2048]{1,0:T(8,128)(2,1)}, u32[]{:S(2)}, u32[]{:S(2)}) %collective-permute-start.24) | collective-permute-done | bytes 524320 | tf_op jit(solution)/shard_map/second_grad_collect/ppermute | solution.py:49
  403.6 15.2 %reduce-scatter.4.cloned.1.call-done = bf16[512,1024]{1,0:T(8,128)(2,1)} async-done(((bf16[2048,1024]{1,0:T(8,128)(2,1)}), bf16[512,1024]{1,0:T(8,128)(2,1)}) %reduce-scatter.4.cloned.1.call-update) | async-done | bytes 1048592 | tf_op jit(solution)/shard_map/down_back/reduce_scatter | solution.py:165
  418.9 2.3 multiply_reduce_fusion
  421.2 3.6 fusion.45
  428.3 10.4 %collective-permute-done.26 = bf16[128,2048]{1,0:T(8,128)(2,1)S(1)} collective-permute-done((bf16[128,2048]{1,0:T(8,128)(2,1)S(1)}, bf16[128,2048]{1,0:T(8,128)(2,1)S(1)}, u32[]{:S(2)}, u32[]{:S(2)}) %collective-permute-start.26) | collective-permute-done | bytes 524320 | tf_op jit(solution)/shard_map/branch_grad_spread/ppermute | solution.py:49
  438.7 2.4 collective-permute-done.27
  441.1 9.8 %collective-permute-done.28 = bf16[128,2048]{1,0:T(8,128)(2,1)S(1)} collective-permute-done((bf16[128,2048]{1,0:T(8,128)(2,1)S(1)}, bf16[128,2048]{1,0:T(8,128)(2,1)S(1)}, u32[]{:S(2)}, u32[]{:S(2)}) %collective-permute-start.28) | collective-permute-done | bytes 524320 | tf_op jit(solution)/shard_map/branch_grad_spread/ppermute | solution.py:49
  452.6 4.5 collective-permute-done.29.far_ref
  457.1 7.5 %join_halves.7 = bf16[1024,2048]{1,0:T(8,128)(2,1)} custom-call(bf16[512,2048]{1,0:T(8,128)(2,1)} %pad_maximum_fusion.7.near_ref, bf16[512,2048]{1,0:T(8,128)(2,1)} %collective-permute-done.29.far_ref), custom_call_target="tpu_custom_call" | custom-call | bytes 8388608 | tf_op jit(solution)/shard_map/branch_grad_spread/join_halves/pallas_call | solution.py:68
  464.6 3.7 convolution_convert_fusion.7
  472.0 12.4 %attend_back.1 = bf16[1024,768]{1,0:T(8,128)(2,1)} custom-call(s32[4]{0:T(128)S(1)} %pad_add_fusion.info_ref, bf16[1024,256]{1,0:T(8,128)(2,1)S(1)} %get-tuple-element.36.q_row, bf16[1024,256]{1,0:T(8,128)(2,1)S(1)} %copy-done.1, bf16[1024,256]{1,0:T(8,128)(2,1)S(1)} %copy-done.3, f32[1024,256]{1,0:T(8,128)S(1)} %get-tuple-element.39.log_ref, ...), custom_call_target="tpu_custom_call" | custom-call | flops 2684354560 | bytes 5242880 | tf_op jit(solution)/shard_map/attend_back/pallas_call | solution.py:424
  484.4 3.2 convolution_convert_fusion.5
  487.7 3.9 convolution_convert_fusion.2
  495.2 3.7 convolution_convert_fusion.3
  499.3 1.8 add_convert_fusion
  507.2 23.3 %collective-permute-done.38 = bf16[4,256,768]{2,1,0:T(8,128)(2,1)} collective-permute-done((bf16[4,256,768]{2,1,0:T(8,128)(2,1)}, bf16[4,256,768]{2,1,0:T(8,128)(2,1)}, u32[]{:S(2)}, u32[]{:S(2)}) %collective-permute-start.38) | collective-permute-done | bytes 1572896 | tf_op jit(solution)/shard_map/qkv_trade/ppermute | solution.py:49
  530.5 3.5 pad_maximum_fusion.2
  534.1 7.7 %collective-permute-done.33 = bf16[128,2048]{1,0:T(8,128)(2,1)} collective-permute-done((bf16[128,2048]{1,0:T(8,128)(2,1)}, bf16[128,2048]{1,0:T(8,128)(2,1)}, u32[]{:S(2)}, u32[]{:S(2)}) %collective-permute-start.33) | collective-permute-done | bytes 524320 | tf_op jit(solution)/shard_map/first_grad_collect/ppermute | solution.py:49
  541.8 11.7 %collective-permute-done.34 = bf16[128,2048]{1,0:T(8,128)(2,1)} collective-permute-done((bf16[128,2048]{1,0:T(8,128)(2,1)}, bf16[128,2048]{1,0:T(8,128)(2,1)}, u32[]{:S(2)}, u32[]{:S(2)}) %collective-permute-start.34) | collective-permute-done | bytes 524320 | tf_op jit(solution)/shard_map/first_grad_collect/ppermute | solution.py:49
  553.5 12.7 %reduce-scatter.6.cloned.1.call-done = bf16[512,2048]{1,0:T(8,128)(2,1)} async-done(((bf16[2048,2048]{1,0:T(8,128)(2,1)}), bf16[512,2048]{1,0:T(8,128)(2,1)}) %reduce-scatter.6.cloned.1.call-update) | async-done | bytes 2097168 | tf_op jit(solution)/shard_map/gate_up_back/reduce_scatter | solution.py:165
  569.7 5.6 add_convert_fusion.1
  580.3 3.2 collective-permute-start.43
  587.5 2.8 fusion.24
  593.8 3.4 collective-permute-done.35
  597.2 5.9 collective-permute-done.36
  603.1 11.2 %collective-permute-done.37 = bf16[128,2048]{1,0:T(8,128)(2,1)S(1)} collective-permute-done((bf16[128,2048]{1,0:T(8,128)(2,1)S(1)}, bf16[128,2048]{1,0:T(8,128)(2,1)S(1)}, u32[]{:S(2)}, u32[]{:S(2)}) %collective-permute-start.37) | collective-permute-done | bytes 524320 | tf_op jit(solution)/shard_map/feed_collect/ppermute | solution.py:49
  615.6 19.4 %collective-permute-done.39 = bf16[256,2048]{1,0:T(8,128)(2,1)S(1)} collective-permute-done((bf16[256,2048]{1,0:T(8,128)(2,1)S(1)}, bf16[256,2048]{1,0:T(8,128)(2,1)S(1)}, u32[]{:S(2)}, u32[]{:S(2)}) %collective-permute-start.39) | collective-permute-done | bytes 1048608 | tf_op jit(solution)/shard_map/gate_up_return/ppermute | solution.py:49
  636.7 5.3 copy.58
  641.9 4.1 reduce-scatter.8.cloned.1.call-done
  (243 shorter events, 94.8 us)
Async XLA Ops:
  7.2 103.4 %all-gather.4.cloned.1.call-start = ((), (), s32[]{:S(2)}) async-start(), calls=%async_computation.5 | async-start | bytes 5242880 | tf_op jit(solution)/shard_map/attention_gather/all_gather | solution.py:161
  8.7 20.1 %copy-start.33 = (f32[2,64]{1,0:T(2,128)S(1)}, f32[2,64]{1,0:T(2,128)}, u32[]{:S(2)}) copy-start(f32[2,64]{1,0:T(2,128)} %param.15) | copy-start | bytes 1540
  28.8 1.2 collective-permute-start
  30.1 11.3 %collective-permute-start.1 = (f32[2,128]{1,0:T(2,128)S(1)}, f32[2,128]{1,0:T(2,128)S(1)}, u32[]{:S(2)}, u32[]{:S(2)}) collective-permute-start(f32[2,128]{1,0:T(2,128)S(1)} %pad_maximum_fusion.18), channel_id=1, source_target_pairs={{0,2},{1,3},{2,0},{3,1},{4,6},{5,7},{6,4},{7,5},{8,10},{9,11},{10,... | collective-permute-start | bytes 3080 | tf_op jit(solution)/shard_map/gain_gather/ppermute | solution.py:49
  41.4 7.6 %collective-permute-start.2 = (f32[2,256]{1,0:T(2,128)S(1)}, f32[2,256]{1,0:T(2,128)S(1)}, u32[]{:S(2)}, u32[]{:S(2)}) collective-permute-start(f32[2,256]{1,0:T(2,128)S(1)} %pad_maximum_fusion.17), channel_id=1, source_target_pairs={{0,4},{4,0},{1,5},{5,1},{2,6},{6,2},{3,7},{7,3},{8,12},{12,8},{9,1... | collective-permute-start | bytes 6152 | tf_op jit(solution)/shard_map/gain_gather/ppermute | solution.py:49
  43.7 41.5 %all-to-all-start = ((bf16[2,256,3072]{1,2,0:T(8,128)(2,1)}), bf16[2,256,3072]{1,2,0:T(8,128)(2,1)}, u32[]{:S(2)}, u32[]{:S(2)}) async-start(bf16[2,256,3072]{1,2,0:T(8,128)(2,1)} %pad_maximum_fusion.4), calls=%async_computation | async-start | bytes 6291456 | tf_op jit(solution)/shard_map/feed_weights/all_to_all | solution.py:139
  49.0 211.2 %all-gather.6.cloned.1.call-start = ((), (), s32[]{:S(2)}) async-start(), calls=%async_computation.6 | async-start | bytes 10485760 | tf_op jit(solution)/shard_map/gate_up_gather/all_gather | solution.py:161
  49.1 4.7 collective-permute-start.3
  53.8 4.8 collective-permute-start.4
  89.9 36.1 %copy-start.32 = (s32[1,3]{1,0:T(1,128)S(1)}, s32[1,3]{1,0:T(1,128)}, u32[]{:S(2)}) copy-start(s32[1,3]{1,0:T(1,128)} %param.10) | copy-start | bytes 40
  89.9 38.9 %copy-start.36 = (s32[8]{0:T(128)S(1)}, s32[8]{0:T(128)}, u32[]{:S(2)}) copy-start(s32[8]{0:T(128)} %constant.44.clone) | copy-start | bytes 100
  90.9 13.6 %collective-permute-start.7 = (bf16[128,2048]{1,0:T(8,128)(2,1)}, bf16[128,2048]{1,0:T(8,128)(2,1)S(1)}, u32[]{:S(2)}, u32[]{:S(2)}) collective-permute-start(bf16[128,2048]{1,0:T(8,128)(2,1)} %fusion.20), channel_id=1, source_target_pairs={{0,6},{1,7},{2,4},{3,5},{4,2},{5,3},{6,0},{7,1},{8,14},{9,15},{10,... | collective-permute-start | bytes 1572872 | tf_op jit(solution)/shard_map/first_spread/ppermute | solution.py:49
  110.6 230.8 %all-gather.8.cloned.1.call-start = ((), (), s32[]{:S(2)}) async-start(), calls=%async_computation.7 | async-start | bytes 5242880 | tf_op jit(solution)/shard_map/down_gather/all_gather | solution.py:161
  110.6 14.0 %collective-permute-start.5 = (bf16[128,2048]{1,0:T(8,128)(2,1)}, bf16[128,2048]{1,0:T(8,128)(2,1)S(1)}, u32[]{:S(2)}, u32[]{:S(2)}) collective-permute-start(bf16[128,2048]{1,0:T(8,128)(2,1)} %fusion.20), channel_id=1, source_target_pairs={{0,2},{1,3},{2,0},{3,1},{4,6},{5,7},{6,4},{7,5},{8,10},{9,11},{10,... | collective-permute-start | bytes 1572872 | tf_op jit(solution)/shard_map/first_spread/ppermute | solution.py:49
  112.2 13.6 %collective-permute-start.6 = (bf16[128,2048]{1,0:T(8,128)(2,1)}, bf16[128,2048]{1,0:T(8,128)(2,1)S(1)}, u32[]{:S(2)}, u32[]{:S(2)}) collective-permute-start(bf16[128,2048]{1,0:T(8,128)(2,1)} %fusion.20), channel_id=1, source_target_pairs={{0,4},{1,5},{2,6},{3,7},{4,0},{5,1},{6,2},{7,3},{8,12},{9,13},{10,... | collective-permute-start | bytes 1572872 | tf_op jit(solution)/shard_map/first_spread/ppermute | solution.py:49
  125.8 7.1 %collective-permute-start.8 = (bf16[512,2048]{1,0:T(8,128)(2,1)S(1)}, bf16[512,2048]{1,0:T(8,128)(2,1)}, u32[]{:S(2)}, u32[]{:S(2)}) collective-permute-start(bf16[512,2048]{1,0:T(8,128)(2,1)S(1)} %constant_dynamic-update-slice_fusion.near_ref), channel_id=1, source_target_pairs={{0,1},{1,0},{2,3},{3,2},{4,5},{5,4},{6,7},{7,6},{8,9},{9,8},{10,11... | collective-permute-start | bytes 6291464 | tf_op jit(solution)/shard_map/first_spread/ppermute | solution.py:49
  160.0 32.7 %copy-start.7 = (bf16[1,128,2048]{2,1,0:T(8,128)(2,1)S(1)}, bf16[1,128,2048]{2,1,0:T(8,128)(2,1)}, u32[]{:S(2)}) copy-start(bf16[1,128,2048]{2,1,0:T(8,128)(2,1)} %param.9) | copy-start | bytes 1572868
  160.0 4.2 collective-permute-start.9
  165.1 15.2 %collective-permute-start.10 = (bf16[128,2048]{1,0:T(8,128)(2,1)S(1)}, bf16[128,2048]{1,0:T(8,128)(2,1)S(1)}, u32[]{:S(2)}, u32[]{:S(2)}) collective-permute-start(bf16[128,2048]{1,0:T(8,128)(2,1)S(1)} %get-tuple-element.106), channel_id=1, source_target_pairs={{0,2},{1,3},{2,0},{3,1},{4,6},{5,7},{6,4},{7,5},{8,10},{9,11},{10,... | collective-permute-start | bytes 1572872 | tf_op jit(solution)/shard_map/branch_collect/ppermute | solution.py:49
  165.8 16.0 %collective-permute-start.11 = (bf16[128,2048]{1,0:T(8,128)(2,1)S(1)}, bf16[128,2048]{1,0:T(8,128)(2,1)S(1)}, u32[]{:S(2)}, u32[]{:S(2)}) collective-permute-start(bf16[128,2048]{1,0:T(8,128)(2,1)S(1)} %get-tuple-element.108), channel_id=1, source_target_pairs={{0,4},{1,5},{2,6},{3,7},{4,0},{5,1},{6,2},{7,3},{8,12},{9,13},{10,... | collective-permute-start | bytes 1572872 | tf_op jit(solution)/shard_map/branch_collect/ppermute | solution.py:49
  167.2 25.5 %collective-permute-start.12 = (bf16[128,2048]{1,0:T(8,128)(2,1)S(1)}, bf16[128,2048]{1,0:T(8,128)(2,1)S(1)}, u32[]{:S(2)}, u32[]{:S(2)}) collective-permute-start(bf16[128,2048]{1,0:T(8,128)(2,1)S(1)} %get-tuple-element.107), channel_id=1, source_target_pairs={{0,6},{1,7},{2,4},{3,5},{4,2},{5,3},{6,0},{7,1},{8,14},{9,15},{10,... | collective-permute-start | bytes 1572872 | tf_op jit(solution)/shard_map/branch_collect/ppermute | solution.py:49
  168.7 34.0 %collective-permute-start.17 = (bf16[128,2048]{1,0:T(8,128)(2,1)S(1)}, bf16[128,2048]{1,0:T(8,128)(2,1)S(1)}, u32[]{:S(2)}, u32[]{:S(2)}) collective-permute-start(bf16[128,2048]{1,0:T(8,128)(2,1)S(1)} %bitcast.132), channel_id=1, source_target_pairs={{0,2},{1,3},{2,0},{3,1},{4,6},{5,7},{6,4},{7,5},{8,10},{9,11},{10,... | collective-permute-start | bytes 1572872 | tf_op jit(solution)/shard_map/cotangent_spread/ppermute | solution.py:49
  169.3 34.9 %collective-permute-start.18 = (bf16[128,2048]{1,0:T(8,128)(2,1)S(1)}, bf16[128,2048]{1,0:T(8,128)(2,1)S(1)}, u32[]{:S(2)}, u32[]{:S(2)}) collective-permute-start(bf16[128,2048]{1,0:T(8,128)(2,1)S(1)} %bitcast.133), channel_id=1, source_target_pairs={{0,4},{1,5},{2,6},{3,7},{4,0},{5,1},{6,2},{7,3},{8,12},{9,13},{10,... | collective-permute-start | bytes 1572872 | tf_op jit(solution)/shard_map/cotangent_spread/ppermute | solution.py:49
  180.3 34.9 %collective-permute-start.19 = (bf16[128,2048]{1,0:T(8,128)(2,1)S(1)}, bf16[128,2048]{1,0:T(8,128)(2,1)S(1)}, u32[]{:S(2)}, u32[]{:S(2)}) collective-permute-start(bf16[128,2048]{1,0:T(8,128)(2,1)S(1)} %bitcast.134), channel_id=1, source_target_pairs={{0,6},{1,7},{2,4},{3,5},{4,2},{5,3},{6,0},{7,1},{8,14},{9,15},{10,... | collective-permute-start | bytes 1572872 | tf_op jit(solution)/shard_map/cotangent_spread/ppermute | solution.py:49
  194.4 29.9 %collective-permute-start.13 = (bf16[128,2048]{1,0:T(8,128)(2,1)S(1)}, bf16[128,2048]{1,0:T(8,128)(2,1)S(1)}, u32[]{:S(2)}, u32[]{:S(2)}) collective-permute-start(bf16[128,2048]{1,0:T(8,128)(2,1)S(1)} %multiply_convert_fusion.3), channel_id=1, source_target_pairs={{0,2},{1,3},{2,0},{3,1},{4,6},{5,7},{6,4},{7,5},{8,10},{9,11},{10,... | collective-permute-start | bytes 1572872 | tf_op jit(solution)/shard_map/second_spread/ppermute | solution.py:49
  195.1 30.5 %collective-permute-start.14 = (bf16[128,2048]{1,0:T(8,128)(2,1)S(1)}, bf16[128,2048]{1,0:T(8,128)(2,1)S(1)}, u32[]{:S(2)}, u32[]{:S(2)}) collective-permute-start(bf16[128,2048]{1,0:T(8,128)(2,1)S(1)} %multiply_convert_fusion.3), channel_id=1, source_target_pairs={{0,4},{1,5},{2,6},{3,7},{4,0},{5,1},{6,2},{7,3},{8,12},{9,13},{10,... | collective-permute-start | bytes 1572872 | tf_op jit(solution)/shard_map/second_spread/ppermute | solution.py:49
  202.7 34.1 %collective-permute-start.15 = (bf16[128,2048]{1,0:T(8,128)(2,1)S(1)}, bf16[128,2048]{1,0:T(8,128)(2,1)S(1)}, u32[]{:S(2)}, u32[]{:S(2)}) collective-permute-start(bf16[128,2048]{1,0:T(8,128)(2,1)S(1)} %multiply_convert_fusion.3), channel_id=1, source_target_pairs={{0,6},{1,7},{2,4},{3,5},{4,2},{5,3},{6,0},{7,1},{8,14},{9,15},{10,... | collective-permute-start | bytes 1572872 | tf_op jit(solution)/shard_map/second_spread/ppermute | solution.py:49
  216.8 21.5 %collective-permute-start.20 = (bf16[512,2048]{1,0:T(8,128)(2,1)S(1)}, bf16[512,2048]{1,0:T(8,128)(2,1)}, u32[]{:S(2)}, u32[]{:S(2)}) collective-permute-start(bf16[512,2048]{1,0:T(8,128)(2,1)S(1)} %pad_maximum_fusion.6.near_ref), channel_id=1, source_target_pairs={{0,1},{1,0},{2,3},{3,2},{4,5},{5,4},{6,7},{7,6},{8,9},{9,8},{10,11... | collective-permute-start | bytes 6291464 | tf_op jit(solution)/shard_map/cotangent_spread/ppermute | solution.py:49
  238.4 7.1 %collective-permute-start.16 = (bf16[512,2048]{1,0:T(8,128)(2,1)}, bf16[512,2048]{1,0:T(8,128)(2,1)}, u32[]{:S(2)}, u32[]{:S(2)}) collective-permute-start(bf16[512,2048]{1,0:T(8,128)(2,1)} %pad_maximum_fusion.5.near_ref), channel_id=1, source_target_pairs={{0,1},{1,0},{2,3},{3,2},{4,5},{5,4},{6,7},{7,6},{8,9},{9,8},{10,11... | collective-permute-start | bytes 6291464 | tf_op jit(solution)/shard_map/second_spread/ppermute | solution.py:49
  260.2 158.6 %reduce-scatter.4.cloned.1.call-start = ((), (), s32[]{:S(2)}) async-start(), calls=%async_computation.8 | async-start | bytes 5242880 | tf_op jit(solution)/shard_map/down_back/reduce_scatter | solution.py:165
  341.4 224.8 %reduce-scatter.6.cloned.1.call-start = ((), (), s32[]{:S(2)}) async-start(), calls=%async_computation.9 | async-start | bytes 10485760 | tf_op jit(solution)/shard_map/gate_up_back/reduce_scatter | solution.py:165
  361.8 4.2 collective-permute-start.21
  376.9 15.9 %collective-permute-start.22 = (bf16[128,2048]{1,0:T(8,128)(2,1)}, bf16[128,2048]{1,0:T(8,128)(2,1)}, u32[]{:S(2)}, u32[]{:S(2)}) collective-permute-start(bf16[128,2048]{1,0:T(8,128)(2,1)} %get-tuple-element.105), channel_id=1, source_target_pairs={{0,2},{1,3},{2,0},{3,1},{4,6},{5,7},{6,4},{7,5},{8,10},{9,11},{10,... | collective-permute-start | bytes 1572872 | tf_op jit(solution)/shard_map/second_grad_collect/ppermute | solution.py:49
  378.4 15.1 %collective-permute-start.23 = (bf16[128,2048]{1,0:T(8,128)(2,1)}, bf16[128,2048]{1,0:T(8,128)(2,1)}, u32[]{:S(2)}, u32[]{:S(2)}) collective-permute-start(bf16[128,2048]{1,0:T(8,128)(2,1)} %get-tuple-element.104), channel_id=1, source_target_pairs={{0,4},{1,5},{2,6},{3,7},{4,0},{5,1},{6,2},{7,3},{8,12},{9,13},{10,... | collective-permute-start | bytes 1572872 | tf_op jit(solution)/shard_map/second_grad_collect/ppermute | solution.py:49
  379.9 23.7 %collective-permute-start.24 = (bf16[128,2048]{1,0:T(8,128)(2,1)}, bf16[128,2048]{1,0:T(8,128)(2,1)}, u32[]{:S(2)}, u32[]{:S(2)}) collective-permute-start(bf16[128,2048]{1,0:T(8,128)(2,1)} %get-tuple-element.103), channel_id=1, source_target_pairs={{0,6},{1,7},{2,4},{3,5},{4,2},{5,3},{6,0},{7,1},{8,14},{9,15},{10,... | collective-permute-start | bytes 1572872 | tf_op jit(solution)/shard_map/second_grad_collect/ppermute | solution.py:49
  418.9 227.1 %reduce-scatter.8.cloned.1.call-start = ((), (), s32[]{:S(2)}) async-start(), calls=%async_computation.10 | async-start | bytes 5242880 | tf_op jit(solution)/shard_map/attention_back/reduce_scatter | solution.py:165
  424.8 13.9 %collective-permute-start.26 = (bf16[128,2048]{1,0:T(8,128)(2,1)S(1)}, bf16[128,2048]{1,0:T(8,128)(2,1)S(1)}, u32[]{:S(2)}, u32[]{:S(2)}) collective-permute-start(bf16[128,2048]{1,0:T(8,128)(2,1)S(1)} %get-tuple-element.81), channel_id=1, source_target_pairs={{0,2},{1,3},{2,0},{3,1},{4,6},{5,7},{6,4},{7,5},{8,10},{9,11},{10,... | collective-permute-start | bytes 1572872 | tf_op jit(solution)/shard_map/branch_grad_spread/ppermute | solution.py:49
  426.3 14.8 %collective-permute-start.27 = (bf16[128,2048]{1,0:T(8,128)(2,1)S(1)}, bf16[128,2048]{1,0:T(8,128)(2,1)S(1)}, u32[]{:S(2)}, u32[]{:S(2)}) collective-permute-start(bf16[128,2048]{1,0:T(8,128)(2,1)S(1)} %get-tuple-element.81), channel_id=1, source_target_pairs={{0,4},{1,5},{2,6},{3,7},{4,0},{5,1},{6,2},{7,3},{8,12},{9,13},{10,... | collective-permute-start | bytes 1572872 | tf_op jit(solution)/shard_map/branch_grad_spread/ppermute | solution.py:49
  427.8 23.2 %collective-permute-start.28 = (bf16[128,2048]{1,0:T(8,128)(2,1)S(1)}, bf16[128,2048]{1,0:T(8,128)(2,1)S(1)}, u32[]{:S(2)}, u32[]{:S(2)}) collective-permute-start(bf16[128,2048]{1,0:T(8,128)(2,1)S(1)} %get-tuple-element.81), channel_id=1, source_target_pairs={{0,6},{1,7},{2,4},{3,5},{4,2},{5,3},{6,0},{7,1},{8,14},{9,15},{10,... | collective-permute-start | bytes 1572872 | tf_op jit(solution)/shard_map/branch_grad_spread/ppermute | solution.py:49
  452.6 4.5 collective-permute-start.29
  469.2 15.2 %collective-permute-start.30 = (bf16[4,256,256]{2,1,0:T(8,128)(2,1)S(1)}, bf16[4,256,256]{2,1,0:T(8,128)(2,1)S(1)}, u32[]{:S(2)}, u32[]{:S(2)}) collective-permute-start(bf16[4,256,256]{2,1,0:T(8,128)(2,1)S(1)} %get-tuple-element.119), channel_id=1, source_target_pairs={{0,4},{4,0},{1,5},{5,1},{2,6},{6,2},{3,7},{7,3},{8,12},{12,8},{9,1... | collective-permute-start | bytes 1572872 | tf_op jit(solution)/shard_map/out_trade/ppermute | solution.py:49
  487.6 11.8 %collective-permute-start.31 = (bf16[512,2048]{1,0:T(8,128)(2,1)S(1)}, bf16[512,2048]{1,0:T(8,128)(2,1)S(1)}, u32[]{:S(2)}, u32[]{:S(2)}) collective-permute-start(bf16[512,2048]{1,0:T(8,128)(2,1)S(1)} %convolution_convert_fusion.5), channel_id=1, source_target_pairs={{0,1},{1,0},{2,3},{3,2},{4,5},{5,4},{6,7},{7,6},{8,9},{9,8},{10,11... | collective-permute-start | bytes 6291464 | tf_op jit(solution)/shard_map/first_grad_collect/ppermute | solution.py:49
  493.0 37.5 %collective-permute-start.38 = (bf16[4,256,768]{2,1,0:T(8,128)(2,1)}, bf16[4,256,768]{2,1,0:T(8,128)(2,1)}, u32[]{:S(2)}, u32[]{:S(2)}) collective-permute-start(bf16[4,256,768]{2,1,0:T(8,128)(2,1)} %get-tuple-element.90), channel_id=1, source_target_pairs={{0,4},{4,0},{1,5},{5,1},{2,6},{6,2},{3,7},{7,3},{8,12},{12,8},{9,1... | collective-permute-start | bytes 4718600 | tf_op jit(solution)/shard_map/qkv_trade/ppermute | solution.py:49
  499.0 31.6 %copy-start.22 = (bf16[4,1,256,256]{3,2,0,1:T(8,128)(2,1)S(1)}, bf16[4,1,256,256]{3,2,0,1:T(8,128)(2,1)}, u32[]{:S(2)}) copy-start(bf16[4,1,256,256]{3,2,0,1:T(8,128)(2,1)} %get-tuple-element.120) | copy-start | bytes 1572868
  499.0 31.6 %copy-start.27 = (bf16[4,256,256]{2,1,0:T(8,128)(2,1)S(1)}, bf16[4,256,256]{2,1,0:T(8,128)(2,1)}, u32[]{:S(2)}) copy-start(bf16[4,256,256]{2,1,0:T(8,128)(2,1)} %copy-done.26) | copy-start | bytes 1572868
  499.0 70.8 %collective-permute-start.25 = (bf16[512,2048]{1,0:T(8,128)(2,1)}, bf16[512,2048]{1,0:T(8,128)(2,1)}, u32[]{:S(2)}, u32[]{:S(2)}) collective-permute-start(bf16[512,2048]{1,0:T(8,128)(2,1)} %convolution_convert_fusion.3), channel_id=1, source_target_pairs={{0,1},{1,0},{2,3},{3,2},{4,5},{5,4},{6,7},{7,6},{8,9},{9,8},{10,11... | collective-permute-start | bytes 6291464 | tf_op jit(solution)/shard_map/feed_collect/ppermute | solution.py:49
  503.7 30.3 %collective-permute-start.32 = (bf16[128,2048]{1,0:T(8,128)(2,1)}, bf16[128,2048]{1,0:T(8,128)(2,1)S(1)}, u32[]{:S(2)}, u32[]{:S(2)}) collective-permute-start(bf16[128,2048]{1,0:T(8,128)(2,1)} %get-tuple-element.102), channel_id=1, source_target_pairs={{0,2},{1,3},{2,0},{3,1},{4,6},{5,7},{6,4},{7,5},{8,10},{9,11},{10,... | collective-permute-start | bytes 1572872 | tf_op jit(solution)/shard_map/first_grad_collect/ppermute | solution.py:49
  505.2 36.6 %collective-permute-start.33 = (bf16[128,2048]{1,0:T(8,128)(2,1)}, bf16[128,2048]{1,0:T(8,128)(2,1)}, u32[]{:S(2)}, u32[]{:S(2)}) collective-permute-start(bf16[128,2048]{1,0:T(8,128)(2,1)} %get-tuple-element.101), channel_id=1, source_target_pairs={{0,4},{1,5},{2,6},{3,7},{4,0},{5,1},{6,2},{7,3},{8,12},{9,13},{10,... | collective-permute-start | bytes 1572872 | tf_op jit(solution)/shard_map/first_grad_collect/ppermute | solution.py:49
  505.9 47.6 %collective-permute-start.34 = (bf16[128,2048]{1,0:T(8,128)(2,1)}, bf16[128,2048]{1,0:T(8,128)(2,1)}, u32[]{:S(2)}, u32[]{:S(2)}) collective-permute-start(bf16[128,2048]{1,0:T(8,128)(2,1)} %get-tuple-element.100), channel_id=1, source_target_pairs={{0,6},{1,7},{2,4},{3,5},{4,2},{5,3},{6,0},{7,1},{8,14},{9,15},{10,... | collective-permute-start | bytes 1572872 | tf_op jit(solution)/shard_map/first_grad_collect/ppermute | solution.py:49
  534.0 32.2 %copy-start.8 = (bf16[1,128,2048]{2,1,0:T(8,128)(2,1)S(1)}, bf16[1,128,2048]{2,1,0:T(8,128)(2,1)}, u32[]{:S(2)}) copy-start(bf16[1,128,2048]{2,1,0:T(8,128)(2,1)} %param.9) | copy-start | bytes 1572868
  534.0 32.2 %copy-start.20 = (bf16[512,2048]{1,0:T(8,128)(2,1)S(1)}, bf16[512,2048]{1,0:T(8,128)(2,1)}, u32[]{:S(2)}) copy-start(bf16[512,2048]{1,0:T(8,128)(2,1)} %copy-done.19) | copy-start | bytes 6291460
  534.0 32.2 %copy-start.29 = (f32[1,2048]{1,0:T(1,128)S(1)}, f32[1,2048]{1,0:T(1,128)}, u32[]{:S(2)}) copy-start(f32[1,2048]{1,0:T(1,128)} %copy-done.28) | copy-start | bytes 24580
  534.0 32.2 %copy-start.31 = (f32[128]{0:T(128)S(1)}, f32[128]{0:T(128)}, u32[]{:S(2)}) copy-start(f32[128]{0:T(128)} %copy-done.30) | copy-start | bytes 1540
  568.2 7.1 %collective-permute-start.40 = (f32[2,1024]{1,0:T(2,128)S(1)}, f32[2,1024]{1,0:T(2,128)S(1)}, u32[]{:S(2)}, u32[]{:S(2)}) collective-permute-start(f32[2,1024]{1,0:T(2,128)S(1)} %broadcast_select_fusion.6), channel_id=1, source_target_pairs={{0,4},{4,0},{1,5},{5,1},{2,6},{6,2},{3,7},{7,3},{8,12},{12,8},{9,1... | collective-permute-start | bytes 24584 | tf_op jit(solution)/shard_map/gain_scatter/ppermute | solution.py:49
  575.4 3.7 collective-permute-start.41
  577.0 15.1 %collective-permute-start.45 = (bf16[256,1024]{1,0:T(8,128)(2,1)S(1)}, bf16[256,1024]{1,0:T(8,128)(2,1)S(1)}, u32[]{:S(2)}, u32[]{:S(2)}) collective-permute-start(bf16[256,1024]{1,0:T(8,128)(2,1)S(1)} %broadcast_select_fusion.3), channel_id=1, source_target_pairs={{0,4},{4,0},{1,5},{5,1},{2,6},{6,2},{3,7},{7,3},{8,12},{12,8},{9,1... | collective-permute-start | bytes 1572872 | tf_op jit(solution)/shard_map/down_return/ppermute | solution.py:49
  579.0 1.2 collective-permute-start.42
  580.3 7.1 %collective-permute-start.43 = (f32[2,128]{1,0:T(2,128)S(1)}, f32[2,128]{1,0:T(2,128)S(1)}, u32[]{:S(2)}, u32[]{:S(2)}) collective-permute-start(f32[2,128]{1,0:T(2,128)S(1)} %broadcast_select_fusion.15), channel_id=1, source_target_pairs={{0,16},{8,24},{16,0},{24,8},{1,17},{9,25},{17,1},{25,9},{2,18},{10... | collective-permute-start | bytes 3080 | tf_op jit(solution)/shard_map/gain_scatter/ppermute | solution.py:49
  583.5 13.7 %collective-permute-start.35 = (bf16[128,2048]{1,0:T(8,128)(2,1)S(1)}, bf16[128,2048]{1,0:T(8,128)(2,1)S(1)}, u32[]{:S(2)}, u32[]{:S(2)}) collective-permute-start(bf16[128,2048]{1,0:T(8,128)(2,1)S(1)} %get-tuple-element.97), channel_id=1, source_target_pairs={{0,2},{1,3},{2,0},{3,1},{4,6},{5,7},{6,4},{7,5},{8,10},{9,11},{10,... | collective-permute-start | bytes 1572872 | tf_op jit(solution)/shard_map/feed_collect/ppermute | solution.py:49
  585.0 18.2 %collective-permute-start.36 = (bf16[128,2048]{1,0:T(8,128)(2,1)S(1)}, bf16[128,2048]{1,0:T(8,128)(2,1)S(1)}, u32[]{:S(2)}, u32[]{:S(2)}) collective-permute-start(bf16[128,2048]{1,0:T(8,128)(2,1)S(1)} %get-tuple-element.99), channel_id=1, source_target_pairs={{0,4},{1,5},{2,6},{3,7},{4,0},{5,1},{6,2},{7,3},{8,12},{9,13},{10,... | collective-permute-start | bytes 1572872 | tf_op jit(solution)/shard_map/feed_collect/ppermute | solution.py:49
  585.5 28.8 %collective-permute-start.37 = (bf16[128,2048]{1,0:T(8,128)(2,1)S(1)}, bf16[128,2048]{1,0:T(8,128)(2,1)S(1)}, u32[]{:S(2)}, u32[]{:S(2)}) collective-permute-start(bf16[128,2048]{1,0:T(8,128)(2,1)S(1)} %get-tuple-element.98), channel_id=1, source_target_pairs={{0,6},{1,7},{2,4},{3,5},{4,2},{5,3},{6,0},{7,1},{8,14},{9,15},{10,... | collective-permute-start | bytes 1572872 | tf_op jit(solution)/shard_map/feed_collect/ppermute | solution.py:49
  587.4 3.6 collective-permute-start.44
  591.8 22.5 %copy-start.5 = (f32[128,2048]{1,0:T(8,128)S(1)}, f32[128,2048]{1,0:T(8,128)}, u32[]{:S(2)}) copy-start(f32[128,2048]{1,0:T(8,128)} %copy-done.4) | copy-start | bytes 3145732
  591.8 43.1 %collective-permute-start.39 = (bf16[256,2048]{1,0:T(8,128)(2,1)S(1)}, bf16[256,2048]{1,0:T(8,128)(2,1)S(1)}, u32[]{:S(2)}, u32[]{:S(2)}) collective-permute-start(bf16[256,2048]{1,0:T(8,128)(2,1)S(1)} %broadcast_select_fusion.1), channel_id=1, source_target_pairs={{0,4},{4,0},{1,5},{5,1},{2,6},{6,2},{3,7},{7,3},{8,12},{12,8},{9,1... | collective-permute-start | bytes 3145736 | tf_op jit(solution)/shard_map/gate_up_return/ppermute | solution.py:49
  (28 other events, 172.5 us)
Sparse Core Ops, SparseCore 0:
  28.9 81.6 all-gather.3
  112.1 148.0 all-gather.5
  262.3 78.9 all-gather.7
  343.5 75.2 reduce-scatter.3
  421.1 144.9 reduce-scatter.5
  568.4 77.5 reduce-scatter.7

commit v6 on v5

--- a/solution.py
+++ b/solution.py
@@ -174,6 +174,12 @@
     split = grads.reshape(size_dp, 2, -1, grads.shape[1])
     own, sent = own_then_other([split[:, 0], split[:, 1]])
     return [part.reshape(-1, grads.shape[1]) for part in (own, swap_by(sent, "blk", 2, 1))]
+
+
+def join_rows(own, sent, size_dp):
+    parts = own_then_other([own, swap_by(sent, "blk", 2, 1)])
+    parts = [part.reshape(size_dp, -1, own.shape[1]) for part in parts]
+    return jnp.stack(parts, axis=1).reshape(-1, own.shape[1])
 
 
 def join_columns(parted, kinds, wide):
@@ -512,17 +518,25 @@
     info = jnp.stack([me] + ends).astype(jnp.int32)
     cosine, sine = rope_tables(within)
 
-    held_attention = named(
-        "attention_weights", swap_columns, [weight_qkv, weight_out[:, None, :]], size_blk
-    )
-    full_attention = jnp.concatenate(held_attention, axis=1)
-    full_attention = named("attention_gather", gather_rows, full_attention)
-    cut = held_attention[0].shape[1]
-    full_qkv, full_out = full_attention[:, :cut], full_attention[:, cut:]
+    kinds = [weight_qkv, weight_out[:, None, :]]
+    if size_blk == 2:
+        sides = [jnp.concatenate(side, axis=1) for side in zip(*(split_columns(k, 2) for k in kinds))]
+        full_attention = named("attention_gather", gather_rows, jnp.concatenate(sides, axis=1))
+        half = full_attention.shape[1] // 2
+        cut = half - split_columns(kinds[1], 2).shape[2]
+        own, sent = own_then_other([full_attention[:, :half], full_attention[:, half:]])
+        full_qkv = named("qkv_join", join_rows, own[:, :cut], sent[:, :cut], size_dp)
+        full_out = named("out_join", join_rows, own[:, cut:], sent[:, cut:], size_dp)
+    else:
+        held_attention = named("attention_weights", swap_columns, kinds, size_blk)
+        full_attention = jnp.concatenate(held_attention, axis=1)
+        full_attention = named("attention_gather", gather_rows, full_attention)
+        cut = held_attention[0].shape[1]
+        full_qkv, full_out = full_attention[:, :cut], full_attention[:, cut:]
     held_gate_up, held_down = named(
         "feed_weights",
         swap_columns,
-        [after(weight_gate_up, *held_attention), weight_down[:, None, :]],
+        [weight_gate_up, weight_down[:, None, :]],
         size_blk,
     )
     gain_pair = named("gain_gather", gather_small, norm_gains, sizes)

time: 664 us -> 686 us (1.033)
  blocking collectives: 17.6 us -> 0 us
  other arithmetic: 40 us -> 53 us
  local copies, waits for them, and re-layouts: 35.6 us -> 48 us
  waiting for transfers between devices: 347 us -> 359 us
    ppermute x46 -> x48, waiting for transfers between devices: 221 us -> 241 us  [swap_by(): return lax.ppermute(value, axes, [(i, i ^ bits) for i in range(size)])]
    all_to_all x1 -> x0, blocking collectives: 17.6 us -> none  [trade(): return lax.all_to_all(blocks, axis, 0, 0, tiled=True)]
    select_n x4 -> x7, other arithmetic: 2.6 us -> 11 us  [own_then_other(): jnp.where(first, blocks[0], blocks[1])]
    reshape x0 -> x4, local copies, waits for them, and re-layouts: none -> 8.35 us  [join_rows(): return jnp.stack(parts, axis=1).reshape(-1, own.shape[1])]
    all_gather x3, waiting for transfers between devices: 67.7 us -> 59.6 us  [gather_rows(): return lax.all_gather(after(weight, *events), 'dp', axis=0, tiled=True)]
    unnamed x85 -> x106, local copies, waits for them, and re-layouts: 17.2 us -> 25 us
    ppermute x46 -> x48, starting transfers between devices: 43.5 us -> 48 us  [swap_by(): return lax.ppermute(value, axes, [(i, i ^ bits) for i in range(size)])]
  transfers between devices with their start and end apart: 53 -> 55, of which waited for: 39 -> 38; matrix products, arithmetic and copies ran while one was open for 25% -> 27% of each run, Pallas kernels for 8% -> 8%
where the time goes in v6:
time: 686 us; the launch traced here: 680 us
  waiting for transfers between devices  359 us (52%)
  matrix products  98.6 us (14%)
  starting transfers between devices  53.8 us (8%)
  other arithmetic  53 us (8%)
  Pallas kernels  51.9 us (8%)
  local copies, waits for them, and re-layouts  48 us (7%)
  between operations  15.5 us (2%)
    ppermute x48, waiting for transfers between devices, swap_by(): return lax.ppermute(value, axes, [(i, i ^ bits) for i in range(size)])  241 us
    all_gather x3, waiting for transfers between devices, gather_rows(): return lax.all_gather(after(weight, *events), 'dp', axis=0, tiled=True)  59.6 us
    ppermute x48, starting transfers between devices, swap_by(): return lax.ppermute(value, axes, [(i, i ^ bits) for i in range(size)])  48 us
    dot_general x5, matrix products, dot_nn(): lax.dot_general(a, b, (((1,), (0,)), ((), ())), preferred_element_type=F32)  37.2 us
    dot_general x8, matrix products, dot_nt(): lax.dot_general(a, b, (((1,), (1,)), ((), ())), preferred_element_type=F32)  33.3 us
    reduce_scatter x3, waiting for transfers between devices, sum_rows(): return lax.psum_scatter(grads, 'dp', scatter_dimension=0, tiled=True)  31.7 us
    pallas_call x4, Pallas kernels, join_halves(): pl.pallas_call(functools.partial(join_kernel, steps), grid=(2 * steps,),...  29.1 us
    dot_general x4, matrix products, dot_tn(): lax.dot_general(a, b, (((0,), (0,)), ((), ())), preferred_element_type=F32)  28.1 us
  transfers between devices with their start and end apart: 55, of which 38 were waited for; matrix products, arithmetic and copies ran while one was open for 27% of the time, Pallas kernels for 8%

profile of v6, /device:TPU:0, one launch (start us, length us, event | category | flops | bytes accessed | tf_op | source)
XLA Modules:
  0.0 679.7 jit_solution(17014648437432765717)
XLA Ops:
  13.1 2.8 collective-permute-start.1
  16.0 4.1 copy.54
  26.9 5.3 all-to-all-start
  36.1 2.7 collective-permute-start.4
  41.9 26.5 %all-to-all-done = bf16[2,256,3072]{1,2,0:T(8,128)(2,1)} async-done(((bf16[2,256,3072]{1,2,0:T(8,128)(2,1)}), bf16[2,256,3072]{1,2,0:T(8,128)(2,1)}, u32[]{:S(2)}, u32[]{:S(2)}) %all-to-all-start) | async-done | bytes 3145760 | tf_op jit(solution)/shard_map/feed_weights/all_to_all | solution.py:139
  68.4 3.2 copy.57
  77.7 12.5 %collective-permute-done.7 = bf16[128,2048]{1,0:T(8,128)(2,1)S(1)} collective-permute-done((bf16[128,2048]{1,0:T(8,128)(2,1)}, bf16[128,2048]{1,0:T(8,128)(2,1)S(1)}, u32[]{:S(2)}, u32[]{:S(2)}) %collective-permute-start.7) | collective-permute-done | bytes 524320 | tf_op jit(solution)/shard_map/first_spread/ppermute | solution.py:49
  90.1 5.3 all-gather.4.cloned.1.call-done
  101.6 3.1 broadcast_select_fusion.1
  115.0 7.3 %join_halves.4 = bf16[1024,2048]{1,0:T(8,128)(2,1)} custom-call(bf16[512,2048]{1,0:T(8,128)(2,1)} %constant_dynamic-update-slice_fusion.near_ref, bf16[512,2048]{1,0:T(8,128)(2,1)} %collective-permute-done.8.far_ref), custom_call_target="tpu_custom_call" | custom-call | bytes 8388608 | tf_op jit(solution)/shard_map/first_spread/join_halves/pallas_call | solution.py:68
  122.3 32.0 %collective-permute-done.10 = bf16[1024,256]{0,1:T(8,128)(2,1)} collective-permute-done((bf16[1024,256]{0,1:T(8,128)(2,1)}, bf16[1024,256]{0,1:T(8,128)(2,1)}, u32[]{:S(2)}, u32[]{:S(2)}) %collective-permute-start.10) | collective-permute-done | bytes 524320 | tf_op jit(solution)/shard_map/out_join/ppermute | solution.py:49
  154.3 2.1 broadcast_select_fusion.11
  160.4 2.3 pad_maximum_fusion.12
  162.7 3.3 broadcast_select_fusion.4
  166.0 2.7 copy.77
  170.2 2.4 pad_maximum_fusion.5
  173.5 5.2 fusion.48.q_ref.k_ref.v_ref
  178.6 10.4 %attend.1 = (bf16[1024,256]{1,0:T(8,128)(2,1)S(1)}, bf16[1024,256]{1,0:T(8,128)(2,1)S(1)}, bf16[1024,256]{1,0:T(8,128)(2,1)S(1)}, bf16[1024,256]{1,0:T(8,128)(2,1)S(1)}, f32[1024,256]{1,0:T(8,128)S(1)}) custom-call(s32[4]{0:T(128)S(1)} %pad_add_fusion.info_ref, f32[1024,768]{1,0:T(8,128)} %fusion.48.q_ref.k_ref.v_ref, f32[1024,768]{1,0:T(8,128)} %fusion.48.q_ref.k_ref.v_ref, ...), custom_call_target="tpu_custom_call" | custom-call | flops 1073741824 | bytes 4718592 | tf_op jit(solution)/shard_map/attend/pallas_call | solution.py:314
  189.9 4.1 collective-permute-done.11
  200.2 10.3 %collective-permute-done.12 = bf16[128,2048]{1,0:T(8,128)(2,1)S(1)} collective-permute-done((bf16[128,2048]{1,0:T(8,128)(2,1)S(1)}, bf16[128,2048]{1,0:T(8,128)(2,1)S(1)}, u32[]{:S(2)}, u32[]{:S(2)}) %collective-permute-start.12) | collective-permute-done | bytes 524320 | tf_op jit(solution)/shard_map/branch_collect/ppermute | solution.py:49
  211.7 10.9 %collective-permute-done.14 = bf16[128,2048]{1,0:T(8,128)(2,1)S(1)} collective-permute-done((bf16[128,2048]{1,0:T(8,128)(2,1)S(1)}, bf16[128,2048]{1,0:T(8,128)(2,1)S(1)}, u32[]{:S(2)}, u32[]{:S(2)}) %collective-permute-start.14) | collective-permute-done | bytes 524320 | tf_op jit(solution)/shard_map/branch_collect/ppermute | solution.py:49
  226.0 6.9 %collective-permute-done.19 = bf16[128,2048]{1,0:T(8,128)(2,1)S(1)} collective-permute-done((bf16[128,2048]{1,0:T(8,128)(2,1)S(1)}, bf16[128,2048]{1,0:T(8,128)(2,1)S(1)}, u32[]{:S(2)}, u32[]{:S(2)}) %collective-permute-start.19) | collective-permute-done | bytes 524320 | tf_op jit(solution)/shard_map/cotangent_spread/ppermute | solution.py:49
  234.1 10.9 %collective-permute-done.21 = bf16[128,2048]{1,0:T(8,128)(2,1)S(1)} collective-permute-done((bf16[128,2048]{1,0:T(8,128)(2,1)S(1)}, bf16[128,2048]{1,0:T(8,128)(2,1)S(1)}, u32[]{:S(2)}, u32[]{:S(2)}) %collective-permute-start.21) | collective-permute-done | bytes 524320 | tf_op jit(solution)/shard_map/cotangent_spread/ppermute | solution.py:49
  246.6 7.3 %collective-permute-done.15 = bf16[128,2048]{1,0:T(8,128)(2,1)S(1)} collective-permute-done((bf16[128,2048]{1,0:T(8,128)(2,1)S(1)}, bf16[128,2048]{1,0:T(8,128)(2,1)S(1)}, u32[]{:S(2)}, u32[]{:S(2)}) %collective-permute-start.15) | collective-permute-done | bytes 524320 | tf_op jit(solution)/shard_map/second_spread/ppermute | solution.py:49
  255.9 10.5 %collective-permute-done.17 = bf16[128,2048]{1,0:T(8,128)(2,1)S(1)} collective-permute-done((bf16[128,2048]{1,0:T(8,128)(2,1)S(1)}, bf16[128,2048]{1,0:T(8,128)(2,1)S(1)}, u32[]{:S(2)}, u32[]{:S(2)}) %collective-permute-start.17) | collective-permute-done | bytes 524320 | tf_op jit(solution)/shard_map/second_spread/ppermute | solution.py:49
  268.0 7.1 %join_halves.6 = bf16[1024,2048]{1,0:T(8,128)(2,1)} custom-call(bf16[512,2048]{1,0:T(8,128)(2,1)} %copy-done.13, bf16[512,2048]{1,0:T(8,128)(2,1)} %collective-permute-done.22.far_ref), custom_call_target="tpu_custom_call" | custom-call | bytes 8388608 | tf_op jit(solution)/shard_map/cotangent_spread/join_halves/pallas_call | solution.py:68
  275.1 7.3 %join_halves.5 = bf16[1024,2048]{1,0:T(8,128)(2,1)} custom-call(bf16[512,2048]{1,0:T(8,128)(2,1)} %pad_maximum_fusion.6.near_ref, bf16[512,2048]{1,0:T(8,128)(2,1)} %collective-permute-done.18.far_ref), custom_call_target="tpu_custom_call" | custom-call | bytes 8388608 | tf_op jit(solution)/shard_map/second_spread/join_halves/pallas_call | solution.py:68
  282.5 10.2 %fusion.2 = f32[1024,1024]{0,1:T(8,128)} fusion(bf16[1024,2048]{1,0:T(8,128)(2,1)} %join_halves.5, bf16[2048,2048]{1,0:T(8,128)(2,1)} %all-gather.6.cloned.1.call-done), kind=kOutput, calls=%fused_computation.8 | convolution fusion | flops 4294967296 | bytes 12582912 | tf_op jit(solution)/shard_map/dot_general | solution.py:24
  292.8 8.6 %multiply_convert_fusion.2 = (bf16[1024,1024]{0,1:T(8,128)(2,1)}, f32[1024,1024]{0,1:T(8,128)}) fusion(f32[1024,1024]{0,1:T(8,128)} %fusion.2, bf16[1024,2048]{1,0:T(8,128)(2,1)S(1)} %copy-done.18, bf16[2048,2048]{1,0:T(8,128)(2,1)S(1)} %copy-done.42), kind=kOutput, calls=%fused_computation.17 | convolution fusion | flops 4301258752 | bytes 18874368 | tf_op jit(solution)/shard_map/dot_general | solution.py:24
  301.4 7.8 %convolution_convert_fusion.1 = bf16[2048,1024]{1,0:T(8,128)(2,1)} fusion(bf16[1024,2048]{1,0:T(8,128)(2,1)S(1)} %copy-done.20, bf16[1024,1024]{0,1:T(8,128)(2,1)} %get-tuple-element.35), kind=kOutput, calls=%fused_computation.21 | convolution fusion | flops 4297064448 | bytes 10485760 | tf_op jit(solution)/shard_map/dot_general | solution.py:32
  309.2 54.3 %all-gather.8.cloned.1.call-done = bf16[2048,1024]{1,0:T(8,128)(2,1)} async-done(((bf16[512,1024]{1,0:T(8,128)(2,1)}), bf16[2048,1024]{1,0:T(8,128)(2,1)}) %all-gather.8.cloned.1.call-update) | async-done | bytes 4194320 | tf_op jit(solution)/shard_map/down_gather/all_gather | solution.py:161
  363.8 11.9 %multiply_convert_fusion = (bf16[1024,1024]{0,1:T(8,128)(2,1)S(1)}, bf16[1024,1024]{0,1:T(8,128)(2,1)S(1)}) fusion(f32[1024,1024]{0,1:T(8,128)} %fusion.2, f32[1024,1024]{0,1:T(8,128)} %get-tuple-element.147, bf16[1024,2048]{1,0:T(8,128)(2,1)} %join_halves.6, bf16[2048,1024]{1,0:T(8,128)(2,1)} %all-gather.8.cloned.1.call-done), kind=kOutput, calls=%fused_computation.15 | convolution fusion | flops 4308598784 | bytes 20971520 | tf_op jit(solution)/shard_map/dot_general | solution.py:24
  375.8 9.0 %convolution_convert_fusion.6 = bf16[512,2048]{1,0:T(8,128)(2,1)S(1)} fusion(bf16[2048,2048]{1,0:T(8,128)(2,1)} %all-gather.6.cloned.1.call-done, bf16[1024,1024]{0,1:T(8,128)(2,1)S(1)} %get-tuple-element.86, bf16[1024,1024]{0,1:T(8,128)(2,1)S(1)} %get-tuple-element.85), kind=kOutput, calls=%fused_computation.28 | convolution fusion | flops 4300210176 | bytes 14680064 | tf_op jit(solution)/shard_map/second_grad_collect/dot_general | solution.py:28
  384.9 4.1 collective-permute-done.23
  389.0 8.5 %add_convert_fusion.2 = bf16[512,2048]{1,0:T(8,128)(2,1)S(1)} fusion(bf16[512,2048]{1,0:T(8,128)(2,1)S(1)} %collective-permute-done.23, bf16[2048,2048]{1,0:T(8,128)(2,1)} %all-gather.6.cloned.1.call-done, bf16[1024,1024]{0,1:T(8,128)(2,1)} %copy-done.47, bf16[1024,1024]{0,1:T(8,128)(2,1)S(1)} %get-tuple-element.85), kind=kOutput, calls=%fused_computation.14 | convolution fusion | flops 4302307328 | bytes 16777216 | tf_op jit(solution)/shard_map/second_grad_collect/dot_general | solution.py:28
  403.6 12.7 %convolution_convert_fusion = bf16[2048,2048]{1,0:T(8,128)(2,1)} fusion(bf16[1024,2048]{1,0:T(8,128)(2,1)S(1)} %copy-done.19, bf16[1024,1024]{0,1:T(8,128)(2,1)S(1)} %get-tuple-element.85, bf16[1024,1024]{0,1:T(8,128)(2,1)S(1)} %copy-done.48), kind=kOutput, calls=%fused_computation | convolution fusion | flops 8602517504 | bytes 16777216 | tf_op jit(solution)/shard_map/dot_general | solution.py:32
  416.7 10.0 %collective-permute-done.26 = bf16[128,2048]{1,0:T(8,128)(2,1)} collective-permute-done((bf16[128,2048]{1,0:T(8,128)(2,1)}, bf16[128,2048]{1,0:T(8,128)(2,1)}, u32[]{:S(2)}, u32[]{:S(2)}) %collective-permute-start.26) | collective-permute-done | bytes 524320 | tf_op jit(solution)/shard_map/second_grad_collect/ppermute | solution.py:49
  426.8 14.2 %reduce-scatter.4.cloned.1.call-done = bf16[512,1024]{1,0:T(8,128)(2,1)} async-done(((bf16[2048,1024]{1,0:T(8,128)(2,1)}), bf16[512,1024]{1,0:T(8,128)(2,1)}) %reduce-scatter.4.cloned.1.call-update) | async-done | bytes 1048592 | tf_op jit(solution)/shard_map/down_back/reduce_scatter | solution.py:165
  441.1 2.4 multiply_reduce_fusion
  443.6 3.1 fusion.38
  450.2 10.4 %collective-permute-done.28 = bf16[128,2048]{1,0:T(8,128)(2,1)S(1)} collective-permute-done((bf16[128,2048]{1,0:T(8,128)(2,1)S(1)}, bf16[128,2048]{1,0:T(8,128)(2,1)S(1)}, u32[]{:S(2)}, u32[]{:S(2)}) %collective-permute-start.28) | collective-permute-done | bytes 524320 | tf_op jit(solution)/shard_map/branch_grad_spread/ppermute | solution.py:49
  460.6 2.4 collective-permute-done.29
  463.0 9.8 %collective-permute-done.30 = bf16[128,2048]{1,0:T(8,128)(2,1)S(1)} collective-permute-done((bf16[128,2048]{1,0:T(8,128)(2,1)S(1)}, bf16[128,2048]{1,0:T(8,128)(2,1)S(1)}, u32[]{:S(2)}, u32[]{:S(2)}) %collective-permute-start.30) | collective-permute-done | bytes 524320 | tf_op jit(solution)/shard_map/branch_grad_spread/ppermute | solution.py:49
  474.4 4.3 collective-permute-done.31.far_ref
  478.7 7.3 %join_halves.7 = bf16[1024,2048]{1,0:T(8,128)(2,1)} custom-call(bf16[512,2048]{1,0:T(8,128)(2,1)} %copy-done.14, bf16[512,2048]{1,0:T(8,128)(2,1)} %collective-permute-done.31.far_ref), custom_call_target="tpu_custom_call" | custom-call | bytes 8388608 | tf_op jit(solution)/shard_map/branch_grad_spread/join_halves/pallas_call | solution.py:68
  486.0 3.7 convolution_convert_fusion.7
  493.4 12.4 %attend_back.1 = bf16[1024,768]{1,0:T(8,128)(2,1)} custom-call(s32[4]{0:T(128)S(1)} %pad_add_fusion.info_ref, bf16[1024,256]{1,0:T(8,128)(2,1)S(1)} %get-tuple-element.36.q_row, bf16[1024,256]{1,0:T(8,128)(2,1)S(1)} %copy-done.1, bf16[1024,256]{1,0:T(8,128)(2,1)S(1)} %copy-done.3, f32[1024,256]{1,0:T(8,128)S(1)} %get-tuple-element.39.log_ref, ...), custom_call_target="tpu_custom_call" | custom-call | flops 2684354560 | bytes 5242880 | tf_op jit(solution)/shard_map/attend_back/pallas_call | solution.py:430
  505.8 3.2 convolution_convert_fusion.5
  509.1 4.0 convolution_convert_fusion.2
  516.8 3.7 convolution_convert_fusion.3
  528.7 23.3 %collective-permute-done.40 = bf16[4,256,768]{2,1,0:T(8,128)(2,1)} collective-permute-done((bf16[4,256,768]{2,1,0:T(8,128)(2,1)}, bf16[4,256,768]{2,1,0:T(8,128)(2,1)}, u32[]{:S(2)}, u32[]{:S(2)}) %collective-permute-start.40) | collective-permute-done | bytes 1572896 | tf_op jit(solution)/shard_map/qkv_trade/ppermute | solution.py:49
  552.0 3.4 pad_maximum_fusion.2
  555.4 7.8 %collective-permute-done.35 = bf16[128,2048]{1,0:T(8,128)(2,1)} collective-permute-done((bf16[128,2048]{1,0:T(8,128)(2,1)}, bf16[128,2048]{1,0:T(8,128)(2,1)}, u32[]{:S(2)}, u32[]{:S(2)}) %collective-permute-start.35) | collective-permute-done | bytes 524320 | tf_op jit(solution)/shard_map/first_grad_collect/ppermute | solution.py:49
  563.2 11.7 %collective-permute-done.36 = bf16[128,2048]{1,0:T(8,128)(2,1)} collective-permute-done((bf16[128,2048]{1,0:T(8,128)(2,1)}, bf16[128,2048]{1,0:T(8,128)(2,1)}, u32[]{:S(2)}, u32[]{:S(2)}) %collective-permute-start.36) | collective-permute-done | bytes 524320 | tf_op jit(solution)/shard_map/first_grad_collect/ppermute | solution.py:49
  575.0 13.4 %reduce-scatter.6.cloned.1.call-done = bf16[512,2048]{1,0:T(8,128)(2,1)} async-done(((bf16[2048,2048]{1,0:T(8,128)(2,1)}), bf16[512,2048]{1,0:T(8,128)(2,1)}) %reduce-scatter.6.cloned.1.call-update) | async-done | bytes 2097168 | tf_op jit(solution)/shard_map/gate_up_back/reduce_scatter | solution.py:165
  591.9 5.6 add_convert_fusion.1
  602.4 3.2 collective-permute-start.45
  609.7 2.8 fusion.17
  616.0 3.4 collective-permute-done.37
  619.4 5.9 collective-permute-done.38
  625.3 11.2 %collective-permute-done.39 = bf16[128,2048]{1,0:T(8,128)(2,1)S(1)} collective-permute-done((bf16[128,2048]{1,0:T(8,128)(2,1)S(1)}, bf16[128,2048]{1,0:T(8,128)(2,1)S(1)}, u32[]{:S(2)}, u32[]{:S(2)}) %collective-permute-start.39) | collective-permute-done | bytes 524320 | tf_op jit(solution)/shard_map/feed_collect/ppermute | solution.py:49
  637.7 19.4 %collective-permute-done.41 = bf16[256,2048]{1,0:T(8,128)(2,1)S(1)} collective-permute-done((bf16[256,2048]{1,0:T(8,128)(2,1)S(1)}, bf16[256,2048]{1,0:T(8,128)(2,1)S(1)}, u32[]{:S(2)}, u32[]{:S(2)}) %collective-permute-start.41) | collective-permute-done | bytes 1048608 | tf_op jit(solution)/shard_map/gate_up_return/ppermute | solution.py:49
  658.8 5.3 copy.74
  664.0 4.1 reduce-scatter.8.cloned.1.call-done
  (277 shorter events, 117.3 us)
Async XLA Ops:
  7.2 88.2 %all-gather.4.cloned.1.call-start = ((), (), s32[]{:S(2)}) async-start(), calls=%async_computation.4 | async-start | bytes 5242880 | tf_op jit(solution)/shard_map/attention_gather/all_gather | solution.py:161
  11.7 1.3 collective-permute-start
  13.1 10.4 %collective-permute-start.1 = (f32[2,128]{1,0:T(2,128)S(1)}, f32[2,128]{1,0:T(2,128)S(1)}, u32[]{:S(2)}, u32[]{:S(2)}) collective-permute-start(f32[2,128]{1,0:T(2,128)S(1)} %pad_maximum_fusion.20), channel_id=1, source_target_pairs={{0,2},{1,3},{2,0},{3,1},{4,6},{5,7},{6,4},{7,5},{8,10},{9,11},{10,... | collective-permute-start | bytes 3080 | tf_op jit(solution)/shard_map/gain_gather/ppermute | solution.py:49
  23.6 8.7 %collective-permute-start.2 = (f32[2,256]{1,0:T(2,128)S(1)}, f32[2,256]{1,0:T(2,128)S(1)}, u32[]{:S(2)}, u32[]{:S(2)}) collective-permute-start(f32[2,256]{1,0:T(2,128)S(1)} %pad_maximum_fusion.19), channel_id=1, source_target_pairs={{0,4},{4,0},{1,5},{5,1},{2,6},{6,2},{3,7},{7,3},{8,12},{12,8},{9,1... | collective-permute-start | bytes 6152 | tf_op jit(solution)/shard_map/gain_gather/ppermute | solution.py:49
  26.9 41.5 %all-to-all-start = ((bf16[2,256,3072]{1,2,0:T(8,128)(2,1)}), bf16[2,256,3072]{1,2,0:T(8,128)(2,1)}, u32[]{:S(2)}, u32[]{:S(2)}) async-start(bf16[2,256,3072]{1,2,0:T(8,128)(2,1)} %pad_maximum_fusion.4), calls=%async_computation | async-start | bytes 6291456 | tf_op jit(solution)/shard_map/feed_weights/all_to_all | solution.py:139
  32.3 250.2 %all-gather.6.cloned.1.call-start = ((), (), s32[]{:S(2)}) async-start(), calls=%async_computation.5 | async-start | bytes 10485760 | tf_op jit(solution)/shard_map/gate_up_gather/all_gather | solution.py:161
  32.3 3.7 collective-permute-start.3
  36.1 4.8 collective-permute-start.4
  74.2 26.8 %copy-start.40 = (s32[1,3]{1,0:T(1,128)S(1)}, s32[1,3]{1,0:T(1,128)}, u32[]{:S(2)}) copy-start(s32[1,3]{1,0:T(1,128)} %param.10) | copy-start | bytes 40
  74.2 16.0 %collective-permute-start.7 = (bf16[128,2048]{1,0:T(8,128)(2,1)}, bf16[128,2048]{1,0:T(8,128)(2,1)S(1)}, u32[]{:S(2)}, u32[]{:S(2)}) collective-permute-start(bf16[128,2048]{1,0:T(8,128)(2,1)} %fusion.13), channel_id=1, source_target_pairs={{0,6},{1,7},{2,4},{3,5},{4,2},{5,3},{6,0},{7,1},{8,14},{9,15},{10,... | collective-permute-start | bytes 1572872 | tf_op jit(solution)/shard_map/first_spread/ppermute | solution.py:49
  74.4 24.0 %collective-permute-start.5 = (bf16[128,2048]{1,0:T(8,128)(2,1)}, bf16[128,2048]{1,0:T(8,128)(2,1)S(1)}, u32[]{:S(2)}, u32[]{:S(2)}) collective-permute-start(bf16[128,2048]{1,0:T(8,128)(2,1)} %fusion.13), channel_id=1, source_target_pairs={{0,2},{1,3},{2,0},{3,1},{4,6},{5,7},{6,4},{7,5},{8,10},{9,11},{10,... | collective-permute-start | bytes 1572872 | tf_op jit(solution)/shard_map/first_spread/ppermute | solution.py:49
  75.9 23.3 %collective-permute-start.6 = (bf16[128,2048]{1,0:T(8,128)(2,1)}, bf16[128,2048]{1,0:T(8,128)(2,1)S(1)}, u32[]{:S(2)}, u32[]{:S(2)}) collective-permute-start(bf16[128,2048]{1,0:T(8,128)(2,1)} %fusion.13), channel_id=1, source_target_pairs={{0,4},{1,5},{2,6},{3,7},{4,0},{5,1},{6,2},{7,3},{8,12},{9,13},{10,... | collective-permute-start | bytes 1572872 | tf_op jit(solution)/shard_map/first_spread/ppermute | solution.py:49
  95.4 268.1 %all-gather.8.cloned.1.call-start = ((), (), s32[]{:S(2)}) async-start(), calls=%async_computation.6 | async-start | bytes 5242880 | tf_op jit(solution)/shard_map/down_gather/all_gather | solution.py:161
  100.9 14.1 %collective-permute-start.8 = (bf16[512,2048]{1,0:T(8,128)(2,1)}, bf16[512,2048]{1,0:T(8,128)(2,1)}, u32[]{:S(2)}, u32[]{:S(2)}) collective-permute-start(bf16[512,2048]{1,0:T(8,128)(2,1)} %constant_dynamic-update-slice_fusion.near_ref), channel_id=1, source_target_pairs={{0,1},{1,0},{2,3},{3,2},{4,5},{5,4},{6,7},{7,6},{8,9},{9,8},{10,11... | collective-permute-start | bytes 6291464 | tf_op jit(solution)/shard_map/first_spread/ppermute | solution.py:49
  105.9 56.8 %collective-permute-start.9 = (bf16[1024,768]{0,1:T(8,128)(2,1)}, bf16[1024,768]{0,1:T(8,128)(2,1)}, u32[]{:S(2)}, u32[]{:S(2)}) collective-permute-start(bf16[1024,768]{0,1:T(8,128)(2,1)} %slice.314), channel_id=1, source_target_pairs={{0,4},{4,0},{1,5},{5,1},{2,6},{6,2},{3,7},{7,3},{8,12},{12,8},{9,1... | collective-permute-start | bytes 4718600 | tf_op jit(solution)/shard_map/qkv_join/ppermute | solution.py:49
  109.9 44.3 %collective-permute-start.10 = (bf16[1024,256]{0,1:T(8,128)(2,1)}, bf16[1024,256]{0,1:T(8,128)(2,1)}, u32[]{:S(2)}, u32[]{:S(2)}) collective-permute-start(bf16[1024,256]{0,1:T(8,128)(2,1)} %slice.316), channel_id=1, source_target_pairs={{0,4},{4,0},{1,5},{5,1},{2,6},{6,2},{3,7},{7,3},{8,12},{12,8},{9,1... | collective-permute-start | bytes 1572872 | tf_op jit(solution)/shard_map/out_join/ppermute | solution.py:49
  189.8 32.8 %copy-start.8 = (bf16[1,128,2048]{2,1,0:T(8,128)(2,1)S(1)}, bf16[1,128,2048]{2,1,0:T(8,128)(2,1)}, u32[]{:S(2)}) copy-start(bf16[1,128,2048]{2,1,0:T(8,128)(2,1)} %param.9) | copy-start | bytes 1572868
  189.8 4.2 collective-permute-start.11
  194.9 15.6 %collective-permute-start.12 = (bf16[128,2048]{1,0:T(8,128)(2,1)S(1)}, bf16[128,2048]{1,0:T(8,128)(2,1)S(1)}, u32[]{:S(2)}, u32[]{:S(2)}) collective-permute-start(bf16[128,2048]{1,0:T(8,128)(2,1)S(1)} %get-tuple-element.112), channel_id=1, source_target_pairs={{0,2},{1,3},{2,0},{3,1},{4,6},{5,7},{6,4},{7,5},{8,10},{9,11},{10,... | collective-permute-start | bytes 1572872 | tf_op jit(solution)/shard_map/branch_collect/ppermute | solution.py:49
  196.1 15.6 %collective-permute-start.13 = (bf16[128,2048]{1,0:T(8,128)(2,1)S(1)}, bf16[128,2048]{1,0:T(8,128)(2,1)S(1)}, u32[]{:S(2)}, u32[]{:S(2)}) collective-permute-start(bf16[128,2048]{1,0:T(8,128)(2,1)S(1)} %get-tuple-element.114), channel_id=1, source_target_pairs={{0,4},{1,5},{2,6},{3,7},{4,0},{5,1},{6,2},{7,3},{8,12},{9,13},{10,... | collective-permute-start | bytes 1572872 | tf_op jit(solution)/shard_map/branch_collect/ppermute | solution.py:49
  196.7 25.8 %collective-permute-start.14 = (bf16[128,2048]{1,0:T(8,128)(2,1)S(1)}, bf16[128,2048]{1,0:T(8,128)(2,1)S(1)}, u32[]{:S(2)}, u32[]{:S(2)}) collective-permute-start(bf16[128,2048]{1,0:T(8,128)(2,1)S(1)} %get-tuple-element.113), channel_id=1, source_target_pairs={{0,6},{1,7},{2,4},{3,5},{4,2},{5,3},{6,0},{7,1},{8,14},{9,15},{10,... | collective-permute-start | bytes 1572872 | tf_op jit(solution)/shard_map/branch_collect/ppermute | solution.py:49
  198.5 34.5 %collective-permute-start.19 = (bf16[128,2048]{1,0:T(8,128)(2,1)S(1)}, bf16[128,2048]{1,0:T(8,128)(2,1)S(1)}, u32[]{:S(2)}, u32[]{:S(2)}) collective-permute-start(bf16[128,2048]{1,0:T(8,128)(2,1)S(1)} %bitcast.154), channel_id=1, source_target_pairs={{0,2},{1,3},{2,0},{3,1},{4,6},{5,7},{6,4},{7,5},{8,10},{9,11},{10,... | collective-permute-start | bytes 1572872 | tf_op jit(solution)/shard_map/cotangent_spread/ppermute | solution.py:49
  199.5 34.5 %collective-permute-start.20 = (bf16[128,2048]{1,0:T(8,128)(2,1)S(1)}, bf16[128,2048]{1,0:T(8,128)(2,1)S(1)}, u32[]{:S(2)}, u32[]{:S(2)}) collective-permute-start(bf16[128,2048]{1,0:T(8,128)(2,1)S(1)} %bitcast.155), channel_id=1, source_target_pairs={{0,4},{1,5},{2,6},{3,7},{4,0},{5,1},{6,2},{7,3},{8,12},{9,13},{10,... | collective-permute-start | bytes 1572872 | tf_op jit(solution)/shard_map/cotangent_spread/ppermute | solution.py:49
  210.5 34.5 %collective-permute-start.21 = (bf16[128,2048]{1,0:T(8,128)(2,1)S(1)}, bf16[128,2048]{1,0:T(8,128)(2,1)S(1)}, u32[]{:S(2)}, u32[]{:S(2)}) collective-permute-start(bf16[128,2048]{1,0:T(8,128)(2,1)S(1)} %bitcast.156), channel_id=1, source_target_pairs={{0,6},{1,7},{2,4},{3,5},{4,2},{5,3},{6,0},{7,1},{8,14},{9,15},{10,... | collective-permute-start | bytes 1572872 | tf_op jit(solution)/shard_map/cotangent_spread/ppermute | solution.py:49
  224.2 29.7 %collective-permute-start.15 = (bf16[128,2048]{1,0:T(8,128)(2,1)S(1)}, bf16[128,2048]{1,0:T(8,128)(2,1)S(1)}, u32[]{:S(2)}, u32[]{:S(2)}) collective-permute-start(bf16[128,2048]{1,0:T(8,128)(2,1)S(1)} %multiply_convert_fusion.3), channel_id=1, source_target_pairs={{0,2},{1,3},{2,0},{3,1},{4,6},{5,7},{6,4},{7,5},{8,10},{9,11},{10,... | collective-permute-start | bytes 1572872 | tf_op jit(solution)/shard_map/second_spread/ppermute | solution.py:49
  225.4 30.5 %collective-permute-start.16 = (bf16[128,2048]{1,0:T(8,128)(2,1)S(1)}, bf16[128,2048]{1,0:T(8,128)(2,1)S(1)}, u32[]{:S(2)}, u32[]{:S(2)}) collective-permute-start(bf16[128,2048]{1,0:T(8,128)(2,1)S(1)} %multiply_convert_fusion.3), channel_id=1, source_target_pairs={{0,4},{1,5},{2,6},{3,7},{4,0},{5,1},{6,2},{7,3},{8,12},{9,13},{10,... | collective-permute-start | bytes 1572872 | tf_op jit(solution)/shard_map/second_spread/ppermute | solution.py:49
  232.9 33.5 %collective-permute-start.17 = (bf16[128,2048]{1,0:T(8,128)(2,1)S(1)}, bf16[128,2048]{1,0:T(8,128)(2,1)S(1)}, u32[]{:S(2)}, u32[]{:S(2)}) collective-permute-start(bf16[128,2048]{1,0:T(8,128)(2,1)S(1)} %multiply_convert_fusion.3), channel_id=1, source_target_pairs={{0,6},{1,7},{2,4},{3,5},{4,2},{5,3},{6,0},{7,1},{8,14},{9,15},{10,... | collective-permute-start | bytes 1572872 | tf_op jit(solution)/shard_map/second_spread/ppermute | solution.py:49
  246.6 21.4 %collective-permute-start.22 = (bf16[512,2048]{1,0:T(8,128)(2,1)S(1)}, bf16[512,2048]{1,0:T(8,128)(2,1)}, u32[]{:S(2)}, u32[]{:S(2)}) collective-permute-start(bf16[512,2048]{1,0:T(8,128)(2,1)S(1)} %pad_maximum_fusion.7.near_ref), channel_id=1, source_target_pairs={{0,1},{1,0},{2,3},{3,2},{4,5},{5,4},{6,7},{7,6},{8,9},{9,8},{10,11... | collective-permute-start | bytes 6291464 | tf_op jit(solution)/shard_map/cotangent_spread/ppermute | solution.py:49
  268.0 7.1 %collective-permute-start.18 = (bf16[512,2048]{1,0:T(8,128)(2,1)}, bf16[512,2048]{1,0:T(8,128)(2,1)}, u32[]{:S(2)}, u32[]{:S(2)}) collective-permute-start(bf16[512,2048]{1,0:T(8,128)(2,1)} %pad_maximum_fusion.6.near_ref), channel_id=1, source_target_pairs={{0,1},{1,0},{2,3},{3,2},{4,5},{5,4},{6,7},{7,6},{8,9},{9,8},{10,11... | collective-permute-start | bytes 6291464 | tf_op jit(solution)/shard_map/second_spread/ppermute | solution.py:49
  282.5 158.5 %reduce-scatter.4.cloned.1.call-start = ((), (), s32[]{:S(2)}) async-start(), calls=%async_computation.7 | async-start | bytes 5242880 | tf_op jit(solution)/shard_map/down_back/reduce_scatter | solution.py:165
  363.5 224.8 %reduce-scatter.6.cloned.1.call-start = ((), (), s32[]{:S(2)}) async-start(), calls=%async_computation.8 | async-start | bytes 10485760 | tf_op jit(solution)/shard_map/gate_up_back/reduce_scatter | solution.py:165
  384.8 4.2 collective-permute-start.23
  400.1 16.2 %collective-permute-start.24 = (bf16[128,2048]{1,0:T(8,128)(2,1)}, bf16[128,2048]{1,0:T(8,128)(2,1)}, u32[]{:S(2)}, u32[]{:S(2)}) collective-permute-start(bf16[128,2048]{1,0:T(8,128)(2,1)} %get-tuple-element.111), channel_id=1, source_target_pairs={{0,2},{1,3},{2,0},{3,1},{4,6},{5,7},{6,4},{7,5},{8,10},{9,11},{10,... | collective-permute-start | bytes 1572872 | tf_op jit(solution)/shard_map/second_grad_collect/ppermute | solution.py:49
  401.6 15.1 %collective-permute-start.25 = (bf16[128,2048]{1,0:T(8,128)(2,1)}, bf16[128,2048]{1,0:T(8,128)(2,1)}, u32[]{:S(2)}, u32[]{:S(2)}) collective-permute-start(bf16[128,2048]{1,0:T(8,128)(2,1)} %get-tuple-element.110), channel_id=1, source_target_pairs={{0,4},{1,5},{2,6},{3,7},{4,0},{5,1},{6,2},{7,3},{8,12},{9,13},{10,... | collective-permute-start | bytes 1572872 | tf_op jit(solution)/shard_map/second_grad_collect/ppermute | solution.py:49
  403.1 23.7 %collective-permute-start.26 = (bf16[128,2048]{1,0:T(8,128)(2,1)}, bf16[128,2048]{1,0:T(8,128)(2,1)}, u32[]{:S(2)}, u32[]{:S(2)}) collective-permute-start(bf16[128,2048]{1,0:T(8,128)(2,1)} %get-tuple-element.109), channel_id=1, source_target_pairs={{0,6},{1,7},{2,4},{3,5},{4,2},{5,3},{6,0},{7,1},{8,14},{9,15},{10,... | collective-permute-start | bytes 1572872 | tf_op jit(solution)/shard_map/second_grad_collect/ppermute | solution.py:49
  441.0 227.1 %reduce-scatter.8.cloned.1.call-start = ((), (), s32[]{:S(2)}) async-start(), calls=%async_computation.9 | async-start | bytes 5242880 | tf_op jit(solution)/shard_map/attention_back/reduce_scatter | solution.py:165
  446.7 13.9 %collective-permute-start.28 = (bf16[128,2048]{1,0:T(8,128)(2,1)S(1)}, bf16[128,2048]{1,0:T(8,128)(2,1)S(1)}, u32[]{:S(2)}, u32[]{:S(2)}) collective-permute-start(bf16[128,2048]{1,0:T(8,128)(2,1)S(1)} %get-tuple-element.81), channel_id=1, source_target_pairs={{0,2},{1,3},{2,0},{3,1},{4,6},{5,7},{6,4},{7,5},{8,10},{9,11},{10,... | collective-permute-start | bytes 1572872 | tf_op jit(solution)/shard_map/branch_grad_spread/ppermute | solution.py:49
  448.2 14.8 %collective-permute-start.29 = (bf16[128,2048]{1,0:T(8,128)(2,1)S(1)}, bf16[128,2048]{1,0:T(8,128)(2,1)S(1)}, u32[]{:S(2)}, u32[]{:S(2)}) collective-permute-start(bf16[128,2048]{1,0:T(8,128)(2,1)S(1)} %get-tuple-element.81), channel_id=1, source_target_pairs={{0,4},{1,5},{2,6},{3,7},{4,0},{5,1},{6,2},{7,3},{8,12},{9,13},{10,... | collective-permute-start | bytes 1572872 | tf_op jit(solution)/shard_map/branch_grad_spread/ppermute | solution.py:49
  449.6 23.2 %collective-permute-start.30 = (bf16[128,2048]{1,0:T(8,128)(2,1)S(1)}, bf16[128,2048]{1,0:T(8,128)(2,1)S(1)}, u32[]{:S(2)}, u32[]{:S(2)}) collective-permute-start(bf16[128,2048]{1,0:T(8,128)(2,1)S(1)} %get-tuple-element.81), channel_id=1, source_target_pairs={{0,6},{1,7},{2,4},{3,5},{4,2},{5,3},{6,0},{7,1},{8,14},{9,15},{10,... | collective-permute-start | bytes 1572872 | tf_op jit(solution)/shard_map/branch_grad_spread/ppermute | solution.py:49
  474.4 4.3 collective-permute-start.31
  490.6 15.2 %collective-permute-start.32 = (bf16[4,256,256]{2,1,0:T(8,128)(2,1)S(1)}, bf16[4,256,256]{2,1,0:T(8,128)(2,1)S(1)}, u32[]{:S(2)}, u32[]{:S(2)}) collective-permute-start(bf16[4,256,256]{2,1,0:T(8,128)(2,1)S(1)} %get-tuple-element.125), channel_id=1, source_target_pairs={{0,4},{4,0},{1,5},{5,1},{2,6},{6,2},{3,7},{7,3},{8,12},{12,8},{9,1... | collective-permute-start | bytes 1572872 | tf_op jit(solution)/shard_map/out_trade/ppermute | solution.py:49
  509.0 11.9 %collective-permute-start.33 = (bf16[512,2048]{1,0:T(8,128)(2,1)S(1)}, bf16[512,2048]{1,0:T(8,128)(2,1)S(1)}, u32[]{:S(2)}, u32[]{:S(2)}) collective-permute-start(bf16[512,2048]{1,0:T(8,128)(2,1)S(1)} %convolution_convert_fusion.5), channel_id=1, source_target_pairs={{0,1},{1,0},{2,3},{3,2},{4,5},{5,4},{6,7},{7,6},{8,9},{9,8},{10,11... | collective-permute-start | bytes 6291464 | tf_op jit(solution)/shard_map/first_grad_collect/ppermute | solution.py:49
  514.5 37.5 %collective-permute-start.40 = (bf16[4,256,768]{2,1,0:T(8,128)(2,1)}, bf16[4,256,768]{2,1,0:T(8,128)(2,1)}, u32[]{:S(2)}, u32[]{:S(2)}) collective-permute-start(bf16[4,256,768]{2,1,0:T(8,128)(2,1)} %get-tuple-element.94), channel_id=1, source_target_pairs={{0,4},{4,0},{1,5},{5,1},{2,6},{6,2},{3,7},{7,3},{8,12},{12,8},{9,1... | collective-permute-start | bytes 4718600 | tf_op jit(solution)/shard_map/qkv_trade/ppermute | solution.py:49
  520.5 71.3 %collective-permute-start.27 = (bf16[512,2048]{1,0:T(8,128)(2,1)}, bf16[512,2048]{1,0:T(8,128)(2,1)}, u32[]{:S(2)}, u32[]{:S(2)}) collective-permute-start(bf16[512,2048]{1,0:T(8,128)(2,1)} %convolution_convert_fusion.3), channel_id=1, source_target_pairs={{0,1},{1,0},{2,3},{3,2},{4,5},{5,4},{6,7},{7,6},{8,9},{9,8},{10,11... | collective-permute-start | bytes 6291464 | tf_op jit(solution)/shard_map/feed_collect/ppermute | solution.py:49
  524.1 27.9 %copy-start.29 = (bf16[4,1,256,256]{3,2,0,1:T(8,128)(2,1)S(1)}, bf16[4,1,256,256]{3,2,0,1:T(8,128)(2,1)}, u32[]{:S(2)}) copy-start(bf16[4,1,256,256]{3,2,0,1:T(8,128)(2,1)} %get-tuple-element.126) | copy-start | bytes 1572868
  524.1 27.9 %copy-start.34 = (bf16[4,256,256]{2,1,0:T(8,128)(2,1)S(1)}, bf16[4,256,256]{2,1,0:T(8,128)(2,1)}, u32[]{:S(2)}) copy-start(bf16[4,256,256]{2,1,0:T(8,128)(2,1)} %copy-done.33) | copy-start | bytes 1572868
  525.2 30.2 %collective-permute-start.34 = (bf16[128,2048]{1,0:T(8,128)(2,1)}, bf16[128,2048]{1,0:T(8,128)(2,1)S(1)}, u32[]{:S(2)}, u32[]{:S(2)}) collective-permute-start(bf16[128,2048]{1,0:T(8,128)(2,1)} %get-tuple-element.108), channel_id=1, source_target_pairs={{0,2},{1,3},{2,0},{3,1},{4,6},{5,7},{6,4},{7,5},{8,10},{9,11},{10,... | collective-permute-start | bytes 1572872 | tf_op jit(solution)/shard_map/first_grad_collect/ppermute | solution.py:49
  526.7 36.5 %collective-permute-start.35 = (bf16[128,2048]{1,0:T(8,128)(2,1)}, bf16[128,2048]{1,0:T(8,128)(2,1)}, u32[]{:S(2)}, u32[]{:S(2)}) collective-permute-start(bf16[128,2048]{1,0:T(8,128)(2,1)} %get-tuple-element.107), channel_id=1, source_target_pairs={{0,4},{1,5},{2,6},{3,7},{4,0},{5,1},{6,2},{7,3},{8,12},{9,13},{10,... | collective-permute-start | bytes 1572872 | tf_op jit(solution)/shard_map/first_grad_collect/ppermute | solution.py:49
  527.4 47.6 %collective-permute-start.36 = (bf16[128,2048]{1,0:T(8,128)(2,1)}, bf16[128,2048]{1,0:T(8,128)(2,1)}, u32[]{:S(2)}, u32[]{:S(2)}) collective-permute-start(bf16[128,2048]{1,0:T(8,128)(2,1)} %get-tuple-element.106), channel_id=1, source_target_pairs={{0,6},{1,7},{2,4},{3,5},{4,2},{5,3},{6,0},{7,1},{8,14},{9,15},{10,... | collective-permute-start | bytes 1572872 | tf_op jit(solution)/shard_map/first_grad_collect/ppermute | solution.py:49
  555.4 33.0 %copy-start.9 = (bf16[1,128,2048]{2,1,0:T(8,128)(2,1)S(1)}, bf16[1,128,2048]{2,1,0:T(8,128)(2,1)}, u32[]{:S(2)}) copy-start(bf16[1,128,2048]{2,1,0:T(8,128)(2,1)} %param.9) | copy-start | bytes 1572868
  555.4 33.0 %copy-start.26 = (bf16[512,2048]{1,0:T(8,128)(2,1)S(1)}, bf16[512,2048]{1,0:T(8,128)(2,1)}, u32[]{:S(2)}) copy-start(bf16[512,2048]{1,0:T(8,128)(2,1)} %copy-done.25) | copy-start | bytes 6291460
  555.4 33.0 %copy-start.37 = (f32[1,2048]{1,0:T(1,128)S(1)}, f32[1,2048]{1,0:T(1,128)}, u32[]{:S(2)}) copy-start(f32[1,2048]{1,0:T(1,128)} %copy-done.36) | copy-start | bytes 24580
  555.4 33.0 %copy-start.39 = (f32[128]{0:T(128)S(1)}, f32[128]{0:T(128)}, u32[]{:S(2)}) copy-start(f32[128]{0:T(128)} %copy-done.38) | copy-start | bytes 1540
  590.4 7.1 %collective-permute-start.42 = (f32[2,1024]{1,0:T(2,128)S(1)}, f32[2,1024]{1,0:T(2,128)S(1)}, u32[]{:S(2)}, u32[]{:S(2)}) collective-permute-start(f32[2,1024]{1,0:T(2,128)S(1)} %broadcast_select_fusion.12), channel_id=1, source_target_pairs={{0,4},{4,0},{1,5},{5,1},{2,6},{6,2},{3,7},{7,3},{8,12},{12,8},{9,1... | collective-permute-start | bytes 24584 | tf_op jit(solution)/shard_map/gain_scatter/ppermute | solution.py:49
  597.5 3.7 collective-permute-start.43
  599.1 15.1 %collective-permute-start.47 = (bf16[256,1024]{1,0:T(8,128)(2,1)S(1)}, bf16[256,1024]{1,0:T(8,128)(2,1)S(1)}, u32[]{:S(2)}, u32[]{:S(2)}) collective-permute-start(bf16[256,1024]{1,0:T(8,128)(2,1)S(1)} %broadcast_select_fusion.7), channel_id=1, source_target_pairs={{0,4},{4,0},{1,5},{5,1},{2,6},{6,2},{3,7},{7,3},{8,12},{12,8},{9,1... | collective-permute-start | bytes 1572872 | tf_op jit(solution)/shard_map/down_return/ppermute | solution.py:49
  601.2 1.2 collective-permute-start.44
  602.4 7.1 %collective-permute-start.45 = (f32[2,128]{1,0:T(2,128)S(1)}, f32[2,128]{1,0:T(2,128)S(1)}, u32[]{:S(2)}, u32[]{:S(2)}) collective-permute-start(f32[2,128]{1,0:T(2,128)S(1)} %broadcast_select_fusion.21), channel_id=1, source_target_pairs={{0,16},{8,24},{16,0},{24,8},{1,17},{9,25},{17,1},{25,9},{2,18},{10... | collective-permute-start | bytes 3080 | tf_op jit(solution)/shard_map/gain_scatter/ppermute | solution.py:49
  605.7 13.7 %collective-permute-start.37 = (bf16[128,2048]{1,0:T(8,128)(2,1)S(1)}, bf16[128,2048]{1,0:T(8,128)(2,1)S(1)}, u32[]{:S(2)}, u32[]{:S(2)}) collective-permute-start(bf16[128,2048]{1,0:T(8,128)(2,1)S(1)} %get-tuple-element.103), channel_id=1, source_target_pairs={{0,2},{1,3},{2,0},{3,1},{4,6},{5,7},{6,4},{7,5},{8,10},{9,11},{10,... | collective-permute-start | bytes 1572872 | tf_op jit(solution)/shard_map/feed_collect/ppermute | solution.py:49
  607.1 18.2 %collective-permute-start.38 = (bf16[128,2048]{1,0:T(8,128)(2,1)S(1)}, bf16[128,2048]{1,0:T(8,128)(2,1)S(1)}, u32[]{:S(2)}, u32[]{:S(2)}) collective-permute-start(bf16[128,2048]{1,0:T(8,128)(2,1)S(1)} %get-tuple-element.105), channel_id=1, source_target_pairs={{0,4},{1,5},{2,6},{3,7},{4,0},{5,1},{6,2},{7,3},{8,12},{9,13},{10,... | collective-permute-start | bytes 1572872 | tf_op jit(solution)/shard_map/feed_collect/ppermute | solution.py:49
  607.7 28.8 %collective-permute-start.39 = (bf16[128,2048]{1,0:T(8,128)(2,1)S(1)}, bf16[128,2048]{1,0:T(8,128)(2,1)S(1)}, u32[]{:S(2)}, u32[]{:S(2)}) collective-permute-start(bf16[128,2048]{1,0:T(8,128)(2,1)S(1)} %get-tuple-element.104), channel_id=1, source_target_pairs={{0,6},{1,7},{2,4},{3,5},{4,2},{5,3},{6,0},{7,1},{8,14},{9,15},{10,... | collective-permute-start | bytes 1572872 | tf_op jit(solution)/shard_map/feed_collect/ppermute | solution.py:49
  609.6 3.6 collective-permute-start.46
  614.0 22.5 %copy-start.6 = (f32[128,2048]{1,0:T(8,128)S(1)}, f32[128,2048]{1,0:T(8,128)}, u32[]{:S(2)}) copy-start(f32[128,2048]{1,0:T(8,128)} %copy-done.4) | copy-start | bytes 3145732
  614.0 43.1 %collective-permute-start.41 = (bf16[256,2048]{1,0:T(8,128)(2,1)S(1)}, bf16[256,2048]{1,0:T(8,128)(2,1)S(1)}, u32[]{:S(2)}, u32[]{:S(2)}) collective-permute-start(bf16[256,2048]{1,0:T(8,128)(2,1)S(1)} %broadcast_select_fusion.5), channel_id=1, source_target_pairs={{0,4},{4,0},{1,5},{5,1},{2,6},{6,2},{3,7},{7,3},{8,12},{12,8},{9,1... | collective-permute-start | bytes 3145736 | tf_op jit(solution)/shard_map/gate_up_return/ppermute | solution.py:49
  (40 other events, 218.0 us)
Sparse Core Ops, SparseCore 0:
  11.8 83.5 all-gather.3
  97.0 147.8 all-gather.5
  282.6 80.9 all-gather.7
  365.7 75.2 reduce-scatter.3
  443.3 144.9 reduce-scatter.5
  590.6 77.5 reduce-scatter.7
